TPU v7x, 512 devices: a whole 4x8x8 slice. The times are simulated.
512 devices in a mesh: dp: 64 (over z_lo, y, core), tensor: 8 (over x, z_hi).
Axes of the slice: x: 4, y: 8, z: 8 (z_hi: 2, z_lo: 4; z = z_hi * 4 + z_lo), core: 2. Of those that a mesh axis runs over, the one named last changes fastest.
Arguments:
- item_cache: bfloat16 [2048, 3584], P('dp', 'tensor'), may hold values from -0.5 to 0.5
- user_cache: bfloat16 [2048, 3584], P('dp', 'tensor'), may hold values from -0.5 to 0.5
- positive: int32 [2048], P('dp'), may hold values from 0 to 2047, each once
- attn_heads: bfloat16 [16384, 2048], P('dp', 'tensor'), may hold values from -6 to 6
- residual: bfloat16 [16384, 3584], P('dp'), may hold values from -2.390625 to 2.390625
- out_proj: bfloat16 [2048, 3584], P('tensor'), may hold values from -0.125 to 0.125
- norm_gain: float32 [3584], replicated, may hold values from 0.1 to 1.9
Outputs:
- loss_mean: float32 [], replicated
- item_grad: float32 [2048, 3584], P('dp', 'tensor')
- user_grad: float32 [2048, 3584], P('dp', 'tensor')
- head_grad: bfloat16 [16384, 2048], P('dp', 'tensor')
- weight_grad: float32 [2048, 3584], P('tensor', 'dp')
All inputs are finite; a program needn't handle non-finite values.
Results may differ from a plain program's by a relative error of at most 0.0051.
Values may be sent and summed in bfloat16 or wider, within the bound.
No kernel may reach another device: no remote copies, remote signals or barrier semaphores. Data moves between devices by JAX's collectives and lax.ppermute only.
A program may use at most 64 MiB of HBM per device.

v0:
```python
import jax
import jax.numpy as jnp
from jax import lax
from jax.sharding import PartitionSpec as P

GROUP = 8


logit_scale = 50.0
norm_eps = 1e-06


def per_device(item_cache, user_cache, positive, attn_heads, residual, out_proj, norm_gain):
    pair_rows = item_cache.shape[0]
    items_all, users_all = (
        lax.all_gather(item_cache, "dp", axis=0, tiled=True),
        lax.all_gather(user_cache, "dp", axis=0, tiled=True),
    )
    total_pairs = users_all.shape[0]
    partial_rows = (
        jnp.einsum("rd,cd->rc", item_cache, users_all, preferred_element_type=jnp.float32)
        * logit_scale
    )
    partial_cols = (
        jnp.einsum("ud,id->ui", user_cache, items_all, preferred_element_type=jnp.float32)
        * logit_scale
    )
    scores, col_scores = lax.psum((partial_rows, partial_cols), "tensor")
    maxima = jnp.max(scores, axis=1, keepdims=True)
    log_total = maxima[:, 0] + jnp.log(jnp.sum(jnp.exp(scores - maxima), axis=1))
    columns = lax.broadcasted_iota(jnp.int32, (1, total_pairs), 1)
    target = positive[:, None] == columns
    picked = jnp.sum(jnp.where(target, scores, jnp.float32(0.0)), axis=1)
    row_loss = log_total - picked
    grad_logits = (jnp.exp(scores - log_total[:, None]) - target.astype(jnp.float32)).astype(
        jnp.bfloat16
    )
    item_grad = jnp.dot(grad_logits, users_all, preferred_element_type=jnp.float32) * logit_scale
    totals_all, losses_all, targets_all = (
        lax.all_gather(log_total, "dp", axis=0, tiled=True),
        lax.all_gather(row_loss, "dp", axis=0, tiled=True),
        lax.all_gather(positive.astype(jnp.float32), "dp", axis=0, tiled=True),
    )
    own_users = lax.axis_index("dp") * pair_rows + lax.broadcasted_iota(
        jnp.int32, (pair_rows, 1), 0
    )
    col_target = targets_all.astype(jnp.int32)[None, :] == own_users
    col_grad = (jnp.exp(col_scores - totals_all[None, :]) - col_target.astype(jnp.float32)).astype(
        jnp.bfloat16
    )
    user_grad = jnp.dot(col_grad, items_all, preferred_element_type=jnp.float32) * logit_scale
    loss_mean = jnp.sum(losses_all) / total_pairs
    partial_hidden = jnp.dot(attn_heads, out_proj, preferred_element_type=jnp.float32)
    mixed = lax.psum(partial_hidden, "tensor")
    hidden = residual.astype(jnp.float32) + mixed
    inverse = lax.rsqrt(jnp.mean(hidden * hidden, axis=1, keepdims=True) + norm_eps)
    group_rows = lax.all_gather(item_grad[:GROUP], "tensor", axis=1, tiled=True)
    token_count = attn_heads.shape[0]
    seq_len = token_count // GROUP
    width = group_rows.shape[1]
    pooled = (
        jnp.broadcast_to(group_rows[:, None, :], (GROUP, seq_len, width)).reshape(
            token_count, width
        )
        / seq_len
    )
    upstream = norm_gain[None, :] * pooled
    inner = jnp.sum(upstream * hidden, axis=1, keepdims=True) / width
    stream_grad = (inverse * upstream - hidden * inverse * inverse * inverse * inner).astype(
        jnp.bfloat16
    )
    head_grad = jnp.einsum(
        "td,hd->th", stream_grad, out_proj, preferred_element_type=jnp.float32
    ).astype(jnp.bfloat16)
    weight_rows = lax.psum_scatter(
        jnp.einsum("tc,th->ch", stream_grad, attn_heads, preferred_element_type=jnp.float32),
        "dp",
        scatter_dimension=0,
        tiled=True,
    )
    weight_grad = weight_rows.T
    return (loss_mean, item_grad, user_grad, head_grad, weight_grad)


def solution(mesh):
    placed = (
        P("dp", "tensor"),
        P("dp", "tensor"),
        P("dp"),
        P("dp", "tensor"),
        P("dp", None),
        P("tensor", None),
        P(),
    )
    return jax.shard_map(
        per_device,
        mesh=mesh,
        in_specs=placed,
        out_specs=(P(), P("dp", "tensor"), P("dp", "tensor"), P("dp", "tensor"), P("tensor", "dp")),
        check_vma=False,
    )
```

profile of v0, /device:TPU:1, one launch (start us, length us, event | category | flops | bytes accessed | tf_op | source)
XLA Modules:
  0.0 951.3 jit_solution(17639845526701563352)
XLA Ops:
  7.2 0.0 all-gather.6.cloned.1.call-start
  7.2 0.7 all-gather.6.cloned.1.call-update
  7.9 0.0 all-gather.4.cloned.1.call-start
  8.0 0.7 all-gather.4.cloned.1.call-update
  8.7 0.0 all-reduce.7.cloned.1.call-start
  8.7 3.4 fusion.11
  12.1 122.5 %all-gather.6.cloned.1.call-done = bf16[2048,448]{1,0:T(8,128)(2,1)} async-done(((bf16[32,448]{1,0:T(8,128)(2,1)}), bf16[2048,448]{1,0:T(8,128)(2,1)}) %all-gather.6.cloned.1.call-update) | async-done | bytes 1835024 | tf_op jit(solution)/shard_map/all_gather | solution.py:16
  134.6 3.0 convolution_multiply_fusion
  137.6 115.2 %all-gather.4.cloned.1.call-done = bf16[2048,448]{1,0:T(8,128)(2,1)} async-done(((bf16[32,448]{1,0:T(8,128)(2,1)}), bf16[2048,448]{1,0:T(8,128)(2,1)}) %all-gather.4.cloned.1.call-update) | async-done | bytes 1835024 | tf_op jit(solution)/shard_map/all_gather | solution.py:17
  252.8 3.0 convolution_multiply_fusion.1
  255.8 0.0 reduce-scatter.2.cloned.1.call-start
  255.9 1.3 dynamic-slice
  257.8 352.3 %all-reduce.7.cloned.1.call-done = (f32[32,2048]{1,0:T(8,128)}, f32[32,2048]{1,0:T(8,128)}, f32[256,3584]{1,0:T(8,128)}) async-done(((f32[32,2048]{1,0:T(8,128)}, f32[32,2048]{1,0:T(8,128)}, f32[256,3584]{1,0:T(8,128)}), (f32[32,2048]{1,0:T(8,128)}, f32[32,2048]{1,0:T(8,128)}, f32[256,3584]{1,0:T(8,128)})) %all-reduce.7.cloned.1.call-update) | async-done | bytes 4194320 | tf_op jit(solution)/shard_map/psum | solution.py:28
  610.1 1.1 reduce_max.9
  611.2 1.2 select_reduce_fusion
  612.4 0.1 fusion.10
  612.5 2.2 convolution_multiply_fusion.3
  614.8 37.6 %all-gather = f32[8,448,8]{1,2,0:T(8,128)S(1)} all-gather(f32[1,448,8]{1,2,0:T(8,128)S(1)} %slice_bitcast_fusion), channel_id=1, replica_groups=mesh['dp'=64,'tensor'=8] {'tensor'}, dimensions={0}, use_global_device_ids=true | all-gather | bytes 129024 | tf_op jit(solution)/shard_map/all_gather | solution.py:57
  652.4 0.1 copy.13
  652.5 0.1 reshape.53
  652.6 3.6 multiply_reduce_fusion
  656.3 0.6 copy-done.4
  656.8 1.4 fusion.3
  658.3 1.2 copy-done.2
  659.5 2.5 fusion.12
  662.1 0.1 convert_dynamic-update-slice_fusion
  662.2 0.1 subtract_dynamic-update-slice_fusion
  662.3 266.1 %all-reduce.3 = (f32[2048]{0:T(1024)S(1)}, f32[2048]{0:T(1024)S(1)}, f32[2048]{0:T(1024)S(1)}) all-reduce(f32[2048]{0:T(1024)S(1)} %subtract_dynamic-update-slice_fusion, f32[2048]{0:T(1024)S(1)} %convert_dynamic-update-slice_fusion, f32[2048]{0:T(1024)S(1)} %get-tuple-element.15), channel_id=1, replica_groups=mesh['dp'=64,'tensor'=8] {'dp'}, use_global_device_ids=true, to_apply=%add | all-reduce | flops 6144 | bytes 49152
  928.4 0.6 reduce_sum.47
  929.6 2.9 convolution_multiply_fusion.2
  932.5 1.3 convolution_convert_fusion
  933.8 9.8 %reduce-scatter.2.cloned.1.call-done = f32[56,256]{1,0:T(8,128)} async-done(((f32[3584,256]{1,0:T(8,128)}), f32[56,256]{1,0:T(8,128)}) %reduce-scatter.2.cloned.1.call-update) | async-done | bytes 57360 | tf_op jit(solution)/shard_map/reduce_scatter | solution.py:75
  (32 shorter events, 0.1 us)
Async XLA Ops:
  7.2 1.6 copy-start
  7.2 127.4 %all-gather.6.cloned.1.call-start = ((), (), s32[]{:S(2)}) async-start(), calls=%async_computation.2 | async-start | bytes 2129920 | tf_op jit(solution)/shard_map/all_gather | solution.py:16
  7.9 244.9 %all-gather.4.cloned.1.call-start = ((), (), s32[]{:S(2)}) async-start(), calls=%async_computation.1 | async-start | bytes 2129920 | tf_op jit(solution)/shard_map/all_gather | solution.py:17
  8.7 126.0 %copy-start.7 = (bf16[32,448]{1,0:T(8,128)(2,1)S(1)}, bf16[32,448]{1,0:T(8,128)(2,1)}, u32[]{:S(2)}) copy-start(bf16[32,448]{1,0:T(8,128)(2,1)} %param.8) | copy-start | bytes 86020
  8.7 601.4 %all-reduce.7.cloned.1.call-start = ((), (), s32[]{:S(2)}) async-start(), calls=%async_computation.4 | async-start | bytes 8388608 | tf_op jit(solution)/shard_map/psum | solution.py:28
  12.1 240.6 %copy-start.8 = (bf16[32,448]{1,0:T(8,128)(2,1)S(1)}, bf16[32,448]{1,0:T(8,128)(2,1)}, u32[]{:S(2)}) copy-start(bf16[32,448]{1,0:T(8,128)(2,1)} %param.7) | copy-start | bytes 86020
  255.8 2.0 copy-start.10
  255.8 355.4 %copy-start.11 = (s32[32]{0:T(128)S(1)}, s32[32]{0:T(128)}, u32[]{:S(2)}) copy-start(s32[32]{0:T(128)} %param.9) | copy-start | bytes 388
  255.8 687.9 %reduce-scatter.2.cloned.1.call-start = ((), (), s32[]{:S(2)}) async-start(), calls=%async_computation.3 | async-start | bytes 3727360 | tf_op jit(solution)/shard_map/reduce_scatter | solution.py:75
  614.7 41.5 %copy-start.9 = (f32[32,448]{1,0:T(8,128)}, f32[32,448]{1,0:T(8,128)S(1)}, u32[]{:S(2)}) copy-start(f32[32,448]{1,0:T(8,128)S(1)} %convolution_multiply_fusion.3) | copy-start | bytes 172036
  652.6 3.7 copy-start.1
  652.6 4.2 copy-start.4
  656.8 2.7 copy-start.5
  658.3 1.2 copy-start.2
  662.0 267.6 %copy-start.6 = (f32[32,2048]{1,0:T(8,128)S(1)}, f32[32,2048]{1,0:T(8,128)}, u32[]{:S(2)}) copy-start(f32[32,2048]{1,0:T(8,128)} %get-tuple-element.13) | copy-start | bytes 786436
  929.6 2.9 copy-start.3
Sparse Core Ops, SparseCore 0:
  10.2 124.3 all-gather.5
  136.8 115.9 all-gather.3
  255.9 354.1 all-reduce.6
  662.2 281.4 reduce-scatter.1
where the time goes:
time: 957 us; the launch traced here: 951 us
  waiting for transfers between devices  601 us (63%)
  blocking collectives  304 us (32%)
  matrix products  18.3 us (2%)
  between operations  16.4 us (2%)
    psum x1, waiting for transfers between devices, per_device(): scores, col_scores = lax.psum((partial_rows, partial_cols), 'tensor')  352 us
    unnamed x1, blocking collectives  266 us
    all_gather x1, waiting for transfers between devices, per_device(): lax.all_gather(item_cache, 'dp', axis=0, tiled=True)  122 us
    all_gather x1, waiting for transfers between devices, per_device(): lax.all_gather(user_cache, 'dp', axis=0, tiled=True)  115 us
    all_gather x1, blocking collectives, per_device(): group_rows = lax.all_gather(item_grad[:GROUP], 'tensor', axis=1, tiled=True)  37.6 us
  transfers between devices with their start and end apart: 4, of which 4 were waited for; matrix products, arithmetic and copies ran while one was open for 1% of the time, Pallas kernels for 0%

commit v1 on v0

v1 whole, which is shorter than its diff:
```python
import jax
import jax.numpy as jnp
from jax import lax
from jax.sharding import Mesh, PartitionSpec as P

BF16 = jnp.bfloat16
F32 = jnp.float32
LOGIT_SCALE = 50.0
NORM_EPS = 1e-06
GROUP = 8
SEQ = 32
AXES = (("zl", 4), ("y", 8), ("c", 2), ("x", 4), ("zh", 2))
TENSOR = ("x", "zh")
PLANE = ("zl", "y")
DP = ("zl", "y", "c")
SWAP = ((0, 1), (1, 0))
N_T = 8
N_P = 32


def three_terms(value):
    high = lax.reduce_precision(value, 8, 7)
    rest = value - high
    middle = lax.reduce_precision(rest, 8, 7)
    low = lax.reduce_precision(rest - middle, 8, 7)
    return high.astype(BF16), middle.astype(BF16), low.astype(BF16)


def to_all(value, axes, count):
    return lax.all_to_all(jnp.broadcast_to(value[None], (count,) + value.shape), axes, 0, 0)


def dot(a, b, dims):
    return lax.dot_general(a, b, (dims, ((), ())), preferred_element_type=F32)


def per_device(item_cache, user_cache, positive, attn_heads, residual, out_proj, norm_gain):
    rows, feats = item_cache.shape
    width = out_proj.shape[1]
    tokens, heads = attn_heads.shape
    half = N_P * rows
    core = lax.axis_index("c")
    dp_index = lax.axis_index(DP)
    t_index = lax.axis_index(TENSOR)

    pair = jnp.concatenate([user_cache, item_cache], axis=1)
    pair_own = to_all(pair, PLANE, N_P).reshape(half, 2 * feats)
    pair_other = lax.ppermute(pair_own, "c", SWAP)
    users = (pair_own[:, :feats], pair_other[:, :feats])
    items = (pair_own[:, feats:], pair_other[:, feats:])

    partial = jnp.concatenate([dot(item_cache, u, ((1,), (1,))) for u in users], axis=1)
    share = 2 * half // N_T
    partial = partial.reshape(rows, N_T, share).transpose(1, 0, 2)
    mixed = dot(attn_heads, out_proj, ((1,), (0,))).astype(BF16).reshape(N_T, tokens // N_T, width)
    got = lax.all_to_all(jnp.concatenate([mixed, *three_terms(partial)], axis=2), TENSOR, 0, 0)
    got = jnp.sum(got.astype(F32), axis=0)
    own_tokens = tokens // N_T
    own_residual = lax.dynamic_slice_in_dim(residual, t_index * own_tokens, own_tokens, 0)
    hidden_own = got[:, :width] + own_residual.astype(F32)
    scores_own = (
        got[:, width : width + share]
        + got[:, width + share : width + 2 * share]
        + got[:, width + 2 * share :]
    ) * LOGIT_SCALE
    back = jnp.concatenate([hidden_own.astype(BF16), *three_terms(scores_own)], axis=1)
    back = to_all(back, TENSOR, N_T)
    hidden = back[:, :, :width].reshape(tokens, width).astype(F32)
    scores = (
        back[:, :, width : width + share].astype(F32)
        + back[:, :, width + share : width + 2 * share].astype(F32)
        + back[:, :, width + 2 * share :].astype(F32)
    )
    scores = scores.transpose(1, 0, 2).reshape(rows, 2 * half)

    owner, row_in = positive // rows, positive % rows
    column = (owner % 2 != core).astype(jnp.int32) * half + (owner // 2) * rows + row_in
    maxima = jnp.max(scores, axis=1, keepdims=True)
    log_total = maxima[:, 0] + jnp.log(jnp.sum(jnp.exp(scores - maxima), axis=1))
    target = column[:, None] == lax.broadcasted_iota(jnp.int32, (1, 2 * half), 1)
    picked = jnp.sum(jnp.where(target, scores, F32(0.0)), axis=1)
    loss = jnp.sum(log_total - picked)
    grad = (jnp.exp(scores - log_total[:, None]) - target.astype(F32)).astype(BF16)
    item_grad = (
        dot(grad[:, :half], users[0], ((1,), (0,))) + dot(grad[:, half:], users[1], ((1,), (0,)))
    ) * LOGIT_SCALE

    group_rows = to_all(item_grad[:GROUP], TENSOR, N_T).transpose(1, 0, 2).reshape(GROUP, width)
    upstream = norm_gain[None, :] * (group_rows / SEQ)
    hidden = hidden.reshape(GROUP, SEQ, width)
    inverse = lax.rsqrt(jnp.mean(hidden * hidden, axis=2, keepdims=True) + NORM_EPS)
    inner = jnp.sum(upstream[:, None, :] * hidden, axis=2, keepdims=True) / width
    stream = inverse * upstream[:, None, :] - hidden * (inverse * inverse * inverse * inner)
    stream = stream.astype(BF16).reshape(tokens, width)
    head_grad = dot(stream, out_proj, ((1,), (1,))).astype(BF16)

    cut = width // (2 * N_P)
    weight = dot(stream, attn_heads, ((0,), (0,))).reshape(N_P, 2, cut, heads)
    give = lax.dynamic_index_in_dim(weight, 1 - core, 1, keepdims=False).astype(BF16)
    keep = lax.dynamic_index_in_dim(weight, core, 1, keepdims=False)
    loss_row = jnp.stack(three_terms(loss))
    loss_rows = jnp.zeros((8, heads), BF16).at[0, :3].set(loss_row)
    grad_give = grad[:, half:].reshape(-1, heads)
    packed = jnp.concatenate([give.reshape(-1, heads), grad_give, loss_rows], axis=0)
    packed = lax.ppermute(packed, "c", SWAP)
    n_w, n_g = N_P * cut, grad_give.shape[0]
    keep = (keep + packed[:n_w].reshape(N_P, cut, heads).astype(F32)).astype(BF16)
    both = jnp.stack([grad[:, :half], packed[n_w : n_w + n_g].reshape(rows, half)])
    both = both.reshape(2, rows, N_P, rows).transpose(2, 0, 1, 3)
    loss = loss + jnp.sum(packed[n_w + n_g, :3].astype(F32))
    loss_rows = jnp.zeros((8, heads), BF16).at[0, :3].set(jnp.stack(three_terms(loss)))
    tile = 2 * rows * rows // heads
    final = jnp.concatenate(
        [
            keep,
            both.reshape(N_P, tile, heads),
            jnp.broadcast_to(loss_rows[None], (N_P, 8, heads)),
        ],
        axis=1,
    )
    final = lax.all_to_all(final, PLANE, 0, 0)
    weight_grad = jnp.sum(final[:, :cut].astype(F32), axis=0).T
    loss_mean = jnp.sum(final[:, cut + tile, :3].astype(F32)) / (2 * half)
    by_user = final[:, cut : cut + tile].reshape(N_P, 2, rows, rows)
    user_grad = (
        dot(by_user[:, 0].reshape(half, rows), items[0], ((0,), (0,)))
        + dot(by_user[:, 1].reshape(half, rows), items[1], ((0,), (0,)))
    ) * LOGIT_SCALE
    return (loss_mean, item_grad, user_grad, head_grad, weight_grad)


def solution(mesh):
    names, sizes = zip(*AXES)
    fine = Mesh(mesh.devices.reshape(sizes), names)
    both = P(DP, TENSOR)
    return jax.shard_map(
        per_device,
        mesh=fine,
        in_specs=(both, both, P(DP), both, P(DP, None), P(TENSOR, None), P()),
        out_specs=(P(), both, both, both, P(TENSOR, DP)),
        check_vma=False,
    )
```

time: 957 us -> 298 us (0.31)
  waiting for transfers between devices: 601 us -> 128 us
  blocking collectives: 304 us -> 55.9 us
  starting transfers between devices: 0.16 us -> 46.8 us
  other arithmetic: 8.28 us -> 22.2 us
  local copies, waits for them, and re-layouts: 3.35 us -> 15.3 us
    psum x1 -> x0, waiting for transfers between devices: 352 us -> none  [per_device(): scores, col_scores = lax.psum((partial_rows, partial_cols), 'tensor')]
    unnamed x1 -> x0, blocking collectives: 266 us -> none
    all_gather x2 -> x0, waiting for transfers between devices: 238 us -> none  [the longest x1 122 us: per_device(): lax.all_gather(item_cache, 'dp', axis=0, tiled=True)]
    all_to_all x0 -> x4, waiting for transfers between devices: none -> 123 us  [the longest x1 52.9 us: per_device(): lax.all_to_all(jnp.concatenate([mixed, *three_terms(partial)], axis=2), T...]
    all_to_all x0 -> x1, blocking collectives: none -> 55.9 us  [to_all(): lax.all_to_all(jnp.broadcast_to(value[None], (count,) + value.shape), axe...]
    all_gather x1 -> x0, blocking collectives: 37.6 us -> none  [per_device(): group_rows = lax.all_gather(item_grad[:GROUP], 'tensor', axis=1, tiled=True)]
    all_to_all x0 -> x4, starting transfers between devices: none -> 36.2 us  [the longest x1 15.5 us: per_device(): final = lax.all_to_all(final, PLANE, 0, 0)]
    ppermute x0 -> x2, starting transfers between devices: none -> 10.6 us  [the longest x1 6.71 us: per_device(): pair_other = lax.ppermute(pair_own, 'c', SWAP)]
  transfers between devices with their start and end apart: 4 -> 6, of which waited for: 4 -> 6; matrix products, arithmetic and copies ran while one was open for 1% -> 2% of each run, Pallas kernels for 0% -> 0%
where the time goes in v1:
time: 298 us; the launch traced here: 294 us
  waiting for transfers between devices  128 us (43%)
  blocking collectives  55.9 us (19%)
  starting transfers between devices  46.8 us (16%)
  other arithmetic  22.2 us (7%)
  local copies, waits for them, and re-layouts  15.3 us (5%)
  between operations  13.6 us (5%)
  matrix products  12.4 us (4%)
    all_to_all x1, blocking collectives, to_all(): lax.all_to_all(jnp.broadcast_to(value[None], (count,) + value.shape), axe...  55.9 us
    all_to_all x1, waiting for transfers between devices, per_device(): lax.all_to_all(jnp.concatenate([mixed, *three_terms(partial)], axis=2), T...  52.9 us
    all_to_all x2, waiting for transfers between devices, to_all(): lax.all_to_all(jnp.broadcast_to(value[None], (count,) + value.shape), axe...  45.3 us
    all_to_all x1, waiting for transfers between devices, per_device(): final = lax.all_to_all(final, PLANE, 0, 0)  25.1 us
    all_to_all x1, starting transfers between devices, per_device(): final = lax.all_to_all(final, PLANE, 0, 0)  15.5 us
    dot_general x9, matrix products, dot(): return lax.dot_general(a, b, (dims, ((), ())), preferred_element_type=F32)  12.4 us
    all_to_all x2, starting transfers between devices, to_all(): lax.all_to_all(jnp.broadcast_to(value[None], (count,) + value.shape), axe...  10.9 us
    all_to_all x1, starting transfers between devices, per_device(): lax.all_to_all(jnp.concatenate([mixed, *three_terms(partial)], axis=2), T...  9.77 us
  transfers between devices with their start and end apart: 6, of which 6 were waited for; matrix products, arithmetic and copies ran while one was open for 2% of the time, Pallas kernels for 0%

profile of v1, /device:TPU:1, one launch (start us, length us, event | category | flops | bytes accessed | tf_op | source)
XLA Modules:
  0.0 293.9 jit_solution(1322754253768694511)
XLA Ops:
  1.8 55.9 %all_to_all.25 = bf16[32,32,896]{2,1,0:T(8,128)(2,1)S(1)} all-to-all(bf16[32,32,896]{2,1,0:T(8,128)(2,1)S(1)} %broadcast_in_dim.16), channel_id=1, replica_groups=mesh['zl'=4,'y'=8,'c'=2,'x'=4,'zh'=2] {'zl','y'}, dimensions={0} | all-to-all | bytes 3670016 | tf_op jit(solution)/shard_map/all_to_all | solution.py:30
  57.6 6.7 %collective-permute-start = (bf16[1024,896]{1,0:T(8,128)(2,1)S(1)}, bf16[1024,896]{1,0:T(8,128)(2,1)S(1)}, u32[]{:S(2)}, u32[]{:S(2)}) collective-permute-start(bf16[1024,896]{1,0:T(8,128)(2,1)S(1)} %bitcast.82), channel_id=1, source_target_pairs={{0,8},{8,0},{1,9},{9,1},{2,10},{10,2},{3,11},{11,3},{4,12},{12,4},... | collective-permute-start | bytes 5505032 | tf_op jit(solution)/shard_map/ppermute | solution.py:48
  65.4 2.3 collective-permute-done
  67.8 1.3 copy-done.4
  69.5 1.5 pad_maximum_fusion
  71.0 9.8 %all-to-all-start.1 = ((bf16[8,32,4352]{2,1,0:T(8,128)(2,1)}), bf16[8,32,4352]{2,1,0:T(8,128)(2,1)}, u32[]{:S(2)}, u32[]{:S(2)}) async-start(bf16[8,32,4352]{2,1,0:T(8,128)(2,1)} %pad_maximum_fusion), calls=%async_computation.1 | async-start | bytes 4456448 | tf_op jit(solution)/shard_map/all_to_all | solution.py:56
  80.8 52.9 %all-to-all-done.1 = bf16[8,32,4352]{2,1,0:T(8,128)(2,1)} async-done(((bf16[8,32,4352]{2,1,0:T(8,128)(2,1)}), bf16[8,32,4352]{2,1,0:T(8,128)(2,1)}, u32[]{:S(2)}, u32[]{:S(2)}) %all-to-all-start.1) | async-done | bytes 2228256 | tf_op jit(solution)/shard_map/all_to_all | solution.py:56
  133.7 2.0 convert_reduce_fusion
  136.7 1.6 broadcast_in_dim.17
  138.3 5.2 %all-to-all-start.2 = ((bf16[8,32,4352]{2,1,0:T(8,128)(2,1)}), bf16[8,32,4352]{2,1,0:T(8,128)(2,1)}, u32[]{:S(2)}, u32[]{:S(2)}) async-start(bf16[8,32,4352]{2,1,0:T(8,128)(2,1)} %broadcast_in_dim.17), calls=%async_computation.2 | async-start | bytes 4456448 | tf_op jit(solution)/shard_map/all_to_all | solution.py:30
  143.5 42.1 %all-to-all-done.2 = bf16[8,32,4352]{2,1,0:T(8,128)(2,1)} async-done(((bf16[8,32,4352]{2,1,0:T(8,128)(2,1)}), bf16[8,32,4352]{2,1,0:T(8,128)(2,1)}, u32[]{:S(2)}, u32[]{:S(2)}) %all-to-all-start.2) | async-done | bytes 2228256 | tf_op jit(solution)/shard_map/all_to_all | solution.py:30
  185.6 1.3 fusion.35
  187.0 1.3 fusion.20
  189.3 1.5 fusion.6
  191.5 5.8 %all-to-all-start.3 = ((f32[8,8,448]{2,1,0:T(8,128)}), f32[8,8,448]{2,1,0:T(8,128)S(1)}, u32[]{:S(2)}, u32[]{:S(2)}) async-start(f32[8,8,448]{2,1,0:T(8,128)} %broadcast_in_dim.18), calls=%async_computation.3 | async-start | bytes 262144 | tf_op jit(solution)/shard_map/all_to_all | solution.py:30
  203.5 3.2 %all-to-all-done.3 = f32[8,8,448]{2,1,0:T(8,128)S(1)} async-done(((f32[8,8,448]{2,1,0:T(8,128)}), f32[8,8,448]{2,1,0:T(8,128)S(1)}, u32[]{:S(2)}, u32[]{:S(2)}) %all-to-all-start.3) | async-done | bytes 114720 | tf_op jit(solution)/shard_map/all_to_all | solution.py:30
  207.0 2.3 fusion
  209.3 3.6 %fusion.3 = bf16[8,32,3584]{2,1,0:T(8,128)(2,1)} fusion(f32[8,32]{1,0:T(8,128)S(1)} %get-tuple-element.49, f32[8,3584]{1,0:T(8,128)S(1)} %broadcast_multiply_fusion, f32[8,32]{1,0:T(8,128)S(1)} %get-tuple-element.48, bf16[8,32,4352]{2,1,0:T(8,128)(2,1)} %all-to-all-done.2), kind=kLoop, calls=%fused_computation.8 | loop fusion | flops 4587520 | bytes 3786752 | tf_op jit(solution)/shard_map/convert_element_type | solution.py:94
  213.0 3.8 %copy.31 = bf16[3584,256]{1,0:T(8,128)(2,1)} copy(bf16[3584,256]{0,1:T(8,128)(2,1)} %bitcast.86) | data formatting | bytes 3670016 | tf_op jit(solution)/shard_map/dot_general | solution.py:34
  216.8 2.1 fusion.23
  218.9 1.9 copy-done.1
  221.0 3.9 %collective-permute-start.1 = (bf16[1928,256]{1,0:T(8,128)(2,1)S(1)}, bf16[1928,256]{1,0:T(8,128)(2,1)}, u32[]{:S(2)}, u32[]{:S(2)}) collective-permute-start(bf16[1928,256]{1,0:T(8,128)(2,1)S(1)} %fusion.11), channel_id=1, source_target_pairs={{0,8},{8,0},{1,9},{9,1},{2,10},{10,2},{3,11},{11,3},{4,12},{12,4},... | collective-permute-start | bytes 2961416 | tf_op jit(solution)/shard_map/ppermute | solution.py:105
  225.1 2.1 collective-permute-done.1
  227.2 1.3 fusion.32
  236.3 1.2 slice.139
  237.6 1.8 fusion.5
  240.5 15.5 %all-to-all-start.4 = ((bf16[32,72,256]{2,1,0:T(8,128)(2,1)}), bf16[32,72,256]{2,1,0:T(8,128)(2,1)S(1)}, u32[]{:S(2)}, u32[]{:S(2)}) async-start(bf16[32,72,256]{2,1,0:T(8,128)(2,1)} %pad_maximum_fusion.1), calls=%async_computation.4 | async-start | bytes 2359296 | tf_op jit(solution)/shard_map/all_to_all | solution.py:121
  256.0 2.8 convolution_convert_fusion.1
  258.8 25.1 %all-to-all-done.4 = bf16[32,72,256]{2,1,0:T(8,128)(2,1)S(1)} async-done(((bf16[32,72,256]{2,1,0:T(8,128)(2,1)}), bf16[32,72,256]{2,1,0:T(8,128)(2,1)S(1)}, u32[]{:S(2)}, u32[]{:S(2)}) %all-to-all-start.4) | async-done | bytes 1179680 | tf_op jit(solution)/shard_map/all_to_all | solution.py:121
  284.6 1.2 reshape.184
  286.5 1.8 fusion.9
  290.3 2.4 fusion.7
  (63 shorter events, 13.2 us)
Async XLA Ops:
  0.6 63.7 %copy-start = (bf16[256,3584]{1,0:T(8,128)(2,1)S(1)}, bf16[256,3584]{1,0:T(8,128)(2,1)}, u32[]{:S(2)}) copy-start(bf16[256,3584]{1,0:T(8,128)(2,1)} %param.16) | copy-start | bytes 5505028
  1.8 62.6 %copy-start.6 = (bf16[256,256]{1,0:T(8,128)(2,1)S(1)}, bf16[256,256]{1,0:T(8,128)(2,1)}, u32[]{:S(2)}) copy-start(bf16[256,256]{1,0:T(8,128)(2,1)} %param.14) | copy-start | bytes 393220
  57.6 7.8 %copy-start.2 = (bf16[32,32,896]{2,1,0:T(8,128)(2,1)}, bf16[32,32,896]{2,1,0:T(8,128)(2,1)S(1)}, u32[]{:S(2)}) copy-start(bf16[32,32,896]{2,1,0:T(8,128)(2,1)S(1)} %all_to_all.25) | copy-start | bytes 5505028
  57.6 7.4 %copy-start.8 = (bf16[32,448]{1,0:T(8,128)(2,1)S(1)}, bf16[32,448]{1,0:T(8,128)(2,1)}, u32[]{:S(2)}) copy-start(bf16[32,448]{1,0:T(8,128)(2,1)} %param.11) | copy-start | bytes 86020
  57.6 10.1 %collective-permute-start = (bf16[1024,896]{1,0:T(8,128)(2,1)S(1)}, bf16[1024,896]{1,0:T(8,128)(2,1)S(1)}, u32[]{:S(2)}, u32[]{:S(2)}) collective-permute-start(bf16[1024,896]{1,0:T(8,128)(2,1)S(1)} %bitcast.82), channel_id=1, source_target_pairs={{0,8},{8,0},{1,9},{9,1},{2,10},{10,2},{3,11},{11,3},{4,12},{12,4},... | collective-permute-start | bytes 5505032 | tf_op jit(solution)/shard_map/ppermute | solution.py:48
  67.8 1.3 copy-start.4
  71.0 62.6 %all-to-all-start.1 = ((bf16[8,32,4352]{2,1,0:T(8,128)(2,1)}), bf16[8,32,4352]{2,1,0:T(8,128)(2,1)}, u32[]{:S(2)}, u32[]{:S(2)}) async-start(bf16[8,32,4352]{2,1,0:T(8,128)(2,1)} %pad_maximum_fusion), calls=%async_computation.1 | async-start | bytes 4456448 | tf_op jit(solution)/shard_map/all_to_all | solution.py:56
  138.3 5.2 %copy-start.10 = (s32[32]{0:T(128)S(1)}, s32[32]{0:T(128)}, u32[]{:S(2)}) copy-start(s32[32]{0:T(128)} %param.13) | copy-start | bytes 388
  138.3 5.2 %copy-start.9 = (f32[3584]{0:T(1024)S(1)}, f32[3584]{0:T(1024)}, u32[]{:S(2)}) copy-start(f32[3584]{0:T(1024)} %param.17) | copy-start | bytes 43012
  138.3 47.3 %all-to-all-start.2 = ((bf16[8,32,4352]{2,1,0:T(8,128)(2,1)}), bf16[8,32,4352]{2,1,0:T(8,128)(2,1)}, u32[]{:S(2)}, u32[]{:S(2)}) async-start(bf16[8,32,4352]{2,1,0:T(8,128)(2,1)} %broadcast_in_dim.17), calls=%async_computation.2 | async-start | bytes 4456448 | tf_op jit(solution)/shard_map/all_to_all | solution.py:30
  185.6 3.4 %copy-start.3 = (bf16[32,32,896]{2,1,0:T(8,128)(2,1)S(1)}, bf16[32,32,896]{2,1,0:T(8,128)(2,1)}, u32[]{:S(2)}) copy-start(bf16[32,32,896]{2,1,0:T(8,128)(2,1)} %copy-done.2) | copy-start | bytes 5505028
  190.8 0.7 copy-start.7
  191.5 15.2 %all-to-all-start.3 = ((f32[8,8,448]{2,1,0:T(8,128)}), f32[8,8,448]{2,1,0:T(8,128)S(1)}, u32[]{:S(2)}, u32[]{:S(2)}) async-start(f32[8,8,448]{2,1,0:T(8,128)} %broadcast_in_dim.18), calls=%async_computation.3 | async-start | bytes 262144 | tf_op jit(solution)/shard_map/all_to_all | solution.py:30
  218.9 1.9 copy-start.1
  221.0 6.2 %collective-permute-start.1 = (bf16[1928,256]{1,0:T(8,128)(2,1)S(1)}, bf16[1928,256]{1,0:T(8,128)(2,1)}, u32[]{:S(2)}, u32[]{:S(2)}) collective-permute-start(bf16[1928,256]{1,0:T(8,128)(2,1)S(1)} %fusion.11), channel_id=1, source_target_pairs={{0,8},{8,0},{1,9},{9,1},{2,10},{10,2},{3,11},{11,3},{4,12},{12,4},... | collective-permute-start | bytes 2961416 | tf_op jit(solution)/shard_map/ppermute | solution.py:105
  240.5 43.4 %all-to-all-start.4 = ((bf16[32,72,256]{2,1,0:T(8,128)(2,1)}), bf16[32,72,256]{2,1,0:T(8,128)(2,1)S(1)}, u32[]{:S(2)}, u32[]{:S(2)}) async-start(bf16[32,72,256]{2,1,0:T(8,128)(2,1)} %pad_maximum_fusion.1), calls=%async_computation.4 | async-start | bytes 2359296 | tf_op jit(solution)/shard_map/all_to_all | solution.py:121
  286.5 3.8 %copy-start.5 = (bf16[32,1,32,32]{3,2,1,0:T(8,128)(2,1)S(1)}, bf16[32,1,32,32]{3,2,1,0:T(8,128)(2,1)}, u32[]{:S(2)}) copy-start(bf16[32,1,32,32]{3,2,1,0:T(8,128)(2,1)} %get-tuple-element.39) | copy-start | bytes 196612

commit v2 on v1

v2 whole, which is shorter than its diff:
```python
import jax
import jax.numpy as jnp
from jax import lax
from jax.sharding import Mesh, PartitionSpec as P

BF16 = jnp.bfloat16
F32 = jnp.float32
LOGIT_SCALE = 50.0
NORM_EPS = 1e-06
GROUP = 8
SEQ = 32
AXES = (("zl", 4), ("y", 8), ("c", 2), ("x", 4), ("zh", 2))
TENSOR = ("x", "zh")
PLANE = ("zl", "y")
DP = ("zl", "y", "c")
N_T = 8
N_P = 32


def xor(axis, size, bits):
    return dict(axis_name=axis, perm=[(i, i ^ bits) for i in range(size)])


def swap(value):
    return lax.ppermute(value, **xor("c", 2, 1))


def three_terms(value):
    high = lax.reduce_precision(value, 8, 7)
    rest = value - high
    middle = lax.reduce_precision(rest, 8, 7)
    low = lax.reduce_precision(rest - middle, 8, 7)
    return high.astype(BF16), middle.astype(BF16), low.astype(BF16)


def to_all(value, axes, count):
    return lax.all_to_all(jnp.broadcast_to(value[None], (count,) + value.shape), axes, 0, 0)


def dot(a, b, dims):
    return lax.dot_general(a, b, (dims, ((), ())), preferred_element_type=F32)


def by_xor(value, index):
    shape = value.shape
    for bit in (1, 2, 4):
        pairs = value.reshape((N_T // (2 * bit), 2, bit) + shape[1:])
        flipped = pairs[:, ::-1].reshape(shape)
        value = jnp.where((index & bit) != 0, flipped, value)
    return value


def core_major(value):
    lead, width = value.shape[:-1], value.shape[-1]
    cut = width // (2 * N_P)
    return value.reshape(lead + (N_P, 2, cut)).swapaxes(-3, -2).reshape(lead + (width,))


def per_device(item_cache, user_cache, positive, attn_heads, residual, out_proj, norm_gain):
    rows, feats = item_cache.shape
    width = out_proj.shape[1]
    tokens, heads = attn_heads.shape
    half = N_P * rows
    core = lax.axis_index("c")
    t_index = lax.axis_index(TENSOR)
    x_block = tokens // 4
    own_tokens = tokens // N_T

    attn = by_xor(attn_heads.reshape(N_T, own_tokens, heads), t_index).reshape(tokens, heads)
    mixed = dot(attn, out_proj, ((1,), (0,))).astype(BF16)
    from_x = [
        lax.ppermute(mixed[k * x_block : (k + 1) * x_block], **xor("x", 4, k)) for k in (1, 2, 3)
    ]

    users_own = to_all(user_cache, PLANE, N_P).reshape(half, feats)
    users_own, *from_x = lax.optimization_barrier((users_own, *from_x))
    users = (users_own, swap(users_own))
    mixed_x = mixed[:x_block].astype(F32) + sum(part.astype(F32) for part in from_x)
    from_z = lax.ppermute(mixed_x[own_tokens:].astype(BF16), **xor("zh", 2, 1))

    partial = jnp.concatenate([dot(item_cache, u, ((1,), (1,))) for u in users], axis=1)
    share = 2 * half // N_T
    partial = partial.reshape(rows, N_T, share).transpose(1, 0, 2)
    scores_own = jnp.sum(lax.all_to_all(partial, TENSOR, 0, 0), axis=0) * LOGIT_SCALE
    scores_own, from_z = lax.optimization_barrier((scores_own, from_z))
    own_residual = lax.dynamic_slice_in_dim(residual, t_index * own_tokens, own_tokens, 0)
    hidden_own = mixed_x[:own_tokens] + from_z.astype(F32) + own_residual.astype(F32)
    hidden_own = core_major(hidden_own.astype(BF16))
    hidden_z = lax.ppermute(hidden_own, **xor("zh", 2, 1))
    scores = to_all(scores_own, TENSOR, N_T).transpose(1, 0, 2).reshape(rows, 2 * half)
    scores, hidden_z = lax.optimization_barrier((scores, hidden_z))
    hidden_x = jnp.concatenate([hidden_own, hidden_z], axis=0)
    hidden_x = [hidden_x] + [lax.ppermute(hidden_x, **xor("x", 4, k)) for k in (1, 2, 3)]

    owner, row_in = positive // rows, positive % rows
    column = (owner % 2 != core).astype(jnp.int32) * half + (owner // 2) * rows + row_in
    maxima = jnp.max(scores, axis=1, keepdims=True)
    log_total = maxima[:, 0] + jnp.log(jnp.sum(jnp.exp(scores - maxima), axis=1))
    target = column[:, None] == lax.broadcasted_iota(jnp.int32, (1, 2 * half), 1)
    picked = jnp.sum(jnp.where(target, scores, F32(0.0)), axis=1)
    losses = jnp.concatenate(three_terms(log_total - picked))
    grad = (jnp.exp(scores - log_total[:, None]) - target.astype(F32)).astype(BF16)
    item_grad = (
        dot(grad[:, :half], users[0], ((1,), (0,))) + dot(grad[:, half:], users[1], ((1,), (0,)))
    ) * LOGIT_SCALE

    group_rows = to_all(item_grad[:GROUP], TENSOR, N_T)
    item_cache, group_rows = lax.optimization_barrier((item_cache, group_rows))
    items_own = to_all(item_cache, PLANE, N_P).reshape(half, feats)
    group_rows = core_major(group_rows.transpose(1, 0, 2).reshape(GROUP, width))
    upstream = core_major(norm_gain)[None, :] * (by_xor(group_rows, t_index) / SEQ)
    hidden = jnp.concatenate(hidden_x, axis=0).reshape(GROUP, SEQ, width).astype(F32)
    inverse = lax.rsqrt(jnp.mean(hidden * hidden, axis=2, keepdims=True) + NORM_EPS)
    inner = jnp.sum(upstream[:, None, :] * hidden, axis=2, keepdims=True) / width
    stream = inverse * upstream[:, None, :] - hidden * (inverse * inverse * inverse * inner)
    stream = stream.astype(BF16).reshape(tokens, width)

    cut = width // (2 * N_P)
    side = width // 2
    grad_losses = jnp.zeros((8, half), BF16).at[0, : 3 * rows].set(losses)
    other = swap(jnp.concatenate([grad[:, half:], grad_losses], axis=0))
    attn_other = swap(attn)
    stream_other = swap(lax.dynamic_slice_in_dim(stream, (1 - core) * side, side, 1))
    stream_keep = lax.dynamic_slice_in_dim(stream, core * side, side, 1)
    weight = dot(stream_keep, attn, ((0,), (0,))) + dot(stream_other, attn_other, ((0,), (0,)))
    weight = weight.astype(BF16).reshape(N_P, cut, heads)
    both = jnp.stack([grad[:, :half], other[:rows]])
    both = both.reshape(2, rows, N_P, rows).transpose(2, 0, 1, 3)
    losses = jnp.concatenate([losses, other[rows, : 3 * rows]])
    losses = jnp.zeros((8, heads), BF16).at[0, : 6 * rows].set(losses)
    tile = 2 * rows * rows // heads
    final = jnp.concatenate(
        [weight, both.reshape(N_P, tile, heads), jnp.broadcast_to(losses[None], (N_P, 8, heads))],
        axis=1,
    )
    final = lax.all_to_all(final, PLANE, 0, 0)
    out_proj = core_major(out_proj)
    head_grad = dot(stream, out_proj, ((1,), (1,))).astype(BF16)
    head_grad = by_xor(head_grad.reshape(N_T, own_tokens, heads), t_index).reshape(tokens, heads)
    weight_grad = jnp.sum(final[:, :cut].astype(F32), axis=0).T
    loss_mean = jnp.sum(final[:, cut + tile].astype(F32)) / (2 * half)
    by_user = final[:, cut : cut + tile].reshape(N_P, 2, rows, rows)
    items = (items_own, swap(items_own))
    user_grad = (
        dot(by_user[:, 0].reshape(half, rows), items[0], ((0,), (0,)))
        + dot(by_user[:, 1].reshape(half, rows), items[1], ((0,), (0,)))
    ) * LOGIT_SCALE
    return (loss_mean, item_grad, user_grad, head_grad, weight_grad)


def solution(mesh):
    names, sizes = zip(*AXES)
    fine = Mesh(mesh.devices.reshape(sizes), names)
    both = P(DP, TENSOR)
    return jax.shard_map(
        per_device,
        mesh=fine,
        in_specs=(both, both, P(DP), both, P(DP, None), P(TENSOR, None), P()),
        out_specs=(P(), both, both, both, P(TENSOR, DP)),
        check_vma=False,
    )
```

time: 298 us -> 238 us (0.80)
  waiting for transfers between devices: 128 us -> 66.3 us
  starting transfers between devices: 46.8 us -> 108 us
  blocking collectives: 55.9 us -> 0 us
  local copies, waits for them, and re-layouts: 15.3 us -> 34.1 us
  between operations: 13.6 us -> 3.18 us
  other arithmetic: 22.2 us -> 12.5 us
    all_to_all x1 -> x0, blocking collectives: 55.9 us -> none  [to_all(): lax.all_to_all(jnp.broadcast_to(value[None], (count,) + value.shape), axe...]
    all_to_all x1, waiting for transfers between devices: 52.9 us -> 1.29 us  [per_device(): lax.all_to_all(partial, TENSOR, 0, 0)]
    ppermute x2 -> x13, starting transfers between devices: 10.6 us -> 49.5 us  [the longest x5 15.8 us: swap(): return lax.ppermute(value, **xor('c', 2, 1))]
    all_to_all x2 -> x4, waiting for transfers between devices: 45.3 us -> 10.2 us  [to_all(): lax.all_to_all(jnp.broadcast_to(value[None], (count,) + value.shape), axe...]
    ppermute x2 -> x13, waiting for transfers between devices: 4.43 us -> 36.5 us  [the longest x3 20.7 us: per_device(): lax.ppermute(mixed[k * x_block:(k + 1) * x_block], **xor('x', 4, k))]
    all_to_all x2 -> x4, starting transfers between devices: 10.9 us -> 41 us  [to_all(): lax.all_to_all(jnp.broadcast_to(value[None], (count,) + value.shape), axe...]
    unnamed x22 -> x34, local copies, waits for them, and re-layouts: 3.16 us -> 10.3 us
    all_to_all x1, waiting for transfers between devices: 25.1 us -> 18.2 us  [per_device(): final = lax.all_to_all(final, PLANE, 0, 0)]
  transfers between devices with their start and end apart: 6 -> 19, of which waited for: 6 -> 9; matrix products, arithmetic and copies ran while one was open for 2% -> 20% of each run, Pallas kernels for 0% -> 0%
where the time goes in v2:
time: 238 us; the launch traced here: 234 us
  starting transfers between devices  108 us (45%)
  waiting for transfers between devices  66.3 us (28%)
  local copies, waits for them, and re-layouts  34.1 us (14%)
  other arithmetic  12.5 us (5%)
  matrix products  10.4 us (4%)
  between operations  3.18 us (1%)
    all_to_all x4, starting transfers between devices, to_all(): lax.all_to_all(jnp.broadcast_to(value[None], (count,) + value.shape), axe...  41 us
    ppermute x3, waiting for transfers between devices, per_device(): lax.ppermute(mixed[k * x_block:(k + 1) * x_block], **xor('x', 4, k))  20.7 us
    all_to_all x1, waiting for transfers between devices, per_device(): final = lax.all_to_all(final, PLANE, 0, 0)  18.2 us
    ppermute x5, starting transfers between devices, swap(): return lax.ppermute(value, **xor('c', 2, 1))  15.8 us
    dot_general x10, matrix products, dot(): return lax.dot_general(a, b, (dims, ((), ())), preferred_element_type=F32)  10.4 us
    unnamed x34, local copies, waits for them, and re-layouts  10.3 us
    all_to_all x4, waiting for transfers between devices, to_all(): lax.all_to_all(jnp.broadcast_to(value[None], (count,) + value.shape), axe...  10.2 us
    all_to_all x1, starting transfers between devices, per_device(): final = lax.all_to_all(final, PLANE, 0, 0)  9.96 us
  transfers between devices with their start and end apart: 19, of which 9 were waited for; matrix products, arithmetic and copies ran while one was open for 20% of the time, Pallas kernels for 0%

profile of v2, /device:TPU:1, one launch (start us, length us, event | category | flops | bytes accessed | tf_op | source)
XLA Modules:
  0.0 234.3 jit_solution(13775271170709995588)
XLA Ops:
  0.6 1.9 broadcast_in_dim.18
  2.5 13.6 %all-to-all-start = ((bf16[32,32,448]{2,1,0:T(8,128)(2,1)}), bf16[32,32,448]{2,1,0:T(8,128)(2,1)S(1)}, u32[]{:S(2)}, u32[]{:S(2)}) async-start(bf16[32,32,448]{2,1,0:T(8,128)(2,1)} %broadcast_in_dim.18), calls=%async_computation | async-start | bytes 2097152 | tf_op jit(solution)/shard_map/all_to_all | solution.py:37
  18.7 3.1 %collective-permute-start = (bf16[64,3584]{1,0:T(8,128)(2,1)S(1)}, bf16[64,3584]{1,0:T(8,128)(2,1)S(1)}, u32[]{:S(2)}, u32[]{:S(2)}) collective-permute-start(bf16[64,3584]{1,0:T(8,128)(2,1)S(1)} %get-tuple-element.55), channel_id=1, source_target_pairs={{0,2},{2,0},{4,6},{6,4},{1,3},{3,1},{5,7},{7,5},{8,10},{10,8},{12,... | collective-permute-start | bytes 1376264 | tf_op jit(solution)/shard_map/ppermute | solution.py:72
  21.8 4.4 %collective-permute-start.1 = (bf16[64,3584]{1,0:T(8,128)(2,1)S(1)}, bf16[64,3584]{1,0:T(8,128)(2,1)S(1)}, u32[]{:S(2)}, u32[]{:S(2)}) collective-permute-start(bf16[64,3584]{1,0:T(8,128)(2,1)S(1)} %get-tuple-element.54), channel_id=1, source_target_pairs={{0,4},{2,6},{4,0},{6,2},{1,5},{3,7},{5,1},{7,3},{8,12},{10,14},{12... | collective-permute-start | bytes 1376264 | tf_op jit(solution)/shard_map/ppermute | solution.py:72
  26.2 2.1 collective-permute-start.2
  28.3 3.4 %collective-permute-done = bf16[64,3584]{1,0:T(8,128)(2,1)S(1)} collective-permute-done((bf16[64,3584]{1,0:T(8,128)(2,1)S(1)}, bf16[64,3584]{1,0:T(8,128)(2,1)S(1)}, u32[]{:S(2)}, u32[]{:S(2)}) %collective-permute-start) | collective-permute-done | bytes 458784 | tf_op jit(solution)/shard_map/ppermute | solution.py:72
  31.7 12.1 %collective-permute-done.1 = bf16[64,3584]{1,0:T(8,128)(2,1)S(1)} collective-permute-done((bf16[64,3584]{1,0:T(8,128)(2,1)S(1)}, bf16[64,3584]{1,0:T(8,128)(2,1)S(1)}, u32[]{:S(2)}, u32[]{:S(2)}) %collective-permute-start.1) | collective-permute-done | bytes 458784 | tf_op jit(solution)/shard_map/ppermute | solution.py:72
  44.5 5.3 %collective-permute-done.2 = bf16[64,3584]{1,0:T(8,128)(2,1)} collective-permute-done((bf16[64,3584]{1,0:T(8,128)(2,1)S(1)}, bf16[64,3584]{1,0:T(8,128)(2,1)}, u32[]{:S(2)}, u32[]{:S(2)}) %collective-permute-start.2) | collective-permute-done | bytes 458784 | tf_op jit(solution)/shard_map/ppermute | solution.py:72
  50.3 4.3 %collective-permute-start.3 = (bf16[1024,448]{0,1:T(8,128)(2,1)S(1)}, bf16[1024,448]{0,1:T(8,128)(2,1)S(1)}, u32[]{:S(2)}, u32[]{:S(2)}) collective-permute-start(bf16[1024,448]{0,1:T(8,128)(2,1)S(1)} %copy.39), channel_id=1, source_target_pairs={{0,8},{8,0},{1,9},{9,1},{2,10},{10,2},{3,11},{11,3},{4,12},{12,4},... | collective-permute-start | bytes 2752520 | tf_op jit(solution)/shard_map/ppermute | solution.py:25
  57.7 7.4 %all-to-all-start.1 = ((f32[8,32,256]{2,1,0:T(8,128)}), f32[8,32,256]{2,1,0:T(8,128)S(1)}, u32[]{:S(2)}, u32[]{:S(2)}) async-start(f32[8,32,256]{2,1,0:T(8,128)} %bitcast.113), calls=%async_computation.1 | async-start | bytes 524288 | tf_op jit(solution)/shard_map/all_to_all | solution.py:84
  66.8 7.3 %collective-permute-start.4 = (bf16[32,3584]{1,0:T(8,128)(2,1)S(1)}, bf16[32,3584]{1,0:T(8,128)(2,1)S(1)}, u32[]{:S(2)}, u32[]{:S(2)}) collective-permute-start(bf16[32,3584]{1,0:T(8,128)(2,1)S(1)} %slice.131), channel_id=1, source_target_pairs={{0,1},{1,0},{2,3},{3,2},{4,5},{5,4},{6,7},{7,6},{8,9},{9,8},{10,11... | collective-permute-start | bytes 688136 | tf_op jit(solution)/shard_map/ppermute | solution.py:79
  75.7 8.6 %collective-permute-done.4 = bf16[32,3584]{1,0:T(8,128)(2,1)S(1)} collective-permute-done((bf16[32,3584]{1,0:T(8,128)(2,1)S(1)}, bf16[32,3584]{1,0:T(8,128)(2,1)S(1)}, u32[]{:S(2)}, u32[]{:S(2)}) %collective-permute-start.4) | collective-permute-done | bytes 229408 | tf_op jit(solution)/shard_map/ppermute | solution.py:79
  85.0 9.0 %all-to-all-start.2 = ((f32[8,32,256]{2,1,0:T(8,128)}), f32[8,32,256]{2,1,0:T(8,128)S(1)}, u32[]{:S(2)}, u32[]{:S(2)}) async-start(f32[8,32,256]{2,1,0:T(8,128)} %broadcast_in_dim.19), calls=%async_computation.2 | async-start | bytes 524288 | tf_op jit(solution)/shard_map/all_to_all | solution.py:37
  97.6 7.3 %collective-permute-start.5 = (bf16[32,3584]{1,0:T(8,128)(2,1)}, bf16[32,3584]{1,0:T(8,128)(2,1)}, u32[]{:S(2)}, u32[]{:S(2)}) collective-permute-start(bf16[32,3584]{1,0:T(8,128)(2,1)} %reshape.440), channel_id=1, source_target_pairs={{0,1},{1,0},{2,3},{3,2},{4,5},{5,4},{6,7},{7,6},{8,9},{9,8},{10,11... | collective-permute-start | bytes 688136 | tf_op jit(solution)/shard_map/ppermute | solution.py:89
  106.6 5.5 %collective-permute-done.5 = bf16[32,3584]{1,0:T(8,128)(2,1)} collective-permute-done((bf16[32,3584]{1,0:T(8,128)(2,1)}, bf16[32,3584]{1,0:T(8,128)(2,1)}, u32[]{:S(2)}, u32[]{:S(2)}) %collective-permute-start.5) | collective-permute-done | bytes 229408 | tf_op jit(solution)/shard_map/ppermute | solution.py:89
  112.1 1.7 constant_dynamic-update-slice_fusion
  113.8 3.1 %collective-permute-start.6 = (bf16[64,3584]{1,0:T(8,128)(2,1)}, bf16[64,3584]{1,0:T(8,128)(2,1)}, u32[]{:S(2)}, u32[]{:S(2)}) collective-permute-start(bf16[64,3584]{1,0:T(8,128)(2,1)} %get-tuple-element.58), channel_id=1, source_target_pairs={{0,2},{2,0},{4,6},{6,4},{1,3},{3,1},{5,7},{7,5},{8,10},{10,8},{12,... | collective-permute-start | bytes 1376264 | tf_op jit(solution)/shard_map/ppermute | solution.py:93
  116.9 4.3 %collective-permute-start.7 = (bf16[64,3584]{1,0:T(8,128)(2,1)}, bf16[64,3584]{1,0:T(8,128)(2,1)}, u32[]{:S(2)}, u32[]{:S(2)}) collective-permute-start(bf16[64,3584]{1,0:T(8,128)(2,1)} %get-tuple-element.58), channel_id=1, source_target_pairs={{0,4},{2,6},{4,0},{6,2},{1,5},{3,7},{5,1},{7,3},{8,12},{10,14},{12... | collective-permute-start | bytes 1376264 | tf_op jit(solution)/shard_map/ppermute | solution.py:93
  121.2 2.2 collective-permute-start.8
  126.5 8.7 %all-to-all-start.3 = ((f32[8,8,448]{2,1,0:T(8,128)}), f32[8,8,448]{2,1,0:T(8,128)S(1)}, u32[]{:S(2)}, u32[]{:S(2)}) async-start(f32[8,8,448]{2,1,0:T(8,128)} %broadcast_in_dim.20), calls=%async_computation.3 | async-start | bytes 262144 | tf_op jit(solution)/shard_map/all_to_all | solution.py:37
  135.8 10.2 %all-to-all-done.3 = f32[8,8,448]{2,1,0:T(8,128)S(1)} async-done(((f32[8,8,448]{2,1,0:T(8,128)}), f32[8,8,448]{2,1,0:T(8,128)S(1)}, u32[]{:S(2)}, u32[]{:S(2)}) %all-to-all-start.3) | async-done | bytes 114720 | tf_op jit(solution)/shard_map/all_to_all | solution.py:37
  150.1 9.7 %all-to-all-start.5 = ((bf16[32,32,448]{2,1,0:T(8,128)(2,1)}), bf16[32,32,448]{2,1,0:T(8,128)(2,1)S(1)}, u32[]{:S(2)}, u32[]{:S(2)}) async-start(bf16[32,32,448]{2,1,0:T(8,128)(2,1)} %broadcast_in_dim.25), calls=%async_computation.5 | async-start | bytes 2097152 | tf_op jit(solution)/shard_map/all_to_all | solution.py:37
  167.3 4.8 %collective-permute-start.9 = (bf16[256,1792]{1,0:T(8,128)(2,1)}, bf16[256,1792]{1,0:T(8,128)(2,1)}, u32[]{:S(2)}, u32[]{:S(2)}) collective-permute-start(bf16[256,1792]{1,0:T(8,128)(2,1)} %constant_dynamic-slice_fusion), channel_id=1, source_target_pairs={{0,8},{8,0},{1,9},{9,1},{2,10},{10,2},{3,11},{11,3},{4,12},{12,4},... | collective-permute-start | bytes 2752520 | tf_op jit(solution)/shard_map/ppermute | solution.py:25
  172.2 1.9 collective-permute-start.11
  174.1 2.6 %collective-permute-start.10 = (bf16[256,256]{1,0:T(8,128)(2,1)}, bf16[256,256]{1,0:T(8,128)(2,1)}, u32[]{:S(2)}, u32[]{:S(2)}) collective-permute-start(bf16[256,256]{1,0:T(8,128)(2,1)} %fusion.14), channel_id=1, source_target_pairs={{0,8},{8,0},{1,9},{9,1},{2,10},{10,2},{3,11},{11,3},{4,12},{12,4},... | collective-permute-start | bytes 393224 | tf_op jit(solution)/shard_map/ppermute | solution.py:25
  181.4 1.8 fusion.30
  185.8 10.0 %all-to-all-start.4 = ((bf16[32,72,256]{2,1,0:T(8,128)(2,1)}), bf16[32,72,256]{2,1,0:T(8,128)(2,1)}, u32[]{:S(2)}, u32[]{:S(2)}) async-start(bf16[32,72,256]{2,1,0:T(8,128)(2,1)} %pad_maximum_fusion), calls=%async_computation.4 | async-start | bytes 2359296 | tf_op jit(solution)/shard_map/all_to_all | solution.py:136
  195.7 3.8 %copy.51 = bf16[256,3584]{0,1:T(8,128)(2,1)} copy(bf16[256,3584]{1,0:T(8,128)(2,1)} %param.16) | data formatting | bytes 3670016 | tf_op args[5]
  204.1 2.2 collective-permute-start.12
  207.0 18.2 %all-to-all-done.4 = bf16[32,72,256]{2,1,0:T(8,128)(2,1)} async-done(((bf16[32,72,256]{2,1,0:T(8,128)(2,1)}), bf16[32,72,256]{2,1,0:T(8,128)(2,1)}, u32[]{:S(2)}, u32[]{:S(2)}) %all-to-all-start.4) | async-done | bytes 1179680 | tf_op jit(solution)/shard_map/all_to_all | solution.py:136
  228.7 1.9 convert_reduce_fusion
  231.0 2.2 fusion.2
  (142 shorter events, 46.7 us)
Async XLA Ops:
  0.6 15.5 %copy-start.5 = (bf16[256,256]{1,0:T(8,128)(2,1)S(1)}, bf16[256,256]{1,0:T(8,128)(2,1)}, u32[]{:S(2)}) copy-start(bf16[256,256]{1,0:T(8,128)(2,1)} %param.14) | copy-start | bytes 393220
  2.5 14.5 %copy-start = (bf16[256,3584]{1,0:T(8,128)(2,1)S(1)}, bf16[256,3584]{1,0:T(8,128)(2,1)}, u32[]{:S(2)}) copy-start(bf16[256,3584]{1,0:T(8,128)(2,1)} %param.16) | copy-start | bytes 5505028
  2.5 47.2 %all-to-all-start = ((bf16[32,32,448]{2,1,0:T(8,128)(2,1)}), bf16[32,32,448]{2,1,0:T(8,128)(2,1)S(1)}, u32[]{:S(2)}, u32[]{:S(2)}) async-start(bf16[32,32,448]{2,1,0:T(8,128)(2,1)} %broadcast_in_dim.18), calls=%async_computation | async-start | bytes 2097152 | tf_op jit(solution)/shard_map/all_to_all | solution.py:37
  18.5 25.2 %copy-start.3 = (bf16[256,3584]{1,0:T(8,128)(2,1)}, bf16[256,3584]{1,0:T(8,128)(2,1)S(1)}, u32[]{:S(2)}) copy-start(bf16[256,3584]{1,0:T(8,128)(2,1)S(1)} %convolution_convert_fusion) | copy-start | bytes 5505028
  18.6 36.0 %copy-start.13 = (f32[3584]{0:T(1024)S(1)}, f32[3584]{0:T(1024)}, u32[]{:S(2)}) copy-start(f32[3584]{0:T(1024)} %param.17) | copy-start | bytes 43012
  18.6 36.1 %copy-start.9 = (bf16[32,448]{1,0:T(8,128)(2,1)S(1)}, bf16[32,448]{1,0:T(8,128)(2,1)}, u32[]{:S(2)}) copy-start(bf16[32,448]{1,0:T(8,128)(2,1)} %param.11) | copy-start | bytes 86020
  18.7 13.0 %collective-permute-start = (bf16[64,3584]{1,0:T(8,128)(2,1)S(1)}, bf16[64,3584]{1,0:T(8,128)(2,1)S(1)}, u32[]{:S(2)}, u32[]{:S(2)}) collective-permute-start(bf16[64,3584]{1,0:T(8,128)(2,1)S(1)} %get-tuple-element.55), channel_id=1, source_target_pairs={{0,2},{2,0},{4,6},{6,4},{1,3},{3,1},{5,7},{7,5},{8,10},{10,8},{12,... | collective-permute-start | bytes 1376264 | tf_op jit(solution)/shard_map/ppermute | solution.py:72
  21.8 21.9 %collective-permute-start.1 = (bf16[64,3584]{1,0:T(8,128)(2,1)S(1)}, bf16[64,3584]{1,0:T(8,128)(2,1)S(1)}, u32[]{:S(2)}, u32[]{:S(2)}) collective-permute-start(bf16[64,3584]{1,0:T(8,128)(2,1)S(1)} %get-tuple-element.54), channel_id=1, source_target_pairs={{0,4},{2,6},{4,0},{6,2},{1,5},{3,7},{5,1},{7,3},{8,12},{10,14},{12... | collective-permute-start | bytes 1376264 | tf_op jit(solution)/shard_map/ppermute | solution.py:72
  26.2 23.6 %collective-permute-start.2 = (bf16[64,3584]{1,0:T(8,128)(2,1)S(1)}, bf16[64,3584]{1,0:T(8,128)(2,1)}, u32[]{:S(2)}, u32[]{:S(2)}) collective-permute-start(bf16[64,3584]{1,0:T(8,128)(2,1)S(1)} %get-tuple-element.53), channel_id=1, source_target_pairs={{0,6},{2,4},{4,2},{6,0},{1,7},{3,5},{5,3},{7,1},{8,14},{10,12},{12... | collective-permute-start | bytes 1376264 | tf_op jit(solution)/shard_map/ppermute | solution.py:72
  31.7 12.1 %copy-start.7 = (bf16[64,3584]{1,0:T(8,128)(2,1)}, bf16[64,3584]{1,0:T(8,128)(2,1)S(1)}, u32[]{:S(2)}) copy-start(bf16[64,3584]{1,0:T(8,128)(2,1)S(1)} %collective-permute-done) | copy-start | bytes 1376260
  43.7 0.8 copy-start.8
  50.3 6.4 %collective-permute-start.3 = (bf16[1024,448]{0,1:T(8,128)(2,1)S(1)}, bf16[1024,448]{0,1:T(8,128)(2,1)S(1)}, u32[]{:S(2)}, u32[]{:S(2)}) collective-permute-start(bf16[1024,448]{0,1:T(8,128)(2,1)S(1)} %copy.39), channel_id=1, source_target_pairs={{0,8},{8,0},{1,9},{9,1},{2,10},{10,2},{3,11},{11,3},{4,12},{12,4},... | collective-permute-start | bytes 2752520 | tf_op jit(solution)/shard_map/ppermute | solution.py:25
  56.7 10.1 %copy-start.4 = (bf16[1024,448]{0,1:T(8,128)(2,1)}, bf16[1024,448]{0,1:T(8,128)(2,1)S(1)}, u32[]{:S(2)}) copy-start(bf16[1024,448]{0,1:T(8,128)(2,1)S(1)} %collective-permute-done.3) | copy-start | bytes 2752516
  57.7 16.4 %copy-start.14 = (s32[32]{0:T(128)S(1)}, s32[32]{0:T(128)}, u32[]{:S(2)}) copy-start(s32[32]{0:T(128)} %param.13) | copy-start | bytes 388
  57.7 18.0 %all-to-all-start.1 = ((f32[8,32,256]{2,1,0:T(8,128)}), f32[8,32,256]{2,1,0:T(8,128)S(1)}, u32[]{:S(2)}, u32[]{:S(2)}) async-start(f32[8,32,256]{2,1,0:T(8,128)} %bitcast.113), calls=%async_computation.1 | async-start | bytes 524288 | tf_op jit(solution)/shard_map/all_to_all | solution.py:84
  66.8 17.5 %collective-permute-start.4 = (bf16[32,3584]{1,0:T(8,128)(2,1)S(1)}, bf16[32,3584]{1,0:T(8,128)(2,1)S(1)}, u32[]{:S(2)}, u32[]{:S(2)}) collective-permute-start(bf16[32,3584]{1,0:T(8,128)(2,1)S(1)} %slice.131), channel_id=1, source_target_pairs={{0,1},{1,0},{2,3},{3,2},{4,5},{5,4},{6,7},{7,6},{8,9},{9,8},{10,11... | collective-permute-start | bytes 688136 | tf_op jit(solution)/shard_map/ppermute | solution.py:79
  85.0 21.6 %all-to-all-start.2 = ((f32[8,32,256]{2,1,0:T(8,128)}), f32[8,32,256]{2,1,0:T(8,128)S(1)}, u32[]{:S(2)}, u32[]{:S(2)}) async-start(f32[8,32,256]{2,1,0:T(8,128)} %broadcast_in_dim.19), calls=%async_computation.2 | async-start | bytes 524288 | tf_op jit(solution)/shard_map/all_to_all | solution.py:37
  97.6 14.5 %collective-permute-start.5 = (bf16[32,3584]{1,0:T(8,128)(2,1)}, bf16[32,3584]{1,0:T(8,128)(2,1)}, u32[]{:S(2)}, u32[]{:S(2)}) collective-permute-start(bf16[32,3584]{1,0:T(8,128)(2,1)} %reshape.440), channel_id=1, source_target_pairs={{0,1},{1,0},{2,3},{3,2},{4,5},{5,4},{6,7},{7,6},{8,9},{9,8},{10,11... | collective-permute-start | bytes 688136 | tf_op jit(solution)/shard_map/ppermute | solution.py:89
  113.8 46.1 %collective-permute-start.6 = (bf16[64,3584]{1,0:T(8,128)(2,1)}, bf16[64,3584]{1,0:T(8,128)(2,1)}, u32[]{:S(2)}, u32[]{:S(2)}) collective-permute-start(bf16[64,3584]{1,0:T(8,128)(2,1)} %get-tuple-element.58), channel_id=1, source_target_pairs={{0,2},{2,0},{4,6},{6,4},{1,3},{3,1},{5,7},{7,5},{8,10},{10,8},{12,... | collective-permute-start | bytes 1376264 | tf_op jit(solution)/shard_map/ppermute | solution.py:93
  116.9 44.1 %collective-permute-start.7 = (bf16[64,3584]{1,0:T(8,128)(2,1)}, bf16[64,3584]{1,0:T(8,128)(2,1)}, u32[]{:S(2)}, u32[]{:S(2)}) collective-permute-start(bf16[64,3584]{1,0:T(8,128)(2,1)} %get-tuple-element.58), channel_id=1, source_target_pairs={{0,4},{2,6},{4,0},{6,2},{1,5},{3,7},{5,1},{7,3},{8,12},{10,14},{12... | collective-permute-start | bytes 1376264 | tf_op jit(solution)/shard_map/ppermute | solution.py:93
  121.2 40.8 %collective-permute-start.8 = (bf16[64,3584]{1,0:T(8,128)(2,1)}, bf16[64,3584]{1,0:T(8,128)(2,1)}, u32[]{:S(2)}, u32[]{:S(2)}) collective-permute-start(bf16[64,3584]{1,0:T(8,128)(2,1)} %get-tuple-element.58), channel_id=1, source_target_pairs={{0,6},{2,4},{4,2},{6,0},{1,7},{3,5},{5,3},{7,1},{8,14},{10,12},{12... | collective-permute-start | bytes 1376264 | tf_op jit(solution)/shard_map/ppermute | solution.py:93
  126.5 19.6 %all-to-all-start.3 = ((f32[8,8,448]{2,1,0:T(8,128)}), f32[8,8,448]{2,1,0:T(8,128)S(1)}, u32[]{:S(2)}, u32[]{:S(2)}) async-start(f32[8,8,448]{2,1,0:T(8,128)} %broadcast_in_dim.20), calls=%async_computation.3 | async-start | bytes 262144 | tf_op jit(solution)/shard_map/all_to_all | solution.py:37
  150.1 35.7 %all-to-all-start.5 = ((bf16[32,32,448]{2,1,0:T(8,128)(2,1)}), bf16[32,32,448]{2,1,0:T(8,128)(2,1)S(1)}, u32[]{:S(2)}, u32[]{:S(2)}) async-start(bf16[32,32,448]{2,1,0:T(8,128)(2,1)} %broadcast_in_dim.25), calls=%async_computation.5 | async-start | bytes 2097152 | tf_op jit(solution)/shard_map/all_to_all | solution.py:37
  165.0 1.3 copy-start.1
  166.3 5.9 %copy-start.10 = (bf16[32,1024]{1,0:T(8,128)(2,1)S(1)}, bf16[32,1024]{1,0:T(8,128)(2,1)}, u32[]{:S(2)}) copy-start(bf16[32,1024]{1,0:T(8,128)(2,1)} %get-tuple-element.63) | copy-start | bytes 196612
  167.3 14.1 %collective-permute-start.9 = (bf16[256,1792]{1,0:T(8,128)(2,1)}, bf16[256,1792]{1,0:T(8,128)(2,1)}, u32[]{:S(2)}, u32[]{:S(2)}) collective-permute-start(bf16[256,1792]{1,0:T(8,128)(2,1)} %constant_dynamic-slice_fusion), channel_id=1, source_target_pairs={{0,8},{8,0},{1,9},{9,1},{2,10},{10,2},{3,11},{11,3},{4,12},{12,4},... | collective-permute-start | bytes 2752520 | tf_op jit(solution)/shard_map/ppermute | solution.py:25
  172.2 4.7 %collective-permute-start.11 = (bf16[40,1024]{1,0:T(8,128)(2,1)S(1)}, bf16[40,1024]{1,0:T(8,128)(2,1)S(1)}, u32[]{:S(2)}, u32[]{:S(2)}) collective-permute-start(bf16[40,1024]{1,0:T(8,128)(2,1)S(1)} %fusion.15), channel_id=1, source_target_pairs={{0,8},{8,0},{1,9},{9,1},{2,10},{10,2},{3,11},{11,3},{4,12},{12,4},... | collective-permute-start | bytes 245768 | tf_op jit(solution)/shard_map/ppermute | solution.py:25
  174.1 7.3 %collective-permute-start.10 = (bf16[256,256]{1,0:T(8,128)(2,1)}, bf16[256,256]{1,0:T(8,128)(2,1)}, u32[]{:S(2)}, u32[]{:S(2)}) collective-permute-start(bf16[256,256]{1,0:T(8,128)(2,1)} %fusion.14), channel_id=1, source_target_pairs={{0,8},{8,0},{1,9},{9,1},{2,10},{10,2},{3,11},{11,3},{4,12},{12,4},... | collective-permute-start | bytes 393224 | tf_op jit(solution)/shard_map/ppermute | solution.py:25
  181.4 1.8 copy-start.2
  183.2 1.4 copy-start.6
  185.8 39.5 %all-to-all-start.4 = ((bf16[32,72,256]{2,1,0:T(8,128)(2,1)}), bf16[32,72,256]{2,1,0:T(8,128)(2,1)}, u32[]{:S(2)}, u32[]{:S(2)}) async-start(bf16[32,72,256]{2,1,0:T(8,128)(2,1)} %pad_maximum_fusion), calls=%async_computation.4 | async-start | bytes 2359296 | tf_op jit(solution)/shard_map/all_to_all | solution.py:136
  204.1 26.8 %collective-permute-start.12 = (bf16[1024,448]{0,1:T(8,128)(2,1)}, bf16[1024,448]{0,1:T(8,128)(2,1)}, u32[]{:S(2)}, u32[]{:S(2)}) collective-permute-start(bf16[1024,448]{0,1:T(8,128)(2,1)} %copy.50), channel_id=1, source_target_pairs={{0,8},{8,0},{1,9},{9,1},{2,10},{10,2},{3,11},{11,3},{4,12},{12,4},... | collective-permute-start | bytes 2752520 | tf_op jit(solution)/shard_map/ppermute | solution.py:25
  (2 other events, 1.3 us)

commit v3 on v2

--- a/solution.py
+++ b/solution.py
@@ -42,12 +42,8 @@
 
 
 def by_xor(value, index):
-    shape = value.shape
-    for bit in (1, 2, 4):
-        pairs = value.reshape((N_T // (2 * bit), 2, bit) + shape[1:])
-        flipped = pairs[:, ::-1].reshape(shape)
-        value = jnp.where((index & bit) != 0, flipped, value)
-    return value
+    parts = [lax.dynamic_slice_in_dim(value, r ^ index, 1, 0) for r in range(value.shape[0])]
+    return jnp.concatenate(parts, axis=0)
 
 
 def core_major(value):
@@ -62,35 +58,30 @@
     tokens, heads = attn_heads.shape
     half = N_P * rows
     core = lax.axis_index("c")
-    t_index = lax.axis_index(TENSOR)
     x_block = tokens // 4
-    own_tokens = tokens // N_T
 
-    attn = by_xor(attn_heads.reshape(N_T, own_tokens, heads), t_index).reshape(tokens, heads)
+    x_index = lax.axis_index("x")
+    attn = by_xor(attn_heads.reshape(4, x_block, heads), x_index).reshape(tokens, heads)
     mixed = dot(attn, out_proj, ((1,), (0,))).astype(BF16)
     from_x = [
         lax.ppermute(mixed[k * x_block : (k + 1) * x_block], **xor("x", 4, k)) for k in (1, 2, 3)
     ]
 
+    mixed_x = mixed[:x_block].astype(F32) + sum(part.astype(F32) for part in from_x)
+    from_z = lax.ppermute(mixed_x.astype(BF16), **xor("zh", 2, 1))
+    residual_x = lax.dynamic_slice_in_dim(residual, x_index * x_block, x_block, 0)
+    hidden_x = core_major((mixed_x + from_z.astype(F32) + residual_x.astype(F32)).astype(BF16))
+    hidden_x = [hidden_x] + [lax.ppermute(hidden_x, **xor("x", 4, k)) for k in (1, 2, 3)]
+
+    items = lax.all_gather(item_cache, DP, axis=0, tiled=True)
     users_own = to_all(user_cache, PLANE, N_P).reshape(half, feats)
-    users_own, *from_x = lax.optimization_barrier((users_own, *from_x))
     users = (users_own, swap(users_own))
-    mixed_x = mixed[:x_block].astype(F32) + sum(part.astype(F32) for part in from_x)
-    from_z = lax.ppermute(mixed_x[own_tokens:].astype(BF16), **xor("zh", 2, 1))
 
     partial = jnp.concatenate([dot(item_cache, u, ((1,), (1,))) for u in users], axis=1)
     share = 2 * half // N_T
     partial = partial.reshape(rows, N_T, share).transpose(1, 0, 2)
     scores_own = jnp.sum(lax.all_to_all(partial, TENSOR, 0, 0), axis=0) * LOGIT_SCALE
-    scores_own, from_z = lax.optimization_barrier((scores_own, from_z))
-    own_residual = lax.dynamic_slice_in_dim(residual, t_index * own_tokens, own_tokens, 0)
-    hidden_own = mixed_x[:own_tokens] + from_z.astype(F32) + own_residual.astype(F32)
-    hidden_own = core_major(hidden_own.astype(BF16))
-    hidden_z = lax.ppermute(hidden_own, **xor("zh", 2, 1))
     scores = to_all(scores_own, TENSOR, N_T).transpose(1, 0, 2).reshape(rows, 2 * half)
-    scores, hidden_z = lax.optimization_barrier((scores, hidden_z))
-    hidden_x = jnp.concatenate([hidden_own, hidden_z], axis=0)
-    hidden_x = [hidden_x] + [lax.ppermute(hidden_x, **xor("x", 4, k)) for k in (1, 2, 3)]
 
     owner, row_in = positive // rows, positive % rows
     column = (owner % 2 != core).astype(jnp.int32) * half + (owner // 2) * rows + row_in
@@ -105,10 +96,10 @@
     ) * LOGIT_SCALE
 
     group_rows = to_all(item_grad[:GROUP], TENSOR, N_T)
-    item_cache, group_rows = lax.optimization_barrier((item_cache, group_rows))
-    items_own = to_all(item_cache, PLANE, N_P).reshape(half, feats)
     group_rows = core_major(group_rows.transpose(1, 0, 2).reshape(GROUP, width))
-    upstream = core_major(norm_gain)[None, :] * (by_xor(group_rows, t_index) / SEQ)
+    upstream = core_major(norm_gain)[None, :] * (
+        by_xor(group_rows.reshape(4, -1), x_index).reshape(GROUP, width) / SEQ
+    )
     hidden = jnp.concatenate(hidden_x, axis=0).reshape(GROUP, SEQ, width).astype(F32)
     inverse = lax.rsqrt(jnp.mean(hidden * hidden, axis=2, keepdims=True) + NORM_EPS)
     inner = jnp.sum(upstream[:, None, :] * hidden, axis=2, keepdims=True) / width
@@ -125,6 +116,7 @@
     weight = dot(stream_keep, attn, ((0,), (0,))) + dot(stream_other, attn_other, ((0,), (0,)))
     weight = weight.astype(BF16).reshape(N_P, cut, heads)
     both = jnp.stack([grad[:, :half], other[:rows]])
+    both = jnp.where(core == 0, both, both[::-1])
     both = both.reshape(2, rows, N_P, rows).transpose(2, 0, 1, 3)
     losses = jnp.concatenate([losses, other[rows, : 3 * rows]])
     losses = jnp.zeros((8, heads), BF16).at[0, : 6 * rows].set(losses)
@@ -136,15 +128,11 @@
     final = lax.all_to_all(final, PLANE, 0, 0)
     out_proj = core_major(out_proj)
     head_grad = dot(stream, out_proj, ((1,), (1,))).astype(BF16)
-    head_grad = by_xor(head_grad.reshape(N_T, own_tokens, heads), t_index).reshape(tokens, heads)
+    head_grad = by_xor(head_grad.reshape(4, x_block, heads), x_index).reshape(tokens, heads)
     weight_grad = jnp.sum(final[:, :cut].astype(F32), axis=0).T
     loss_mean = jnp.sum(final[:, cut + tile].astype(F32)) / (2 * half)
-    by_user = final[:, cut : cut + tile].reshape(N_P, 2, rows, rows)
-    items = (items_own, swap(items_own))
-    user_grad = (
-        dot(by_user[:, 0].reshape(half, rows), items[0], ((0,), (0,)))
-        + dot(by_user[:, 1].reshape(half, rows), items[1], ((0,), (0,)))
-    ) * LOGIT_SCALE
+    by_user = final[:, cut : cut + tile].reshape(2 * half, rows)
+    user_grad = dot(by_user, items, ((0,), (0,))) * LOGIT_SCALE
     return (loss_mean, item_grad, user_grad, head_grad, weight_grad)
 
 

time: 238 us -> 248 us (1.042)
  starting transfers between devices: 108 us -> 86.3 us
  between operations: 3.18 us -> 16.5 us
  waiting for transfers between devices: 66.3 us -> 78.3 us
  other arithmetic: 12.5 us -> 23.5 us
  local copies, waits for them, and re-layouts: 34.1 us -> 28.1 us
    all_to_all x4 -> x3, starting transfers between devices: 41 us -> 19.7 us  [to_all(): lax.all_to_all(jnp.broadcast_to(value[None], (count,) + value.shape), axe...]
    ppermute x3, waiting for transfers between devices: 0.01 us -> 16.9 us  [per_device(): lax.ppermute(hidden_x, **xor('x', 4, k))]
    ppermute x3, waiting for transfers between devices: 20.7 us -> 6.38 us  [per_device(): lax.ppermute(mixed[k * x_block:(k + 1) * x_block], **xor('x', 4, k))]
    all_to_all x4 -> x3, waiting for transfers between devices: 10.2 us -> 17.3 us  [to_all(): lax.all_to_all(jnp.broadcast_to(value[None], (count,) + value.shape), axe...]
    unnamed x34 -> x45, local copies, waits for them, and re-layouts: 10.3 us -> 3.88 us
    convert_element_type x1 -> x3, other arithmetic: 1.01 us -> 6.36 us  [the longest x1 2.26 us: per_device(): jnp.concatenate(hidden_x, axis=0).reshape(GROUP, SEQ, width).astype(F32)]
    ppermute x5 -> x4, starting transfers between devices: 15.8 us -> 20.1 us  [swap(): return lax.ppermute(value, **xor('c', 2, 1))]
    all_to_all x1, starting transfers between devices: 7.44 us -> 3.62 us  [per_device(): lax.all_to_all(partial, TENSOR, 0, 0)]
  transfers between devices with their start and end apart: 19 -> 17, of which waited for: 9 -> 8; matrix products, arithmetic and copies ran while one was open for 20% -> 23% of each run, Pallas kernels for 0% -> 0%
where the time goes in v3:
time: 248 us; the launch traced here: 244 us
  starting transfers between devices  86.3 us (35%)
  waiting for transfers between devices  78.3 us (32%)
  local copies, waits for them, and re-layouts  28.1 us (11%)
  other arithmetic  23.5 us (9%)
  between operations  16.5 us (7%)
  matrix products  11.3 us (5%)
    all_to_all x1, waiting for transfers between devices, per_device(): final = lax.all_to_all(final, PLANE, 0, 0)  21.1 us
    ppermute x4, starting transfers between devices, swap(): return lax.ppermute(value, **xor('c', 2, 1))  20.1 us
    all_to_all x3, starting transfers between devices, to_all(): lax.all_to_all(jnp.broadcast_to(value[None], (count,) + value.shape), axe...  19.7 us
    all_to_all x3, waiting for transfers between devices, to_all(): lax.all_to_all(jnp.broadcast_to(value[None], (count,) + value.shape), axe...  17.3 us
    ppermute x3, waiting for transfers between devices, per_device(): lax.ppermute(hidden_x, **xor('x', 4, k))  16.9 us
    ppermute x1, waiting for transfers between devices, per_device(): from_z = lax.ppermute(mixed_x.astype(BF16), **xor('zh', 2, 1))  16.6 us
    ppermute x1, starting transfers between devices, per_device(): from_z = lax.ppermute(mixed_x.astype(BF16), **xor('zh', 2, 1))  12.2 us
    dot_general x9, matrix products, dot(): return lax.dot_general(a, b, (dims, ((), ())), preferred_element_type=F32)  11.3 us
  transfers between devices with their start and end apart: 17, of which 8 were waited for; matrix products, arithmetic and copies ran while one was open for 23% of the time, Pallas kernels for 0%

profile of v3, /device:TPU:1, one launch (start us, length us, event | category | flops | bytes accessed | tf_op | source)
XLA Modules:
  0.0 244.0 jit_solution(8018109603402792605)
XLA Ops:
  8.0 2.1 convolution_convert_fusion
  11.3 3.9 %collective-permute-start = (bf16[64,3584]{1,0:T(8,128)(2,1)}, bf16[64,3584]{1,0:T(8,128)(2,1)S(1)}, u32[]{:S(2)}, u32[]{:S(2)}) collective-permute-start(bf16[64,3584]{1,0:T(8,128)(2,1)} %get-tuple-element.33), channel_id=1, source_target_pairs={{0,2},{2,0},{4,6},{6,4},{1,3},{3,1},{5,7},{7,5},{8,10},{10,8},{12,... | collective-permute-start | bytes 1376264 | tf_op jit(solution)/shard_map/ppermute | solution.py:67
  15.3 4.4 %collective-permute-start.1 = (bf16[64,3584]{1,0:T(8,128)(2,1)}, bf16[64,3584]{1,0:T(8,128)(2,1)}, u32[]{:S(2)}, u32[]{:S(2)}) collective-permute-start(bf16[64,3584]{1,0:T(8,128)(2,1)} %get-tuple-element.35), channel_id=1, source_target_pairs={{0,4},{2,6},{4,0},{6,2},{1,5},{3,7},{5,1},{7,3},{8,12},{10,14},{12... | collective-permute-start | bytes 1376264 | tf_op jit(solution)/shard_map/ppermute | solution.py:67
  22.7 13.0 %all-to-all-start = ((bf16[32,32,448]{2,1,0:T(8,128)(2,1)}), bf16[32,32,448]{2,1,0:T(8,128)(2,1)S(1)}, u32[]{:S(2)}, u32[]{:S(2)}) async-start(bf16[32,32,448]{2,1,0:T(8,128)(2,1)} %broadcast_in_dim.16), calls=%async_computation | async-start | bytes 2097152 | tf_op jit(solution)/shard_map/all_to_all | solution.py:37
  37.8 4.3 %collective-permute-done.2 = bf16[64,3584]{1,0:T(8,128)(2,1)} collective-permute-done((bf16[64,3584]{1,0:T(8,128)(2,1)}, bf16[64,3584]{1,0:T(8,128)(2,1)}, u32[]{:S(2)}, u32[]{:S(2)}) %collective-permute-start.2) | collective-permute-done | bytes 458784 | tf_op jit(solution)/shard_map/ppermute | solution.py:67
  42.1 2.2 fusion.9
  44.3 12.2 %collective-permute-start.3 = (bf16[64,3584]{1,0:T(8,128)(2,1)}, bf16[64,3584]{1,0:T(8,128)(2,1)}, u32[]{:S(2)}, u32[]{:S(2)}) collective-permute-start(bf16[64,3584]{1,0:T(8,128)(2,1)} %fusion.9), channel_id=1, source_target_pairs={{0,1},{1,0},{2,3},{3,2},{4,5},{5,4},{6,7},{7,6},{8,9},{9,8},{10,11... | collective-permute-start | bytes 1376264 | tf_op jit(solution)/shard_map/ppermute | solution.py:71
  56.4 4.4 %collective-permute-start.9 = (bf16[256,256]{1,0:T(8,128)(2,1)S(1)}, bf16[256,256]{1,0:T(8,128)(2,1)}, u32[]{:S(2)}, u32[]{:S(2)}) collective-permute-start(bf16[256,256]{1,0:T(8,128)(2,1)S(1)} %bitcast.86), channel_id=1, source_target_pairs={{0,8},{8,0},{1,9},{9,1},{2,10},{10,2},{3,11},{11,3},{4,12},{12,4},... | collective-permute-start | bytes 393224 | tf_op jit(solution)/shard_map/ppermute | solution.py:25
  62.7 7.2 %collective-permute-start.7 = (bf16[1024,448]{0,1:T(8,128)(2,1)}, bf16[1024,448]{0,1:T(8,128)(2,1)}, u32[]{:S(2)}, u32[]{:S(2)}) collective-permute-start(bf16[1024,448]{0,1:T(8,128)(2,1)} %copy.33), channel_id=1, source_target_pairs={{0,8},{8,0},{1,9},{9,1},{2,10},{10,2},{3,11},{11,3},{4,12},{12,4},... | collective-permute-start | bytes 2752520 | tf_op jit(solution)/shard_map/ppermute | solution.py:25
  69.9 16.6 %collective-permute-done.3 = bf16[64,3584]{1,0:T(8,128)(2,1)} collective-permute-done((bf16[64,3584]{1,0:T(8,128)(2,1)}, bf16[64,3584]{1,0:T(8,128)(2,1)}, u32[]{:S(2)}, u32[]{:S(2)}) %collective-permute-start.3) | collective-permute-done | bytes 458784 | tf_op jit(solution)/shard_map/ppermute | solution.py:71
  88.4 2.1 reshape.282
  91.7 2.6 %reshape.283 = bf16[64,3584]{1,0:T(8,128)(2,1)S(1)} reshape(bf16[64,2,32,56]{3,2,1,0:T(8,128)(2,1)} %copy.32) | data formatting | bytes 917504 | tf_op jit(solution)/shard_map/reshape | solution.py:52
  96.3 5.4 %collective-permute-start.5 = (bf16[64,3584]{1,0:T(8,128)(2,1)S(1)}, bf16[64,3584]{1,0:T(8,128)(2,1)S(1)}, u32[]{:S(2)}, u32[]{:S(2)}) collective-permute-start(bf16[64,3584]{1,0:T(8,128)(2,1)S(1)} %reshape.283), channel_id=1, source_target_pairs={{0,4},{2,6},{4,0},{6,2},{1,5},{3,7},{5,1},{7,3},{8,12},{10,14},{12... | collective-permute-start | bytes 1376264 | tf_op jit(solution)/shard_map/ppermute | solution.py:74
  101.7 2.2 collective-permute-start.6
  106.6 3.6 %all-to-all-start.1 = ((f32[8,32,256]{2,1,0:T(8,128)}), f32[8,32,256]{2,1,0:T(8,128)S(1)}, u32[]{:S(2)}, u32[]{:S(2)}) async-start(f32[8,32,256]{2,1,0:T(8,128)} %bitcast.88), calls=%async_computation.1 | async-start | bytes 524288 | tf_op jit(solution)/shard_map/all_to_all | solution.py:83
  110.4 8.8 %collective-permute-done.5 = bf16[64,3584]{1,0:T(8,128)(2,1)S(1)} collective-permute-done((bf16[64,3584]{1,0:T(8,128)(2,1)S(1)}, bf16[64,3584]{1,0:T(8,128)(2,1)S(1)}, u32[]{:S(2)}, u32[]{:S(2)}) %collective-permute-start.5) | collective-permute-done | bytes 458784 | tf_op jit(solution)/shard_map/ppermute | solution.py:74
  119.3 8.1 %collective-permute-done.6 = bf16[64,3584]{1,0:T(8,128)(2,1)S(1)} collective-permute-done((bf16[64,3584]{1,0:T(8,128)(2,1)S(1)}, bf16[64,3584]{1,0:T(8,128)(2,1)S(1)}, u32[]{:S(2)}, u32[]{:S(2)}) %collective-permute-start.6) | collective-permute-done | bytes 458784 | tf_op jit(solution)/shard_map/ppermute | solution.py:74
  129.2 3.4 %all-to-all-start.2 = ((f32[8,32,256]{2,1,0:T(8,128)}), f32[8,32,256]{2,1,0:T(8,128)S(1)}, u32[]{:S(2)}, u32[]{:S(2)}) async-start(f32[8,32,256]{2,1,0:T(8,128)} %broadcast_in_dim.17), calls=%async_computation.2 | async-start | bytes 524288 | tf_op jit(solution)/shard_map/all_to_all | solution.py:37
  132.6 2.3 maximum_convert_fusion
  134.9 8.0 %all-to-all-done.2 = f32[8,32,256]{2,1,0:T(8,128)S(1)} async-done(((f32[8,32,256]{2,1,0:T(8,128)}), f32[8,32,256]{2,1,0:T(8,128)S(1)}, u32[]{:S(2)}, u32[]{:S(2)}) %all-to-all-start.2) | async-done | bytes 262176 | tf_op jit(solution)/shard_map/all_to_all | solution.py:37
  145.6 5.6 %collective-permute-start.10 = (bf16[40,1024]{1,0:T(8,128)(2,1)S(1)}, bf16[40,1024]{1,0:T(8,128)(2,1)S(1)}, u32[]{:S(2)}, u32[]{:S(2)}) collective-permute-start(bf16[40,1024]{1,0:T(8,128)(2,1)S(1)} %fusion.11), channel_id=1, source_target_pairs={{0,8},{8,0},{1,9},{9,1},{2,10},{10,2},{3,11},{11,3},{4,12},{12,4},... | collective-permute-start | bytes 245768 | tf_op jit(solution)/shard_map/ppermute | solution.py:25
  153.4 3.4 %all-to-all-start.3 = ((f32[8,8,448]{2,1,0:T(8,128)}), f32[8,8,448]{2,1,0:T(8,128)S(1)}, u32[]{:S(2)}, u32[]{:S(2)}) async-start(f32[8,8,448]{2,1,0:T(8,128)} %broadcast_in_dim.18), calls=%async_computation.3 | async-start | bytes 262144 | tf_op jit(solution)/shard_map/all_to_all | solution.py:37
  157.5 9.3 %all-to-all-done.3 = f32[8,8,448]{2,1,0:T(8,128)S(1)} async-done(((f32[8,8,448]{2,1,0:T(8,128)}), f32[8,8,448]{2,1,0:T(8,128)S(1)}, u32[]{:S(2)}, u32[]{:S(2)}) %all-to-all-start.3) | async-done | bytes 114720 | tf_op jit(solution)/shard_map/all_to_all | solution.py:37
  167.9 2.4 multiply_reduce_fusion
  170.4 3.0 %fusion.1 = bf16[256,3584]{1,0:T(8,128)(2,1)S(1)} fusion(f32[256]{0:T(256)S(1)} %fusion.17, f32[8,3584]{1,0:T(8,128)S(1)} %broadcast_multiply_fusion, f32[256]{0:T(256)} %copy-done.11, bf16[64,3584]{1,0:T(8,128)(2,1)} %copy-done, bf16[64,3584]{1,0:T(8,128)(2,1)S(1)} %collective-permute-done.5, bf16[64,3584]{1,0:T(8,128)(2,1)S(1)} %collective-permute-done.4, ...), kind=kLoop, calls=%fused_computation.3 | loop fusion | flops 11010048 | bytes 3786752 | tf_op jit(solution)/shard_map/convert_element_type | solution.py:107
  174.5 2.9 %collective-permute-start.8 = (bf16[256,1792]{1,0:T(8,128)(2,1)}, bf16[256,1792]{1,0:T(8,128)(2,1)}, u32[]{:S(2)}, u32[]{:S(2)}) collective-permute-start(bf16[256,1792]{1,0:T(8,128)(2,1)} %constant_dynamic-slice_fusion.4), channel_id=1, source_target_pairs={{0,8},{8,0},{1,9},{9,1},{2,10},{10,2},{3,11},{11,3},{4,12},{12,4},... | collective-permute-start | bytes 2752520 | tf_op jit(solution)/shard_map/ppermute | solution.py:25
  182.9 2.1 reshape.291
  188.4 10.8 %all-to-all-start.4 = ((bf16[32,72,256]{2,1,0:T(8,128)(2,1)}), bf16[32,72,256]{2,1,0:T(8,128)(2,1)}, u32[]{:S(2)}, u32[]{:S(2)}) async-start(bf16[32,72,256]{2,1,0:T(8,128)(2,1)} %pad_maximum_fusion), calls=%async_computation.4 | async-start | bytes 2359296 | tf_op jit(solution)/shard_map/all_to_all | solution.py:128
  199.3 2.9 %copy.40 = bf16[256,3584]{0,1:T(8,128)(2,1)S(1)} copy(bf16[256,3584]{1,0:T(8,128)(2,1)} %param.16) | data formatting | bytes 3670016 | tf_op args[5]
  203.2 2.3 subtract_convert_fusion
  206.8 21.1 %all-to-all-done.4 = bf16[32,72,256]{2,1,0:T(8,128)(2,1)} async-done(((bf16[32,72,256]{2,1,0:T(8,128)(2,1)}), bf16[32,72,256]{2,1,0:T(8,128)(2,1)}, u32[]{:S(2)}, u32[]{:S(2)}) %all-to-all-start.4) | async-done | bytes 1179680 | tf_op jit(solution)/shard_map/all_to_all | solution.py:128
  233.3 2.7 %convolution_multiply_fusion = f32[32,448]{1,0:T(8,128)} fusion(bf16[2048,32]{1,0:T(8,128)(2,1)S(1)} %reshape.292, bf16[2048,448]{1,0:T(8,128)(2,1)} %all-gather.2.cloned.1.call-done), kind=kOutput, calls=%fused_computation.15 | convolution fusion | flops 58734592 | bytes 2023424 | tf_op jit(solution)/shard_map/dot_general | solution.py:41
  (127 shorter events, 42.3 us)
Async XLA Ops:
  10.2 11.4 %copy-start.9 = (bf16[32,448]{1,0:T(8,128)(2,1)S(1)}, bf16[32,448]{1,0:T(8,128)(2,1)}, u32[]{:S(2)}) copy-start(bf16[32,448]{1,0:T(8,128)(2,1)} %param.12) | copy-start | bytes 86020
  11.3 24.4 %collective-permute-start = (bf16[64,3584]{1,0:T(8,128)(2,1)}, bf16[64,3584]{1,0:T(8,128)(2,1)S(1)}, u32[]{:S(2)}, u32[]{:S(2)}) collective-permute-start(bf16[64,3584]{1,0:T(8,128)(2,1)} %get-tuple-element.33), channel_id=1, source_target_pairs={{0,2},{2,0},{4,6},{6,4},{1,3},{3,1},{5,7},{7,5},{8,10},{10,8},{12,... | collective-permute-start | bytes 1376264 | tf_op jit(solution)/shard_map/ppermute | solution.py:67
  15.3 22.5 %collective-permute-start.1 = (bf16[64,3584]{1,0:T(8,128)(2,1)}, bf16[64,3584]{1,0:T(8,128)(2,1)}, u32[]{:S(2)}, u32[]{:S(2)}) collective-permute-start(bf16[64,3584]{1,0:T(8,128)(2,1)} %get-tuple-element.35), channel_id=1, source_target_pairs={{0,4},{2,6},{4,0},{6,2},{1,5},{3,7},{5,1},{7,3},{8,12},{10,14},{12... | collective-permute-start | bytes 1376264 | tf_op jit(solution)/shard_map/ppermute | solution.py:67
  19.6 22.5 %collective-permute-start.2 = (bf16[64,3584]{1,0:T(8,128)(2,1)}, bf16[64,3584]{1,0:T(8,128)(2,1)}, u32[]{:S(2)}, u32[]{:S(2)}) collective-permute-start(bf16[64,3584]{1,0:T(8,128)(2,1)} %get-tuple-element.34), channel_id=1, source_target_pairs={{0,6},{2,4},{4,2},{6,0},{1,7},{3,5},{5,3},{7,1},{8,14},{10,12},{12... | collective-permute-start | bytes 1376264 | tf_op jit(solution)/shard_map/ppermute | solution.py:67
  22.7 38.2 %copy-start.21 = (s32[32]{0:T(128)S(1)}, s32[32]{0:T(128)}, u32[]{:S(2)}) copy-start(s32[32]{0:T(128)} %param.13) | copy-start | bytes 388
  22.7 38.7 %copy-start.10 = (f32[3584]{0:T(1024)S(1)}, f32[3584]{0:T(1024)}, u32[]{:S(2)}) copy-start(f32[3584]{0:T(1024)} %param.17) | copy-start | bytes 43012
  22.7 38.7 %all-to-all-start = ((bf16[32,32,448]{2,1,0:T(8,128)(2,1)}), bf16[32,32,448]{2,1,0:T(8,128)(2,1)S(1)}, u32[]{:S(2)}, u32[]{:S(2)}) async-start(bf16[32,32,448]{2,1,0:T(8,128)(2,1)} %broadcast_in_dim.16), calls=%async_computation | async-start | bytes 2097152 | tf_op jit(solution)/shard_map/all_to_all | solution.py:37
  35.6 197.7 %all-gather.2.cloned.1.call-start = ((), (), s32[]{:S(2)}) async-start(), calls=%async_computation.5 | async-start | bytes 2129920 | tf_op jit(solution)/shard_map/all_gather | solution.py:76
  35.7 27.0 %copy-start.2 = (bf16[64,3584]{1,0:T(8,128)(2,1)}, bf16[64,3584]{1,0:T(8,128)(2,1)S(1)}, u32[]{:S(2)}) copy-start(bf16[64,3584]{1,0:T(8,128)(2,1)S(1)} %collective-permute-done) | copy-start | bytes 1376260
  44.3 42.2 %collective-permute-start.3 = (bf16[64,3584]{1,0:T(8,128)(2,1)}, bf16[64,3584]{1,0:T(8,128)(2,1)}, u32[]{:S(2)}, u32[]{:S(2)}) collective-permute-start(bf16[64,3584]{1,0:T(8,128)(2,1)} %fusion.9), channel_id=1, source_target_pairs={{0,1},{1,0},{2,3},{3,2},{4,5},{5,4},{6,7},{7,6},{8,9},{9,8},{10,11... | collective-permute-start | bytes 1376264 | tf_op jit(solution)/shard_map/ppermute | solution.py:71
  56.4 129.1 %collective-permute-start.9 = (bf16[256,256]{1,0:T(8,128)(2,1)S(1)}, bf16[256,256]{1,0:T(8,128)(2,1)}, u32[]{:S(2)}, u32[]{:S(2)}) collective-permute-start(bf16[256,256]{1,0:T(8,128)(2,1)S(1)} %bitcast.86), channel_id=1, source_target_pairs={{0,8},{8,0},{1,9},{9,1},{2,10},{10,2},{3,11},{11,3},{4,12},{12,4},... | collective-permute-start | bytes 393224 | tf_op jit(solution)/shard_map/ppermute | solution.py:25
  62.7 41.7 %collective-permute-start.7 = (bf16[1024,448]{0,1:T(8,128)(2,1)}, bf16[1024,448]{0,1:T(8,128)(2,1)}, u32[]{:S(2)}, u32[]{:S(2)}) collective-permute-start(bf16[1024,448]{0,1:T(8,128)(2,1)} %copy.33), channel_id=1, source_target_pairs={{0,8},{8,0},{1,9},{9,1},{2,10},{10,2},{3,11},{11,3},{4,12},{12,4},... | collective-permute-start | bytes 2752520 | tf_op jit(solution)/shard_map/ppermute | solution.py:25
  90.5 13.4 %copy-start.5 = (bf16[32,448]{1,0:T(8,128)(2,1)S(1)}, bf16[32,448]{1,0:T(8,128)(2,1)}, u32[]{:S(2)}) copy-start(bf16[32,448]{1,0:T(8,128)(2,1)} %param.11) | copy-start | bytes 86020
  94.3 16.1 %collective-permute-start.4 = (bf16[64,3584]{1,0:T(8,128)(2,1)S(1)}, bf16[64,3584]{1,0:T(8,128)(2,1)S(1)}, u32[]{:S(2)}, u32[]{:S(2)}) collective-permute-start(bf16[64,3584]{1,0:T(8,128)(2,1)S(1)} %reshape.283), channel_id=1, source_target_pairs={{0,2},{2,0},{4,6},{6,4},{1,3},{3,1},{5,7},{7,5},{8,10},{10,8},{12,... | collective-permute-start | bytes 1376264 | tf_op jit(solution)/shard_map/ppermute | solution.py:74
  96.3 23.0 %collective-permute-start.5 = (bf16[64,3584]{1,0:T(8,128)(2,1)S(1)}, bf16[64,3584]{1,0:T(8,128)(2,1)S(1)}, u32[]{:S(2)}, u32[]{:S(2)}) collective-permute-start(bf16[64,3584]{1,0:T(8,128)(2,1)S(1)} %reshape.283), channel_id=1, source_target_pairs={{0,4},{2,6},{4,0},{6,2},{1,5},{3,7},{5,1},{7,3},{8,12},{10,14},{12... | collective-permute-start | bytes 1376264 | tf_op jit(solution)/shard_map/ppermute | solution.py:74
  101.7 25.6 %collective-permute-start.6 = (bf16[64,3584]{1,0:T(8,128)(2,1)S(1)}, bf16[64,3584]{1,0:T(8,128)(2,1)S(1)}, u32[]{:S(2)}, u32[]{:S(2)}) collective-permute-start(bf16[64,3584]{1,0:T(8,128)(2,1)S(1)} %reshape.283), channel_id=1, source_target_pairs={{0,6},{2,4},{4,2},{6,0},{1,7},{3,5},{5,3},{7,1},{8,14},{10,12},{12... | collective-permute-start | bytes 1376264 | tf_op jit(solution)/shard_map/ppermute | solution.py:74
  106.6 21.9 %all-to-all-start.1 = ((f32[8,32,256]{2,1,0:T(8,128)}), f32[8,32,256]{2,1,0:T(8,128)S(1)}, u32[]{:S(2)}, u32[]{:S(2)}) async-start(f32[8,32,256]{2,1,0:T(8,128)} %bitcast.88), calls=%async_computation.1 | async-start | bytes 524288 | tf_op jit(solution)/shard_map/all_to_all | solution.py:83
  127.3 25.4 %copy-start = (bf16[64,3584]{1,0:T(8,128)(2,1)}, bf16[64,3584]{1,0:T(8,128)(2,1)S(1)}, u32[]{:S(2)}) copy-start(bf16[64,3584]{1,0:T(8,128)(2,1)S(1)} %collective-permute-done.6) | copy-start | bytes 1376260
  127.8 7.2 %copy-start.12 = (f32[256]{0:T(256)}, f32[256]{0:T(256)S(1)}, u32[]{:S(2)}) copy-start(f32[256]{0:T(256)S(1)} %multiply_reduce_fusion.1) | copy-start | bytes 3076
  127.8 7.1 %copy-start.11 = (f32[256]{0:T(256)}, f32[256]{0:T(256)S(1)}, u32[]{:S(2)}) copy-start(f32[256]{0:T(256)S(1)} %add_rsqrt_fusion) | copy-start | bytes 3076
  129.2 13.7 %all-to-all-start.2 = ((f32[8,32,256]{2,1,0:T(8,128)}), f32[8,32,256]{2,1,0:T(8,128)S(1)}, u32[]{:S(2)}, u32[]{:S(2)}) async-start(f32[8,32,256]{2,1,0:T(8,128)} %broadcast_in_dim.17), calls=%async_computation.2 | async-start | bytes 524288 | tf_op jit(solution)/shard_map/all_to_all | solution.py:37
  132.6 11.1 %copy-start.20 = (s32[32]{0:T(128)S(1)}, s32[32]{0:T(128)}, u32[]{:S(2)}) copy-start(s32[32]{0:T(128)} %fusion.18) | copy-start | bytes 388
  145.6 11.2 %collective-permute-start.10 = (bf16[40,1024]{1,0:T(8,128)(2,1)S(1)}, bf16[40,1024]{1,0:T(8,128)(2,1)S(1)}, u32[]{:S(2)}, u32[]{:S(2)}) collective-permute-start(bf16[40,1024]{1,0:T(8,128)(2,1)S(1)} %fusion.11), channel_id=1, source_target_pairs={{0,8},{8,0},{1,9},{9,1},{2,10},{10,2},{3,11},{11,3},{4,12},{12,4},... | collective-permute-start | bytes 245768 | tf_op jit(solution)/shard_map/ppermute | solution.py:25
  152.8 17.6 %copy-start.6 = (f32[32,448]{1,0:T(8,128)}, f32[32,448]{1,0:T(8,128)S(1)}, u32[]{:S(2)}) copy-start(f32[32,448]{1,0:T(8,128)S(1)} %fusion.3) | copy-start | bytes 172036
  153.4 13.3 %all-to-all-start.3 = ((f32[8,8,448]{2,1,0:T(8,128)}), f32[8,8,448]{2,1,0:T(8,128)S(1)}, u32[]{:S(2)}, u32[]{:S(2)}) async-start(f32[8,8,448]{2,1,0:T(8,128)} %broadcast_in_dim.18), calls=%async_computation.3 | async-start | bytes 262144 | tf_op jit(solution)/shard_map/all_to_all | solution.py:37
  156.8 10.0 %copy-start.7 = (bf16[40,1024]{1,0:T(8,128)(2,1)}, bf16[40,1024]{1,0:T(8,128)(2,1)S(1)}, u32[]{:S(2)}) copy-start(bf16[40,1024]{1,0:T(8,128)(2,1)S(1)} %collective-permute-done.10) | copy-start | bytes 245764
  170.4 7.0 %copy-start.4 = (bf16[2,32,1024]{2,1,0:T(8,128)(2,1)S(1)}, bf16[2,32,1024]{2,1,0:T(8,128)(2,1)}, u32[]{:S(2)}) copy-start(bf16[2,32,1024]{2,1,0:T(8,128)(2,1)} %pad_maximum_fusion.3) | copy-start | bytes 393220
  173.4 11.6 %copy-start.15 = (bf16[32]{0:T(256)(128)(2,1)S(1)}, bf16[32]{0:T(256)(128)(2,1)}, u32[]{:S(2)}) copy-start(bf16[32]{0:T(256)(128)(2,1)} %copy-done.14) | copy-start | bytes 196
  173.4 11.6 %copy-start.17 = (bf16[32]{0:T(256)(128)(2,1)S(1)}, bf16[32]{0:T(256)(128)(2,1)}, u32[]{:S(2)}) copy-start(bf16[32]{0:T(256)(128)(2,1)} %copy-done.16) | copy-start | bytes 196
  173.5 11.6 %copy-start.19 = (bf16[32]{0:T(256)(128)(2,1)S(1)}, bf16[32]{0:T(256)(128)(2,1)}, u32[]{:S(2)}) copy-start(bf16[32]{0:T(256)(128)(2,1)} %copy-done.18) | copy-start | bytes 196
  174.5 11.1 %collective-permute-start.8 = (bf16[256,1792]{1,0:T(8,128)(2,1)}, bf16[256,1792]{1,0:T(8,128)(2,1)}, u32[]{:S(2)}, u32[]{:S(2)}) collective-permute-start(bf16[256,1792]{1,0:T(8,128)(2,1)} %constant_dynamic-slice_fusion.4), channel_id=1, source_target_pairs={{0,8},{8,0},{1,9},{9,1},{2,10},{10,2},{3,11},{11,3},{4,12},{12,4},... | collective-permute-start | bytes 2752520 | tf_op jit(solution)/shard_map/ppermute | solution.py:25
  188.4 39.6 %all-to-all-start.4 = ((bf16[32,72,256]{2,1,0:T(8,128)(2,1)}), bf16[32,72,256]{2,1,0:T(8,128)(2,1)}, u32[]{:S(2)}, u32[]{:S(2)}) async-start(bf16[32,72,256]{2,1,0:T(8,128)(2,1)} %pad_maximum_fusion), calls=%async_computation.4 | async-start | bytes 2359296 | tf_op jit(solution)/shard_map/all_to_all | solution.py:128
  (7 other events, 12.4 us)
Sparse Core Ops, SparseCore 0:
  61.0 120.1 all-gather.1

commit v4 on v3

--- a/solution.py
+++ b/solution.py
@@ -52,28 +52,33 @@
     return value.reshape(lead + (N_P, 2, cut)).swapaxes(-3, -2).reshape(lead + (width,))
 
 
+def after(value, *others):
+    return lax.optimization_barrier((value, *others))[0]
+
+
 def per_device(item_cache, user_cache, positive, attn_heads, residual, out_proj, norm_gain):
     rows, feats = item_cache.shape
     width = out_proj.shape[1]
     tokens, heads = attn_heads.shape
     half = N_P * rows
     core = lax.axis_index("c")
+    x_index = lax.axis_index("x")
+    z_index = lax.axis_index("zh")
     x_block = tokens // 4
+    z_block = x_block // 2
 
-    x_index = lax.axis_index("x")
     attn = by_xor(attn_heads.reshape(4, x_block, heads), x_index).reshape(tokens, heads)
+    attn_other = swap(attn)
     mixed = dot(attn, out_proj, ((1,), (0,))).astype(BF16)
     from_x = [
         lax.ppermute(mixed[k * x_block : (k + 1) * x_block], **xor("x", 4, k)) for k in (1, 2, 3)
     ]
+    mixed_x = mixed[:x_block].astype(F32) + sum(part.astype(F32) for part in from_x)
+    mixed_x = mixed_x.reshape(2, z_block, width)
+    mixed_give = lax.dynamic_index_in_dim(mixed_x, 1 - z_index, 0, keepdims=False)
+    mixed_keep = lax.dynamic_index_in_dim(mixed_x, z_index, 0, keepdims=False)
+    from_z = lax.ppermute(mixed_give.astype(BF16), **xor("zh", 2, 1))
 
-    mixed_x = mixed[:x_block].astype(F32) + sum(part.astype(F32) for part in from_x)
-    from_z = lax.ppermute(mixed_x.astype(BF16), **xor("zh", 2, 1))
-    residual_x = lax.dynamic_slice_in_dim(residual, x_index * x_block, x_block, 0)
-    hidden_x = core_major((mixed_x + from_z.astype(F32) + residual_x.astype(F32)).astype(BF16))
-    hidden_x = [hidden_x] + [lax.ppermute(hidden_x, **xor("x", 4, k)) for k in (1, 2, 3)]
-
-    items = lax.all_gather(item_cache, DP, axis=0, tiled=True)
     users_own = to_all(user_cache, PLANE, N_P).reshape(half, feats)
     users = (users_own, swap(users_own))
 
@@ -82,6 +87,15 @@
     partial = partial.reshape(rows, N_T, share).transpose(1, 0, 2)
     scores_own = jnp.sum(lax.all_to_all(partial, TENSOR, 0, 0), axis=0) * LOGIT_SCALE
     scores = to_all(scores_own, TENSOR, N_T).transpose(1, 0, 2).reshape(rows, 2 * half)
+
+    own_tokens = (2 * x_index + z_index) * z_block
+    own_residual = lax.dynamic_slice_in_dim(residual, own_tokens, z_block, 0).astype(F32)
+    hidden_own = mixed_keep + after(from_z, partial).astype(F32) + own_residual
+    hidden_own = core_major(hidden_own.astype(BF16))
+    hidden_z = after(lax.ppermute(hidden_own, **xor("zh", 2, 1)), scores_own)
+    pair = jnp.stack([hidden_own, hidden_z])
+    hidden_x = jnp.where(z_index == 0, pair, pair[::-1]).reshape(x_block, width)
+    hidden_x = [hidden_x] + [lax.ppermute(hidden_x, **xor("x", 4, k)) for k in (1, 2, 3)]
 
     owner, row_in = positive // rows, positive % rows
     column = (owner % 2 != core).astype(jnp.int32) * half + (owner // 2) * rows + row_in
@@ -94,8 +108,20 @@
     item_grad = (
         dot(grad[:, :half], users[0], ((1,), (0,))) + dot(grad[:, half:], users[1], ((1,), (0,)))
     ) * LOGIT_SCALE
+    group_rows = to_all(item_grad[:GROUP], TENSOR, N_T)
 
-    group_rows = to_all(item_grad[:GROUP], TENSOR, N_T)
+    grad_losses = jnp.zeros((8, half), BF16).at[0, : 3 * rows].set(losses)
+    other = swap(jnp.concatenate([grad[:, half:], grad_losses], axis=0))
+    losses = jnp.concatenate([losses, other[rows, : 3 * rows]])
+    losses = jnp.zeros((8, heads), BF16).at[0, : 6 * rows].set(losses)
+    both = jnp.concatenate([grad[:, :half], other[:rows]], axis=0)
+    both = both.T.reshape(N_P, rows, 2 * rows)
+    by_plane = jnp.concatenate(
+        [jnp.broadcast_to(item_cache[None], (N_P, rows, feats)), both], axis=2
+    )
+    group_rows = after(group_rows, by_plane, losses)
+    by_plane = lax.all_to_all(after(by_plane, group_rows), PLANE, 0, 0)
+
     group_rows = core_major(group_rows.transpose(1, 0, 2).reshape(GROUP, width))
     upstream = core_major(norm_gain)[None, :] * (
         by_xor(group_rows.reshape(4, -1), x_index).reshape(GROUP, width) / SEQ
@@ -108,31 +134,24 @@
 
     cut = width // (2 * N_P)
     side = width // 2
-    grad_losses = jnp.zeros((8, half), BF16).at[0, : 3 * rows].set(losses)
-    other = swap(jnp.concatenate([grad[:, half:], grad_losses], axis=0))
-    attn_other = swap(attn)
     stream_other = swap(lax.dynamic_slice_in_dim(stream, (1 - core) * side, side, 1))
     stream_keep = lax.dynamic_slice_in_dim(stream, core * side, side, 1)
     weight = dot(stream_keep, attn, ((0,), (0,))) + dot(stream_other, attn_other, ((0,), (0,)))
     weight = weight.astype(BF16).reshape(N_P, cut, heads)
-    both = jnp.stack([grad[:, :half], other[:rows]])
-    both = jnp.where(core == 0, both, both[::-1])
-    both = both.reshape(2, rows, N_P, rows).transpose(2, 0, 1, 3)
-    losses = jnp.concatenate([losses, other[rows, : 3 * rows]])
-    losses = jnp.zeros((8, heads), BF16).at[0, : 6 * rows].set(losses)
-    tile = 2 * rows * rows // heads
-    final = jnp.concatenate(
-        [weight, both.reshape(N_P, tile, heads), jnp.broadcast_to(losses[None], (N_P, 8, heads))],
-        axis=1,
-    )
+    weight, by_plane = lax.optimization_barrier((weight, by_plane))
+    final = jnp.concatenate([weight, jnp.broadcast_to(losses[None], (N_P, 8, heads))], axis=1)
     final = lax.all_to_all(final, PLANE, 0, 0)
     out_proj = core_major(out_proj)
     head_grad = dot(stream, out_proj, ((1,), (1,))).astype(BF16)
     head_grad = by_xor(head_grad.reshape(4, x_block, heads), x_index).reshape(tokens, heads)
+    items_own = by_plane[:, :, :feats].reshape(half, feats)
+    by_item = by_plane[:, :, feats:].reshape(N_P, rows, 2, rows).transpose(2, 0, 3, 1)
+    by_item = by_item.reshape(2, half, rows)
+    user_grad = (
+        dot(by_item[0], items_own, ((0,), (0,))) + dot(by_item[1], swap(items_own), ((0,), (0,)))
+    ) * LOGIT_SCALE
     weight_grad = jnp.sum(final[:, :cut].astype(F32), axis=0).T
-    loss_mean = jnp.sum(final[:, cut + tile].astype(F32)) / (2 * half)
-    by_user = final[:, cut : cut + tile].reshape(2 * half, rows)
-    user_grad = dot(by_user, items, ((0,), (0,))) * LOGIT_SCALE
+    loss_mean = jnp.sum(final[:, cut].astype(F32)) / (2 * half)
     return (loss_mean, item_grad, user_grad, head_grad, weight_grad)
 
 

time: 248 us -> 234 us (0.944)
  the two profiles are of different devices: /device:TPU:1 before, /device:TPU:8 now
where the time goes in v4:
time: 234 us; the launch traced here: 232 us
  starting transfers between devices  98.1 us (42%)
  waiting for transfers between devices  70.1 us (30%)
  other arithmetic  25.2 us (11%)
  local copies, waits for them, and re-layouts  23.4 us (10%)
  matrix products  12.3 us (5%)
  between operations  3.19 us (1%)
    all_to_all x3, waiting for transfers between devices, to_all(): lax.all_to_all(jnp.broadcast_to(value[None], (count,) + value.shape), axe...  24.3 us
    all_to_all x3, starting transfers between devices, to_all(): lax.all_to_all(jnp.broadcast_to(value[None], (count,) + value.shape), axe...  23.8 us
    all_to_all x1, starting transfers between devices, per_device(): by_plane = lax.all_to_all(after(by_plane, group_rows), PLANE, 0, 0)  18 us
    all_to_all x1, waiting for transfers between devices, per_device(): final = lax.all_to_all(final, PLANE, 0, 0)  15.2 us
    dot_general x10, matrix products, dot(): return lax.dot_general(a, b, (dims, ((), ())), preferred_element_type=F32)  12.3 us
    ppermute x3, starting transfers between devices, per_device(): lax.ppermute(hidden_x, **xor('x', 4, k))  10.4 us
    ppermute x3, starting transfers between devices, per_device(): lax.ppermute(mixed[k * x_block:(k + 1) * x_block], **xor('x', 4, k))  10.4 us
    ppermute x5, starting transfers between devices, swap(): return lax.ppermute(value, **xor('c', 2, 1))  10.1 us
  transfers between devices with their start and end apart: 19, of which 10 were waited for; matrix products, arithmetic and copies ran while one was open for 18% of the time, Pallas kernels for 0%

profile of v4, /device:TPU:8, one launch (start us, length us, event | category | flops | bytes accessed | tf_op | source)
XLA Modules:
  0.0 232.3 jit_solution(14707017595059311273)
XLA Ops:
  0.7 2.0 broadcast_in_dim.14
  2.7 13.1 %all-to-all-start = ((bf16[32,32,448]{2,1,0:T(8,128)(2,1)}), bf16[32,32,448]{2,1,0:T(8,128)(2,1)S(1)}, u32[]{:S(2)}, u32[]{:S(2)}) async-start(bf16[32,32,448]{2,1,0:T(8,128)(2,1)} %broadcast_in_dim.14), calls=%async_computation | async-start | bytes 2097152 | tf_op jit(solution)/shard_map/all_to_all | solution.py:37
  20.3 3.4 %collective-permute-start = (bf16[64,3584]{1,0:T(8,128)(2,1)}, bf16[64,3584]{1,0:T(8,128)(2,1)S(1)}, u32[]{:S(2)}, u32[]{:S(2)}) collective-permute-start(bf16[64,3584]{1,0:T(8,128)(2,1)} %get-tuple-element.43), channel_id=1, source_target_pairs={{0,2},{2,0},{4,6},{6,4},{1,3},{3,1},{5,7},{7,5},{8,10},{10,8},{12,... | collective-permute-start | bytes 1376264 | tf_op jit(solution)/shard_map/ppermute | solution.py:74
  23.7 4.6 %collective-permute-start.1 = (bf16[64,3584]{1,0:T(8,128)(2,1)}, bf16[64,3584]{1,0:T(8,128)(2,1)S(1)}, u32[]{:S(2)}, u32[]{:S(2)}) collective-permute-start(bf16[64,3584]{1,0:T(8,128)(2,1)} %get-tuple-element.45), channel_id=1, source_target_pairs={{0,4},{2,6},{4,0},{6,2},{1,5},{3,7},{5,1},{7,3},{8,12},{10,14},{12... | collective-permute-start | bytes 1376264 | tf_op jit(solution)/shard_map/ppermute | solution.py:74
  28.4 2.4 %collective-permute-start.2 = (bf16[64,3584]{1,0:T(8,128)(2,1)S(1)}, bf16[64,3584]{1,0:T(8,128)(2,1)}, u32[]{:S(2)}, u32[]{:S(2)}) collective-permute-start(bf16[64,3584]{1,0:T(8,128)(2,1)S(1)} %get-tuple-element.44), channel_id=1, source_target_pairs={{0,6},{2,4},{4,2},{6,0},{1,7},{3,5},{5,3},{7,1},{8,14},{10,12},{12... | collective-permute-start | bytes 1376264 | tf_op jit(solution)/shard_map/ppermute | solution.py:74
  30.8 13.6 %all-to-all-done = bf16[32,32,448]{2,1,0:T(8,128)(2,1)S(1)} async-done(((bf16[32,32,448]{2,1,0:T(8,128)(2,1)}), bf16[32,32,448]{2,1,0:T(8,128)(2,1)S(1)}, u32[]{:S(2)}, u32[]{:S(2)}) %all-to-all-start) | async-done | bytes 917536 | tf_op jit(solution)/shard_map/all_to_all | solution.py:37
  46.8 5.7 %collective-permute-done.2 = bf16[64,3584]{1,0:T(8,128)(2,1)} collective-permute-done((bf16[64,3584]{1,0:T(8,128)(2,1)S(1)}, bf16[64,3584]{1,0:T(8,128)(2,1)}, u32[]{:S(2)}, u32[]{:S(2)}) %collective-permute-start.2) | collective-permute-done | bytes 458784 | tf_op jit(solution)/shard_map/ppermute | solution.py:74
  54.0 8.2 %collective-permute-start.3 = (bf16[32,3584]{1,0:T(8,128)(2,1)S(1)}, bf16[32,3584]{1,0:T(8,128)(2,1)S(1)}, u32[]{:S(2)}, u32[]{:S(2)}) collective-permute-start(bf16[32,3584]{1,0:T(8,128)(2,1)S(1)} %fusion.14), channel_id=1, source_target_pairs={{0,1},{1,0},{2,3},{3,2},{4,5},{5,4},{6,7},{7,6},{8,9},{9,8},{10,11... | collective-permute-start | bytes 688136 | tf_op jit(solution)/shard_map/ppermute | solution.py:80
  64.6 5.8 %collective-permute-done.3 = bf16[32,3584]{1,0:T(8,128)(2,1)S(1)} collective-permute-done((bf16[32,3584]{1,0:T(8,128)(2,1)S(1)}, bf16[32,3584]{1,0:T(8,128)(2,1)S(1)}, u32[]{:S(2)}, u32[]{:S(2)}) %collective-permute-start.3) | collective-permute-done | bytes 229408 | tf_op jit(solution)/shard_map/ppermute | solution.py:80
  73.4 8.3 %collective-permute-start.5 = (bf16[32,3584]{1,0:T(8,128)(2,1)S(1)}, bf16[32,3584]{1,0:T(8,128)(2,1)S(1)}, u32[]{:S(2)}, u32[]{:S(2)}) collective-permute-start(bf16[32,3584]{1,0:T(8,128)(2,1)S(1)} %reshape.299), channel_id=1, source_target_pairs={{0,1},{1,0},{2,3},{3,2},{4,5},{5,4},{6,7},{7,6},{8,9},{9,8},{10,11... | collective-permute-start | bytes 688136 | tf_op jit(solution)/shard_map/ppermute | solution.py:95
  81.7 3.4 %all-to-all-start.1 = ((f32[8,32,256]{2,1,0:T(8,128)}), f32[8,32,256]{2,1,0:T(8,128)S(1)}, u32[]{:S(2)}, u32[]{:S(2)}) async-start(f32[8,32,256]{2,1,0:T(8,128)} %bitcast.92), calls=%async_computation.1 | async-start | bytes 524288 | tf_op jit(solution)/shard_map/all_to_all | solution.py:88
  85.9 3.6 %collective-permute-done.5 = bf16[32,3584]{1,0:T(8,128)(2,1)S(1)} collective-permute-done((bf16[32,3584]{1,0:T(8,128)(2,1)S(1)}, bf16[32,3584]{1,0:T(8,128)(2,1)S(1)}, u32[]{:S(2)}, u32[]{:S(2)}) %collective-permute-start.5) | collective-permute-done | bytes 229408 | tf_op jit(solution)/shard_map/ppermute | solution.py:95
  91.5 2.9 %collective-permute-start.7 = (bf16[64,3584]{1,0:T(8,128)(2,1)S(1)}, bf16[64,3584]{1,0:T(8,128)(2,1)S(1)}, u32[]{:S(2)}, u32[]{:S(2)}) collective-permute-start(bf16[64,3584]{1,0:T(8,128)(2,1)S(1)} %bitcast.100), channel_id=1, source_target_pairs={{0,4},{2,6},{4,0},{6,2},{1,5},{3,7},{5,1},{7,3},{8,12},{10,14},{12... | collective-permute-start | bytes 1376264 | tf_op jit(solution)/shard_map/ppermute | solution.py:98
  94.5 5.6 %collective-permute-start.8 = (bf16[64,3584]{1,0:T(8,128)(2,1)S(1)}, bf16[64,3584]{1,0:T(8,128)(2,1)S(1)}, u32[]{:S(2)}, u32[]{:S(2)}) collective-permute-start(bf16[64,3584]{1,0:T(8,128)(2,1)S(1)} %bitcast.101), channel_id=1, source_target_pairs={{0,6},{2,4},{4,2},{6,0},{1,7},{3,5},{5,3},{7,1},{8,14},{10,12},{12... | collective-permute-start | bytes 1376264 | tf_op jit(solution)/shard_map/ppermute | solution.py:98
  101.1 5.7 %all-to-all-start.2 = ((f32[8,32,256]{2,1,0:T(8,128)}), f32[8,32,256]{2,1,0:T(8,128)S(1)}, u32[]{:S(2)}, u32[]{:S(2)}) async-start(f32[8,32,256]{2,1,0:T(8,128)} %broadcast_in_dim.15), calls=%async_computation.2 | async-start | bytes 524288 | tf_op jit(solution)/shard_map/all_to_all | solution.py:37
  108.2 5.2 %collective-permute-done.8 = bf16[64,3584]{1,0:T(8,128)(2,1)S(1)} collective-permute-done((bf16[64,3584]{1,0:T(8,128)(2,1)S(1)}, bf16[64,3584]{1,0:T(8,128)(2,1)S(1)}, u32[]{:S(2)}, u32[]{:S(2)}) %collective-permute-start.8) | collective-permute-done | bytes 458784 | tf_op jit(solution)/shard_map/ppermute | solution.py:98
  113.9 2.2 maximum_convert_fusion
  127.8 5.0 %all-to-all-start.3 = ((f32[8,8,448]{2,1,0:T(8,128)}), f32[8,8,448]{2,1,0:T(8,128)S(1)}, u32[]{:S(2)}, u32[]{:S(2)}) async-start(f32[8,8,448]{2,1,0:T(8,128)} %broadcast_in_dim.16), calls=%async_computation.3 | async-start | bytes 262144 | tf_op jit(solution)/shard_map/all_to_all | solution.py:37
  134.6 8.8 %all-to-all-done.3 = f32[8,8,448]{2,1,0:T(8,128)S(1)} async-done(((f32[8,8,448]{2,1,0:T(8,128)}), f32[8,8,448]{2,1,0:T(8,128)S(1)}, u32[]{:S(2)}, u32[]{:S(2)}) %all-to-all-start.3) | async-done | bytes 114720 | tf_op jit(solution)/shard_map/all_to_all | solution.py:37
  144.5 18.0 %all-to-all-start.4 = ((bf16[32,32,512]{2,1,0:T(8,128)(2,1)}), bf16[32,32,512]{2,1,0:T(8,128)(2,1)S(1)}, u32[]{:S(2)}, u32[]{:S(2)}) async-start(bf16[32,32,512]{2,1,0:T(8,128)(2,1)} %pad_maximum_fusion), calls=%async_computation.4 | async-start | bytes 2097152 | tf_op jit(solution)/shard_map/all_to_all | solution.py:123
  162.5 2.4 %multiply_reduce_fusion = f32[8,32]{1,0:T(8,128)S(1)} fusion(f32[8,32,3584]{2,1,0:T(8,128)} %bitcast.98, f32[8,3584]{1,0:T(8,128)S(1)} %broadcast_multiply_fusion), kind=kLoop, calls=%fused_computation.5 | loop fusion | flops 1834752 | bytes 3785728 | tf_op jit(solution)/shard_map/reduce_sum | solution.py:131
  165.1 2.4 %fusion.1 = bf16[256,3584]{1,0:T(8,128)(2,1)S(1)} fusion(f32[256]{0:T(256)S(1)} %fusion.18, f32[8,3584]{1,0:T(8,128)S(1)} %broadcast_multiply_fusion, f32[256]{0:T(256)S(1)} %add_rsqrt_fusion, bf16[64,3584]{1,0:T(8,128)(2,1)S(1)} %collective-permute-done.8, bf16[64,3584]{1,0:T(8,128)(2,1)S(1)} %collective-permute-done.7, ...), kind=kLoop, calls=%fused_computation.3 | loop fusion | flops 11010048 | bytes 3786752 | tf_op jit(solution)/shard_map/convert_element_type | solution.py:133
  170.5 2.4 %collective-permute-start.11 = (bf16[256,256]{1,0:T(8,128)(2,1)}, bf16[256,256]{1,0:T(8,128)(2,1)}, u32[]{:S(2)}, u32[]{:S(2)}) collective-permute-start(bf16[256,256]{1,0:T(8,128)(2,1)} %bitcast.1), channel_id=1, source_target_pairs={{0,8},{8,0},{1,9},{9,1},{2,10},{10,2},{3,11},{11,3},{4,12},{12,4},... | collective-permute-start | bytes 393224 | tf_op jit(solution)/shard_map/ppermute | solution.py:25
  172.9 2.9 %copy.67 = bf16[256,3584]{0,1:T(8,128)(2,1)S(1)} copy(bf16[256,3584]{1,0:T(8,128)(2,1)} %param.16) | data formatting | bytes 3670016 | tf_op args[5]
  178.9 2.6 %fusion.2 = bf16[1792,256]{1,0:T(8,128)(2,1)} fusion(f32[1792,256]{1,0:T(8,128)S(1)} %fusion.8, bf16[256,1792]{1,0:T(8,128)(2,1)} %collective-permute-done.10, bf16[256,256]{1,0:T(8,128)(2,1)} %collective-permute-done.11), kind=kOutput, calls=%fused_computation.8 | convolution fusion | flops 235798528 | bytes 3801088 | tf_op jit(solution)/shard_map/dot_general | solution.py:41
  181.4 8.9 %all-to-all-done.4 = bf16[32,32,512]{2,1,0:T(8,128)(2,1)S(1)} async-done(((bf16[32,32,512]{2,1,0:T(8,128)(2,1)}), bf16[32,32,512]{2,1,0:T(8,128)(2,1)S(1)}, u32[]{:S(2)}, u32[]{:S(2)}) %all-to-all-start.4) | async-done | bytes 1048608 | tf_op jit(solution)/shard_map/all_to_all | solution.py:123
  190.4 2.4 %pad_maximum_fusion.1 = bf16[32,64,256]{2,1,0:T(8,128)(2,1)} fusion(bf16[32,8,256]{2,1,0:T(8,128)(2,1)S(1)} %broadcast_in_dim.19, bf16[32,56,256]{2,1,0:T(8,128)(2,1)} %bitcast.113), kind=kLoop, calls=%fused_computation.17 | loop fusion | flops 2097152 | bytes 2097152 | tf_op jit(solution)/shard_map/concatenate | solution.py:142
  192.8 5.4 %all-to-all-start.5 = ((bf16[32,64,256]{2,1,0:T(8,128)(2,1)}), bf16[32,64,256]{2,1,0:T(8,128)(2,1)}, u32[]{:S(2)}, u32[]{:S(2)}) async-start(bf16[32,64,256]{2,1,0:T(8,128)(2,1)} %pad_maximum_fusion.1), calls=%async_computation.5 | async-start | bytes 2097152 | tf_op jit(solution)/shard_map/all_to_all | solution.py:143
  198.3 3.2 %subtract_convert_fusion = bf16[8,32,3584]{2,1,0:T(8,128)(2,1)} fusion(f32[8,32]{1,0:T(8,128)S(1)} %get-tuple-element.62, f32[8,32]{1,0:T(8,128)S(1)} %rsqrt.17, f32[8,3584]{1,0:T(8,128)S(1)} %broadcast_multiply_fusion, bf16[64,3584]{1,0:T(8,128)(2,1)S(1)} %copy-done.8, bf16[64,3584]{1,0:T(8,128)(2,1)S(1)} %copy-done.6, bf16[64,3584]{1,0:T(8,128)(2,1)S(1)} %copy-done.4, ...), kind=kLoop, calls=%fused_computation.4 | loop fusion | flops 11010048 | bytes 3786752 | tf_op jit(solution)/shard_map/convert_element_type | solution.py:133
  204.7 2.7 %convolution_convert_fusion.1 = bf16[256,256]{1,0:T(8,128)(2,1)S(1)} fusion(bf16[256,3584]{1,0:T(8,128)(2,1)} %bitcast.117, bf16[256,3584]{0,1:T(8,128)(2,1)} %bitcast.116), kind=kOutput, calls=%fused_computation.11 | convolution fusion | flops 469827584 | bytes 3801088 | tf_op jit(solution)/shard_map/dot_general | solution.py:41
  211.8 15.2 %all-to-all-done.5 = bf16[32,64,256]{2,1,0:T(8,128)(2,1)} async-done(((bf16[32,64,256]{2,1,0:T(8,128)(2,1)}), bf16[32,64,256]{2,1,0:T(8,128)(2,1)}, u32[]{:S(2)}, u32[]{:S(2)}) %all-to-all-start.5) | async-done | bytes 1048608 | tf_op jit(solution)/shard_map/all_to_all | solution.py:143
  229.2 1.9 convert_reduce_fusion
  (127 shorter events, 49.0 us)
Async XLA Ops:
  0.6 15.2 %copy-start.12 = (bf16[256,256]{1,0:T(8,128)(2,1)S(1)}, bf16[256,256]{1,0:T(8,128)(2,1)}, u32[]{:S(2)}) copy-start(bf16[256,256]{1,0:T(8,128)(2,1)} %param.14) | copy-start | bytes 393220
  0.6 15.9 %copy-start = (bf16[256,3584]{1,0:T(8,128)(2,1)S(1)}, bf16[256,3584]{1,0:T(8,128)(2,1)}, u32[]{:S(2)}) copy-start(bf16[256,3584]{1,0:T(8,128)(2,1)} %param.16) | copy-start | bytes 5505028
  2.7 41.7 %all-to-all-start = ((bf16[32,32,448]{2,1,0:T(8,128)(2,1)}), bf16[32,32,448]{2,1,0:T(8,128)(2,1)S(1)}, u32[]{:S(2)}, u32[]{:S(2)}) async-start(bf16[32,32,448]{2,1,0:T(8,128)(2,1)} %broadcast_in_dim.14), calls=%async_computation | async-start | bytes 2097152 | tf_op jit(solution)/shard_map/all_to_all | solution.py:37
  20.3 26.5 %collective-permute-start = (bf16[64,3584]{1,0:T(8,128)(2,1)}, bf16[64,3584]{1,0:T(8,128)(2,1)S(1)}, u32[]{:S(2)}, u32[]{:S(2)}) collective-permute-start(bf16[64,3584]{1,0:T(8,128)(2,1)} %get-tuple-element.43), channel_id=1, source_target_pairs={{0,2},{2,0},{4,6},{6,4},{1,3},{3,1},{5,7},{7,5},{8,10},{10,8},{12,... | collective-permute-start | bytes 1376264 | tf_op jit(solution)/shard_map/ppermute | solution.py:74
  23.7 23.1 %collective-permute-start.1 = (bf16[64,3584]{1,0:T(8,128)(2,1)}, bf16[64,3584]{1,0:T(8,128)(2,1)S(1)}, u32[]{:S(2)}, u32[]{:S(2)}) collective-permute-start(bf16[64,3584]{1,0:T(8,128)(2,1)} %get-tuple-element.45), channel_id=1, source_target_pairs={{0,4},{2,6},{4,0},{6,2},{1,5},{3,7},{5,1},{7,3},{8,12},{10,14},{12... | collective-permute-start | bytes 1376264 | tf_op jit(solution)/shard_map/ppermute | solution.py:74
  28.4 24.2 %collective-permute-start.2 = (bf16[64,3584]{1,0:T(8,128)(2,1)S(1)}, bf16[64,3584]{1,0:T(8,128)(2,1)}, u32[]{:S(2)}, u32[]{:S(2)}) collective-permute-start(bf16[64,3584]{1,0:T(8,128)(2,1)S(1)} %get-tuple-element.44), channel_id=1, source_target_pairs={{0,6},{2,4},{4,2},{6,0},{1,7},{3,5},{5,3},{7,1},{8,14},{10,12},{12... | collective-permute-start | bytes 1376264 | tf_op jit(solution)/shard_map/ppermute | solution.py:74
  44.9 17.3 %copy-start.11 = (bf16[32,448]{1,0:T(8,128)(2,1)S(1)}, bf16[32,448]{1,0:T(8,128)(2,1)}, u32[]{:S(2)}) copy-start(bf16[32,448]{1,0:T(8,128)(2,1)} %param.11) | copy-start | bytes 86020
  44.9 17.7 %collective-permute-start.4 = (bf16[1024,448]{0,1:T(8,128)(2,1)S(1)}, bf16[1024,448]{0,1:T(8,128)(2,1)S(1)}, u32[]{:S(2)}, u32[]{:S(2)}) collective-permute-start(bf16[1024,448]{0,1:T(8,128)(2,1)S(1)} %copy.55), channel_id=1, source_target_pairs={{0,8},{8,0},{1,9},{9,1},{2,10},{10,2},{3,11},{11,3},{4,12},{12,4},... | collective-permute-start | bytes 2752520 | tf_op jit(solution)/shard_map/ppermute | solution.py:25
  54.0 16.5 %collective-permute-start.3 = (bf16[32,3584]{1,0:T(8,128)(2,1)S(1)}, bf16[32,3584]{1,0:T(8,128)(2,1)S(1)}, u32[]{:S(2)}, u32[]{:S(2)}) collective-permute-start(bf16[32,3584]{1,0:T(8,128)(2,1)S(1)} %fusion.14), channel_id=1, source_target_pairs={{0,1},{1,0},{2,3},{3,2},{4,5},{5,4},{6,7},{7,6},{8,9},{9,8},{10,11... | collective-permute-start | bytes 688136 | tf_op jit(solution)/shard_map/ppermute | solution.py:80
  63.9 17.8 %copy-start.14 = (f32[3584]{0:T(1024)S(1)}, f32[3584]{0:T(1024)}, u32[]{:S(2)}) copy-start(f32[3584]{0:T(1024)} %param.17) | copy-start | bytes 43012
  72.7 27.6 %copy-start.15 = (s32[32]{0:T(128)S(1)}, s32[32]{0:T(128)}, u32[]{:S(2)}) copy-start(s32[32]{0:T(128)} %param.13) | copy-start | bytes 388
  73.4 16.0 %collective-permute-start.5 = (bf16[32,3584]{1,0:T(8,128)(2,1)S(1)}, bf16[32,3584]{1,0:T(8,128)(2,1)S(1)}, u32[]{:S(2)}, u32[]{:S(2)}) collective-permute-start(bf16[32,3584]{1,0:T(8,128)(2,1)S(1)} %reshape.299), channel_id=1, source_target_pairs={{0,1},{1,0},{2,3},{3,2},{4,5},{5,4},{6,7},{7,6},{8,9},{9,8},{10,11... | collective-permute-start | bytes 688136 | tf_op jit(solution)/shard_map/ppermute | solution.py:95
  81.7 18.6 %all-to-all-start.1 = ((f32[8,32,256]{2,1,0:T(8,128)}), f32[8,32,256]{2,1,0:T(8,128)S(1)}, u32[]{:S(2)}, u32[]{:S(2)}) async-start(f32[8,32,256]{2,1,0:T(8,128)} %bitcast.92), calls=%async_computation.1 | async-start | bytes 524288 | tf_op jit(solution)/shard_map/all_to_all | solution.py:88
  89.6 17.2 %collective-permute-start.6 = (bf16[64,3584]{1,0:T(8,128)(2,1)S(1)}, bf16[64,3584]{1,0:T(8,128)(2,1)S(1)}, u32[]{:S(2)}, u32[]{:S(2)}) collective-permute-start(bf16[64,3584]{1,0:T(8,128)(2,1)S(1)} %bitcast.99), channel_id=1, source_target_pairs={{0,2},{2,0},{4,6},{6,4},{1,3},{3,1},{5,7},{7,5},{8,10},{10,8},{12,... | collective-permute-start | bytes 1376264 | tf_op jit(solution)/shard_map/ppermute | solution.py:98
  91.5 16.6 %collective-permute-start.7 = (bf16[64,3584]{1,0:T(8,128)(2,1)S(1)}, bf16[64,3584]{1,0:T(8,128)(2,1)S(1)}, u32[]{:S(2)}, u32[]{:S(2)}) collective-permute-start(bf16[64,3584]{1,0:T(8,128)(2,1)S(1)} %bitcast.100), channel_id=1, source_target_pairs={{0,4},{2,6},{4,0},{6,2},{1,5},{3,7},{5,1},{7,3},{8,12},{10,14},{12... | collective-permute-start | bytes 1376264 | tf_op jit(solution)/shard_map/ppermute | solution.py:98
  94.5 18.9 %collective-permute-start.8 = (bf16[64,3584]{1,0:T(8,128)(2,1)S(1)}, bf16[64,3584]{1,0:T(8,128)(2,1)S(1)}, u32[]{:S(2)}, u32[]{:S(2)}) collective-permute-start(bf16[64,3584]{1,0:T(8,128)(2,1)S(1)} %bitcast.101), channel_id=1, source_target_pairs={{0,6},{2,4},{4,2},{6,0},{1,7},{3,5},{5,3},{7,1},{8,14},{10,12},{12... | collective-permute-start | bytes 1376264 | tf_op jit(solution)/shard_map/ppermute | solution.py:98
  101.1 16.9 %all-to-all-start.2 = ((f32[8,32,256]{2,1,0:T(8,128)}), f32[8,32,256]{2,1,0:T(8,128)S(1)}, u32[]{:S(2)}, u32[]{:S(2)}) async-start(f32[8,32,256]{2,1,0:T(8,128)} %broadcast_in_dim.15), calls=%async_computation.2 | async-start | bytes 524288 | tf_op jit(solution)/shard_map/all_to_all | solution.py:37
  106.8 58.3 %copy-start.3 = (bf16[64,3584]{1,0:T(8,128)(2,1)}, bf16[64,3584]{1,0:T(8,128)(2,1)S(1)}, u32[]{:S(2)}) copy-start(bf16[64,3584]{1,0:T(8,128)(2,1)S(1)} %collective-permute-done.6) | copy-start | bytes 1376260
  108.2 56.9 %copy-start.5 = (bf16[64,3584]{1,0:T(8,128)(2,1)}, bf16[64,3584]{1,0:T(8,128)(2,1)S(1)}, u32[]{:S(2)}) copy-start(bf16[64,3584]{1,0:T(8,128)(2,1)S(1)} %collective-permute-done.7) | copy-start | bytes 1376260
  113.3 51.7 %copy-start.7 = (bf16[64,3584]{1,0:T(8,128)(2,1)}, bf16[64,3584]{1,0:T(8,128)(2,1)S(1)}, u32[]{:S(2)}) copy-start(bf16[64,3584]{1,0:T(8,128)(2,1)S(1)} %collective-permute-done.8) | copy-start | bytes 1376260
  122.3 10.8 %copy-start.10 = (bf16[32,1024]{0,1:T(8,128)(2,1)S(1)}, bf16[32,1024]{0,1:T(8,128)(2,1)}, u32[]{:S(2)}) copy-start(bf16[32,1024]{0,1:T(8,128)(2,1)} %get-tuple-element.48) | copy-start | bytes 196612
  123.6 9.2 %collective-permute-start.9 = (bf16[40,1024]{0,1:T(8,128)(2,1)S(1)}, bf16[40,1024]{0,1:T(8,128)(2,1)S(1)}, u32[]{:S(2)}, u32[]{:S(2)}) collective-permute-start(bf16[40,1024]{0,1:T(8,128)(2,1)S(1)} %fusion.13), channel_id=1, source_target_pairs={{0,8},{8,0},{1,9},{9,1},{2,10},{10,2},{3,11},{11,3},{4,12},{12,4},... | collective-permute-start | bytes 245768 | tf_op jit(solution)/shard_map/ppermute | solution.py:25
  127.1 6.2 %copy-start.13 = (f32[32,448]{1,0:T(8,128)}, f32[32,448]{1,0:T(8,128)S(1)}, u32[]{:S(2)}) copy-start(f32[32,448]{1,0:T(8,128)S(1)} %fusion.4) | copy-start | bytes 172036
  127.8 15.6 %all-to-all-start.3 = ((f32[8,8,448]{2,1,0:T(8,128)}), f32[8,8,448]{2,1,0:T(8,128)S(1)}, u32[]{:S(2)}, u32[]{:S(2)}) async-start(f32[8,8,448]{2,1,0:T(8,128)} %broadcast_in_dim.16), calls=%async_computation.3 | async-start | bytes 262144 | tf_op jit(solution)/shard_map/all_to_all | solution.py:37
  144.5 45.9 %all-to-all-start.4 = ((bf16[32,32,512]{2,1,0:T(8,128)(2,1)}), bf16[32,32,512]{2,1,0:T(8,128)(2,1)S(1)}, u32[]{:S(2)}, u32[]{:S(2)}) async-start(bf16[32,32,512]{2,1,0:T(8,128)(2,1)} %pad_maximum_fusion), calls=%async_computation.4 | async-start | bytes 2097152 | tf_op jit(solution)/shard_map/all_to_all | solution.py:123
  168.6 10.3 %collective-permute-start.10 = (bf16[256,1792]{1,0:T(8,128)(2,1)}, bf16[256,1792]{1,0:T(8,128)(2,1)}, u32[]{:S(2)}, u32[]{:S(2)}) collective-permute-start(bf16[256,1792]{1,0:T(8,128)(2,1)} %constant_dynamic-slice_fusion.3), channel_id=1, source_target_pairs={{0,8},{8,0},{1,9},{9,1},{2,10},{10,2},{3,11},{11,3},{4,12},{12,4},... | collective-permute-start | bytes 2752520 | tf_op jit(solution)/shard_map/ppermute | solution.py:25
  170.5 8.3 %collective-permute-start.11 = (bf16[256,256]{1,0:T(8,128)(2,1)}, bf16[256,256]{1,0:T(8,128)(2,1)}, u32[]{:S(2)}, u32[]{:S(2)}) collective-permute-start(bf16[256,256]{1,0:T(8,128)(2,1)} %bitcast.1), channel_id=1, source_target_pairs={{0,8},{8,0},{1,9},{9,1},{2,10},{10,2},{3,11},{11,3},{4,12},{12,4},... | collective-permute-start | bytes 393224 | tf_op jit(solution)/shard_map/ppermute | solution.py:25
  190.4 7.9 %copy-start.4 = (bf16[64,3584]{1,0:T(8,128)(2,1)S(1)}, bf16[64,3584]{1,0:T(8,128)(2,1)}, u32[]{:S(2)}) copy-start(bf16[64,3584]{1,0:T(8,128)(2,1)} %copy-done.3) | copy-start | bytes 1376260
  190.4 7.9 %copy-start.6 = (bf16[64,3584]{1,0:T(8,128)(2,1)S(1)}, bf16[64,3584]{1,0:T(8,128)(2,1)}, u32[]{:S(2)}) copy-start(bf16[64,3584]{1,0:T(8,128)(2,1)} %copy-done.5) | copy-start | bytes 1376260
  190.4 7.9 %copy-start.8 = (bf16[64,3584]{1,0:T(8,128)(2,1)S(1)}, bf16[64,3584]{1,0:T(8,128)(2,1)}, u32[]{:S(2)}) copy-start(bf16[64,3584]{1,0:T(8,128)(2,1)} %copy-done.7) | copy-start | bytes 1376260
  192.8 34.1 %all-to-all-start.5 = ((bf16[32,64,256]{2,1,0:T(8,128)(2,1)}), bf16[32,64,256]{2,1,0:T(8,128)(2,1)}, u32[]{:S(2)}, u32[]{:S(2)}) async-start(bf16[32,64,256]{2,1,0:T(8,128)(2,1)} %pad_maximum_fusion.1), calls=%async_computation.5 | async-start | bytes 2097152 | tf_op jit(solution)/shard_map/all_to_all | solution.py:143
  202.8 7.9 %collective-permute-start.12 = (bf16[1024,448]{0,1:T(8,128)(2,1)}, bf16[1024,448]{0,1:T(8,128)(2,1)S(1)}, u32[]{:S(2)}, u32[]{:S(2)}) collective-permute-start(bf16[1024,448]{0,1:T(8,128)(2,1)} %copy.66), channel_id=1, source_target_pairs={{0,8},{8,0},{1,9},{9,1},{2,10},{10,2},{3,11},{11,3},{4,12},{12,4},... | collective-permute-start | bytes 2752520 | tf_op jit(solution)/shard_map/ppermute | solution.py:25
  (3 other events, 5.2 us)

commit v5 on v4

--- a/solution.py
+++ b/solution.py
@@ -52,8 +52,9 @@
     return value.reshape(lead + (N_P, 2, cut)).swapaxes(-3, -2).reshape(lead + (width,))
 
 
-def after(value, *others):
-    return lax.optimization_barrier((value, *others))[0]
+def tie(value, other):
+    corner = other.reshape(-1, other.shape[-1])[:1, :1].reshape((1,) * value.ndim)
+    return value + (corner * 0).astype(value.dtype)
 
 
 def per_device(item_cache, user_cache, positive, attn_heads, residual, out_proj, norm_gain):
@@ -68,35 +69,44 @@
     z_block = x_block // 2
 
     attn = by_xor(attn_heads.reshape(4, x_block, heads), x_index).reshape(tokens, heads)
-    attn_other = swap(attn)
     mixed = dot(attn, out_proj, ((1,), (0,))).astype(BF16)
+    mixed = mixed.reshape(4, 2, z_block, width)
+    toward = [
+        lax.ppermute(mixed[2, 0], **xor("x", 4, 1)),
+        lax.ppermute(mixed[2, 1], **xor("x", 4, 3)),
+    ]
+    toward = [part.astype(F32) for part in toward]
+    mixed_3 = jnp.stack([mixed[3, 0].astype(F32) + toward[0], mixed[3, 1].astype(F32)])
+    mixed_1 = jnp.stack([mixed[1, 0].astype(F32), mixed[1, 1].astype(F32) + toward[1]])
     from_x = [
-        lax.ppermute(mixed[k * x_block : (k + 1) * x_block], **xor("x", 4, k)) for k in (1, 2, 3)
+        lax.ppermute(mixed_1.astype(BF16), **xor("x", 4, 1)),
+        lax.ppermute(mixed_3.astype(BF16), **xor("x", 4, 3)),
     ]
-    mixed_x = mixed[:x_block].astype(F32) + sum(part.astype(F32) for part in from_x)
-    mixed_x = mixed_x.reshape(2, z_block, width)
+    mixed_x = mixed[0].astype(F32) + sum(part.astype(F32) for part in from_x)
     mixed_give = lax.dynamic_index_in_dim(mixed_x, 1 - z_index, 0, keepdims=False)
     mixed_keep = lax.dynamic_index_in_dim(mixed_x, z_index, 0, keepdims=False)
-    from_z = lax.ppermute(mixed_give.astype(BF16), **xor("zh", 2, 1))
+    mixed_give = mixed_give.astype(BF16)
+    from_z = lax.ppermute(mixed_give, **xor("zh", 2, 1))
 
-    users_own = to_all(user_cache, PLANE, N_P).reshape(half, feats)
+    users_own = to_all(tie(user_cache, mixed), PLANE, N_P).reshape(half, feats)
     users = (users_own, swap(users_own))
 
     partial = jnp.concatenate([dot(item_cache, u, ((1,), (1,))) for u in users], axis=1)
     share = 2 * half // N_T
+    attn_other = swap(tie(attn, partial))
     partial = partial.reshape(rows, N_T, share).transpose(1, 0, 2)
     scores_own = jnp.sum(lax.all_to_all(partial, TENSOR, 0, 0), axis=0) * LOGIT_SCALE
     scores = to_all(scores_own, TENSOR, N_T).transpose(1, 0, 2).reshape(rows, 2 * half)
 
     own_tokens = (2 * x_index + z_index) * z_block
     own_residual = lax.dynamic_slice_in_dim(residual, own_tokens, z_block, 0).astype(F32)
-    hidden_own = mixed_keep + after(from_z, partial).astype(F32) + own_residual
+    hidden_own = mixed_keep + tie(from_z, partial).astype(F32) + own_residual
     hidden_own = core_major(hidden_own.astype(BF16))
-    hidden_z = after(lax.ppermute(hidden_own, **xor("zh", 2, 1)), scores_own)
+    hidden_z = tie(lax.ppermute(hidden_own, **xor("zh", 2, 1)), scores_own)
     pair = jnp.stack([hidden_own, hidden_z])
-    hidden_x = jnp.where(z_index == 0, pair, pair[::-1]).reshape(x_block, width)
-    hidden_x = [hidden_x] + [lax.ppermute(hidden_x, **xor("x", 4, k)) for k in (1, 2, 3)]
-
+    hidden_0 = jnp.where(z_index == 0, pair, pair[::-1])
+    hidden_1 = lax.ppermute(hidden_0, **xor("x", 4, 1))
+    hidden_3 = lax.ppermute(hidden_0, **xor("x", 4, 3))
     owner, row_in = positive // rows, positive % rows
     column = (owner % 2 != core).astype(jnp.int32) * half + (owner // 2) * rows + row_in
     maxima = jnp.max(scores, axis=1, keepdims=True)
@@ -109,6 +119,10 @@
         dot(grad[:, :half], users[0], ((1,), (0,))) + dot(grad[:, half:], users[1], ((1,), (0,)))
     ) * LOGIT_SCALE
     group_rows = to_all(item_grad[:GROUP], TENSOR, N_T)
+    hidden_2 = [
+        lax.ppermute(tie(hidden_1[0], item_grad), **xor("x", 4, 3)),
+        lax.ppermute(tie(hidden_3[1], item_grad), **xor("x", 4, 1)),
+    ]
 
     grad_losses = jnp.zeros((8, half), BF16).at[0, : 3 * rows].set(losses)
     other = swap(jnp.concatenate([grad[:, half:], grad_losses], axis=0))
@@ -119,14 +133,14 @@
     by_plane = jnp.concatenate(
         [jnp.broadcast_to(item_cache[None], (N_P, rows, feats)), both], axis=2
     )
-    group_rows = after(group_rows, by_plane, losses)
-    by_plane = lax.all_to_all(after(by_plane, group_rows), PLANE, 0, 0)
+    by_plane = lax.all_to_all(by_plane, PLANE, 0, 0)
 
     group_rows = core_major(group_rows.transpose(1, 0, 2).reshape(GROUP, width))
     upstream = core_major(norm_gain)[None, :] * (
         by_xor(group_rows.reshape(4, -1), x_index).reshape(GROUP, width) / SEQ
     )
-    hidden = jnp.concatenate(hidden_x, axis=0).reshape(GROUP, SEQ, width).astype(F32)
+    hidden_2 = tie(jnp.stack(hidden_2), group_rows)
+    hidden = jnp.concatenate([hidden_0, hidden_1, hidden_2, hidden_3], axis=0).astype(F32)
     inverse = lax.rsqrt(jnp.mean(hidden * hidden, axis=2, keepdims=True) + NORM_EPS)
     inner = jnp.sum(upstream[:, None, :] * hidden, axis=2, keepdims=True) / width
     stream = inverse * upstream[:, None, :] - hidden * (inverse * inverse * inverse * inner)
@@ -136,13 +150,12 @@
     side = width // 2
     stream_other = swap(lax.dynamic_slice_in_dim(stream, (1 - core) * side, side, 1))
     stream_keep = lax.dynamic_slice_in_dim(stream, core * side, side, 1)
+    attn_other = tie(attn_other, scores)
     weight = dot(stream_keep, attn, ((0,), (0,))) + dot(stream_other, attn_other, ((0,), (0,)))
     weight = weight.astype(BF16).reshape(N_P, cut, heads)
-    weight, by_plane = lax.optimization_barrier((weight, by_plane))
     final = jnp.concatenate([weight, jnp.broadcast_to(losses[None], (N_P, 8, heads))], axis=1)
     final = lax.all_to_all(final, PLANE, 0, 0)
-    out_proj = core_major(out_proj)
-    head_grad = dot(stream, out_proj, ((1,), (1,))).astype(BF16)
+    head_grad = dot(stream, core_major(tie(out_proj, weight[0])), ((1,), (1,))).astype(BF16)
     head_grad = by_xor(head_grad.reshape(4, x_block, heads), x_index).reshape(tokens, heads)
     items_own = by_plane[:, :, :feats].reshape(half, feats)
     by_item = by_plane[:, :, feats:].reshape(N_P, rows, 2, rows).transpose(2, 0, 3, 1)

time: 234 us -> 209 us (0.89)
  the two profiles are of different devices: /device:TPU:8 before, /device:TPU:1 now
where the time goes in v5:
time: 209 us; the launch traced here: 205 us
  starting transfers between devices  95.6 us (46%)
  waiting for transfers between devices  46.5 us (22%)
  local copies, waits for them, and re-layouts  24.1 us (12%)
  other arithmetic  20.5 us (10%)
  matrix products  9.91 us (5%)
  between operations  8.51 us (4%)
    all_to_all x3, starting transfers between devices, to_all(): lax.all_to_all(jnp.broadcast_to(value[None], (count,) + value.shape), axe...  21.7 us
    ppermute x5, starting transfers between devices, swap(): return lax.ppermute(value, **xor('c', 2, 1))  19.8 us
    all_to_all x3, waiting for transfers between devices, to_all(): lax.all_to_all(jnp.broadcast_to(value[None], (count,) + value.shape), axe...  17.5 us
    all_to_all x1, waiting for transfers between devices, per_device(): final = lax.all_to_all(final, PLANE, 0, 0)  13.5 us
    all_to_all x1, waiting for transfers between devices, per_device(): by_plane = lax.all_to_all(by_plane, PLANE, 0, 0)  10.6 us
    dot_general x10, matrix products, dot(): return lax.dot_general(a, b, (dims, ((), ())), preferred_element_type=F32)  9.91 us
    ppermute x1, starting transfers between devices, per_device(): from_z = lax.ppermute(mixed_give, **xor('zh', 2, 1))  7.94 us
    all_to_all x1, starting transfers between devices, per_device(): final = lax.all_to_all(final, PLANE, 0, 0)  7.81 us
  transfers between devices with their start and end apart: 21, of which 6 were waited for; matrix products, arithmetic and copies ran while one was open for 22% of the time, Pallas kernels for 0%

profile of v5, /device:TPU:1, one launch (start us, length us, event | category | flops | bytes accessed | tf_op | source)
XLA Modules:
  0.0 205.1 jit_solution(13641106560701580981)
XLA Ops:
  1.5 2.1 %convolution_convert_fusion = bf16[256,3584]{1,0:T(8,128)(2,1)S(1)} fusion(bf16[256,256]{1,0:T(8,128)(2,1)S(1)} %bitcast.158, bf16[256,3584]{1,0:T(8,128)(2,1)} %param.16), kind=kOutput, calls=%fused_computation | convolution fusion | flops 470679552 | bytes 3801088 | tf_op jit(solution)/shard_map/dot_general | solution.py:41
  4.6 3.9 %collective-permute-start.2 = (bf16[32,3584]{1,0:T(8,128)(2,1)}, bf16[32,3584]{1,0:T(8,128)(2,1)}, u32[]{:S(2)}, u32[]{:S(2)}) collective-permute-start(bf16[32,3584]{1,0:T(8,128)(2,1)} %get-tuple-element.37), channel_id=1, source_target_pairs={{0,2},{2,0},{4,6},{6,4},{1,3},{3,1},{5,7},{7,5},{8,10},{10,8},{12,... | collective-permute-start | bytes 688136 | tf_op jit(solution)/shard_map/ppermute | solution.py:75
  8.6 3.7 %collective-permute-start = (bf16[32,3584]{1,0:T(8,128)(2,1)}, bf16[32,3584]{1,0:T(8,128)(2,1)}, u32[]{:S(2)}, u32[]{:S(2)}) collective-permute-start(bf16[32,3584]{1,0:T(8,128)(2,1)} %get-tuple-element.38), channel_id=1, source_target_pairs={{0,6},{2,4},{4,2},{6,0},{1,7},{3,5},{5,3},{7,1},{8,14},{10,12},{12... | collective-permute-start | bytes 688136 | tf_op jit(solution)/shard_map/ppermute | solution.py:76
  14.6 12.6 %all-to-all-start = ((bf16[32,32,448]{2,1,0:T(8,128)(2,1)}), bf16[32,32,448]{2,1,0:T(8,128)(2,1)S(1)}, u32[]{:S(2)}, u32[]{:S(2)}) async-start(bf16[32,32,448]{2,1,0:T(8,128)(2,1)} %broadcast_in_dim.16), calls=%async_computation | async-start | bytes 2097152 | tf_op jit(solution)/shard_map/all_to_all | solution.py:37
  28.3 2.3 %copy.56 = bf16[256,3584]{0,1:T(8,128)(2,1)} copy(bf16[256,3584]{1,0:T(8,128)(2,1)S(1)} %copy-done) | data formatting | bytes 3670016 | tf_op args[5]
  33.8 2.8 %collective-permute-start.3 = (bf16[2,32,3584]{2,1,0:T(8,128)(2,1)}, bf16[2,32,3584]{2,1,0:T(8,128)(2,1)}, u32[]{:S(2)}, u32[]{:S(2)}) collective-permute-start(bf16[2,32,3584]{2,1,0:T(8,128)(2,1)} %pad_maximum_fusion.4), channel_id=1, source_target_pairs={{0,6},{2,4},{4,2},{6,0},{1,7},{3,5},{5,3},{7,1},{8,14},{10,12},{12... | collective-permute-start | bytes 1376264 | tf_op jit(solution)/shard_map/ppermute | solution.py:83
  36.6 1.9 collective-permute-start.1
  38.8 13.4 %all-to-all-done = bf16[32,32,448]{2,1,0:T(8,128)(2,1)S(1)} async-done(((bf16[32,32,448]{2,1,0:T(8,128)(2,1)}), bf16[32,32,448]{2,1,0:T(8,128)(2,1)S(1)}, u32[]{:S(2)}, u32[]{:S(2)}) %all-to-all-start) | async-done | bytes 917536 | tf_op jit(solution)/shard_map/all_to_all | solution.py:37
  52.8 7.5 %collective-permute-start.5 = (bf16[1024,448]{0,1:T(8,128)(2,1)S(1)}, bf16[1024,448]{0,1:T(8,128)(2,1)S(1)}, u32[]{:S(2)}, u32[]{:S(2)}) collective-permute-start(bf16[1024,448]{0,1:T(8,128)(2,1)S(1)} %copy.44), channel_id=1, source_target_pairs={{0,8},{8,0},{1,9},{9,1},{2,10},{10,2},{3,11},{11,3},{4,12},{12,4},... | collective-permute-start | bytes 2752520 | tf_op jit(solution)/shard_map/ppermute | solution.py:25
  62.4 7.9 %collective-permute-start.4 = (bf16[32,3584]{1,0:T(8,128)(2,1)S(1)}, bf16[32,3584]{1,0:T(8,128)(2,1)S(1)}, u32[]{:S(2)}, u32[]{:S(2)}) collective-permute-start(bf16[32,3584]{1,0:T(8,128)(2,1)S(1)} %fusion.14), channel_id=1, source_target_pairs={{0,1},{1,0},{2,3},{3,2},{4,5},{5,4},{6,7},{7,6},{8,9},{9,8},{10,11... | collective-permute-start | bytes 688136 | tf_op jit(solution)/shard_map/ppermute | solution.py:89
  75.8 3.4 %all-to-all-start.1 = ((f32[8,32,256]{2,1,0:T(8,128)}), f32[8,32,256]{2,1,0:T(8,128)S(1)}, u32[]{:S(2)}, u32[]{:S(2)}) async-start(f32[8,32,256]{2,1,0:T(8,128)} %bitcast.115.clone.2), calls=%async_computation.1 | async-start | bytes 524288 | tf_op jit(solution)/shard_map/all_to_all | solution.py:98
  79.2 2.0 collective-permute-done.4
  84.2 5.2 %collective-permute-start.6 = (bf16[32,3584]{1,0:T(8,128)(2,1)S(1)}, bf16[32,3584]{1,0:T(8,128)(2,1)S(1)}, u32[]{:S(2)}, u32[]{:S(2)}) collective-permute-start(bf16[32,3584]{1,0:T(8,128)(2,1)S(1)} %reshape.331), channel_id=1, source_target_pairs={{0,1},{1,0},{2,3},{3,2},{4,5},{5,4},{6,7},{7,6},{8,9},{9,8},{10,11... | collective-permute-start | bytes 688136 | tf_op jit(solution)/shard_map/ppermute | solution.py:105
  90.1 2.7 %collective-permute-start.12 = (bf16[256,256]{1,0:T(8,128)(2,1)}, bf16[256,256]{1,0:T(8,128)(2,1)}, u32[]{:S(2)}, u32[]{:S(2)}) collective-permute-start(bf16[256,256]{1,0:T(8,128)(2,1)} %broadcast_add_fusion.1), channel_id=1, source_target_pairs={{0,8},{8,0},{1,9},{9,1},{2,10},{10,2},{3,11},{11,3},{4,12},{12,4},... | collective-permute-start | bytes 393224 | tf_op jit(solution)/shard_map/ppermute | solution.py:25
  95.5 4.0 %all-to-all-start.2 = ((f32[8,32,256]{2,1,0:T(8,128)}), f32[8,32,256]{2,1,0:T(8,128)S(1)}, u32[]{:S(2)}, u32[]{:S(2)}) async-start(f32[8,32,256]{2,1,0:T(8,128)} %broadcast_in_dim.17), calls=%async_computation.2 | async-start | bytes 524288 | tf_op jit(solution)/shard_map/all_to_all | solution.py:37
  99.5 2.9 %collective-permute-done.6 = bf16[32,3584]{1,0:T(8,128)(2,1)S(1)} collective-permute-done((bf16[32,3584]{1,0:T(8,128)(2,1)S(1)}, bf16[32,3584]{1,0:T(8,128)(2,1)S(1)}, u32[]{:S(2)}, u32[]{:S(2)}) %collective-permute-start.6) | collective-permute-done | bytes 229408 | tf_op jit(solution)/shard_map/ppermute | solution.py:105
  102.6 1.9 collective-permute-start.9
  104.5 1.9 collective-permute-start.7
  106.4 4.1 %all-to-all-done.2 = f32[8,32,256]{2,1,0:T(8,128)S(1)} async-done(((f32[8,32,256]{2,1,0:T(8,128)}), f32[8,32,256]{2,1,0:T(8,128)S(1)}, u32[]{:S(2)}, u32[]{:S(2)}) %all-to-all-start.2) | async-done | bytes 262176 | tf_op jit(solution)/shard_map/all_to_all | solution.py:37
  114.7 3.1 %collective-permute-start.13 = (bf16[40,1024]{1,0:T(8,128)(2,1)S(1)}, bf16[40,1024]{1,0:T(8,128)(2,1)S(1)}, u32[]{:S(2)}, u32[]{:S(2)}) collective-permute-start(bf16[40,1024]{1,0:T(8,128)(2,1)S(1)} %fusion.21), channel_id=1, source_target_pairs={{0,8},{8,0},{1,9},{9,1},{2,10},{10,2},{3,11},{11,3},{4,12},{12,4},... | collective-permute-start | bytes 245768 | tf_op jit(solution)/shard_map/ppermute | solution.py:25
  118.5 5.0 %all-to-all-start.3 = ((f32[8,8,448]{2,1,0:T(8,128)}), f32[8,8,448]{2,1,0:T(8,128)S(1)}, u32[]{:S(2)}, u32[]{:S(2)}) async-start(f32[8,8,448]{2,1,0:T(8,128)} %broadcast_in_dim.18), calls=%async_computation.3 | async-start | bytes 262144 | tf_op jit(solution)/shard_map/all_to_all | solution.py:37
  124.2 3.4 %collective-permute-start.10 = (bf16[32,3584]{1,0:T(8,128)(2,1)}, bf16[32,3584]{1,0:T(8,128)(2,1)}, u32[]{:S(2)}, u32[]{:S(2)}) collective-permute-start(bf16[32,3584]{1,0:T(8,128)(2,1)} %fusion.17), channel_id=1, source_target_pairs={{0,2},{2,0},{4,6},{6,4},{1,3},{3,1},{5,7},{7,5},{8,10},{10,8},{12,... | collective-permute-start | bytes 688136 | tf_op jit(solution)/shard_map/ppermute | solution.py:124
  128.3 3.7 %collective-permute-start.8 = (bf16[32,3584]{1,0:T(8,128)(2,1)}, bf16[32,3584]{1,0:T(8,128)(2,1)}, u32[]{:S(2)}, u32[]{:S(2)}) collective-permute-start(bf16[32,3584]{1,0:T(8,128)(2,1)} %fusion.18), channel_id=1, source_target_pairs={{0,6},{2,4},{4,2},{6,0},{1,7},{3,5},{5,3},{7,1},{8,14},{10,12},{12... | collective-permute-start | bytes 688136 | tf_op jit(solution)/shard_map/ppermute | solution.py:123
  133.6 6.6 %all-to-all-start.5 = ((bf16[32,32,512]{2,1,0:T(8,128)(2,1)}), bf16[32,32,512]{2,1,0:T(8,128)(2,1)S(1)}, u32[]{:S(2)}, u32[]{:S(2)}) async-start(bf16[32,32,512]{2,1,0:T(8,128)(2,1)} %pad_maximum_fusion.2), calls=%async_computation.5 | async-start | bytes 2097152 | tf_op jit(solution)/shard_map/all_to_all | solution.py:136
  146.4 3.3 %collective-permute-start.11 = (bf16[256,1792]{1,0:T(8,128)(2,1)S(1)}, bf16[256,1792]{1,0:T(8,128)(2,1)S(1)}, u32[]{:S(2)}, u32[]{:S(2)}) collective-permute-start(bf16[256,1792]{1,0:T(8,128)(2,1)S(1)} %constant_dynamic-slice_fusion.3), channel_id=1, source_target_pairs={{0,8},{8,0},{1,9},{9,1},{2,10},{10,2},{3,11},{11,3},{4,12},{12,4},... | collective-permute-start | bytes 2752520 | tf_op jit(solution)/shard_map/ppermute | solution.py:25
  155.5 10.6 %all-to-all-done.5 = bf16[32,32,512]{2,1,0:T(8,128)(2,1)S(1)} async-done(((bf16[32,32,512]{2,1,0:T(8,128)(2,1)}), bf16[32,32,512]{2,1,0:T(8,128)(2,1)S(1)}, u32[]{:S(2)}, u32[]{:S(2)}) %all-to-all-start.5) | async-done | bytes 1048608 | tf_op jit(solution)/shard_map/all_to_all | solution.py:136
  166.1 7.8 %all-to-all-start.4 = ((bf16[32,64,256]{2,1,0:T(8,128)(2,1)}), bf16[32,64,256]{2,1,0:T(8,128)(2,1)}, u32[]{:S(2)}, u32[]{:S(2)}) async-start(bf16[32,64,256]{2,1,0:T(8,128)(2,1)} %pad_maximum_fusion.1), calls=%async_computation.4 | async-start | bytes 2097152 | tf_op jit(solution)/shard_map/all_to_all | solution.py:157
  175.5 3.2 %collective-permute-start.14 = (bf16[1024,448]{0,1:T(8,128)(2,1)}, bf16[1024,448]{0,1:T(8,128)(2,1)}, u32[]{:S(2)}, u32[]{:S(2)}) collective-permute-start(bf16[1024,448]{0,1:T(8,128)(2,1)} %copy.55), channel_id=1, source_target_pairs={{0,8},{8,0},{1,9},{9,1},{2,10},{10,2},{3,11},{11,3},{4,12},{12,4},... | collective-permute-start | bytes 2752520 | tf_op jit(solution)/shard_map/ppermute | solution.py:25
  178.7 2.1 %convolution_convert_fusion.1 = bf16[256,256]{1,0:T(8,128)(2,1)S(1)} fusion(bf16[256,3584]{1,0:T(8,128)(2,1)} %bitcast.161, bf16[256,3584]{0,1:T(8,128)(2,1)S(1)} %bitcast.160), kind=kOutput, calls=%fused_computation.12 | convolution fusion | flops 469827584 | bytes 3801088 | tf_op jit(solution)/shard_map/dot_general | solution.py:41
  184.1 2.2 %fusion.3 = f32[32,448]{1,0:T(8,128)} fusion(f32[32,448]{1,0:T(8,128)S(1)} %fusion.37, bf16[1024,32]{0,1:T(8,128)(2,1)S(1)} %squeeze.34, bf16[1024,448]{0,1:T(8,128)(2,1)} %collective-permute-done.14), kind=kOutput, calls=%fused_computation.16 | convolution fusion | flops 29388800 | bytes 1097728 | tf_op jit(solution)/shard_map/dot_general | solution.py:41
  186.3 13.5 %all-to-all-done.4 = bf16[32,64,256]{2,1,0:T(8,128)(2,1)} async-done(((bf16[32,64,256]{2,1,0:T(8,128)(2,1)}), bf16[32,64,256]{2,1,0:T(8,128)(2,1)}, u32[]{:S(2)}, u32[]{:S(2)}) %all-to-all-start.4) | async-done | bytes 1048608 | tf_op jit(solution)/shard_map/all_to_all | solution.py:157
  202.0 1.9 convert_reduce_fusion
  (141 shorter events, 43.8 us)
Async XLA Ops:
  3.7 9.8 %copy-start.2 = (bf16[256,3584]{1,0:T(8,128)(2,1)}, bf16[256,3584]{1,0:T(8,128)(2,1)S(1)}, u32[]{:S(2)}) copy-start(bf16[256,3584]{1,0:T(8,128)(2,1)S(1)} %convolution_convert_fusion) | copy-start | bytes 5505028
  3.7 9.8 %copy-start.9 = (bf16[32,448]{1,0:T(8,128)(2,1)S(1)}, bf16[32,448]{1,0:T(8,128)(2,1)}, u32[]{:S(2)}) copy-start(bf16[32,448]{1,0:T(8,128)(2,1)} %param.12) | copy-start | bytes 86020
  4.6 26.0 %collective-permute-start.2 = (bf16[32,3584]{1,0:T(8,128)(2,1)}, bf16[32,3584]{1,0:T(8,128)(2,1)}, u32[]{:S(2)}, u32[]{:S(2)}) collective-permute-start(bf16[32,3584]{1,0:T(8,128)(2,1)} %get-tuple-element.37), channel_id=1, source_target_pairs={{0,2},{2,0},{4,6},{6,4},{1,3},{3,1},{5,7},{7,5},{8,10},{10,8},{12,... | collective-permute-start | bytes 688136 | tf_op jit(solution)/shard_map/ppermute | solution.py:75
  8.6 22.1 %collective-permute-start = (bf16[32,3584]{1,0:T(8,128)(2,1)}, bf16[32,3584]{1,0:T(8,128)(2,1)}, u32[]{:S(2)}, u32[]{:S(2)}) collective-permute-start(bf16[32,3584]{1,0:T(8,128)(2,1)} %get-tuple-element.38), channel_id=1, source_target_pairs={{0,6},{2,4},{4,2},{6,0},{1,7},{3,5},{5,3},{7,1},{8,14},{10,12},{12... | collective-permute-start | bytes 688136 | tf_op jit(solution)/shard_map/ppermute | solution.py:76
  13.5 14.8 %copy-start = (bf16[256,3584]{1,0:T(8,128)(2,1)S(1)}, bf16[256,3584]{1,0:T(8,128)(2,1)}, u32[]{:S(2)}) copy-start(bf16[256,3584]{1,0:T(8,128)(2,1)} %param.16) | copy-start | bytes 5505028
  14.6 37.6 %all-to-all-start = ((bf16[32,32,448]{2,1,0:T(8,128)(2,1)}), bf16[32,32,448]{2,1,0:T(8,128)(2,1)S(1)}, u32[]{:S(2)}, u32[]{:S(2)}) async-start(bf16[32,32,448]{2,1,0:T(8,128)(2,1)} %broadcast_in_dim.16), calls=%async_computation | async-start | bytes 2097152 | tf_op jit(solution)/shard_map/all_to_all | solution.py:37
  30.6 6.0 %copy-start.5 = (bf16[1,32,3584]{2,1,0:T(8,128)(2,1)S(1)}, bf16[1,32,3584]{2,1,0:T(8,128)(2,1)}, u32[]{:S(2)}) copy-start(bf16[1,32,3584]{2,1,0:T(8,128)(2,1)} %get-tuple-element.35) | copy-start | bytes 688132
  30.6 8.0 %copy-start.10 = (f32[3584]{0:T(1024)S(1)}, f32[3584]{0:T(1024)}, u32[]{:S(2)}) copy-start(f32[3584]{0:T(1024)} %param.17) | copy-start | bytes 43012
  30.6 8.2 %copy-start.11 = (s32[32]{0:T(128)S(1)}, s32[32]{0:T(128)}, u32[]{:S(2)}) copy-start(s32[32]{0:T(128)} %param.13) | copy-start | bytes 388
  33.8 26.5 %collective-permute-start.3 = (bf16[2,32,3584]{2,1,0:T(8,128)(2,1)}, bf16[2,32,3584]{2,1,0:T(8,128)(2,1)}, u32[]{:S(2)}, u32[]{:S(2)}) collective-permute-start(bf16[2,32,3584]{2,1,0:T(8,128)(2,1)} %pad_maximum_fusion.4), channel_id=1, source_target_pairs={{0,6},{2,4},{4,2},{6,0},{1,7},{3,5},{5,3},{7,1},{8,14},{10,12},{12... | collective-permute-start | bytes 1376264 | tf_op jit(solution)/shard_map/ppermute | solution.py:83
  36.6 23.7 %collective-permute-start.1 = (bf16[2,32,3584]{2,1,0:T(8,128)(2,1)S(1)}, bf16[2,32,3584]{2,1,0:T(8,128)(2,1)S(1)}, u32[]{:S(2)}, u32[]{:S(2)}) collective-permute-start(bf16[2,32,3584]{2,1,0:T(8,128)(2,1)S(1)} %pad_maximum_fusion.3), channel_id=1, source_target_pairs={{0,2},{2,0},{4,6},{6,4},{1,3},{3,1},{5,7},{7,5},{8,10},{10,8},{12,... | collective-permute-start | bytes 1376264 | tf_op jit(solution)/shard_map/ppermute | solution.py:82
  52.8 17.6 %copy-start.7 = (bf16[32,448]{1,0:T(8,128)(2,1)S(1)}, bf16[32,448]{1,0:T(8,128)(2,1)}, u32[]{:S(2)}) copy-start(bf16[32,448]{1,0:T(8,128)(2,1)} %param.11) | copy-start | bytes 86020
  52.8 19.2 %collective-permute-start.5 = (bf16[1024,448]{0,1:T(8,128)(2,1)S(1)}, bf16[1024,448]{0,1:T(8,128)(2,1)S(1)}, u32[]{:S(2)}, u32[]{:S(2)}) collective-permute-start(bf16[1024,448]{0,1:T(8,128)(2,1)S(1)} %copy.44), channel_id=1, source_target_pairs={{0,8},{8,0},{1,9},{9,1},{2,10},{10,2},{3,11},{11,3},{4,12},{12,4},... | collective-permute-start | bytes 2752520 | tf_op jit(solution)/shard_map/ppermute | solution.py:25
  62.4 18.8 %collective-permute-start.4 = (bf16[32,3584]{1,0:T(8,128)(2,1)S(1)}, bf16[32,3584]{1,0:T(8,128)(2,1)S(1)}, u32[]{:S(2)}, u32[]{:S(2)}) collective-permute-start(bf16[32,3584]{1,0:T(8,128)(2,1)S(1)} %fusion.14), channel_id=1, source_target_pairs={{0,1},{1,0},{2,3},{3,2},{4,5},{5,4},{6,7},{7,6},{8,9},{9,8},{10,11... | collective-permute-start | bytes 688136 | tf_op jit(solution)/shard_map/ppermute | solution.py:89
  72.0 1.0 copy-start.3
  75.8 17.7 %all-to-all-start.1 = ((f32[8,32,256]{2,1,0:T(8,128)}), f32[8,32,256]{2,1,0:T(8,128)S(1)}, u32[]{:S(2)}, u32[]{:S(2)}) async-start(f32[8,32,256]{2,1,0:T(8,128)} %bitcast.115.clone.2), calls=%async_computation.1 | async-start | bytes 524288 | tf_op jit(solution)/shard_map/all_to_all | solution.py:98
  84.2 18.2 %collective-permute-start.6 = (bf16[32,3584]{1,0:T(8,128)(2,1)S(1)}, bf16[32,3584]{1,0:T(8,128)(2,1)S(1)}, u32[]{:S(2)}, u32[]{:S(2)}) collective-permute-start(bf16[32,3584]{1,0:T(8,128)(2,1)S(1)} %reshape.331), channel_id=1, source_target_pairs={{0,1},{1,0},{2,3},{3,2},{4,5},{5,4},{6,7},{7,6},{8,9},{9,8},{10,11... | collective-permute-start | bytes 688136 | tf_op jit(solution)/shard_map/ppermute | solution.py:105
  90.1 61.7 %collective-permute-start.12 = (bf16[256,256]{1,0:T(8,128)(2,1)}, bf16[256,256]{1,0:T(8,128)(2,1)}, u32[]{:S(2)}, u32[]{:S(2)}) collective-permute-start(bf16[256,256]{1,0:T(8,128)(2,1)} %broadcast_add_fusion.1), channel_id=1, source_target_pairs={{0,8},{8,0},{1,9},{9,1},{2,10},{10,2},{3,11},{11,3},{4,12},{12,4},... | collective-permute-start | bytes 393224 | tf_op jit(solution)/shard_map/ppermute | solution.py:25
  95.5 15.1 %all-to-all-start.2 = ((f32[8,32,256]{2,1,0:T(8,128)}), f32[8,32,256]{2,1,0:T(8,128)S(1)}, u32[]{:S(2)}, u32[]{:S(2)}) async-start(f32[8,32,256]{2,1,0:T(8,128)} %broadcast_in_dim.17), calls=%async_computation.2 | async-start | bytes 524288 | tf_op jit(solution)/shard_map/all_to_all | solution.py:37
  102.6 20.9 %collective-permute-start.9 = (bf16[2,32,3584]{2,1,0:T(8,128)(2,1)S(1)}, bf16[2,32,3584]{2,1,0:T(8,128)(2,1)S(1)}, u32[]{:S(2)}, u32[]{:S(2)}) collective-permute-start(bf16[2,32,3584]{2,1,0:T(8,128)(2,1)S(1)} %reverse_select_fusion), channel_id=1, source_target_pairs={{0,6},{2,4},{4,2},{6,0},{1,7},{3,5},{5,3},{7,1},{8,14},{10,12},{12... | collective-permute-start | bytes 1376264 | tf_op jit(solution)/shard_map/ppermute | solution.py:109
  104.5 23.1 %collective-permute-start.7 = (bf16[2,32,3584]{2,1,0:T(8,128)(2,1)S(1)}, bf16[2,32,3584]{2,1,0:T(8,128)(2,1)S(1)}, u32[]{:S(2)}, u32[]{:S(2)}) collective-permute-start(bf16[2,32,3584]{2,1,0:T(8,128)(2,1)S(1)} %reverse_select_fusion), channel_id=1, source_target_pairs={{0,2},{2,0},{4,6},{6,4},{1,3},{3,1},{5,7},{7,5},{8,10},{10,8},{12,... | collective-permute-start | bytes 1376264 | tf_op jit(solution)/shard_map/ppermute | solution.py:108
  110.7 1.2 copy-start.4
  112.2 20.2 %copy-start.8 = (f32[32,448]{1,0:T(8,128)}, f32[32,448]{1,0:T(8,128)S(1)}, u32[]{:S(2)}) copy-start(f32[32,448]{1,0:T(8,128)S(1)} %fusion.4) | copy-start | bytes 172036
  114.7 17.2 %collective-permute-start.13 = (bf16[40,1024]{1,0:T(8,128)(2,1)S(1)}, bf16[40,1024]{1,0:T(8,128)(2,1)S(1)}, u32[]{:S(2)}, u32[]{:S(2)}) collective-permute-start(bf16[40,1024]{1,0:T(8,128)(2,1)S(1)} %fusion.21), channel_id=1, source_target_pairs={{0,8},{8,0},{1,9},{9,1},{2,10},{10,2},{3,11},{11,3},{4,12},{12,4},... | collective-permute-start | bytes 245768 | tf_op jit(solution)/shard_map/ppermute | solution.py:25
  118.5 15.1 %all-to-all-start.3 = ((f32[8,8,448]{2,1,0:T(8,128)}), f32[8,8,448]{2,1,0:T(8,128)S(1)}, u32[]{:S(2)}, u32[]{:S(2)}) async-start(f32[8,8,448]{2,1,0:T(8,128)} %broadcast_in_dim.18), calls=%async_computation.3 | async-start | bytes 262144 | tf_op jit(solution)/shard_map/all_to_all | solution.py:37
  124.2 18.5 %collective-permute-start.10 = (bf16[32,3584]{1,0:T(8,128)(2,1)}, bf16[32,3584]{1,0:T(8,128)(2,1)}, u32[]{:S(2)}, u32[]{:S(2)}) collective-permute-start(bf16[32,3584]{1,0:T(8,128)(2,1)} %fusion.17), channel_id=1, source_target_pairs={{0,2},{2,0},{4,6},{6,4},{1,3},{3,1},{5,7},{7,5},{8,10},{10,8},{12,... | collective-permute-start | bytes 688136 | tf_op jit(solution)/shard_map/ppermute | solution.py:124
  128.3 14.4 %collective-permute-start.8 = (bf16[32,3584]{1,0:T(8,128)(2,1)}, bf16[32,3584]{1,0:T(8,128)(2,1)}, u32[]{:S(2)}, u32[]{:S(2)}) collective-permute-start(bf16[32,3584]{1,0:T(8,128)(2,1)} %fusion.18), channel_id=1, source_target_pairs={{0,6},{2,4},{4,2},{6,0},{1,7},{3,5},{5,3},{7,1},{8,14},{10,12},{12... | collective-permute-start | bytes 688136 | tf_op jit(solution)/shard_map/ppermute | solution.py:123
  133.6 32.4 %all-to-all-start.5 = ((bf16[32,32,512]{2,1,0:T(8,128)(2,1)}), bf16[32,32,512]{2,1,0:T(8,128)(2,1)S(1)}, u32[]{:S(2)}, u32[]{:S(2)}) async-start(bf16[32,32,512]{2,1,0:T(8,128)(2,1)} %pad_maximum_fusion.2), calls=%async_computation.5 | async-start | bytes 2097152 | tf_op jit(solution)/shard_map/all_to_all | solution.py:136
  146.4 5.4 %collective-permute-start.11 = (bf16[256,1792]{1,0:T(8,128)(2,1)S(1)}, bf16[256,1792]{1,0:T(8,128)(2,1)S(1)}, u32[]{:S(2)}, u32[]{:S(2)}) collective-permute-start(bf16[256,1792]{1,0:T(8,128)(2,1)S(1)} %constant_dynamic-slice_fusion.3), channel_id=1, source_target_pairs={{0,8},{8,0},{1,9},{9,1},{2,10},{10,2},{3,11},{11,3},{4,12},{12,4},... | collective-permute-start | bytes 2752520 | tf_op jit(solution)/shard_map/ppermute | solution.py:25
  154.4 19.5 %copy-start.1 = (bf16[256,3584]{0,1:T(8,128)(2,1)S(1)}, bf16[256,3584]{0,1:T(8,128)(2,1)}, u32[]{:S(2)}) copy-start(bf16[256,3584]{0,1:T(8,128)(2,1)} %copy.56) | copy-start | bytes 5505028
  166.1 33.7 %all-to-all-start.4 = ((bf16[32,64,256]{2,1,0:T(8,128)(2,1)}), bf16[32,64,256]{2,1,0:T(8,128)(2,1)}, u32[]{:S(2)}, u32[]{:S(2)}) async-start(bf16[32,64,256]{2,1,0:T(8,128)(2,1)} %pad_maximum_fusion.1), calls=%async_computation.4 | async-start | bytes 2097152 | tf_op jit(solution)/shard_map/all_to_all | solution.py:157
  175.5 8.6 %collective-permute-start.14 = (bf16[1024,448]{0,1:T(8,128)(2,1)}, bf16[1024,448]{0,1:T(8,128)(2,1)}, u32[]{:S(2)}, u32[]{:S(2)}) collective-permute-start(bf16[1024,448]{0,1:T(8,128)(2,1)} %copy.55), channel_id=1, source_target_pairs={{0,8},{8,0},{1,9},{9,1},{2,10},{10,2},{3,11},{11,3},{4,12},{12,4},... | collective-permute-start | bytes 2752520 | tf_op jit(solution)/shard_map/ppermute | solution.py:25
  (1 other events, 0.8 us)

commit v6 on v5

--- a/solution.py
+++ b/solution.py
@@ -13,8 +13,8 @@
 TENSOR = ("x", "zh")
 PLANE = ("zl", "y")
 DP = ("zl", "y", "c")
-N_T = 8
-N_P = 32
+N_T, N_Y, N_Z = 8, 8, 4
+N_P = N_Y * N_Z
 
 
 def xor(axis, size, bits):
@@ -61,7 +61,6 @@
     rows, feats = item_cache.shape
     width = out_proj.shape[1]
     tokens, heads = attn_heads.shape
-    half = N_P * rows
     core = lax.axis_index("c")
     x_index = lax.axis_index("x")
     z_index = lax.axis_index("zh")
@@ -86,60 +85,81 @@
     mixed_give = lax.dynamic_index_in_dim(mixed_x, 1 - z_index, 0, keepdims=False)
     mixed_keep = lax.dynamic_index_in_dim(mixed_x, z_index, 0, keepdims=False)
     mixed_give = mixed_give.astype(BF16)
+
+    users_own = to_all(tie(user_cache, mixed[0, 0]), "y", N_Y).reshape(N_Y * rows, feats)
+    users = (users_own, swap(users_own))
+    place = lax.broadcasted_iota(jnp.int32, (rows, 64), 1)
+    place = jnp.where(place == 0, positive[:, None] // 64, positive[:, None] % 64).astype(BF16)
+    items = jnp.concatenate([item_cache, place], axis=1)
+    items = to_all(tie(items, users_own), "zl", N_Z).reshape(N_Z * rows, feats + 64)
+    place = items[:, feats : feats + 2].astype(jnp.int32)
+    items = items[:, :feats]
+    columns = 2 * N_Y * rows
+    own = N_Z * rows // N_T
+
+    partial = jnp.concatenate([dot(items, u, ((1,), (1,))) for u in users], axis=1)
+    partial = partial.reshape(N_T, own, columns)
+    scores = jnp.sum(lax.all_to_all(partial, TENSOR, 0, 0), axis=0) * LOGIT_SCALE
+
+    place = lax.dynamic_slice_in_dim(place, (2 * x_index + z_index) * own, own, 0)
+    place = place[:, :1] * 64 + place[:, 1:]
+    owner, row_in = place // rows, place % rows
+    column = (owner % 2 != core).astype(jnp.int32) * N_Y * rows + (owner // 2 % N_Y) * rows + row_in
+    column = jnp.where(owner // (2 * N_Y) == lax.axis_index("zl"), column, -1)
+    target = column == lax.broadcasted_iota(jnp.int32, (1, columns), 1)
+    maxima = jnp.max(scores, axis=1, keepdims=True)
+    sums = jnp.sum(jnp.exp(scores - maxima), axis=1, keepdims=True)
+    picked = jnp.sum(jnp.where(target, scores, F32(0.0)), axis=1, keepdims=True)
+    lane = lax.broadcasted_iota(jnp.int32, (own, 128), 1)
+    stats = jnp.where(lane == 0, maxima, jnp.where(lane == 1, sums, picked))
+    stats = to_all(stats, "zl", N_Z)
+    top = jnp.max(stats[:, :, :1], axis=0)
+    log_total = top + jnp.log(jnp.sum(stats[:, :, 1:2] * jnp.exp(stats[:, :, :1] - top), axis=0))
+    losses = log_total - jnp.sum(stats[:, :, 2:3], axis=0)
+    grad = (jnp.exp(scores - log_total) - target.astype(F32)).astype(BF16)
+    high, middle, low = three_terms(losses)
+    losses = jnp.where(lane == 0, high, jnp.where(lane == 1, middle, low))
+    losses = jnp.where(lane < 3, losses, BF16(0.0))
+    tile = to_all(jnp.concatenate([grad, losses], axis=1), TENSOR, N_T)
+    tile = tile.reshape(N_Z * rows, columns + 128)
+    losses = jnp.sum(tile[:, columns:].astype(F32), axis=0, keepdims=True)
+    tile = tile[:, :columns]
+    item_part = dot(tile[:, : columns // 2], users[0], ((1,), (0,)))
+    item_part += dot(tile[:, columns // 2 :], users[1], ((1,), (0,)))
+    item_part = lax.all_to_all(item_part.reshape(N_Z, rows, feats), "zl", 0, 0)
+    item_grad = jnp.sum(item_part, axis=0) * LOGIT_SCALE
+    group_rows = to_all(item_grad[:GROUP], TENSOR, N_T)
+
+    user_part = dot(tile, items, ((0,), (0,)))
+    losses = jnp.pad(jnp.concatenate(three_terms(losses)), ((0, 13), (0, feats - 128)))
+    give = jnp.concatenate([user_part[columns // 2 :].astype(BF16), losses], axis=0)
+    give = swap(tie(give, item_part))
+    losses = losses[:8].astype(F32) + give[columns // 2 : columns // 2 + 8].astype(F32)
+    user_part = (user_part[: columns // 2] + give[: columns // 2].astype(F32)).astype(BF16)
+    user_part = tie(user_part.reshape(N_Y, rows, feats), group_rows)
+    user_grad = jnp.sum(lax.all_to_all(user_part, "y", 0, 0).astype(F32), axis=0) * LOGIT_SCALE
+
     from_z = lax.ppermute(mixed_give, **xor("zh", 2, 1))
-
-    users_own = to_all(tie(user_cache, mixed), PLANE, N_P).reshape(half, feats)
-    users = (users_own, swap(users_own))
-
-    partial = jnp.concatenate([dot(item_cache, u, ((1,), (1,))) for u in users], axis=1)
-    share = 2 * half // N_T
-    attn_other = swap(tie(attn, partial))
-    partial = partial.reshape(rows, N_T, share).transpose(1, 0, 2)
-    scores_own = jnp.sum(lax.all_to_all(partial, TENSOR, 0, 0), axis=0) * LOGIT_SCALE
-    scores = to_all(scores_own, TENSOR, N_T).transpose(1, 0, 2).reshape(rows, 2 * half)
-
     own_tokens = (2 * x_index + z_index) * z_block
     own_residual = lax.dynamic_slice_in_dim(residual, own_tokens, z_block, 0).astype(F32)
     hidden_own = mixed_keep + tie(from_z, partial).astype(F32) + own_residual
     hidden_own = core_major(hidden_own.astype(BF16))
-    hidden_z = tie(lax.ppermute(hidden_own, **xor("zh", 2, 1)), scores_own)
+    hidden_z = tie(lax.ppermute(hidden_own, **xor("zh", 2, 1)), scores)
     pair = jnp.stack([hidden_own, hidden_z])
     hidden_0 = jnp.where(z_index == 0, pair, pair[::-1])
     hidden_1 = lax.ppermute(hidden_0, **xor("x", 4, 1))
     hidden_3 = lax.ppermute(hidden_0, **xor("x", 4, 3))
-    owner, row_in = positive // rows, positive % rows
-    column = (owner % 2 != core).astype(jnp.int32) * half + (owner // 2) * rows + row_in
-    maxima = jnp.max(scores, axis=1, keepdims=True)
-    log_total = maxima[:, 0] + jnp.log(jnp.sum(jnp.exp(scores - maxima), axis=1))
-    target = column[:, None] == lax.broadcasted_iota(jnp.int32, (1, 2 * half), 1)
-    picked = jnp.sum(jnp.where(target, scores, F32(0.0)), axis=1)
-    losses = jnp.concatenate(three_terms(log_total - picked))
-    grad = (jnp.exp(scores - log_total[:, None]) - target.astype(F32)).astype(BF16)
-    item_grad = (
-        dot(grad[:, :half], users[0], ((1,), (0,))) + dot(grad[:, half:], users[1], ((1,), (0,)))
-    ) * LOGIT_SCALE
-    group_rows = to_all(item_grad[:GROUP], TENSOR, N_T)
     hidden_2 = [
-        lax.ppermute(tie(hidden_1[0], item_grad), **xor("x", 4, 3)),
-        lax.ppermute(tie(hidden_3[1], item_grad), **xor("x", 4, 1)),
+        lax.ppermute(tie(hidden_1[0], grad), **xor("x", 4, 3)),
+        lax.ppermute(tie(hidden_3[1], grad), **xor("x", 4, 1)),
     ]
-
-    grad_losses = jnp.zeros((8, half), BF16).at[0, : 3 * rows].set(losses)
-    other = swap(jnp.concatenate([grad[:, half:], grad_losses], axis=0))
-    losses = jnp.concatenate([losses, other[rows, : 3 * rows]])
-    losses = jnp.zeros((8, heads), BF16).at[0, : 6 * rows].set(losses)
-    both = jnp.concatenate([grad[:, :half], other[:rows]], axis=0)
-    both = both.T.reshape(N_P, rows, 2 * rows)
-    by_plane = jnp.concatenate(
-        [jnp.broadcast_to(item_cache[None], (N_P, rows, feats)), both], axis=2
-    )
-    by_plane = lax.all_to_all(by_plane, PLANE, 0, 0)
+    attn_other = swap(tie(attn, partial))
 
     group_rows = core_major(group_rows.transpose(1, 0, 2).reshape(GROUP, width))
     upstream = core_major(norm_gain)[None, :] * (
         by_xor(group_rows.reshape(4, -1), x_index).reshape(GROUP, width) / SEQ
     )
-    hidden_2 = tie(jnp.stack(hidden_2), group_rows)
+    hidden_2 = tie(jnp.stack(hidden_2), item_grad)
     hidden = jnp.concatenate([hidden_0, hidden_1, hidden_2, hidden_3], axis=0).astype(F32)
     inverse = lax.rsqrt(jnp.mean(hidden * hidden, axis=2, keepdims=True) + NORM_EPS)
     inner = jnp.sum(upstream[:, None, :] * hidden, axis=2, keepdims=True) / width
@@ -153,18 +173,15 @@
     attn_other = tie(attn_other, scores)
     weight = dot(stream_keep, attn, ((0,), (0,))) + dot(stream_other, attn_other, ((0,), (0,)))
     weight = weight.astype(BF16).reshape(N_P, cut, heads)
+    losses = losses[:1, :heads] + losses[1:2, :heads] + losses[2:3, :heads]
+    losses = jnp.pad(jnp.concatenate(three_terms(losses)), ((0, 5), (0, 0)))
     final = jnp.concatenate([weight, jnp.broadcast_to(losses[None], (N_P, 8, heads))], axis=1)
     final = lax.all_to_all(final, PLANE, 0, 0)
     head_grad = dot(stream, core_major(tie(out_proj, weight[0])), ((1,), (1,))).astype(BF16)
     head_grad = by_xor(head_grad.reshape(4, x_block, heads), x_index).reshape(tokens, heads)
-    items_own = by_plane[:, :, :feats].reshape(half, feats)
-    by_item = by_plane[:, :, feats:].reshape(N_P, rows, 2, rows).transpose(2, 0, 3, 1)
-    by_item = by_item.reshape(2, half, rows)
-    user_grad = (
-        dot(by_item[0], items_own, ((0,), (0,))) + dot(by_item[1], swap(items_own), ((0,), (0,)))
-    ) * LOGIT_SCALE
     weight_grad = jnp.sum(final[:, :cut].astype(F32), axis=0).T
-    loss_mean = jnp.sum(final[:, cut].astype(F32)) / (2 * half)
+    loss_mean = jnp.sum(final[:, cut].astype(F32)) / (N_Z * 2 * N_P * rows)
+    loss_mean += jnp.sum(final[:, cut + 1 : cut + 3].astype(F32)) / (N_Z * 2 * N_P * rows)
     return (loss_mean, item_grad, user_grad, head_grad, weight_grad)
 
 

time: 209 us -> 220 us (1.053)
  starting transfers between devices: 95.6 us -> 116 us
  waiting for transfers between devices: 46.5 us -> 38.1 us
  matrix products: 9.91 us -> 6.18 us
  other arithmetic: 20.5 us -> 23.5 us
    all_to_all x3 -> x5, waiting for transfers between devices: 17.5 us -> 5.62 us  [to_all(): lax.all_to_all(jnp.broadcast_to(value[None], (count,) + value.shape), axe...]
    all_to_all x3 -> x5, starting transfers between devices: 21.7 us -> 32 us  [to_all(): lax.all_to_all(jnp.broadcast_to(value[None], (count,) + value.shape), axe...]
    all_to_all x1, waiting for transfers between devices: 13.5 us -> 20.2 us  [per_device(): final = lax.all_to_all(final, PLANE, 0, 0)]
    all_to_all x1 -> x2, starting transfers between devices: 6.57 us -> 13 us  [the longest x1 6.64 us: per_device(): lax.all_to_all(user_part, 'y', 0, 0).astype(F32)]
    all_to_all x1, starting transfers between devices: 3.42 us -> 8.27 us  [per_device(): lax.all_to_all(partial, TENSOR, 0, 0)]
    dot_general x10 -> x9, matrix products: 9.91 us -> 6.18 us  [dot(): return lax.dot_general(a, b, (dims, ((), ())), preferred_element_type=F32)]
    ppermute x3, waiting for transfers between devices: 2.9 us -> 0.01 us  [the longest x1 0.01 us: per_device(): hidden_z = tie(lax.ppermute(hidden_own, **xor('zh', 2, 1)), scores)]
    reshape x5 -> x0, local copies, waits for them, and re-layouts: 2.8 us -> none  [the longest x1 1.32 us: per_device(): items_own = by_plane[:, :, :feats].reshape(half, feats)]
  transfers between devices with their start and end apart: 21 -> 23, of which waited for: 6 -> 8; matrix products, arithmetic and copies ran while one was open for 22% -> 20% of each run, Pallas kernels for 0% -> 0%
where the time goes in v6:
time: 220 us; the launch traced here: 216 us
  starting transfers between devices  116 us (53%)
  waiting for transfers between devices  38.1 us (17%)
  other arithmetic  23.5 us (11%)
  local copies, waits for them, and re-layouts  22.4 us (10%)
  between operations  9.76 us (4%)
  matrix products  6.18 us (3%)
    all_to_all x5, starting transfers between devices, to_all(): lax.all_to_all(jnp.broadcast_to(value[None], (count,) + value.shape), axe...  32 us
    all_to_all x1, waiting for transfers between devices, per_device(): final = lax.all_to_all(final, PLANE, 0, 0)  20.2 us
    ppermute x4, starting transfers between devices, swap(): return lax.ppermute(value, **xor('c', 2, 1))  19 us
    all_to_all x1, waiting for transfers between devices, per_device(): lax.all_to_all(user_part, 'y', 0, 0).astype(F32)  8.75 us
    all_to_all x1, starting transfers between devices, per_device(): lax.all_to_all(partial, TENSOR, 0, 0)  8.27 us
    ppermute x1, starting transfers between devices, per_device(): from_z = lax.ppermute(mixed_give, **xor('zh', 2, 1))  7.27 us
    ppermute x1, starting transfers between devices, per_device(): hidden_z = tie(lax.ppermute(hidden_own, **xor('zh', 2, 1)), scores)  6.98 us
    all_to_all x1, starting transfers between devices, per_device(): lax.all_to_all(user_part, 'y', 0, 0).astype(F32)  6.64 us
  transfers between devices with their start and end apart: 23, of which 8 were waited for; matrix products, arithmetic and copies ran while one was open for 20% of the time, Pallas kernels for 0%

profile of v6, /device:TPU:1, one launch (start us, length us, event | category | flops | bytes accessed | tf_op | source)
XLA Modules:
  0.0 215.9 jit_solution(5570849547146957908)
XLA Ops:
  1.5 2.1 convolution_convert_fusion
  6.5 7.7 %all-to-all-start = ((bf16[8,32,448]{2,1,0:T(8,128)(2,1)}), bf16[8,32,448]{2,1,0:T(8,128)(2,1)S(1)}, u32[]{:S(2)}, u32[]{:S(2)}) async-start(bf16[8,32,448]{2,1,0:T(8,128)(2,1)} %broadcast_in_dim.88), calls=%async_computation | async-start | bytes 524288 | tf_op jit(solution)/shard_map/all_to_all | solution.py:37
  14.1 3.1 %collective-permute-start.2 = (bf16[32,3584]{1,0:T(8,128)(2,1)}, bf16[32,3584]{1,0:T(8,128)(2,1)}, u32[]{:S(2)}, u32[]{:S(2)}) collective-permute-start(bf16[32,3584]{1,0:T(8,128)(2,1)} %get-tuple-element.18), channel_id=1, source_target_pairs={{0,2},{2,0},{4,6},{6,4},{1,3},{3,1},{5,7},{7,5},{8,10},{10,8},{12,... | collective-permute-start | bytes 688136 | tf_op jit(solution)/shard_map/ppermute | solution.py:74
  17.3 3.7 %collective-permute-start = (bf16[32,3584]{1,0:T(8,128)(2,1)}, bf16[32,3584]{1,0:T(8,128)(2,1)}, u32[]{:S(2)}, u32[]{:S(2)}) collective-permute-start(bf16[32,3584]{1,0:T(8,128)(2,1)} %get-tuple-element.19), channel_id=1, source_target_pairs={{0,6},{2,4},{4,2},{6,0},{1,7},{3,5},{5,3},{7,1},{8,14},{10,12},{12... | collective-permute-start | bytes 688136 | tf_op jit(solution)/shard_map/ppermute | solution.py:75
  21.1 3.8 %copy.87 = bf16[256,3584]{0,1:T(8,128)(2,1)} copy(bf16[256,3584]{1,0:T(8,128)(2,1)} %param.12) | data formatting | bytes 3670016 | tf_op args[5]
  26.3 1.8 fusion.12
  28.2 3.9 %collective-permute-start.3 = (bf16[2,32,3584]{2,1,0:T(8,128)(2,1)S(1)}, bf16[2,32,3584]{2,1,0:T(8,128)(2,1)S(1)}, u32[]{:S(2)}, u32[]{:S(2)}) collective-permute-start(bf16[2,32,3584]{2,1,0:T(8,128)(2,1)S(1)} %pad_maximum_fusion.3), channel_id=1, source_target_pairs={{0,6},{2,4},{4,2},{6,0},{1,7},{3,5},{5,3},{7,1},{8,14},{10,12},{12... | collective-permute-start | bytes 1376264 | tf_op jit(solution)/shard_map/ppermute | solution.py:82
  34.1 7.0 %all-to-all-start.1 = ((bf16[4,32,512]{2,1,0:T(8,128)(2,1)}), bf16[4,32,512]{2,1,0:T(8,128)(2,1)S(1)}, u32[]{:S(2)}, u32[]{:S(2)}) async-start(bf16[4,32,512]{2,1,0:T(8,128)(2,1)} %broadcast_in_dim.124), calls=%async_computation.1 | async-start | bytes 262144 | tf_op jit(solution)/shard_map/all_to_all | solution.py:37
  42.0 1.9 collective-permute-start.1
  44.0 4.6 %collective-permute-start.6 = (bf16[256,448]{1,0:T(8,128)(2,1)S(1)}, bf16[256,448]{1,0:T(8,128)(2,1)S(1)}, u32[]{:S(2)}, u32[]{:S(2)}) collective-permute-start(bf16[256,448]{1,0:T(8,128)(2,1)S(1)} %bitcast.122), channel_id=1, source_target_pairs={{0,8},{8,0},{1,9},{9,1},{2,10},{10,2},{3,11},{11,3},{4,12},{12,4},... | collective-permute-start | bytes 688136 | tf_op jit(solution)/shard_map/ppermute | solution.py:25
  50.8 3.0 %collective-permute-start.12 = (bf16[256,256]{1,0:T(8,128)(2,1)}, bf16[256,256]{1,0:T(8,128)(2,1)}, u32[]{:S(2)}, u32[]{:S(2)}) collective-permute-start(bf16[256,256]{1,0:T(8,128)(2,1)} %broadcast_add_fusion.1), channel_id=1, source_target_pairs={{0,8},{8,0},{1,9},{9,1},{2,10},{10,2},{3,11},{11,3},{4,12},{12,4},... | collective-permute-start | bytes 393224 | tf_op jit(solution)/shard_map/ppermute | solution.py:25
  55.0 8.3 %all-to-all-start.2 = ((f32[8,16,512]{2,1,0:T(8,128)}), f32[8,16,512]{2,1,0:T(8,128)S(1)}, u32[]{:S(2)}, u32[]{:S(2)}) async-start(f32[8,16,512]{2,1,0:T(8,128)} %bitcast.21), calls=%async_computation.2 | async-start | bytes 524288 | tf_op jit(solution)/shard_map/all_to_all | solution.py:102
  64.5 7.3 %collective-permute-start.4 = (bf16[32,3584]{1,0:T(8,128)(2,1)S(1)}, bf16[32,3584]{1,0:T(8,128)(2,1)S(1)}, u32[]{:S(2)}, u32[]{:S(2)}) collective-permute-start(bf16[32,3584]{1,0:T(8,128)(2,1)S(1)} %fusion.11), channel_id=1, source_target_pairs={{0,1},{1,0},{2,3},{3,2},{4,5},{5,4},{6,7},{7,6},{8,9},{9,8},{10,11... | collective-permute-start | bytes 688136 | tf_op jit(solution)/shard_map/ppermute | solution.py:142
  71.8 1.8 all-to-all-done.2
  74.6 7.6 %all-to-all-start.3 = ((f32[4,16,128]{2,1,0:T(8,128)}), f32[4,16,128]{2,1,0:T(8,128)S(1)}, u32[]{:S(2)}, u32[]{:S(2)}) async-start(f32[4,16,128]{2,1,0:T(8,128)} %broadcast_in_dim.129), calls=%async_computation.3 | async-start | bytes 65536 | tf_op jit(solution)/shard_map/all_to_all | solution.py:37
  86.1 7.0 %collective-permute-start.5 = (bf16[32,3584]{1,0:T(8,128)(2,1)S(1)}, bf16[32,3584]{1,0:T(8,128)(2,1)S(1)}, u32[]{:S(2)}, u32[]{:S(2)}) collective-permute-start(bf16[32,3584]{1,0:T(8,128)(2,1)S(1)} %reshape.447), channel_id=1, source_target_pairs={{0,1},{1,0},{2,3},{3,2},{4,5},{5,4},{6,7},{7,6},{8,9},{9,8},{10,11... | collective-permute-start | bytes 688136 | tf_op jit(solution)/shard_map/ppermute | solution.py:147
  96.8 4.2 %all-to-all-start.4 = ((bf16[8,16,640]{2,1,0:T(8,128)(2,1)}), bf16[8,16,640]{2,1,0:T(8,128)(2,1)S(1)}, u32[]{:S(2)}, u32[]{:S(2)}) async-start(bf16[8,16,640]{2,1,0:T(8,128)(2,1)} %broadcast_in_dim.134), calls=%async_computation.4 | async-start | bytes 327680 | tf_op jit(solution)/shard_map/all_to_all | solution.py:37
  101.2 4.6 %collective-permute-start.9 = (bf16[2,32,3584]{2,1,0:T(8,128)(2,1)S(1)}, bf16[2,32,3584]{2,1,0:T(8,128)(2,1)S(1)}, u32[]{:S(2)}, u32[]{:S(2)}) collective-permute-start(bf16[2,32,3584]{2,1,0:T(8,128)(2,1)S(1)} %reverse_select_fusion), channel_id=1, source_target_pairs={{0,6},{2,4},{4,2},{6,0},{1,7},{3,5},{5,3},{7,1},{8,14},{10,12},{12... | collective-permute-start | bytes 1376264 | tf_op jit(solution)/shard_map/ppermute | solution.py:151
  105.8 1.9 collective-permute-start.7
  107.7 3.0 %all-to-all-done.4 = bf16[8,16,640]{2,1,0:T(8,128)(2,1)S(1)} async-done(((bf16[8,16,640]{2,1,0:T(8,128)(2,1)}), bf16[8,16,640]{2,1,0:T(8,128)(2,1)S(1)}, u32[]{:S(2)}, u32[]{:S(2)}) %all-to-all-start.4) | async-done | bytes 163872 | tf_op jit(solution)/shard_map/all_to_all | solution.py:37
  112.8 6.4 %all-to-all-start.5 = ((f32[4,32,448]{2,1,0:T(8,128)}), f32[4,32,448]{2,1,0:T(8,128)}, u32[]{:S(2)}, u32[]{:S(2)}) async-start(f32[4,32,448]{2,1,0:T(8,128)} %bitcast.30), calls=%async_computation.5 | async-start | bytes 524288 | tf_op jit(solution)/shard_map/all_to_all | solution.py:129
  120.0 2.0 collective-permute-start.10
  122.7 3.0 %collective-permute-start.8 = (bf16[32,3584]{1,0:T(8,128)(2,1)}, bf16[32,3584]{1,0:T(8,128)(2,1)}, u32[]{:S(2)}, u32[]{:S(2)}) collective-permute-start(bf16[32,3584]{1,0:T(8,128)(2,1)} %fusion.15), channel_id=1, source_target_pairs={{0,6},{2,4},{4,2},{6,0},{1,7},{3,5},{5,3},{7,1},{8,14},{10,12},{12... | collective-permute-start | bytes 688136 | tf_op jit(solution)/shard_map/ppermute | solution.py:153
  130.8 5.6 %all-to-all-start.6 = ((f32[8,8,448]{2,1,0:T(8,128)}), f32[8,8,448]{2,1,0:T(8,128)S(1)}, u32[]{:S(2)}, u32[]{:S(2)}) async-start(f32[8,8,448]{2,1,0:T(8,128)} %broadcast_in_dim.135), calls=%async_computation.6 | async-start | bytes 262144 | tf_op jit(solution)/shard_map/all_to_all | solution.py:37
  137.2 5.1 %collective-permute-start.13 = (bf16[272,448]{1,0:T(8,128)(2,1)}, bf16[272,448]{1,0:T(8,128)(2,1)}, u32[]{:S(2)}, u32[]{:S(2)}) collective-permute-start(bf16[272,448]{1,0:T(8,128)(2,1)} %maximum_add_fusion.1), channel_id=1, source_target_pairs={{0,8},{8,0},{1,9},{9,1},{2,10},{10,2},{3,11},{11,3},{4,12},{12,4},... | collective-permute-start | bytes 731144 | tf_op jit(solution)/shard_map/ppermute | solution.py:25
  143.2 2.6 %all-to-all-done.6 = f32[8,8,448]{2,1,0:T(8,128)S(1)} async-done(((f32[8,8,448]{2,1,0:T(8,128)}), f32[8,8,448]{2,1,0:T(8,128)S(1)}, u32[]{:S(2)}, u32[]{:S(2)}) %all-to-all-start.6) | async-done | bytes 114720 | tf_op jit(solution)/shard_map/all_to_all | solution.py:37
  151.7 6.3 %collective-permute-start.11 = (bf16[256,1792]{1,0:T(8,128)(2,1)}, bf16[256,1792]{1,0:T(8,128)(2,1)}, u32[]{:S(2)}, u32[]{:S(2)}) collective-permute-start(bf16[256,1792]{1,0:T(8,128)(2,1)} %constant_dynamic-slice_fusion.4), channel_id=1, source_target_pairs={{0,8},{8,0},{1,9},{9,1},{2,10},{10,2},{3,11},{11,3},{4,12},{12,4},... | collective-permute-start | bytes 2752520 | tf_op jit(solution)/shard_map/ppermute | solution.py:25
  159.2 1.7 fusion.10
  161.0 6.6 %all-to-all-start.8 = ((bf16[8,32,448]{2,1,0:T(8,128)(2,1)}), bf16[8,32,448]{2,1,0:T(8,128)(2,1)}, u32[]{:S(2)}, u32[]{:S(2)}) async-start(bf16[8,32,448]{2,1,0:T(8,128)(2,1)} %bitcast.135), calls=%async_computation.8 | async-start | bytes 524288 | tf_op jit(solution)/shard_map/all_to_all | solution.py:140
  171.3 8.7 %all-to-all-done.8 = bf16[8,32,448]{2,1,0:T(8,128)(2,1)} async-done(((bf16[8,32,448]{2,1,0:T(8,128)(2,1)}), bf16[8,32,448]{2,1,0:T(8,128)(2,1)}, u32[]{:S(2)}, u32[]{:S(2)}) %all-to-all-start.8) | async-done | bytes 229408 | tf_op jit(solution)/shard_map/all_to_all | solution.py:140
  180.1 5.3 %all-to-all-start.7 = ((bf16[32,64,256]{2,1,0:T(8,128)(2,1)}), bf16[32,64,256]{2,1,0:T(8,128)(2,1)S(1)}, u32[]{:S(2)}, u32[]{:S(2)}) async-start(bf16[32,64,256]{2,1,0:T(8,128)(2,1)} %pad_maximum_fusion.1), calls=%async_computation.7 | async-start | bytes 2097152 | tf_op jit(solution)/shard_map/all_to_all | solution.py:179
  191.2 20.2 %all-to-all-done.7 = bf16[32,64,256]{2,1,0:T(8,128)(2,1)S(1)} async-done(((bf16[32,64,256]{2,1,0:T(8,128)(2,1)}), bf16[32,64,256]{2,1,0:T(8,128)(2,1)S(1)}, u32[]{:S(2)}, u32[]{:S(2)}) %all-to-all-start.7) | async-done | bytes 1048608 | tf_op jit(solution)/shard_map/all_to_all | solution.py:179
  (154 shorter events, 44.3 us)
Async XLA Ops:
  3.7 17.3 %copy-start.12 = (s32[32]{0:T(128)S(1)}, s32[32]{0:T(128)}, u32[]{:S(2)}) copy-start(s32[32]{0:T(128)} %param.9) | copy-start | bytes 388
  3.7 17.4 %copy-start.11 = (f32[3584]{0:T(1024)S(1)}, f32[3584]{0:T(1024)}, u32[]{:S(2)}) copy-start(f32[3584]{0:T(1024)} %param.13) | copy-start | bytes 43012
  6.5 25.7 %all-to-all-start = ((bf16[8,32,448]{2,1,0:T(8,128)(2,1)}), bf16[8,32,448]{2,1,0:T(8,128)(2,1)S(1)}, u32[]{:S(2)}, u32[]{:S(2)}) async-start(bf16[8,32,448]{2,1,0:T(8,128)(2,1)} %broadcast_in_dim.88), calls=%async_computation | async-start | bytes 524288 | tf_op jit(solution)/shard_map/all_to_all | solution.py:37
  14.1 11.1 %collective-permute-start.2 = (bf16[32,3584]{1,0:T(8,128)(2,1)}, bf16[32,3584]{1,0:T(8,128)(2,1)}, u32[]{:S(2)}, u32[]{:S(2)}) collective-permute-start(bf16[32,3584]{1,0:T(8,128)(2,1)} %get-tuple-element.18), channel_id=1, source_target_pairs={{0,2},{2,0},{4,6},{6,4},{1,3},{3,1},{5,7},{7,5},{8,10},{10,8},{12,... | collective-permute-start | bytes 688136 | tf_op jit(solution)/shard_map/ppermute | solution.py:74
  17.3 9.1 %collective-permute-start = (bf16[32,3584]{1,0:T(8,128)(2,1)}, bf16[32,3584]{1,0:T(8,128)(2,1)}, u32[]{:S(2)}, u32[]{:S(2)}) collective-permute-start(bf16[32,3584]{1,0:T(8,128)(2,1)} %get-tuple-element.19), channel_id=1, source_target_pairs={{0,6},{2,4},{4,2},{6,0},{1,7},{3,5},{5,3},{7,1},{8,14},{10,12},{12... | collective-permute-start | bytes 688136 | tf_op jit(solution)/shard_map/ppermute | solution.py:75
  24.9 8.4 %copy-start.9 = (bf16[32,448]{1,0:T(8,128)(2,1)S(1)}, bf16[32,448]{1,0:T(8,128)(2,1)}, u32[]{:S(2)}) copy-start(bf16[32,448]{1,0:T(8,128)(2,1)} %param.7) | copy-start | bytes 86020
  28.2 35.1 %collective-permute-start.3 = (bf16[2,32,3584]{2,1,0:T(8,128)(2,1)S(1)}, bf16[2,32,3584]{2,1,0:T(8,128)(2,1)S(1)}, u32[]{:S(2)}, u32[]{:S(2)}) collective-permute-start(bf16[2,32,3584]{2,1,0:T(8,128)(2,1)S(1)} %pad_maximum_fusion.3), channel_id=1, source_target_pairs={{0,6},{2,4},{4,2},{6,0},{1,7},{3,5},{5,3},{7,1},{8,14},{10,12},{12... | collective-permute-start | bytes 1376264 | tf_op jit(solution)/shard_map/ppermute | solution.py:82
  34.1 14.5 %all-to-all-start.1 = ((bf16[4,32,512]{2,1,0:T(8,128)(2,1)}), bf16[4,32,512]{2,1,0:T(8,128)(2,1)S(1)}, u32[]{:S(2)}, u32[]{:S(2)}) async-start(bf16[4,32,512]{2,1,0:T(8,128)(2,1)} %broadcast_in_dim.124), calls=%async_computation.1 | async-start | bytes 262144 | tf_op jit(solution)/shard_map/all_to_all | solution.py:37
  42.0 21.2 %collective-permute-start.1 = (bf16[2,32,3584]{2,1,0:T(8,128)(2,1)S(1)}, bf16[2,32,3584]{2,1,0:T(8,128)(2,1)}, u32[]{:S(2)}, u32[]{:S(2)}) collective-permute-start(bf16[2,32,3584]{2,1,0:T(8,128)(2,1)S(1)} %pad_maximum_fusion.2), channel_id=1, source_target_pairs={{0,2},{2,0},{4,6},{6,4},{1,3},{3,1},{5,7},{7,5},{8,10},{10,8},{12,... | collective-permute-start | bytes 1376264 | tf_op jit(solution)/shard_map/ppermute | solution.py:81
  44.0 10.0 %collective-permute-start.6 = (bf16[256,448]{1,0:T(8,128)(2,1)S(1)}, bf16[256,448]{1,0:T(8,128)(2,1)S(1)}, u32[]{:S(2)}, u32[]{:S(2)}) collective-permute-start(bf16[256,448]{1,0:T(8,128)(2,1)S(1)} %bitcast.122), channel_id=1, source_target_pairs={{0,8},{8,0},{1,9},{9,1},{2,10},{10,2},{3,11},{11,3},{4,12},{12,4},... | collective-permute-start | bytes 688136 | tf_op jit(solution)/shard_map/ppermute | solution.py:25
  50.8 116.8 %collective-permute-start.12 = (bf16[256,256]{1,0:T(8,128)(2,1)}, bf16[256,256]{1,0:T(8,128)(2,1)}, u32[]{:S(2)}, u32[]{:S(2)}) collective-permute-start(bf16[256,256]{1,0:T(8,128)(2,1)} %broadcast_add_fusion.1), channel_id=1, source_target_pairs={{0,8},{8,0},{1,9},{9,1},{2,10},{10,2},{3,11},{11,3},{4,12},{12,4},... | collective-permute-start | bytes 393224 | tf_op jit(solution)/shard_map/ppermute | solution.py:25
  54.0 47.0 %copy-start.6 = (bf16[256,448]{1,0:T(8,128)(2,1)}, bf16[256,448]{1,0:T(8,128)(2,1)S(1)}, u32[]{:S(2)}) copy-start(bf16[256,448]{1,0:T(8,128)(2,1)S(1)} %collective-permute-done.6) | copy-start | bytes 688132
  55.0 18.6 %all-to-all-start.2 = ((f32[8,16,512]{2,1,0:T(8,128)}), f32[8,16,512]{2,1,0:T(8,128)S(1)}, u32[]{:S(2)}, u32[]{:S(2)}) async-start(f32[8,16,512]{2,1,0:T(8,128)} %bitcast.21), calls=%async_computation.2 | async-start | bytes 524288 | tf_op jit(solution)/shard_map/all_to_all | solution.py:102
  64.5 17.9 %collective-permute-start.4 = (bf16[32,3584]{1,0:T(8,128)(2,1)S(1)}, bf16[32,3584]{1,0:T(8,128)(2,1)S(1)}, u32[]{:S(2)}, u32[]{:S(2)}) collective-permute-start(bf16[32,3584]{1,0:T(8,128)(2,1)S(1)} %fusion.11), channel_id=1, source_target_pairs={{0,1},{1,0},{2,3},{3,2},{4,5},{5,4},{6,7},{7,6},{8,9},{9,8},{10,11... | collective-permute-start | bytes 688136 | tf_op jit(solution)/shard_map/ppermute | solution.py:142
  74.6 19.6 %all-to-all-start.3 = ((f32[4,16,128]{2,1,0:T(8,128)}), f32[4,16,128]{2,1,0:T(8,128)S(1)}, u32[]{:S(2)}, u32[]{:S(2)}) async-start(f32[4,16,128]{2,1,0:T(8,128)} %broadcast_in_dim.129), calls=%async_computation.3 | async-start | bytes 65536 | tf_op jit(solution)/shard_map/all_to_all | solution.py:37
  86.1 14.9 %collective-permute-start.5 = (bf16[32,3584]{1,0:T(8,128)(2,1)S(1)}, bf16[32,3584]{1,0:T(8,128)(2,1)S(1)}, u32[]{:S(2)}, u32[]{:S(2)}) collective-permute-start(bf16[32,3584]{1,0:T(8,128)(2,1)S(1)} %reshape.447), channel_id=1, source_target_pairs={{0,1},{1,0},{2,3},{3,2},{4,5},{5,4},{6,7},{7,6},{8,9},{9,8},{10,11... | collective-permute-start | bytes 688136 | tf_op jit(solution)/shard_map/ppermute | solution.py:147
  96.8 13.9 %all-to-all-start.4 = ((bf16[8,16,640]{2,1,0:T(8,128)(2,1)}), bf16[8,16,640]{2,1,0:T(8,128)(2,1)S(1)}, u32[]{:S(2)}, u32[]{:S(2)}) async-start(bf16[8,16,640]{2,1,0:T(8,128)(2,1)} %broadcast_in_dim.134), calls=%async_computation.4 | async-start | bytes 327680 | tf_op jit(solution)/shard_map/all_to_all | solution.py:37
  101.2 18.0 %collective-permute-start.9 = (bf16[2,32,3584]{2,1,0:T(8,128)(2,1)S(1)}, bf16[2,32,3584]{2,1,0:T(8,128)(2,1)S(1)}, u32[]{:S(2)}, u32[]{:S(2)}) collective-permute-start(bf16[2,32,3584]{2,1,0:T(8,128)(2,1)S(1)} %reverse_select_fusion), channel_id=1, source_target_pairs={{0,6},{2,4},{4,2},{6,0},{1,7},{3,5},{5,3},{7,1},{8,14},{10,12},{12... | collective-permute-start | bytes 1376264 | tf_op jit(solution)/shard_map/ppermute | solution.py:151
  105.8 16.2 %collective-permute-start.7 = (bf16[2,32,3584]{2,1,0:T(8,128)(2,1)S(1)}, bf16[2,32,3584]{2,1,0:T(8,128)(2,1)S(1)}, u32[]{:S(2)}, u32[]{:S(2)}) collective-permute-start(bf16[2,32,3584]{2,1,0:T(8,128)(2,1)S(1)} %reverse_select_fusion), channel_id=1, source_target_pairs={{0,2},{2,0},{4,6},{6,4},{1,3},{3,1},{5,7},{7,5},{8,10},{10,8},{12,... | collective-permute-start | bytes 1376264 | tf_op jit(solution)/shard_map/ppermute | solution.py:150
  111.6 15.4 %copy-start.4 = (f32[512,448]{1,0:T(8,128)}, f32[512,448]{1,0:T(8,128)S(1)}, u32[]{:S(2)}) copy-start(f32[512,448]{1,0:T(8,128)S(1)} %fusion.16) | copy-start | bytes 2752516
  112.8 13.3 %all-to-all-start.5 = ((f32[4,32,448]{2,1,0:T(8,128)}), f32[4,32,448]{2,1,0:T(8,128)}, u32[]{:S(2)}, u32[]{:S(2)}) async-start(f32[4,32,448]{2,1,0:T(8,128)} %bitcast.30), calls=%async_computation.5 | async-start | bytes 524288 | tf_op jit(solution)/shard_map/all_to_all | solution.py:129
  120.0 22.3 %collective-permute-start.10 = (bf16[32,3584]{1,0:T(8,128)(2,1)}, bf16[32,3584]{1,0:T(8,128)(2,1)S(1)}, u32[]{:S(2)}, u32[]{:S(2)}) collective-permute-start(bf16[32,3584]{1,0:T(8,128)(2,1)} %fusion.14), channel_id=1, source_target_pairs={{0,2},{2,0},{4,6},{6,4},{1,3},{3,1},{5,7},{7,5},{8,10},{10,8},{12,... | collective-permute-start | bytes 688136 | tf_op jit(solution)/shard_map/ppermute | solution.py:154
  121.9 27.2 %copy-start.1 = (bf16[2,32,3584]{2,1,0:T(8,128)(2,1)}, bf16[2,32,3584]{2,1,0:T(8,128)(2,1)S(1)}, u32[]{:S(2)}) copy-start(bf16[2,32,3584]{2,1,0:T(8,128)(2,1)S(1)} %collective-permute-done.7) | copy-start | bytes 1376260
  122.7 19.5 %collective-permute-start.8 = (bf16[32,3584]{1,0:T(8,128)(2,1)}, bf16[32,3584]{1,0:T(8,128)(2,1)}, u32[]{:S(2)}, u32[]{:S(2)}) collective-permute-start(bf16[32,3584]{1,0:T(8,128)(2,1)} %fusion.15), channel_id=1, source_target_pairs={{0,6},{2,4},{4,2},{6,0},{1,7},{3,5},{5,3},{7,1},{8,14},{10,12},{12... | collective-permute-start | bytes 688136 | tf_op jit(solution)/shard_map/ppermute | solution.py:153
  127.1 20.9 %copy-start.8 = (f32[32,448]{1,0:T(8,128)}, f32[32,448]{1,0:T(8,128)S(1)}, u32[]{:S(2)}) copy-start(f32[32,448]{1,0:T(8,128)S(1)} %broadcast_multiply_fusion.2) | copy-start | bytes 172036
  130.8 15.1 %all-to-all-start.6 = ((f32[8,8,448]{2,1,0:T(8,128)}), f32[8,8,448]{2,1,0:T(8,128)S(1)}, u32[]{:S(2)}, u32[]{:S(2)}) async-start(f32[8,8,448]{2,1,0:T(8,128)} %broadcast_in_dim.135), calls=%async_computation.6 | async-start | bytes 262144 | tf_op jit(solution)/shard_map/all_to_all | solution.py:37
  137.2 21.3 %collective-permute-start.13 = (bf16[272,448]{1,0:T(8,128)(2,1)}, bf16[272,448]{1,0:T(8,128)(2,1)}, u32[]{:S(2)}, u32[]{:S(2)}) collective-permute-start(bf16[272,448]{1,0:T(8,128)(2,1)} %maximum_add_fusion.1), channel_id=1, source_target_pairs={{0,8},{8,0},{1,9},{9,1},{2,10},{10,2},{3,11},{11,3},{4,12},{12,4},... | collective-permute-start | bytes 731144 | tf_op jit(solution)/shard_map/ppermute | solution.py:25
  151.7 7.5 %copy-start.5 = (f32[512,448]{1,0:T(8,128)S(1)}, f32[512,448]{1,0:T(8,128)}, u32[]{:S(2)}) copy-start(f32[512,448]{1,0:T(8,128)} %copy-done.4) | copy-start | bytes 2752516
  151.7 16.0 %collective-permute-start.11 = (bf16[256,1792]{1,0:T(8,128)(2,1)}, bf16[256,1792]{1,0:T(8,128)(2,1)}, u32[]{:S(2)}, u32[]{:S(2)}) collective-permute-start(bf16[256,1792]{1,0:T(8,128)(2,1)} %constant_dynamic-slice_fusion.4), channel_id=1, source_target_pairs={{0,8},{8,0},{1,9},{9,1},{2,10},{10,2},{3,11},{11,3},{4,12},{12,4},... | collective-permute-start | bytes 2752520 | tf_op jit(solution)/shard_map/ppermute | solution.py:25
  161.0 19.1 %all-to-all-start.8 = ((bf16[8,32,448]{2,1,0:T(8,128)(2,1)}), bf16[8,32,448]{2,1,0:T(8,128)(2,1)}, u32[]{:S(2)}, u32[]{:S(2)}) async-start(bf16[8,32,448]{2,1,0:T(8,128)(2,1)} %bitcast.135), calls=%async_computation.8 | async-start | bytes 524288 | tf_op jit(solution)/shard_map/all_to_all | solution.py:140
  170.2 15.1 %copy-start.2 = (bf16[2,32,3584]{2,1,0:T(8,128)(2,1)S(1)}, bf16[2,32,3584]{2,1,0:T(8,128)(2,1)}, u32[]{:S(2)}) copy-start(bf16[2,32,3584]{2,1,0:T(8,128)(2,1)} %copy-done.1) | copy-start | bytes 1376260
  180.1 31.3 %all-to-all-start.7 = ((bf16[32,64,256]{2,1,0:T(8,128)(2,1)}), bf16[32,64,256]{2,1,0:T(8,128)(2,1)S(1)}, u32[]{:S(2)}, u32[]{:S(2)}) async-start(bf16[32,64,256]{2,1,0:T(8,128)(2,1)} %pad_maximum_fusion.1), calls=%async_computation.7 | async-start | bytes 2097152 | tf_op jit(solution)/shard_map/all_to_all | solution.py:179
  (4 other events, 8.2 us)

commit v7 on v4

--- a/solution.py
+++ b/solution.py
@@ -52,8 +52,8 @@
     return value.reshape(lead + (N_P, 2, cut)).swapaxes(-3, -2).reshape(lead + (width,))
 
 
-def after(value, *others):
-    return lax.optimization_barrier((value, *others))[0]
+def tie(value, column):
+    return value + (column * 0).astype(value.dtype)
 
 
 def per_device(item_cache, user_cache, positive, attn_heads, residual, out_proj, norm_gain):
@@ -68,16 +68,12 @@
     z_block = x_block // 2
 
     attn = by_xor(attn_heads.reshape(4, x_block, heads), x_index).reshape(tokens, heads)
-    attn_other = swap(attn)
+    out_proj = core_major(out_proj)
     mixed = dot(attn, out_proj, ((1,), (0,))).astype(BF16)
+    attn_other = swap(tie(attn, mixed[:1, :1]))
     from_x = [
         lax.ppermute(mixed[k * x_block : (k + 1) * x_block], **xor("x", 4, k)) for k in (1, 2, 3)
     ]
-    mixed_x = mixed[:x_block].astype(F32) + sum(part.astype(F32) for part in from_x)
-    mixed_x = mixed_x.reshape(2, z_block, width)
-    mixed_give = lax.dynamic_index_in_dim(mixed_x, 1 - z_index, 0, keepdims=False)
-    mixed_keep = lax.dynamic_index_in_dim(mixed_x, z_index, 0, keepdims=False)
-    from_z = lax.ppermute(mixed_give.astype(BF16), **xor("zh", 2, 1))
 
     users_own = to_all(user_cache, PLANE, N_P).reshape(half, feats)
     users = (users_own, swap(users_own))
@@ -88,14 +84,19 @@
     scores_own = jnp.sum(lax.all_to_all(partial, TENSOR, 0, 0), axis=0) * LOGIT_SCALE
     scores = to_all(scores_own, TENSOR, N_T).transpose(1, 0, 2).reshape(rows, 2 * half)
 
+    mixed_x = tie(mixed[:x_block].astype(F32), partial.reshape(-1, share)[:x_block, :1])
+    mixed_x = mixed_x + sum(part.astype(F32) for part in from_x)
+    mixed_x = mixed_x.reshape(2, z_block, width)
+    mixed_give = lax.dynamic_index_in_dim(mixed_x, 1 - z_index, 0, keepdims=False)
+    mixed_keep = lax.dynamic_index_in_dim(mixed_x, z_index, 0, keepdims=False)
     own_tokens = (2 * x_index + z_index) * z_block
-    own_residual = lax.dynamic_slice_in_dim(residual, own_tokens, z_block, 0).astype(F32)
-    hidden_own = mixed_keep + after(from_z, partial).astype(F32) + own_residual
-    hidden_own = core_major(hidden_own.astype(BF16))
-    hidden_z = after(lax.ppermute(hidden_own, **xor("zh", 2, 1)), scores_own)
-    pair = jnp.stack([hidden_own, hidden_z])
-    hidden_x = jnp.where(z_index == 0, pair, pair[::-1]).reshape(x_block, width)
-    hidden_x = [hidden_x] + [lax.ppermute(hidden_x, **xor("x", 4, k)) for k in (1, 2, 3)]
+    own_residual = lax.dynamic_slice_in_dim(residual, own_tokens, z_block, 0)
+    own_residual = lax.optimization_barrier(core_major(own_residual))
+    own_residual = tie(own_residual, attn_other[:z_block, :1])
+    mixed_give = tie(mixed_give, own_residual[:, :1]).astype(BF16)
+    from_z = lax.ppermute(mixed_give, **xor("zh", 2, 1))
+    hidden_own = mixed_keep + tie(from_z.astype(F32), scores_own[:, :1]) + own_residual.astype(F32)
+    hidden_own = hidden_own.astype(BF16)
 
     owner, row_in = positive // rows, positive % rows
     column = (owner % 2 != core).astype(jnp.int32) * half + (owner // 2) * rows + row_in
@@ -112,6 +113,11 @@
 
     grad_losses = jnp.zeros((8, half), BF16).at[0, : 3 * rows].set(losses)
     other = swap(jnp.concatenate([grad[:, half:], grad_losses], axis=0))
+    hidden_z = tie(lax.ppermute(hidden_own, **xor("zh", 2, 1)), other[:rows, :1])
+    pair = jnp.stack([hidden_own, hidden_z])
+    hidden_0 = jnp.where(z_index == 0, pair, pair[::-1])
+    hidden_1 = lax.ppermute(hidden_0, **xor("x", 4, 1))
+    hidden_3 = lax.ppermute(hidden_0, **xor("x", 4, 3))
     losses = jnp.concatenate([losses, other[rows, : 3 * rows]])
     losses = jnp.zeros((8, heads), BF16).at[0, : 6 * rows].set(losses)
     both = jnp.concatenate([grad[:, :half], other[:rows]], axis=0)
@@ -119,14 +125,18 @@
     by_plane = jnp.concatenate(
         [jnp.broadcast_to(item_cache[None], (N_P, rows, feats)), both], axis=2
     )
-    group_rows = after(group_rows, by_plane, losses)
-    by_plane = lax.all_to_all(after(by_plane, group_rows), PLANE, 0, 0)
+    by_plane = lax.all_to_all(by_plane, PLANE, 0, 0)
 
     group_rows = core_major(group_rows.transpose(1, 0, 2).reshape(GROUP, width))
     upstream = core_major(norm_gain)[None, :] * (
         by_xor(group_rows.reshape(4, -1), x_index).reshape(GROUP, width) / SEQ
     )
-    hidden = jnp.concatenate(hidden_x, axis=0).reshape(GROUP, SEQ, width).astype(F32)
+    hidden_2 = [
+        lax.ppermute(hidden_1[0], **xor("x", 4, 3)),
+        lax.ppermute(hidden_3[1], **xor("x", 4, 1)),
+    ]
+    hidden_2 = jnp.stack(hidden_2)
+    hidden = jnp.concatenate([hidden_0, hidden_1, hidden_2, hidden_3], axis=0).astype(F32)
     inverse = lax.rsqrt(jnp.mean(hidden * hidden, axis=2, keepdims=True) + NORM_EPS)
     inner = jnp.sum(upstream[:, None, :] * hidden, axis=2, keepdims=True) / width
     stream = inverse * upstream[:, None, :] - hidden * (inverse * inverse * inverse * inner)
@@ -138,10 +148,8 @@
     stream_keep = lax.dynamic_slice_in_dim(stream, core * side, side, 1)
     weight = dot(stream_keep, attn, ((0,), (0,))) + dot(stream_other, attn_other, ((0,), (0,)))
     weight = weight.astype(BF16).reshape(N_P, cut, heads)
-    weight, by_plane = lax.optimization_barrier((weight, by_plane))
     final = jnp.concatenate([weight, jnp.broadcast_to(losses[None], (N_P, 8, heads))], axis=1)
     final = lax.all_to_all(final, PLANE, 0, 0)
-    out_proj = core_major(out_proj)
     head_grad = dot(stream, out_proj, ((1,), (1,))).astype(BF16)
     head_grad = by_xor(head_grad.reshape(4, x_block, heads), x_index).reshape(tokens, heads)
     items_own = by_plane[:, :, :feats].reshape(half, feats)

time: 234 us -> 211 us (0.902)
  waiting for transfers between devices: 70.1 us -> 17.6 us
  local copies, waits for them, and re-layouts: 23.4 us -> 39.9 us
  starting transfers between devices: 98.1 us -> 106 us
  other arithmetic: 25.2 us -> 31.5 us
    all_to_all x3, waiting for transfers between devices: 24.3 us -> 0.42 us  [to_all(): lax.all_to_all(jnp.broadcast_to(value[None], (count,) + value.shape), axe...]
    ppermute x5 -> x6, waiting for transfers between devices: 16 us -> 3.78 us  [the longest x1 1.93 us: per_device(): lax.ppermute(hidden_1[0], **xor('x', 4, 3))]
    all_to_all x1, waiting for transfers between devices: 8.94 us -> 0.01 us  [per_device(): by_plane = lax.all_to_all(by_plane, PLANE, 0, 0)]
    all_to_all x1, starting transfers between devices: 3.42 us -> 9.8 us  [per_device(): lax.all_to_all(partial, TENSOR, 0, 0)]
    all_to_all x1, starting transfers between devices: 18 us -> 11.6 us  [per_device(): by_plane = lax.all_to_all(by_plane, PLANE, 0, 0)]
    ppermute x3, waiting for transfers between devices: 5.74 us -> 0.01 us  [per_device(): lax.ppermute(mixed[k * x_block:(k + 1) * x_block], **xor('x', 4, k))]
    ppermute x5 -> x6, starting transfers between devices: 26.9 us -> 32.6 us  [the longest x1 12 us: per_device(): lax.ppermute(hidden_own, **xor('zh', 2, 1))]
    unnamed x34 -> x48, local copies, waits for them, and re-layouts: 5.28 us -> 10.2 us
  transfers between devices with their start and end apart: 19 -> 20, of which waited for: 10 -> 6; matrix products, arithmetic and copies ran while one was open for 18% -> 35% of each run, Pallas kernels for 0% -> 0%
where the time goes in v7:
time: 211 us; the launch traced here: 209 us
  starting transfers between devices  106 us (50%)
  local copies, waits for them, and re-layouts  39.9 us (19%)
  other arithmetic  31.5 us (15%)
  waiting for transfers between devices  17.6 us (8%)
  matrix products  10.8 us (5%)
  between operations  3.82 us (2%)
    all_to_all x3, starting transfers between devices, to_all(): lax.all_to_all(jnp.broadcast_to(value[None], (count,) + value.shape), axe...  20.8 us
    ppermute x1, starting transfers between devices, per_device(): lax.ppermute(hidden_own, **xor('zh', 2, 1))  12 us
    all_to_all x1, starting transfers between devices, per_device(): by_plane = lax.all_to_all(by_plane, PLANE, 0, 0)  11.6 us
    dot_general x10, matrix products, dot(): return lax.dot_general(a, b, (dims, ((), ())), preferred_element_type=F32)  10.8 us
    all_to_all x1, waiting for transfers between devices, per_device(): final = lax.all_to_all(final, PLANE, 0, 0)  10.5 us
    ppermute x3, starting transfers between devices, per_device(): lax.ppermute(mixed[k * x_block:(k + 1) * x_block], **xor('x', 4, k))  10.4 us
    ppermute x5, starting transfers between devices, swap(): return lax.ppermute(value, **xor('c', 2, 1))  10.2 us
    unnamed x48, local copies, waits for them, and re-layouts  10.2 us
  transfers between devices with their start and end apart: 20, of which 6 were waited for; matrix products, arithmetic and copies ran while one was open for 35% of the time, Pallas kernels for 0%

profile of v7, /device:TPU:8, one launch (start us, length us, event | category | flops | bytes accessed | tf_op | source)
XLA Modules:
  0.0 209.2 jit_solution(2311640344064732137)
XLA Ops:
  0.6 2.0 broadcast_in_dim.18
  2.6 13.1 %all-to-all-start = ((bf16[32,32,448]{2,1,0:T(8,128)(2,1)}), bf16[32,32,448]{2,1,0:T(8,128)(2,1)S(1)}, u32[]{:S(2)}, u32[]{:S(2)}) async-start(bf16[32,32,448]{2,1,0:T(8,128)(2,1)} %broadcast_in_dim.18), calls=%async_computation | async-start | bytes 2097152 | tf_op jit(solution)/shard_map/all_to_all | solution.py:37
  15.8 3.8 %copy.48 = bf16[256,3584]{0,1:T(8,128)(2,1)} copy(bf16[256,3584]{1,0:T(8,128)(2,1)} %param.16) | data formatting | bytes 3670016 | tf_op args[5]
  19.6 2.9 %copy.49 = bf16[256,2,32,56]{0,3,2,1:T(8,128)(2,1)} copy(bf16[256,2,32,56]{0,3,1,2:T(8,128)(2,1)} %bitcast.117) | data formatting | bytes 3670016 | tf_op jit(solution)/shard_map/transpose | solution.py:52
  22.6 2.2 %convolution_convert_fusion = bf16[256,3584]{1,0:T(8,128)(2,1)S(1)} fusion(bf16[256,256]{1,0:T(8,128)(2,1)S(1)} %bitcast.126, bf16[256,3584]{0,1:T(8,128)(2,1)} %bitcast.118), kind=kOutput, calls=%fused_computation | convolution fusion | flops 470679552 | bytes 3801088 | tf_op jit(solution)/shard_map/dot_general | solution.py:41
  25.9 3.4 %collective-permute-start.1 = (bf16[64,3584]{1,0:T(8,128)(2,1)}, bf16[64,3584]{1,0:T(8,128)(2,1)}, u32[]{:S(2)}, u32[]{:S(2)}) collective-permute-start(bf16[64,3584]{1,0:T(8,128)(2,1)} %get-tuple-element.37), channel_id=1, source_target_pairs={{0,2},{2,0},{4,6},{6,4},{1,3},{3,1},{5,7},{7,5},{8,10},{10,8},{12,... | collective-permute-start | bytes 1376264 | tf_op jit(solution)/shard_map/ppermute | solution.py:75
  29.3 4.6 %collective-permute-start.2 = (bf16[64,3584]{1,0:T(8,128)(2,1)}, bf16[64,3584]{1,0:T(8,128)(2,1)}, u32[]{:S(2)}, u32[]{:S(2)}) collective-permute-start(bf16[64,3584]{1,0:T(8,128)(2,1)} %get-tuple-element.39), channel_id=1, source_target_pairs={{0,4},{2,6},{4,0},{6,2},{1,5},{3,7},{5,1},{7,3},{8,12},{10,14},{12... | collective-permute-start | bytes 1376264 | tf_op jit(solution)/shard_map/ppermute | solution.py:75
  33.9 2.4 %collective-permute-start.3 = (bf16[64,3584]{1,0:T(8,128)(2,1)}, bf16[64,3584]{1,0:T(8,128)(2,1)}, u32[]{:S(2)}, u32[]{:S(2)}) collective-permute-start(bf16[64,3584]{1,0:T(8,128)(2,1)} %get-tuple-element.38), channel_id=1, source_target_pairs={{0,6},{2,4},{4,2},{6,0},{1,7},{3,5},{5,3},{7,1},{8,14},{10,12},{12... | collective-permute-start | bytes 1376264 | tf_op jit(solution)/shard_map/ppermute | solution.py:75
  41.6 2.0 reshape.282
  49.0 2.4 %collective-permute-start = (bf16[1024,448]{0,1:T(8,128)(2,1)}, bf16[1024,448]{0,1:T(8,128)(2,1)S(1)}, u32[]{:S(2)}, u32[]{:S(2)}) collective-permute-start(bf16[1024,448]{0,1:T(8,128)(2,1)} %copy.50), channel_id=1, source_target_pairs={{0,8},{8,0},{1,9},{9,1},{2,10},{10,2},{3,11},{11,3},{4,12},{12,4},... | collective-permute-start | bytes 2752520 | tf_op jit(solution)/shard_map/ppermute | solution.py:25
  55.7 9.8 %all-to-all-start.1 = ((f32[8,32,256]{2,1,0:T(8,128)}), f32[8,32,256]{2,1,0:T(8,128)S(1)}, u32[]{:S(2)}, u32[]{:S(2)}) async-start(f32[8,32,256]{2,1,0:T(8,128)} %bitcast.84.clone.2), calls=%async_computation.1 | async-start | bytes 524288 | tf_op jit(solution)/shard_map/all_to_all | solution.py:84
  69.8 7.8 %collective-permute-start.5 = (bf16[32,3584]{1,0:T(8,128)(2,1)}, bf16[32,3584]{1,0:T(8,128)(2,1)}, u32[]{:S(2)}, u32[]{:S(2)}) collective-permute-start(bf16[32,3584]{1,0:T(8,128)(2,1)} %fusion.8), channel_id=1, source_target_pairs={{0,1},{1,0},{2,3},{3,2},{4,5},{5,4},{6,7},{7,6},{8,9},{9,8},{10,11... | collective-permute-start | bytes 688136 | tf_op jit(solution)/shard_map/ppermute | solution.py:97
  79.8 4.2 %all-to-all-start.2 = ((f32[8,32,256]{2,1,0:T(8,128)}), f32[8,32,256]{2,1,0:T(8,128)S(1)}, u32[]{:S(2)}, u32[]{:S(2)}) async-start(f32[8,32,256]{2,1,0:T(8,128)} %broadcast_in_dim.19), calls=%async_computation.2 | async-start | bytes 524288 | tf_op jit(solution)/shard_map/all_to_all | solution.py:37
  84.2 2.0 fusion.10
  86.1 12.0 %collective-permute-start.6 = (bf16[32,3584]{1,0:T(8,128)(2,1)}, bf16[32,3584]{1,0:T(8,128)(2,1)}, u32[]{:S(2)}, u32[]{:S(2)}) collective-permute-start(bf16[32,3584]{1,0:T(8,128)(2,1)} %fusion.10), channel_id=1, source_target_pairs={{0,1},{1,0},{2,3},{3,2},{4,5},{5,4},{6,7},{7,6},{8,9},{9,8},{10,11... | collective-permute-start | bytes 688136 | tf_op jit(solution)/shard_map/ppermute | solution.py:116
  102.2 1.9 collective-permute-start.7
  105.2 3.4 %all-to-all-start.3 = ((f32[8,8,448]{2,1,0:T(8,128)}), f32[8,8,448]{2,1,0:T(8,128)S(1)}, u32[]{:S(2)}, u32[]{:S(2)}) async-start(f32[8,8,448]{2,1,0:T(8,128)} %broadcast_in_dim.21), calls=%async_computation.3 | async-start | bytes 262144 | tf_op jit(solution)/shard_map/all_to_all | solution.py:37
  111.8 3.8 %collective-permute-start.8 = (bf16[2,32,3584]{2,1,0:T(8,128)(2,1)}, bf16[2,32,3584]{2,1,0:T(8,128)(2,1)}, u32[]{:S(2)}, u32[]{:S(2)}) collective-permute-start(bf16[2,32,3584]{2,1,0:T(8,128)(2,1)} %get-tuple-element.34), channel_id=1, source_target_pairs={{0,2},{2,0},{4,6},{6,4},{1,3},{3,1},{5,7},{7,5},{8,10},{10,8},{12,... | collective-permute-start | bytes 1376264 | tf_op jit(solution)/shard_map/ppermute | solution.py:119
  115.6 4.0 %collective-permute-start.10 = (bf16[2,32,3584]{2,1,0:T(8,128)(2,1)}, bf16[2,32,3584]{2,1,0:T(8,128)(2,1)}, u32[]{:S(2)}, u32[]{:S(2)}) collective-permute-start(bf16[2,32,3584]{2,1,0:T(8,128)(2,1)} %get-tuple-element.34), channel_id=1, source_target_pairs={{0,6},{2,4},{4,2},{6,0},{1,7},{3,5},{5,3},{7,1},{8,14},{10,12},{12... | collective-permute-start | bytes 1376264 | tf_op jit(solution)/shard_map/ppermute | solution.py:120
  121.1 11.6 %all-to-all-start.5 = ((bf16[32,32,512]{2,1,0:T(8,128)(2,1)}), bf16[32,32,512]{2,1,0:T(8,128)(2,1)S(1)}, u32[]{:S(2)}, u32[]{:S(2)}) async-start(bf16[32,32,512]{2,1,0:T(8,128)(2,1)} %pad_maximum_fusion.1), calls=%async_computation.5 | async-start | bytes 2097152 | tf_op jit(solution)/shard_map/all_to_all | solution.py:128
  134.8 3.1 %collective-permute-start.9 = (bf16[32,3584]{1,0:T(8,128)(2,1)S(1)}, bf16[32,3584]{1,0:T(8,128)(2,1)S(1)}, u32[]{:S(2)}, u32[]{:S(2)}) collective-permute-start(bf16[32,3584]{1,0:T(8,128)(2,1)S(1)} %slice_bitcast_fusion.1), channel_id=1, source_target_pairs={{0,6},{2,4},{4,2},{6,0},{1,7},{3,5},{5,3},{7,1},{8,14},{10,12},{12... | collective-permute-start | bytes 688136 | tf_op jit(solution)/shard_map/ppermute | solution.py:135
  138.9 1.9 collective-permute-start.11
  142.6 1.9 collective-permute-done.9
  149.6 2.2 %multiply_reduce_fusion.1 = (f32[8,32]{1,0:T(8,128)S(1)}, f32[8,32]{1,0:T(8,128)S(1)}) fusion(bf16[8,32,3584]{2,1,0:T(8,128)(2,1)} %constant_dynamic-update-slice_fusion, f32[8,3584]{1,0:T(8,128)S(1)} %broadcast_multiply_fusion), kind=kLoop, calls=%fused_computation.7 | loop fusion | flops 4587008 | bytes 1951744 | tf_op jit(solution)/shard_map/reduce_sum | solution.py:140
  152.0 2.4 %fusion.1 = bf16[256,3584]{1,0:T(8,128)(2,1)S(1)} fusion(bf16[8,32,3584]{2,1,0:T(8,128)(2,1)} %constant_dynamic-update-slice_fusion, f32[256]{0:T(256)S(1)} %fusion.23, f32[8,3584]{1,0:T(8,128)S(1)} %broadcast_multiply_fusion, f32[256]{0:T(256)S(1)} %rsqrt.17), kind=kLoop, calls=%fused_computation.3 | loop fusion | flops 4587520 | bytes 3786752 | tf_op jit(solution)/shard_map/convert_element_type | solution.py:143
  156.7 2.1 collective-permute-start.12
  164.7 10.2 %all-to-all-start.4 = ((bf16[32,64,256]{2,1,0:T(8,128)(2,1)}), bf16[32,64,256]{2,1,0:T(8,128)(2,1)}, u32[]{:S(2)}, u32[]{:S(2)}) async-start(bf16[32,64,256]{2,1,0:T(8,128)(2,1)} %pad_maximum_fusion), calls=%async_computation.4 | async-start | bytes 2097152 | tf_op jit(solution)/shard_map/all_to_all | solution.py:152
  174.9 3.6 %subtract_convert_fusion = bf16[8,32,3584]{2,1,0:T(8,128)(2,1)} fusion(bf16[8,32,3584]{2,1,0:T(8,128)(2,1)} %constant_dynamic-update-slice_fusion, f32[8,32]{1,0:T(8,128)S(1)} %get-tuple-element.58, f32[8,32]{1,0:T(8,128)S(1)} %get-tuple-element.59, f32[8,3584]{1,0:T(8,128)S(1)} %broadcast_multiply_fusion), kind=kLoop, calls=%fused_computation.5 | loop fusion | flops 4587520 | bytes 3786752 | tf_op jit(solution)/shard_map/convert_element_type | solution.py:143
  181.7 2.7 %convolution_convert_fusion.1 = bf16[256,256]{1,0:T(8,128)(2,1)S(1)} fusion(bf16[256,3584]{1,0:T(8,128)(2,1)} %bitcast.128, bf16[256,3584]{0,1:T(8,128)(2,1)} %bitcast.119), kind=kOutput, calls=%fused_computation.10 | convolution fusion | flops 469827584 | bytes 3801088 | tf_op jit(solution)/shard_map/dot_general | solution.py:41
  191.2 2.2 %fusion.2 = f32[32,448]{1,0:T(8,128)} fusion(f32[32,448]{1,0:T(8,128)S(1)} %fusion.38, bf16[1024,32]{0,1:T(8,128)(2,1)S(1)} %squeeze.29, bf16[1024,448]{0,1:T(8,128)(2,1)} %collective-permute-done.13), kind=kOutput, calls=%fused_computation.12 | convolution fusion | flops 29388800 | bytes 1097728 | tf_op jit(solution)/shard_map/dot_general | solution.py:41
  193.4 10.5 %all-to-all-done.4 = bf16[32,64,256]{2,1,0:T(8,128)(2,1)} async-done(((bf16[32,64,256]{2,1,0:T(8,128)(2,1)}), bf16[32,64,256]{2,1,0:T(8,128)(2,1)}, u32[]{:S(2)}, u32[]{:S(2)}) %all-to-all-start.4) | async-done | bytes 1048608 | tf_op jit(solution)/shard_map/all_to_all | solution.py:152
  206.2 1.9 convert_reduce_fusion
  (154 shorter events, 61.3 us)
Async XLA Ops:
  0.6 39.5 %copy-start = (bf16[256,3584]{1,0:T(8,128)(2,1)S(1)}, bf16[256,3584]{1,0:T(8,128)(2,1)}, u32[]{:S(2)}) copy-start(bf16[256,3584]{1,0:T(8,128)(2,1)} %param.15) | copy-start | bytes 5505028
  2.6 45.0 %all-to-all-start = ((bf16[32,32,448]{2,1,0:T(8,128)(2,1)}), bf16[32,32,448]{2,1,0:T(8,128)(2,1)S(1)}, u32[]{:S(2)}, u32[]{:S(2)}) async-start(bf16[32,32,448]{2,1,0:T(8,128)(2,1)} %broadcast_in_dim.18), calls=%async_computation | async-start | bytes 2097152 | tf_op jit(solution)/shard_map/all_to_all | solution.py:37
  24.7 11.6 %copy-start.1 = (bf16[256,3584]{1,0:T(8,128)(2,1)}, bf16[256,3584]{1,0:T(8,128)(2,1)S(1)}, u32[]{:S(2)}) copy-start(bf16[256,3584]{1,0:T(8,128)(2,1)S(1)} %convolution_convert_fusion) | copy-start | bytes 5505028
  24.7 15.4 %copy-start.12 = (f32[3584]{0:T(1024)S(1)}, f32[3584]{0:T(1024)}, u32[]{:S(2)}) copy-start(f32[3584]{0:T(1024)} %param.17) | copy-start | bytes 43012
  24.8 16.1 %copy-start.21 = (s32[32]{0:T(128)S(1)}, s32[32]{0:T(128)}, u32[]{:S(2)}) copy-start(s32[32]{0:T(128)} %param.13) | copy-start | bytes 388
  25.9 40.5 %collective-permute-start.1 = (bf16[64,3584]{1,0:T(8,128)(2,1)}, bf16[64,3584]{1,0:T(8,128)(2,1)}, u32[]{:S(2)}, u32[]{:S(2)}) collective-permute-start(bf16[64,3584]{1,0:T(8,128)(2,1)} %get-tuple-element.37), channel_id=1, source_target_pairs={{0,2},{2,0},{4,6},{6,4},{1,3},{3,1},{5,7},{7,5},{8,10},{10,8},{12,... | collective-permute-start | bytes 1376264 | tf_op jit(solution)/shard_map/ppermute | solution.py:75
  29.3 37.1 %collective-permute-start.2 = (bf16[64,3584]{1,0:T(8,128)(2,1)}, bf16[64,3584]{1,0:T(8,128)(2,1)}, u32[]{:S(2)}, u32[]{:S(2)}) collective-permute-start(bf16[64,3584]{1,0:T(8,128)(2,1)} %get-tuple-element.39), channel_id=1, source_target_pairs={{0,4},{2,6},{4,0},{6,2},{1,5},{3,7},{5,1},{7,3},{8,12},{10,14},{12... | collective-permute-start | bytes 1376264 | tf_op jit(solution)/shard_map/ppermute | solution.py:75
  33.9 32.4 %collective-permute-start.3 = (bf16[64,3584]{1,0:T(8,128)(2,1)}, bf16[64,3584]{1,0:T(8,128)(2,1)}, u32[]{:S(2)}, u32[]{:S(2)}) collective-permute-start(bf16[64,3584]{1,0:T(8,128)(2,1)} %get-tuple-element.38), channel_id=1, source_target_pairs={{0,6},{2,4},{4,2},{6,0},{1,7},{3,5},{5,3},{7,1},{8,14},{10,12},{12... | collective-permute-start | bytes 1376264 | tf_op jit(solution)/shard_map/ppermute | solution.py:75
  38.2 8.7 %collective-permute-start.4 = (bf16[256,256]{1,0:T(8,128)(2,1)}, bf16[256,256]{1,0:T(8,128)(2,1)}, u32[]{:S(2)}, u32[]{:S(2)}) collective-permute-start(bf16[256,256]{1,0:T(8,128)(2,1)} %broadcast_add_fusion.1), channel_id=1, source_target_pairs={{0,8},{8,0},{1,9},{9,1},{2,10},{10,2},{3,11},{11,3},{4,12},{12,4},... | collective-permute-start | bytes 393224 | tf_op jit(solution)/shard_map/ppermute | solution.py:25
  44.5 7.6 %copy-start.7 = (bf16[32,448]{1,0:T(8,128)(2,1)S(1)}, bf16[32,448]{1,0:T(8,128)(2,1)}, u32[]{:S(2)}) copy-start(bf16[32,448]{1,0:T(8,128)(2,1)} %param.11) | copy-start | bytes 86020
  47.6 6.0 %copy-start.13 = (bf16[32]{0:T(256)(128)(2,1)}, bf16[32]{0:T(256)(128)(2,1)S(1)}, u32[]{:S(2)}) copy-start(bf16[32]{0:T(256)(128)(2,1)S(1)} %fusion.20) | copy-start | bytes 196
  49.0 4.7 %collective-permute-start = (bf16[1024,448]{0,1:T(8,128)(2,1)}, bf16[1024,448]{0,1:T(8,128)(2,1)S(1)}, u32[]{:S(2)}, u32[]{:S(2)}) collective-permute-start(bf16[1024,448]{0,1:T(8,128)(2,1)} %copy.50), channel_id=1, source_target_pairs={{0,8},{8,0},{1,9},{9,1},{2,10},{10,2},{3,11},{11,3},{4,12},{12,4},... | collective-permute-start | bytes 2752520 | tf_op jit(solution)/shard_map/ppermute | solution.py:25
  54.9 14.1 %copy-start.20 = (f32[32]{0:T(128)S(1)}, f32[32]{0:T(128)}, u32[]{:S(2)}) copy-start(f32[32]{0:T(128)} %convert_reduce_fusion.1) | copy-start | bytes 388
  55.7 22.0 %all-to-all-start.1 = ((f32[8,32,256]{2,1,0:T(8,128)}), f32[8,32,256]{2,1,0:T(8,128)S(1)}, u32[]{:S(2)}, u32[]{:S(2)}) async-start(f32[8,32,256]{2,1,0:T(8,128)} %bitcast.84.clone.2), calls=%async_computation.1 | async-start | bytes 524288 | tf_op jit(solution)/shard_map/all_to_all | solution.py:84
  69.8 14.3 %collective-permute-start.5 = (bf16[32,3584]{1,0:T(8,128)(2,1)}, bf16[32,3584]{1,0:T(8,128)(2,1)}, u32[]{:S(2)}, u32[]{:S(2)}) collective-permute-start(bf16[32,3584]{1,0:T(8,128)(2,1)} %fusion.8), channel_id=1, source_target_pairs={{0,1},{1,0},{2,3},{3,2},{4,5},{5,4},{6,7},{7,6},{8,9},{9,8},{10,11... | collective-permute-start | bytes 688136 | tf_op jit(solution)/shard_map/ppermute | solution.py:97
  79.8 18.7 %all-to-all-start.2 = ((f32[8,32,256]{2,1,0:T(8,128)}), f32[8,32,256]{2,1,0:T(8,128)S(1)}, u32[]{:S(2)}, u32[]{:S(2)}) async-start(f32[8,32,256]{2,1,0:T(8,128)} %broadcast_in_dim.19), calls=%async_computation.2 | async-start | bytes 524288 | tf_op jit(solution)/shard_map/all_to_all | solution.py:37
  86.1 22.6 %collective-permute-start.6 = (bf16[32,3584]{1,0:T(8,128)(2,1)}, bf16[32,3584]{1,0:T(8,128)(2,1)}, u32[]{:S(2)}, u32[]{:S(2)}) collective-permute-start(bf16[32,3584]{1,0:T(8,128)(2,1)} %fusion.10), channel_id=1, source_target_pairs={{0,1},{1,0},{2,3},{3,2},{4,5},{5,4},{6,7},{7,6},{8,9},{9,8},{10,11... | collective-permute-start | bytes 688136 | tf_op jit(solution)/shard_map/ppermute | solution.py:116
  99.2 4.9 %copy-start.6 = (bf16[1024,448]{0,1:T(8,128)(2,1)S(1)}, bf16[1024,448]{0,1:T(8,128)(2,1)}, u32[]{:S(2)}) copy-start(bf16[1024,448]{0,1:T(8,128)(2,1)} %copy-done.5) | copy-start | bytes 2752516
  102.2 6.4 %collective-permute-start.7 = (bf16[40,1024]{1,0:T(8,128)(2,1)S(1)}, bf16[40,1024]{1,0:T(8,128)(2,1)S(1)}, u32[]{:S(2)}, u32[]{:S(2)}) collective-permute-start(bf16[40,1024]{1,0:T(8,128)(2,1)S(1)} %fusion.15), channel_id=1, source_target_pairs={{0,8},{8,0},{1,9},{9,1},{2,10},{10,2},{3,11},{11,3},{4,12},{12,4},... | collective-permute-start | bytes 245768 | tf_op jit(solution)/shard_map/ppermute | solution.py:25
  104.5 15.3 %copy-start.10 = (f32[32,448]{1,0:T(8,128)}, f32[32,448]{1,0:T(8,128)S(1)}, u32[]{:S(2)}) copy-start(f32[32,448]{1,0:T(8,128)S(1)} %fusion.3) | copy-start | bytes 172036
  105.2 15.9 %all-to-all-start.3 = ((f32[8,8,448]{2,1,0:T(8,128)}), f32[8,8,448]{2,1,0:T(8,128)S(1)}, u32[]{:S(2)}, u32[]{:S(2)}) async-start(f32[8,8,448]{2,1,0:T(8,128)} %broadcast_in_dim.21), calls=%async_computation.3 | async-start | bytes 262144 | tf_op jit(solution)/shard_map/all_to_all | solution.py:37
  108.6 11.2 %copy-start.8 = (bf16[32,448]{1,0:T(8,128)(2,1)S(1)}, bf16[32,448]{1,0:T(8,128)(2,1)}, u32[]{:S(2)}) copy-start(bf16[32,448]{1,0:T(8,128)(2,1)} %param.11) | copy-start | bytes 86020
  108.6 11.0 %copy-start.11 = (bf16[40,1024]{1,0:T(8,128)(2,1)}, bf16[40,1024]{1,0:T(8,128)(2,1)S(1)}, u32[]{:S(2)}) copy-start(bf16[40,1024]{1,0:T(8,128)(2,1)S(1)} %collective-permute-done.7) | copy-start | bytes 245764
  111.8 22.1 %collective-permute-start.8 = (bf16[2,32,3584]{2,1,0:T(8,128)(2,1)}, bf16[2,32,3584]{2,1,0:T(8,128)(2,1)}, u32[]{:S(2)}, u32[]{:S(2)}) collective-permute-start(bf16[2,32,3584]{2,1,0:T(8,128)(2,1)} %get-tuple-element.34), channel_id=1, source_target_pairs={{0,2},{2,0},{4,6},{6,4},{1,3},{3,1},{5,7},{7,5},{8,10},{10,8},{12,... | collective-permute-start | bytes 1376264 | tf_op jit(solution)/shard_map/ppermute | solution.py:119
  115.6 22.3 %collective-permute-start.10 = (bf16[2,32,3584]{2,1,0:T(8,128)(2,1)}, bf16[2,32,3584]{2,1,0:T(8,128)(2,1)}, u32[]{:S(2)}, u32[]{:S(2)}) collective-permute-start(bf16[2,32,3584]{2,1,0:T(8,128)(2,1)} %get-tuple-element.34), channel_id=1, source_target_pairs={{0,6},{2,4},{4,2},{6,0},{1,7},{3,5},{5,3},{7,1},{8,14},{10,12},{12... | collective-permute-start | bytes 1376264 | tf_op jit(solution)/shard_map/ppermute | solution.py:120
  121.1 43.5 %all-to-all-start.5 = ((bf16[32,32,512]{2,1,0:T(8,128)(2,1)}), bf16[32,32,512]{2,1,0:T(8,128)(2,1)S(1)}, u32[]{:S(2)}, u32[]{:S(2)}) async-start(bf16[32,32,512]{2,1,0:T(8,128)(2,1)} %pad_maximum_fusion.1), calls=%async_computation.5 | async-start | bytes 2097152 | tf_op jit(solution)/shard_map/all_to_all | solution.py:128
  134.8 9.7 %collective-permute-start.9 = (bf16[32,3584]{1,0:T(8,128)(2,1)S(1)}, bf16[32,3584]{1,0:T(8,128)(2,1)S(1)}, u32[]{:S(2)}, u32[]{:S(2)}) collective-permute-start(bf16[32,3584]{1,0:T(8,128)(2,1)S(1)} %slice_bitcast_fusion.1), channel_id=1, source_target_pairs={{0,6},{2,4},{4,2},{6,0},{1,7},{3,5},{5,3},{7,1},{8,14},{10,12},{12... | collective-permute-start | bytes 688136 | tf_op jit(solution)/shard_map/ppermute | solution.py:135
  138.9 8.2 %collective-permute-start.11 = (bf16[32,3584]{1,0:T(8,128)(2,1)S(1)}, bf16[32,3584]{1,0:T(8,128)(2,1)S(1)}, u32[]{:S(2)}, u32[]{:S(2)}) collective-permute-start(bf16[32,3584]{1,0:T(8,128)(2,1)S(1)} %slice_bitcast_fusion), channel_id=1, source_target_pairs={{0,2},{2,0},{4,6},{6,4},{1,3},{3,1},{5,7},{7,5},{8,10},{10,8},{12,... | collective-permute-start | bytes 688136 | tf_op jit(solution)/shard_map/ppermute | solution.py:136
  156.7 4.7 %collective-permute-start.12 = (bf16[256,1792]{1,0:T(8,128)(2,1)}, bf16[256,1792]{1,0:T(8,128)(2,1)}, u32[]{:S(2)}, u32[]{:S(2)}) collective-permute-start(bf16[256,1792]{1,0:T(8,128)(2,1)} %constant_dynamic-slice_fusion.4), channel_id=1, source_target_pairs={{0,8},{8,0},{1,9},{9,1},{2,10},{10,2},{3,11},{11,3},{4,12},{12,4},... | collective-permute-start | bytes 2752520 | tf_op jit(solution)/shard_map/ppermute | solution.py:25
  158.8 4.2 %copy-start.3 = (bf16[256,3584]{1,0:T(8,128)(2,1)S(1)}, bf16[256,3584]{1,0:T(8,128)(2,1)}, u32[]{:S(2)}) copy-start(bf16[256,3584]{1,0:T(8,128)(2,1)} %copy-done.2) | copy-start | bytes 5505028
  164.7 39.3 %all-to-all-start.4 = ((bf16[32,64,256]{2,1,0:T(8,128)(2,1)}), bf16[32,64,256]{2,1,0:T(8,128)(2,1)}, u32[]{:S(2)}, u32[]{:S(2)}) async-start(bf16[32,64,256]{2,1,0:T(8,128)(2,1)} %pad_maximum_fusion), calls=%async_computation.4 | async-start | bytes 2097152 | tf_op jit(solution)/shard_map/all_to_all | solution.py:152
  179.8 11.4 %collective-permute-start.13 = (bf16[1024,448]{0,1:T(8,128)(2,1)}, bf16[1024,448]{0,1:T(8,128)(2,1)}, u32[]{:S(2)}, u32[]{:S(2)}) collective-permute-start(bf16[1024,448]{0,1:T(8,128)(2,1)} %copy.60), channel_id=1, source_target_pairs={{0,8},{8,0},{1,9},{9,1},{2,10},{10,2},{3,11},{11,3},{4,12},{12,4},... | collective-permute-start | bytes 2752520 | tf_op jit(solution)/shard_map/ppermute | solution.py:25
  (10 other events, 21.5 us)

commit v8 on v4

v8 whole, which is shorter than its diff:
```python
import jax
import jax.numpy as jnp
from jax import lax
from jax.experimental import pallas as pl
from jax.experimental.pallas import tpu as pltpu
from jax.sharding import Mesh, PartitionSpec as P

BF16 = jnp.bfloat16
F32 = jnp.float32
LOGIT_SCALE = 50.0
NORM_EPS = 1e-06
GROUP = 8
SEQ = 32
AXES = (("zl", 4), ("y", 8), ("c", 2), ("x", 4), ("zh", 2))
TENSOR = ("x", "zh")
PLANE = ("zl", "y")
DP = ("zl", "y", "c")
N_T = 8
N_P = 32


def xor(axis, size, bits):
    return dict(axis_name=axis, perm=[(i, i ^ bits) for i in range(size)])


def swap(value):
    return lax.ppermute(value, **xor("c", 2, 1))


def three_terms(value):
    high = lax.reduce_precision(value, 8, 7)
    rest = value - high
    middle = lax.reduce_precision(rest, 8, 7)
    low = lax.reduce_precision(rest - middle, 8, 7)
    return high.astype(BF16), middle.astype(BF16), low.astype(BF16)


def to_all(value, axes, count):
    return lax.all_to_all(jnp.broadcast_to(value[None], (count,) + value.shape), axes, 0, 0)


def dot(a, b, dims):
    return lax.dot_general(a, b, (dims, ((), ())), preferred_element_type=F32)


def by_xor(value, index):
    parts = [lax.dynamic_slice_in_dim(value, r ^ index, 1, 0) for r in range(value.shape[0])]
    return jnp.concatenate(parts, axis=0)


def tie(value, column):
    return value + (column * 0).astype(value.dtype)


def stream_kernel(x_ref, gain_ref, group_ref, *refs):
    first, second, third_0, third_1, fourth, out_ref = refs
    halves = (first, first, second, second, third_0, third_1, fourth, fourth)
    width = out_ref.shape[1]
    for item in range(GROUP):
        start = 0 if halves[item].shape[0] == SEQ else item % 2 * SEQ
        tokens = halves[item][start : start + SEQ, :].astype(F32)
        which = (x_ref[0] ^ (item // 2)) * 2 + item % 2
        up = gain_ref[...] * (group_ref[pl.ds(which, 1), :] / SEQ)
        mean = jnp.sum(tokens * tokens, axis=1, keepdims=True) / width
        inverse = lax.rsqrt(mean + NORM_EPS)
        inner = jnp.sum(up * tokens, axis=1, keepdims=True) / width
        stream = inverse * up - tokens * (inverse * inverse * inverse * inner)
        out_ref[item * SEQ : (item + 1) * SEQ, :] = stream.astype(BF16)


def stream_gradient(x_index, norm_gain, group_rows, blocks):
    tokens, width = GROUP * SEQ, norm_gain.shape[0]
    whole = pl.BlockSpec(memory_space=pltpu.VMEM)
    return pl.pallas_call(
        stream_kernel,
        out_shape=jax.ShapeDtypeStruct((tokens, width), BF16),
        in_specs=[pl.BlockSpec(memory_space=pltpu.SMEM)] + [whole] * 7,
        out_specs=whole,
        compiler_params=pltpu.CompilerParams(vmem_limit_bytes=24 * 2**20),
        cost_estimate=pl.CostEstimate(
            flops=12 * tokens * width, bytes_accessed=4 * tokens * width, transcendentals=0
        ),
    )(x_index.reshape(1), norm_gain.reshape(1, width), group_rows, *blocks)


def per_device(item_cache, user_cache, positive, attn_heads, residual, out_proj, norm_gain):
    rows, feats = item_cache.shape
    width = out_proj.shape[1]
    tokens, heads = attn_heads.shape
    half = N_P * rows
    core = lax.axis_index("c")
    x_index = lax.axis_index("x")
    z_index = lax.axis_index("zh")
    x_block = tokens // 4

    attn = by_xor(attn_heads.reshape(4, x_block, heads), x_index).reshape(tokens, heads)
    mixed = dot(attn, out_proj, ((1,), (0,))).astype(BF16)
    from_x = [
        lax.ppermute(mixed[k * x_block : (k + 1) * x_block], **xor("x", 4, k)) for k in (1, 2, 3)
    ]
    mixed_x = mixed[:x_block].astype(F32) + sum(part.astype(F32) for part in from_x)
    mixed_x = mixed_x.reshape(2, rows, width)
    mixed_give = lax.dynamic_index_in_dim(mixed_x, 1 - z_index, 0, keepdims=False)
    mixed_keep = lax.dynamic_index_in_dim(mixed_x, z_index, 0, keepdims=False)
    from_z = lax.ppermute(mixed_give.astype(BF16), **xor("zh", 2, 1))

    users_own = to_all(user_cache, PLANE, N_P).reshape(half, feats)
    users = (users_own, swap(users_own))

    partial = [dot(item_cache, u, ((1,), (1,))) for u in users]
    partial = jnp.concatenate(partial, axis=1)
    share = 2 * half // N_T
    partial = partial.reshape(rows, N_T, share).transpose(1, 0, 2)
    scores_own = jnp.sum(lax.all_to_all(partial, TENSOR, 0, 0), axis=0) * LOGIT_SCALE
    scores = to_all(scores_own, TENSOR, N_T).transpose(1, 0, 2).reshape(rows, 2 * half)

    own_residual = lax.dynamic_slice_in_dim(residual, (2 * x_index + z_index) * rows, rows, 0)
    hidden_own = tie(from_z.astype(F32), partial[0, :, :1]) + own_residual.astype(F32)
    hidden_own = (mixed_keep + hidden_own).astype(BF16)

    hidden_z = tie(lax.ppermute(hidden_own, **xor("zh", 2, 1)), scores_own[:, :1])
    hidden_0 = jnp.stack([hidden_own, hidden_z])
    hidden_0 = jnp.where(z_index == 0, hidden_0, hidden_0[::-1]).reshape(x_block, width)
    hidden_1 = lax.ppermute(hidden_0, **xor("x", 4, 1))
    hidden_3 = lax.ppermute(hidden_0, **xor("x", 4, 3))

    owner, row_in = positive // rows, positive % rows
    column = (owner % 2 != core).astype(jnp.int32) * half + (owner // 2) * rows + row_in
    maxima = jnp.max(scores, axis=1, keepdims=True)
    log_total = maxima[:, 0] + jnp.log(jnp.sum(jnp.exp(scores - maxima), axis=1))
    target = column[:, None] == lax.broadcasted_iota(jnp.int32, (1, 2 * half), 1)
    picked = jnp.sum(jnp.where(target, scores, F32(0.0)), axis=1)
    losses = jnp.concatenate(three_terms(log_total - picked))
    grad = (jnp.exp(scores - log_total[:, None]) - target.astype(F32)).astype(BF16)
    item_grad = (
        dot(grad[:, :half], users[0], ((1,), (0,))) + dot(grad[:, half:], users[1], ((1,), (0,)))
    ) * LOGIT_SCALE
    group_rows = to_all(item_grad[:GROUP], TENSOR, N_T)
    hidden_2 = [
        lax.ppermute(tie(hidden_1[:rows], item_grad[:, :1]), **xor("x", 4, 3)),
        lax.ppermute(tie(hidden_3[rows:], item_grad[:, :1]), **xor("x", 4, 1)),
    ]
    hidden = (hidden_0, hidden_1, *hidden_2, hidden_3)

    grad_losses = jnp.zeros((8, half), BF16).at[0, : 3 * rows].set(losses)
    other = swap(jnp.concatenate([grad[:, half:], grad_losses], axis=0))
    losses = jnp.concatenate([losses, other[rows, : 3 * rows]])
    losses = jnp.pad(losses, (0, 2 * rows)).reshape(2, heads // 2)
    losses = jnp.pad(losses, ((0, 6), (0, 0)))
    both = jnp.concatenate([grad[:, :half], other[:rows]], axis=0)
    both = both.T.reshape(N_P, rows, 2 * rows)
    by_plane = jnp.concatenate(
        [jnp.broadcast_to(item_cache[None], (N_P, rows, feats)), both], axis=2
    )
    by_plane = lax.all_to_all(by_plane, PLANE, 0, 0)

    group_rows = group_rows.transpose(1, 0, 2).reshape(GROUP, width)
    stream = stream_gradient(x_index, norm_gain, group_rows, hidden)

    side = heads // 2
    cut = width // N_P
    attn_give = lax.dynamic_slice_in_dim(attn, (1 - core) * side, side, 1)
    attn_keep = lax.dynamic_slice_in_dim(attn, core * side, side, 1)
    weight_give = swap(dot(stream, attn_give, ((0,), (0,))).astype(BF16))
    weight = dot(stream, attn_keep, ((0,), (0,))) + weight_give.astype(F32)
    weight = weight.astype(BF16).reshape(N_P, cut, side)
    final = jnp.concatenate([weight, jnp.broadcast_to(losses[None], (N_P, 8, side))], axis=1)
    final = lax.all_to_all(final, PLANE, 0, 0)
    head_grad = dot(stream, out_proj, ((1,), (1,))).astype(BF16)
    head_grad = by_xor(head_grad.reshape(4, x_block, heads), x_index).reshape(tokens, heads)
    items_own = by_plane[:, :, :feats].reshape(half, feats)
    by_item = by_plane[:, :, feats:].reshape(N_P, rows, 2, rows).transpose(2, 0, 3, 1)
    by_item = by_item.reshape(2, half, rows)
    user_grad = (
        dot(by_item[0], items_own, ((0,), (0,))) + dot(by_item[1], swap(items_own), ((0,), (0,)))
    ) * LOGIT_SCALE
    weight = jnp.sum(final[:, :cut].astype(F32), axis=0).reshape(2, cut // 2, side)
    weight_keep = lax.dynamic_index_in_dim(weight, core, 0, keepdims=False)
    weight_other = swap(lax.dynamic_index_in_dim(weight, 1 - core, 0, keepdims=False))
    lower = jnp.where(core == 0, weight_keep, weight_other)
    upper = jnp.where(core == 0, weight_other, weight_keep)
    weight_grad = jnp.concatenate([lower, upper], axis=1).T
    loss_mean = jnp.sum(final[:, cut:].astype(F32)) / (2 * half)
    return (loss_mean, item_grad, user_grad, head_grad, weight_grad)


def solution(mesh):
    names, sizes = zip(*AXES)
    fine = Mesh(mesh.devices.reshape(sizes), names)
    both = P(DP, TENSOR)
    return jax.shard_map(
        per_device,
        mesh=fine,
        in_specs=(both, both, P(DP), both, P(DP, None), P(TENSOR, None), P()),
        out_specs=(P(), both, both, both, P(TENSOR, DP)),
        check_vma=False,
    )
```

time: 234 us -> 204 us (0.87)
  the two profiles are of different devices: /device:TPU:8 before, /device:TPU:1 now
where the time goes in v8:
time: 204 us; the launch traced here: 202 us
  starting transfers between devices  112 us (55%)
  waiting for transfers between devices  29.4 us (14%)
  local copies, waits for them, and re-layouts  27.5 us (13%)
  matrix products  14.3 us (7%)
  other arithmetic  13.2 us (6%)
  between operations  3.07 us (2%)
  Pallas kernels  2.43 us (1%)
    ppermute x5, starting transfers between devices, swap(): return lax.ppermute(value, **xor('c', 2, 1))  25.9 us
    all_to_all x3, starting transfers between devices, to_all(): lax.all_to_all(jnp.broadcast_to(value[None], (count,) + value.shape), axe...  23.5 us
    dot_general x10, matrix products, dot(): return lax.dot_general(a, b, (dims, ((), ())), preferred_element_type=F32)  14.3 us
    all_to_all x3, waiting for transfers between devices, to_all(): lax.all_to_all(jnp.broadcast_to(value[None], (count,) + value.shape), axe...  13.8 us
    all_to_all x1, starting transfers between devices, per_device(): by_plane = lax.all_to_all(by_plane, PLANE, 0, 0)  11.5 us
    all_to_all x1, starting transfers between devices, per_device(): final = lax.all_to_all(final, PLANE, 0, 0)  9.78 us
    ppermute x3, starting transfers between devices, per_device(): lax.ppermute(mixed[k * x_block:(k + 1) * x_block], **xor('x', 4, k))  9.39 us
    ppermute x1, starting transfers between devices, per_device(): from_z = lax.ppermute(mixed_give.astype(BF16), **xor('zh', 2, 1))  7.94 us
  transfers between devices with their start and end apart: 20, of which 9 were waited for; matrix products, arithmetic and copies ran while one was open for 23% of the time, Pallas kernels for 1%

profile of v8, /device:TPU:1, one launch (start us, length us, event | category | flops | bytes accessed | tf_op | source)
XLA Modules:
  0.0 201.9 jit_solution(2167672881509644729)
XLA Ops:
  0.7 2.0 broadcast_in_dim.14
  2.7 13.5 %all-to-all-start = ((bf16[32,32,448]{2,1,0:T(8,128)(2,1)}), bf16[32,32,448]{2,1,0:T(8,128)(2,1)S(1)}, u32[]{:S(2)}, u32[]{:S(2)}) async-start(bf16[32,32,448]{2,1,0:T(8,128)(2,1)} %broadcast_in_dim.14), calls=%async_computation | async-start | bytes 2097152 | tf_op jit(solution)/shard_map/all_to_all | solution.py:39
  19.3 3.1 %collective-permute-start.1 = (bf16[64,3584]{1,0:T(8,128)(2,1)}, bf16[64,3584]{1,0:T(8,128)(2,1)S(1)}, u32[]{:S(2)}, u32[]{:S(2)}) collective-permute-start(bf16[64,3584]{1,0:T(8,128)(2,1)} %get-tuple-element.21), channel_id=1, source_target_pairs={{0,2},{2,0},{4,6},{6,4},{1,3},{3,1},{5,7},{7,5},{8,10},{10,8},{12,... | collective-permute-start | bytes 1376264 | tf_op jit(solution)/shard_map/ppermute | solution.py:99
  22.4 3.7 %collective-permute-start.3 = (bf16[64,3584]{1,0:T(8,128)(2,1)}, bf16[64,3584]{1,0:T(8,128)(2,1)}, u32[]{:S(2)}, u32[]{:S(2)}) collective-permute-start(bf16[64,3584]{1,0:T(8,128)(2,1)} %get-tuple-element.22), channel_id=1, source_target_pairs={{0,6},{2,4},{4,2},{6,0},{1,7},{3,5},{5,3},{7,1},{8,14},{10,12},{12... | collective-permute-start | bytes 1376264 | tf_op jit(solution)/shard_map/ppermute | solution.py:99
  26.1 2.6 %collective-permute-start.2 = (bf16[64,3584]{1,0:T(8,128)(2,1)}, bf16[64,3584]{1,0:T(8,128)(2,1)}, u32[]{:S(2)}, u32[]{:S(2)}) collective-permute-start(bf16[64,3584]{1,0:T(8,128)(2,1)} %get-tuple-element.23), channel_id=1, source_target_pairs={{0,4},{2,6},{4,0},{6,2},{1,5},{3,7},{5,1},{7,3},{8,12},{10,14},{12... | collective-permute-start | bytes 1376264 | tf_op jit(solution)/shard_map/ppermute | solution.py:99
  28.8 13.2 %all-to-all-done = bf16[32,32,448]{2,1,0:T(8,128)(2,1)S(1)} async-done(((bf16[32,32,448]{2,1,0:T(8,128)(2,1)}), bf16[32,32,448]{2,1,0:T(8,128)(2,1)S(1)}, u32[]{:S(2)}, u32[]{:S(2)}) %all-to-all-start) | async-done | bytes 917536 | tf_op jit(solution)/shard_map/all_to_all | solution.py:39
  43.3 6.3 %collective-permute-start = (bf16[1024,448]{0,1:T(8,128)(2,1)}, bf16[1024,448]{0,1:T(8,128)(2,1)S(1)}, u32[]{:S(2)}, u32[]{:S(2)}) collective-permute-start(bf16[1024,448]{0,1:T(8,128)(2,1)} %copy.44), channel_id=1, source_target_pairs={{0,8},{8,0},{1,9},{9,1},{2,10},{10,2},{3,11},{11,3},{4,12},{12,4},... | collective-permute-start | bytes 2752520 | tf_op jit(solution)/shard_map/ppermute | solution.py:27
  51.2 7.9 %collective-permute-start.4 = (bf16[32,3584]{1,0:T(8,128)(2,1)S(1)}, bf16[32,3584]{1,0:T(8,128)(2,1)S(1)}, u32[]{:S(2)}, u32[]{:S(2)}) collective-permute-start(bf16[32,3584]{1,0:T(8,128)(2,1)S(1)} %fusion.9), channel_id=1, source_target_pairs={{0,1},{1,0},{2,3},{3,2},{4,5},{5,4},{6,7},{7,6},{8,9},{9,8},{10,11... | collective-permute-start | bytes 688136 | tf_op jit(solution)/shard_map/ppermute | solution.py:105
  61.6 4.0 %all-to-all-start.1 = ((f32[8,32,256]{2,1,0:T(8,128)}), f32[8,32,256]{2,1,0:T(8,128)S(1)}, u32[]{:S(2)}, u32[]{:S(2)}) async-start(f32[8,32,256]{2,1,0:T(8,128)} %bitcast.77), calls=%async_computation.1 | async-start | bytes 524288 | tf_op jit(solution)/shard_map/all_to_all | solution.py:114
  69.2 6.3 %collective-permute-start.5 = (bf16[32,3584]{1,0:T(8,128)(2,1)S(1)}, bf16[32,3584]{1,0:T(8,128)(2,1)S(1)}, u32[]{:S(2)}, u32[]{:S(2)}) collective-permute-start(bf16[32,3584]{1,0:T(8,128)(2,1)S(1)} %fusion.7), channel_id=1, source_target_pairs={{0,1},{1,0},{2,3},{3,2},{4,5},{5,4},{6,7},{7,6},{8,9},{9,8},{10,11... | collective-permute-start | bytes 688136 | tf_op jit(solution)/shard_map/ppermute | solution.py:121
  76.9 4.2 %all-to-all-start.2 = ((f32[8,32,256]{2,1,0:T(8,128)}), f32[8,32,256]{2,1,0:T(8,128)S(1)}, u32[]{:S(2)}, u32[]{:S(2)}) async-start(f32[8,32,256]{2,1,0:T(8,128)} %broadcast_in_dim.15), calls=%async_computation.2 | async-start | bytes 524288 | tf_op jit(solution)/shard_map/all_to_all | solution.py:39
  81.1 3.9 %collective-permute-done.5 = bf16[32,3584]{1,0:T(8,128)(2,1)S(1)} collective-permute-done((bf16[32,3584]{1,0:T(8,128)(2,1)S(1)}, bf16[32,3584]{1,0:T(8,128)(2,1)S(1)}, u32[]{:S(2)}, u32[]{:S(2)}) %collective-permute-start.5) | collective-permute-done | bytes 229408 | tf_op jit(solution)/shard_map/ppermute | solution.py:121
  85.2 4.4 %collective-permute-start.8 = (bf16[64,3584]{1,0:T(8,128)(2,1)S(1)}, bf16[64,3584]{1,0:T(8,128)(2,1)S(1)}, u32[]{:S(2)}, u32[]{:S(2)}) collective-permute-start(bf16[64,3584]{1,0:T(8,128)(2,1)S(1)} %bitcast.80), channel_id=1, source_target_pairs={{0,6},{2,4},{4,2},{6,0},{1,7},{3,5},{5,3},{7,1},{8,14},{10,12},{12... | collective-permute-start | bytes 1376264 | tf_op jit(solution)/shard_map/ppermute | solution.py:125
  89.6 1.9 collective-permute-start.6
  94.8 2.4 %fusion.32 = f32[32,448]{1,0:T(8,128)} fusion(bf16[1024,448]{1,0:T(8,128)(2,1)} %bitcast.85, bf16[32,2048]{0,1:T(8,128)(2,1)S(1)} %fusion.5), kind=kOutput, calls=%fused_computation.96 | convolution fusion | flops 29360128 | bytes 1236992 | tf_op jit(solution)/shard_map/dot_general | solution.py:43
  101.1 5.9 %all-to-all-start.3 = ((f32[8,8,448]{2,1,0:T(8,128)}), f32[8,8,448]{2,1,0:T(8,128)}, u32[]{:S(2)}, u32[]{:S(2)}) async-start(f32[8,8,448]{2,1,0:T(8,128)} %broadcast_in_dim.16), calls=%async_computation.3 | async-start | bytes 262144 | tf_op jit(solution)/shard_map/all_to_all | solution.py:39
  108.0 4.8 %collective-permute-start.11 = (bf16[40,1024]{0,1:T(8,128)(2,1)S(1)}, bf16[40,1024]{0,1:T(8,128)(2,1)S(1)}, u32[]{:S(2)}, u32[]{:S(2)}) collective-permute-start(bf16[40,1024]{0,1:T(8,128)(2,1)S(1)} %fusion.8), channel_id=1, source_target_pairs={{0,8},{8,0},{1,9},{9,1},{2,10},{10,2},{3,11},{11,3},{4,12},{12,4},... | collective-permute-start | bytes 245768 | tf_op jit(solution)/shard_map/ppermute | solution.py:27
  116.5 11.5 %all-to-all-start.5 = ((bf16[32,32,512]{2,1,0:T(8,128)(2,1)}), bf16[32,32,512]{2,1,0:T(8,128)(2,1)}, u32[]{:S(2)}, u32[]{:S(2)}) async-start(bf16[32,32,512]{2,1,0:T(8,128)(2,1)} %pad_maximum_fusion), calls=%async_computation.5 | async-start | bytes 2097152 | tf_op jit(solution)/shard_map/all_to_all | solution.py:155
  128.9 3.6 %collective-permute-start.9 = (bf16[32,3584]{1,0:T(8,128)(2,1)}, bf16[32,3584]{1,0:T(8,128)(2,1)S(1)}, u32[]{:S(2)}, u32[]{:S(2)}) collective-permute-start(bf16[32,3584]{1,0:T(8,128)(2,1)} %get-tuple-element.40), channel_id=1, source_target_pairs={{0,2},{2,0},{4,6},{6,4},{1,3},{3,1},{5,7},{7,5},{8,10},{10,8},{12,... | collective-permute-start | bytes 688136 | tf_op jit(solution)/shard_map/ppermute | solution.py:141
  132.6 3.7 %collective-permute-start.7 = (bf16[32,3584]{1,0:T(8,128)(2,1)}, bf16[32,3584]{1,0:T(8,128)(2,1)}, u32[]{:S(2)}, u32[]{:S(2)}) collective-permute-start(bf16[32,3584]{1,0:T(8,128)(2,1)} %get-tuple-element.41), channel_id=1, source_target_pairs={{0,6},{2,4},{4,2},{6,0},{1,7},{3,5},{5,3},{7,1},{8,14},{10,12},{12... | collective-permute-start | bytes 688136 | tf_op jit(solution)/shard_map/ppermute | solution.py:140
  136.9 1.6 copy.49
  141.9 2.4 %shard_map.110 = bf16[256,3584]{1,0:T(8,128)(2,1)S(1)} custom-call(s32[1]{0:T(128)} %bitcast.x_ref, f32[1,3584]{1,0:T(1,128)S(1)} %copy-done.2, f32[8,3584]{1,0:T(8,128)S(1)} %reshape.147.group_ref, bf16[64,3584]{1,0:T(8,128)(2,1)S(1)} %bitcast.82, bf16[64,3584]{1,0:T(8,128)(2,1)S(1)} %collective-permute-done.6.refs_1_, ...), custom_call_target="tpu_custom_call" | custom-call | flops 11010048 | bytes 3670016 | tf_op jit(solution)/shard_map/pallas_call | solution.py:74
  146.3 6.2 %collective-permute-start.10 = (bf16[3584,128]{1,0:T(8,128)(2,1)S(1)}, bf16[3584,128]{1,0:T(8,128)(2,1)}, u32[]{:S(2)}, u32[]{:S(2)}) collective-permute-start(bf16[3584,128]{1,0:T(8,128)(2,1)S(1)} %convolution_convert_fusion.1), channel_id=1, source_target_pairs={{0,8},{8,0},{1,9},{9,1},{2,10},{10,2},{3,11},{11,3},{4,12},{12,4},... | collective-permute-start | bytes 2752520 | tf_op jit(solution)/shard_map/ppermute | solution.py:27
  154.7 2.4 %fusion = bf16[3584,128]{1,0:T(8,128)(2,1)S(1)} fusion(bf16[256,3584]{1,0:T(8,128)(2,1)} %copy-done.1, bf16[3584,128]{1,0:T(8,128)(2,1)} %collective-permute-done.10, bf16[256,256]{1,0:T(8,128)(2,1)S(1)} %bitcast.93, s32[]{:T(128)S(6)} %select_n.96), kind=kOutput, calls=%fused_computation.2 | convolution fusion | flops 236257280 | bytes 3735556 | tf_op jit(solution)/shard_map/dot_general | solution.py:43
  158.1 9.8 %all-to-all-start.4 = ((bf16[32,120,128]{2,1,0:T(8,128)(2,1)}), bf16[32,120,128]{2,1,0:T(8,128)(2,1)S(1)}, u32[]{:S(2)}, u32[]{:S(2)}) async-start(bf16[32,120,128]{2,1,0:T(8,128)(2,1)} %pad_maximum_fusion.1), calls=%async_computation.4 | async-start | bytes 1966080 | tf_op jit(solution)/shard_map/all_to_all | solution.py:168
  167.9 2.2 %copy.53 = bf16[1024,448]{0,1:T(8,128)(2,1)} copy(bf16[1024,448]{1,0:T(8,128)(2,1)} %bitcast.20) | data formatting | bytes 1835008 | tf_op jit(solution)/shard_map/reshape | solution.py:171
  170.2 2.7 %collective-permute-start.12 = (bf16[1024,448]{0,1:T(8,128)(2,1)}, bf16[1024,448]{0,1:T(8,128)(2,1)}, u32[]{:S(2)}, u32[]{:S(2)}) collective-permute-start(bf16[1024,448]{0,1:T(8,128)(2,1)} %copy.53), channel_id=1, source_target_pairs={{0,8},{8,0},{1,9},{9,1},{2,10},{10,2},{3,11},{11,3},{4,12},{12,4},... | collective-permute-start | bytes 2752520 | tf_op jit(solution)/shard_map/ppermute | solution.py:27
  172.9 2.2 %convolution_convert_fusion.2 = bf16[256,256]{1,0:T(8,128)(2,1)S(1)} fusion(bf16[256,3584]{1,0:T(8,128)(2,1)} %copy-done.1, bf16[256,3584]{1,0:T(8,128)(2,1)S(1)} %copy-done), kind=kOutput, calls=%fused_computation.5 | convolution fusion | flops 469827584 | bytes 3801088 | tf_op jit(solution)/shard_map/dot_general | solution.py:43
  175.8 1.8 slice.116
  184.1 2.2 %fusion.1 = f32[32,448]{1,0:T(8,128)} fusion(f32[32,448]{1,0:T(8,128)S(1)} %fusion.39, bf16[1024,32]{0,1:T(8,128)(2,1)S(1)} %squeeze.25, bf16[1024,448]{0,1:T(8,128)(2,1)} %collective-permute-done.12), kind=kOutput, calls=%fused_computation.7 | convolution fusion | flops 29388800 | bytes 1097728 | tf_op jit(solution)/shard_map/dot_general | solution.py:43
  186.3 6.5 %all-to-all-done.4 = bf16[32,120,128]{2,1,0:T(8,128)(2,1)S(1)} async-done(((bf16[32,120,128]{2,1,0:T(8,128)(2,1)}), bf16[32,120,128]{2,1,0:T(8,128)(2,1)S(1)}, u32[]{:S(2)}, u32[]{:S(2)}) %all-to-all-start.4) | async-done | bytes 983072 | tf_op jit(solution)/shard_map/all_to_all | solution.py:168
  193.0 5.9 %collective-permute-start.13 = (f32[56,128]{1,0:T(8,128)S(1)}, f32[56,128]{1,0:T(8,128)S(1)}, u32[]{:S(2)}, u32[]{:S(2)}) collective-permute-start(f32[56,128]{1,0:T(8,128)S(1)} %dynamic-slice_bitcast_fusion), channel_id=1, source_target_pairs={{0,8},{8,0},{1,9},{9,1},{2,10},{10,2},{3,11},{11,3},{4,12},{12,4},... | collective-permute-start | bytes 86024 | tf_op jit(solution)/shard_map/ppermute | solution.py:27
  (125 shorter events, 44.0 us)
Async XLA Ops:
  0.6 15.6 %copy-start = (bf16[256,3584]{1,0:T(8,128)(2,1)S(1)}, bf16[256,3584]{1,0:T(8,128)(2,1)}, u32[]{:S(2)}) copy-start(bf16[256,3584]{1,0:T(8,128)(2,1)} %param.14) | copy-start | bytes 5505028
  0.6 15.5 %copy-start.14 = (bf16[256,256]{1,0:T(8,128)(2,1)S(1)}, bf16[256,256]{1,0:T(8,128)(2,1)}, u32[]{:S(2)}) copy-start(bf16[256,256]{1,0:T(8,128)(2,1)} %param.12) | copy-start | bytes 393220
  2.7 39.3 %all-to-all-start = ((bf16[32,32,448]{2,1,0:T(8,128)(2,1)}), bf16[32,32,448]{2,1,0:T(8,128)(2,1)S(1)}, u32[]{:S(2)}, u32[]{:S(2)}) async-start(bf16[32,32,448]{2,1,0:T(8,128)(2,1)} %broadcast_in_dim.14), calls=%async_computation | async-start | bytes 2097152 | tf_op jit(solution)/shard_map/all_to_all | solution.py:39
  18.1 10.6 %copy-start.22 = (s32[32]{0:T(128)S(1)}, s32[32]{0:T(128)}, u32[]{:S(2)}) copy-start(s32[32]{0:T(128)} %param.11) | copy-start | bytes 388
  19.3 30.3 %collective-permute-start.1 = (bf16[64,3584]{1,0:T(8,128)(2,1)}, bf16[64,3584]{1,0:T(8,128)(2,1)S(1)}, u32[]{:S(2)}, u32[]{:S(2)}) collective-permute-start(bf16[64,3584]{1,0:T(8,128)(2,1)} %get-tuple-element.21), channel_id=1, source_target_pairs={{0,2},{2,0},{4,6},{6,4},{1,3},{3,1},{5,7},{7,5},{8,10},{10,8},{12,... | collective-permute-start | bytes 1376264 | tf_op jit(solution)/shard_map/ppermute | solution.py:99
  22.4 27.2 %collective-permute-start.3 = (bf16[64,3584]{1,0:T(8,128)(2,1)}, bf16[64,3584]{1,0:T(8,128)(2,1)}, u32[]{:S(2)}, u32[]{:S(2)}) collective-permute-start(bf16[64,3584]{1,0:T(8,128)(2,1)} %get-tuple-element.22), channel_id=1, source_target_pairs={{0,6},{2,4},{4,2},{6,0},{1,7},{3,5},{5,3},{7,1},{8,14},{10,12},{12... | collective-permute-start | bytes 1376264 | tf_op jit(solution)/shard_map/ppermute | solution.py:99
  26.1 23.5 %collective-permute-start.2 = (bf16[64,3584]{1,0:T(8,128)(2,1)}, bf16[64,3584]{1,0:T(8,128)(2,1)}, u32[]{:S(2)}, u32[]{:S(2)}) collective-permute-start(bf16[64,3584]{1,0:T(8,128)(2,1)} %get-tuple-element.23), channel_id=1, source_target_pairs={{0,4},{2,6},{4,0},{6,2},{1,5},{3,7},{5,1},{7,3},{8,12},{10,14},{12... | collective-permute-start | bytes 1376264 | tf_op jit(solution)/shard_map/ppermute | solution.py:99
  42.0 17.2 %copy-start.3 = (bf16[32,32,448]{2,1,0:T(8,128)(2,1)}, bf16[32,32,448]{2,1,0:T(8,128)(2,1)S(1)}, u32[]{:S(2)}) copy-start(bf16[32,32,448]{2,1,0:T(8,128)(2,1)S(1)} %all-to-all-done) | copy-start | bytes 2752516
  43.3 15.9 %copy-start.12 = (bf16[32,448]{1,0:T(8,128)(2,1)S(1)}, bf16[32,448]{1,0:T(8,128)(2,1)}, u32[]{:S(2)}) copy-start(bf16[32,448]{1,0:T(8,128)(2,1)} %param.9) | copy-start | bytes 86020
  43.3 16.3 %collective-permute-start = (bf16[1024,448]{0,1:T(8,128)(2,1)}, bf16[1024,448]{0,1:T(8,128)(2,1)S(1)}, u32[]{:S(2)}, u32[]{:S(2)}) collective-permute-start(bf16[1024,448]{0,1:T(8,128)(2,1)} %copy.44), channel_id=1, source_target_pairs={{0,8},{8,0},{1,9},{9,1},{2,10},{10,2},{3,11},{11,3},{4,12},{12,4},... | collective-permute-start | bytes 2752520 | tf_op jit(solution)/shard_map/ppermute | solution.py:27
  51.2 10.4 %copy-start.7 = (f32[64,3584]{1,0:T(8,128)}, f32[64,3584]{1,0:T(8,128)S(1)}, u32[]{:S(2)}) copy-start(f32[64,3584]{1,0:T(8,128)S(1)} %add_add_fusion) | copy-start | bytes 2752516
  51.2 16.8 %collective-permute-start.4 = (bf16[32,3584]{1,0:T(8,128)(2,1)S(1)}, bf16[32,3584]{1,0:T(8,128)(2,1)S(1)}, u32[]{:S(2)}, u32[]{:S(2)}) collective-permute-start(bf16[32,3584]{1,0:T(8,128)(2,1)S(1)} %fusion.9), channel_id=1, source_target_pairs={{0,1},{1,0},{2,3},{3,2},{4,5},{5,4},{6,7},{7,6},{8,9},{9,8},{10,11... | collective-permute-start | bytes 688136 | tf_op jit(solution)/shard_map/ppermute | solution.py:105
  61.6 14.5 %all-to-all-start.1 = ((f32[8,32,256]{2,1,0:T(8,128)}), f32[8,32,256]{2,1,0:T(8,128)S(1)}, u32[]{:S(2)}, u32[]{:S(2)}) async-start(f32[8,32,256]{2,1,0:T(8,128)} %bitcast.77), calls=%async_computation.1 | async-start | bytes 524288 | tf_op jit(solution)/shard_map/all_to_all | solution.py:114
  69.2 15.8 %collective-permute-start.5 = (bf16[32,3584]{1,0:T(8,128)(2,1)S(1)}, bf16[32,3584]{1,0:T(8,128)(2,1)S(1)}, u32[]{:S(2)}, u32[]{:S(2)}) collective-permute-start(bf16[32,3584]{1,0:T(8,128)(2,1)S(1)} %fusion.7), channel_id=1, source_target_pairs={{0,1},{1,0},{2,3},{3,2},{4,5},{5,4},{6,7},{7,6},{8,9},{9,8},{10,11... | collective-permute-start | bytes 688136 | tf_op jit(solution)/shard_map/ppermute | solution.py:121
  76.9 14.7 %all-to-all-start.2 = ((f32[8,32,256]{2,1,0:T(8,128)}), f32[8,32,256]{2,1,0:T(8,128)S(1)}, u32[]{:S(2)}, u32[]{:S(2)}) async-start(f32[8,32,256]{2,1,0:T(8,128)} %broadcast_in_dim.15), calls=%async_computation.2 | async-start | bytes 524288 | tf_op jit(solution)/shard_map/all_to_all | solution.py:39
  85.2 42.8 %collective-permute-start.8 = (bf16[64,3584]{1,0:T(8,128)(2,1)S(1)}, bf16[64,3584]{1,0:T(8,128)(2,1)S(1)}, u32[]{:S(2)}, u32[]{:S(2)}) collective-permute-start(bf16[64,3584]{1,0:T(8,128)(2,1)S(1)} %bitcast.80), channel_id=1, source_target_pairs={{0,6},{2,4},{4,2},{6,0},{1,7},{3,5},{5,3},{7,1},{8,14},{10,12},{12... | collective-permute-start | bytes 1376264 | tf_op jit(solution)/shard_map/ppermute | solution.py:125
  89.6 38.4 %collective-permute-start.6 = (bf16[64,3584]{1,0:T(8,128)(2,1)S(1)}, bf16[64,3584]{1,0:T(8,128)(2,1)S(1)}, u32[]{:S(2)}, u32[]{:S(2)}) collective-permute-start(bf16[64,3584]{1,0:T(8,128)(2,1)S(1)} %bitcast.81), channel_id=1, source_target_pairs={{0,2},{2,0},{4,6},{6,4},{1,3},{3,1},{5,7},{7,5},{8,10},{10,8},{12,... | collective-permute-start | bytes 1376264 | tf_op jit(solution)/shard_map/ppermute | solution.py:124
  91.9 6.0 %copy-start.16 = (bf16[32]{0:T(256)(128)(2,1)}, bf16[32]{0:T(256)(128)(2,1)S(1)}, u32[]{:S(2)}) copy-start(bf16[32]{0:T(256)(128)(2,1)S(1)} %get-tuple-element.19) | copy-start | bytes 196
  101.1 15.4 %all-to-all-start.3 = ((f32[8,8,448]{2,1,0:T(8,128)}), f32[8,8,448]{2,1,0:T(8,128)}, u32[]{:S(2)}, u32[]{:S(2)}) async-start(f32[8,8,448]{2,1,0:T(8,128)} %broadcast_in_dim.16), calls=%async_computation.3 | async-start | bytes 262144 | tf_op jit(solution)/shard_map/all_to_all | solution.py:39
  108.0 6.0 %collective-permute-start.11 = (bf16[40,1024]{0,1:T(8,128)(2,1)S(1)}, bf16[40,1024]{0,1:T(8,128)(2,1)S(1)}, u32[]{:S(2)}, u32[]{:S(2)}) collective-permute-start(bf16[40,1024]{0,1:T(8,128)(2,1)S(1)} %fusion.8), channel_id=1, source_target_pairs={{0,8},{8,0},{1,9},{9,1},{2,10},{10,2},{3,11},{11,3},{4,12},{12,4},... | collective-permute-start | bytes 245768 | tf_op jit(solution)/shard_map/ppermute | solution.py:27
  116.0 20.3 %copy-start.15 = (f32[3584]{0:T(1024)S(1)}, f32[3584]{0:T(1024)}, u32[]{:S(2)}) copy-start(f32[3584]{0:T(1024)} %param.15) | copy-start | bytes 43012
  116.5 41.6 %all-to-all-start.5 = ((bf16[32,32,512]{2,1,0:T(8,128)(2,1)}), bf16[32,32,512]{2,1,0:T(8,128)(2,1)}, u32[]{:S(2)}, u32[]{:S(2)}) async-start(bf16[32,32,512]{2,1,0:T(8,128)(2,1)} %pad_maximum_fusion), calls=%async_computation.5 | async-start | bytes 2097152 | tf_op jit(solution)/shard_map/all_to_all | solution.py:155
  128.9 10.6 %collective-permute-start.9 = (bf16[32,3584]{1,0:T(8,128)(2,1)}, bf16[32,3584]{1,0:T(8,128)(2,1)S(1)}, u32[]{:S(2)}, u32[]{:S(2)}) collective-permute-start(bf16[32,3584]{1,0:T(8,128)(2,1)} %get-tuple-element.40), channel_id=1, source_target_pairs={{0,2},{2,0},{4,6},{6,4},{1,3},{3,1},{5,7},{7,5},{8,10},{10,8},{12,... | collective-permute-start | bytes 688136 | tf_op jit(solution)/shard_map/ppermute | solution.py:141
  132.6 8.6 %collective-permute-start.7 = (bf16[32,3584]{1,0:T(8,128)(2,1)}, bf16[32,3584]{1,0:T(8,128)(2,1)}, u32[]{:S(2)}, u32[]{:S(2)}) collective-permute-start(bf16[32,3584]{1,0:T(8,128)(2,1)} %get-tuple-element.41), channel_id=1, source_target_pairs={{0,6},{2,4},{4,2},{6,0},{1,7},{3,5},{5,3},{7,1},{8,14},{10,12},{12... | collective-permute-start | bytes 688136 | tf_op jit(solution)/shard_map/ppermute | solution.py:140
  145.6 7.8 %copy-start.17 = (bf16[32]{0:T(256)(128)(2,1)S(1)}, bf16[32]{0:T(256)(128)(2,1)}, u32[]{:S(2)}) copy-start(bf16[32]{0:T(256)(128)(2,1)} %copy-done.16) | copy-start | bytes 196
  145.6 7.8 %copy-start.19 = (bf16[32]{0:T(256)(128)(2,1)S(1)}, bf16[32]{0:T(256)(128)(2,1)}, u32[]{:S(2)}) copy-start(bf16[32]{0:T(256)(128)(2,1)} %copy-done.18) | copy-start | bytes 196
  145.6 7.8 %copy-start.21 = (bf16[32]{0:T(256)(128)(2,1)S(1)}, bf16[32]{0:T(256)(128)(2,1)}, u32[]{:S(2)}) copy-start(bf16[32]{0:T(256)(128)(2,1)} %copy-done.20) | copy-start | bytes 196
  145.6 9.1 %copy-start.10 = (bf16[4,64,256]{2,1,0:T(8,128)(2,1)S(1)}, bf16[4,64,256]{2,1,0:T(8,128)(2,1)}, u32[]{:S(2)}) copy-start(bf16[4,64,256]{2,1,0:T(8,128)(2,1)} %copy-done.8) | copy-start | bytes 393220
  146.3 8.4 %collective-permute-start.10 = (bf16[3584,128]{1,0:T(8,128)(2,1)S(1)}, bf16[3584,128]{1,0:T(8,128)(2,1)}, u32[]{:S(2)}, u32[]{:S(2)}) collective-permute-start(bf16[3584,128]{1,0:T(8,128)(2,1)S(1)} %convolution_convert_fusion.1), channel_id=1, source_target_pairs={{0,8},{8,0},{1,9},{9,1},{2,10},{10,2},{3,11},{11,3},{4,12},{12,4},... | collective-permute-start | bytes 2752520 | tf_op jit(solution)/shard_map/ppermute | solution.py:27
  158.1 34.7 %all-to-all-start.4 = ((bf16[32,120,128]{2,1,0:T(8,128)(2,1)}), bf16[32,120,128]{2,1,0:T(8,128)(2,1)S(1)}, u32[]{:S(2)}, u32[]{:S(2)}) async-start(bf16[32,120,128]{2,1,0:T(8,128)(2,1)} %pad_maximum_fusion.1), calls=%async_computation.4 | async-start | bytes 1966080 | tf_op jit(solution)/shard_map/all_to_all | solution.py:168
  170.2 13.9 %collective-permute-start.12 = (bf16[1024,448]{0,1:T(8,128)(2,1)}, bf16[1024,448]{0,1:T(8,128)(2,1)}, u32[]{:S(2)}, u32[]{:S(2)}) collective-permute-start(bf16[1024,448]{0,1:T(8,128)(2,1)} %copy.53), channel_id=1, source_target_pairs={{0,8},{8,0},{1,9},{9,1},{2,10},{10,2},{3,11},{11,3},{4,12},{12,4},... | collective-permute-start | bytes 2752520 | tf_op jit(solution)/shard_map/ppermute | solution.py:27
  193.0 7.1 %collective-permute-start.13 = (f32[56,128]{1,0:T(8,128)S(1)}, f32[56,128]{1,0:T(8,128)S(1)}, u32[]{:S(2)}, u32[]{:S(2)}) collective-permute-start(f32[56,128]{1,0:T(8,128)S(1)} %dynamic-slice_bitcast_fusion), channel_id=1, source_target_pairs={{0,8},{8,0},{1,9},{9,1},{2,10},{10,2},{3,11},{11,3},{4,12},{12,4},... | collective-permute-start | bytes 86024 | tf_op jit(solution)/shard_map/ppermute | solution.py:27
  (11 other events, 24.1 us)

commit v9 on v8

--- a/solution.py
+++ b/solution.py
@@ -52,15 +52,16 @@
     return value + (column * 0).astype(value.dtype)
 
 
-def stream_kernel(x_ref, gain_ref, group_ref, *refs):
-    first, second, third_0, third_1, fourth, out_ref = refs
+def stream_kernel(x_ref, group_ref, *refs):
+    first, second, third_0, third_1, fourth, out_ref, up_ref = refs
     halves = (first, first, second, second, third_0, third_1, fourth, fourth)
     width = out_ref.shape[1]
+    up_ref[...] = jnp.concatenate([group_ref[t] for t in range(N_T)], axis=1)
     for item in range(GROUP):
         start = 0 if halves[item].shape[0] == SEQ else item % 2 * SEQ
         tokens = halves[item][start : start + SEQ, :].astype(F32)
         which = (x_ref[0] ^ (item // 2)) * 2 + item % 2
-        up = gain_ref[...] * (group_ref[pl.ds(which, 1), :] / SEQ)
+        up = up_ref[pl.ds(which, 1), :]
         mean = jnp.sum(tokens * tokens, axis=1, keepdims=True) / width
         inverse = lax.rsqrt(mean + NORM_EPS)
         inner = jnp.sum(up * tokens, axis=1, keepdims=True) / width
@@ -68,19 +69,43 @@
         out_ref[item * SEQ : (item + 1) * SEQ, :] = stream.astype(BF16)
 
 
-def stream_gradient(x_index, norm_gain, group_rows, blocks):
-    tokens, width = GROUP * SEQ, norm_gain.shape[0]
+def stream_gradient(x_index, group_rows, blocks):
+    tokens, width = GROUP * SEQ, blocks[0].shape[1]
     whole = pl.BlockSpec(memory_space=pltpu.VMEM)
     return pl.pallas_call(
         stream_kernel,
         out_shape=jax.ShapeDtypeStruct((tokens, width), BF16),
-        in_specs=[pl.BlockSpec(memory_space=pltpu.SMEM)] + [whole] * 7,
+        in_specs=[pl.BlockSpec(memory_space=pltpu.SMEM)] + [whole] * 6,
         out_specs=whole,
+        scratch_shapes=[pltpu.VMEM((GROUP, width), F32)],
         compiler_params=pltpu.CompilerParams(vmem_limit_bytes=24 * 2**20),
         cost_estimate=pl.CostEstimate(
             flops=12 * tokens * width, bytes_accessed=4 * tokens * width, transcendentals=0
         ),
-    )(x_index.reshape(1), norm_gain.reshape(1, width), group_rows, *blocks)
+    )(x_index.reshape(1), group_rows, *blocks)
+
+
+def payload_kernel(item_ref, own_ref, other_ref, out_ref):
+    rows, feats = item_ref.shape
+    both = jnp.concatenate([own_ref[...].astype(F32), other_ref[:rows, :].astype(F32)], axis=0)
+    both = both.T.astype(BF16)
+    for place in range(N_P):
+        out_ref[place, :, :feats] = item_ref[...]
+        out_ref[place, :, feats:] = both[place * rows : (place + 1) * rows, :]
+
+
+def plane_payload(item_cache, own, other):
+    rows, feats = item_cache.shape
+    whole = pl.BlockSpec(memory_space=pltpu.VMEM)
+    size = N_P * rows * (feats + 2 * rows)
+    return pl.pallas_call(
+        payload_kernel,
+        out_shape=jax.ShapeDtypeStruct((N_P, rows, feats + 2 * rows), BF16),
+        in_specs=[whole] * 3,
+        out_specs=whole,
+        compiler_params=pltpu.CompilerParams(vmem_limit_bytes=12 * 2**20),
+        cost_estimate=pl.CostEstimate(flops=0, bytes_accessed=2 * size, transcendentals=0),
+    )(item_cache, own, other)
 
 
 def per_device(item_cache, user_cache, positive, attn_heads, residual, out_proj, norm_gain):
@@ -135,7 +160,9 @@
     item_grad = (
         dot(grad[:, :half], users[0], ((1,), (0,))) + dot(grad[:, half:], users[1], ((1,), (0,)))
     ) * LOGIT_SCALE
-    group_rows = to_all(item_grad[:GROUP], TENSOR, N_T)
+    t_index = 2 * x_index + z_index
+    own_gain = lax.dynamic_slice_in_dim(norm_gain, t_index * feats, feats, 0) / SEQ
+    group_rows = to_all(own_gain[None, :] * item_grad[:GROUP], TENSOR, N_T)
     hidden_2 = [
         lax.ppermute(tie(hidden_1[:rows], item_grad[:, :1]), **xor("x", 4, 3)),
         lax.ppermute(tie(hidden_3[rows:], item_grad[:, :1]), **xor("x", 4, 1)),
@@ -147,15 +174,10 @@
     losses = jnp.concatenate([losses, other[rows, : 3 * rows]])
     losses = jnp.pad(losses, (0, 2 * rows)).reshape(2, heads // 2)
     losses = jnp.pad(losses, ((0, 6), (0, 0)))
-    both = jnp.concatenate([grad[:, :half], other[:rows]], axis=0)
-    both = both.T.reshape(N_P, rows, 2 * rows)
-    by_plane = jnp.concatenate(
-        [jnp.broadcast_to(item_cache[None], (N_P, rows, feats)), both], axis=2
-    )
+    by_plane = plane_payload(item_cache, grad[:, :half], other)
     by_plane = lax.all_to_all(by_plane, PLANE, 0, 0)
 
-    group_rows = group_rows.transpose(1, 0, 2).reshape(GROUP, width)
-    stream = stream_gradient(x_index, norm_gain, group_rows, hidden)
+    stream = stream_gradient(x_index, group_rows, hidden)
 
     side = heads // 2
     cut = width // N_P

time: 204 us -> 202 us (level)
  local copies, waits for them, and re-layouts: 27.5 us -> 18 us
  waiting for transfers between devices: 29.4 us -> 38.8 us
  matrix products: 14.3 us -> 12.2 us
    all_to_all x3, waiting for transfers between devices: 13.8 us -> 17.9 us  [to_all(): lax.all_to_all(jnp.broadcast_to(value[None], (count,) + value.shape), axe...]
    ppermute x1, waiting for transfers between devices: 0.01 us -> 3.67 us  [per_device(): lax.ppermute(tie(hidden_3[rows:], item_grad[:, :1]), **xor('x', 4, 1))]
    ppermute x1, waiting for transfers between devices: 3.85 us -> 0.71 us  [per_device(): lax.ppermute(hidden_own, **xor('zh', 2, 1))]
    all_to_all x1, starting transfers between devices: 11.5 us -> 8.38 us  [per_device(): by_plane = lax.all_to_all(by_plane, PLANE, 0, 0)]
    all_to_all x1, waiting for transfers between devices: 6.52 us -> 9.51 us  [per_device(): final = lax.all_to_all(final, PLANE, 0, 0)]
    transpose x2 -> x0, local copies, waits for them, and re-layouts: 2.97 us -> none  [the longest x1 1.64 us: per_device(): group_rows = group_rows.transpose(1, 0, 2).reshape(GROUP, width)]
    slice x4 -> x0, local copies, waits for them, and re-layouts: 2.78 us -> none  [the longest x2 1.86 us: per_device(): by_item[1]]
    dot_general x10, matrix products: 14.3 us -> 12.2 us  [dot(): return lax.dot_general(a, b, (dims, ((), ())), preferred_element_type=F32)]
  transfers between devices with their start and end apart: 20 -> 20, of which waited for: 9 -> 11; matrix products, arithmetic and copies ran while one was open for 23% -> 18% of each run, Pallas kernels for 1% -> 2%
where the time goes in v9:
time: 202 us; the launch traced here: 201 us
  starting transfers between devices  112 us (55%)
  waiting for transfers between devices  38.8 us (19%)
  local copies, waits for them, and re-layouts  18 us (9%)
  other arithmetic  13.2 us (7%)
  matrix products  12.2 us (6%)
  Pallas kernels  3.62 us (2%)
  between operations  2.99 us (1%)
    ppermute x5, starting transfers between devices, swap(): return lax.ppermute(value, **xor('c', 2, 1))  26.6 us
    all_to_all x3, starting transfers between devices, to_all(): lax.all_to_all(jnp.broadcast_to(value[None], (count,) + value.shape), axe...  24.3 us
    all_to_all x3, waiting for transfers between devices, to_all(): lax.all_to_all(jnp.broadcast_to(value[None], (count,) + value.shape), axe...  17.9 us
    dot_general x10, matrix products, dot(): return lax.dot_general(a, b, (dims, ((), ())), preferred_element_type=F32)  12.2 us
    all_to_all x1, starting transfers between devices, per_device(): final = lax.all_to_all(final, PLANE, 0, 0)  9.78 us
    ppermute x3, starting transfers between devices, per_device(): lax.ppermute(mixed[k * x_block:(k + 1) * x_block], **xor('x', 4, k))  9.57 us
    all_to_all x1, waiting for transfers between devices, per_device(): final = lax.all_to_all(final, PLANE, 0, 0)  9.51 us
    all_to_all x1, starting transfers between devices, per_device(): by_plane = lax.all_to_all(by_plane, PLANE, 0, 0)  8.38 us
  transfers between devices with their start and end apart: 20, of which 11 were waited for; matrix products, arithmetic and copies ran while one was open for 18% of the time, Pallas kernels for 2%

profile of v9, /device:TPU:1, one launch (start us, length us, event | category | flops | bytes accessed | tf_op | source)
XLA Modules:
  0.0 200.6 jit_solution(6599878377828299346)
XLA Ops:
  0.7 2.0 %broadcast_in_dim.11 = bf16[32,32,448]{2,1,0:T(8,128)(2,1)} broadcast(bf16[32,448]{1,0:T(8,128)(2,1)} %param.10), dimensions={1,2} | broadcast | bytes 946176 | tf_op jit(solution)/shard_map/broadcast_in_dim | solution.py:39
  2.7 13.5 %all-to-all-start = ((bf16[32,32,448]{2,1,0:T(8,128)(2,1)}), bf16[32,32,448]{2,1,0:T(8,128)(2,1)S(1)}, u32[]{:S(2)}, u32[]{:S(2)}) async-start(bf16[32,32,448]{2,1,0:T(8,128)(2,1)} %broadcast_in_dim.11), calls=%async_computation | async-start | bytes 2097152 | tf_op jit(solution)/shard_map/all_to_all | solution.py:39
  19.3 3.1 %collective-permute-start.1 = (bf16[64,3584]{1,0:T(8,128)(2,1)}, bf16[64,3584]{1,0:T(8,128)(2,1)S(1)}, u32[]{:S(2)}, u32[]{:S(2)}) collective-permute-start(bf16[64,3584]{1,0:T(8,128)(2,1)} %get-tuple-element.21), channel_id=1, source_target_pairs={{0,2},{2,0},{4,6},{6,4},{1,3},{3,1},{5,7},{7,5},{8,10},{10,8},{12,... | collective-permute-start | bytes 1376264 | tf_op jit(solution)/shard_map/ppermute | solution.py:124
  22.4 4.4 %collective-permute-start.2 = (bf16[64,3584]{1,0:T(8,128)(2,1)}, bf16[64,3584]{1,0:T(8,128)(2,1)}, u32[]{:S(2)}, u32[]{:S(2)}) collective-permute-start(bf16[64,3584]{1,0:T(8,128)(2,1)} %get-tuple-element.23), channel_id=1, source_target_pairs={{0,4},{2,6},{4,0},{6,2},{1,5},{3,7},{5,1},{7,3},{8,12},{10,14},{12... | collective-permute-start | bytes 1376264 | tf_op jit(solution)/shard_map/ppermute | solution.py:124
  26.8 2.1 %collective-permute-start.3 = (bf16[64,3584]{1,0:T(8,128)(2,1)}, bf16[64,3584]{1,0:T(8,128)(2,1)}, u32[]{:S(2)}, u32[]{:S(2)}) collective-permute-start(bf16[64,3584]{1,0:T(8,128)(2,1)} %get-tuple-element.22), channel_id=1, source_target_pairs={{0,6},{2,4},{4,2},{6,0},{1,7},{3,5},{5,3},{7,1},{8,14},{10,12},{12... | collective-permute-start | bytes 1376264 | tf_op jit(solution)/shard_map/ppermute | solution.py:124
  29.7 12.3 %all-to-all-done = bf16[32,32,448]{2,1,0:T(8,128)(2,1)S(1)} async-done(((bf16[32,32,448]{2,1,0:T(8,128)(2,1)}), bf16[32,32,448]{2,1,0:T(8,128)(2,1)S(1)}, u32[]{:S(2)}, u32[]{:S(2)}) %all-to-all-start) | async-done | bytes 917536 | tf_op jit(solution)/shard_map/all_to_all | solution.py:39
  43.3 6.3 %collective-permute-start = (bf16[1024,448]{0,1:T(8,128)(2,1)}, bf16[1024,448]{0,1:T(8,128)(2,1)S(1)}, u32[]{:S(2)}, u32[]{:S(2)}) collective-permute-start(bf16[1024,448]{0,1:T(8,128)(2,1)} %copy.22), channel_id=1, source_target_pairs={{0,8},{8,0},{1,9},{9,1},{2,10},{10,2},{3,11},{11,3},{4,12},{12,4},... | collective-permute-start | bytes 2752520 | tf_op jit(solution)/shard_map/ppermute | solution.py:27
  52.2 7.9 %collective-permute-start.4 = (bf16[32,3584]{1,0:T(8,128)(2,1)S(1)}, bf16[32,3584]{1,0:T(8,128)(2,1)S(1)}, u32[]{:S(2)}, u32[]{:S(2)}) collective-permute-start(bf16[32,3584]{1,0:T(8,128)(2,1)S(1)} %fusion.7), channel_id=1, source_target_pairs={{0,1},{1,0},{2,3},{3,2},{4,5},{5,4},{6,7},{7,6},{8,9},{9,8},{10,11... | collective-permute-start | bytes 688136 | tf_op jit(solution)/shard_map/ppermute | solution.py:130
  62.5 3.4 %all-to-all-start.1 = ((f32[8,32,256]{2,1,0:T(8,128)}), f32[8,32,256]{2,1,0:T(8,128)S(1)}, u32[]{:S(2)}, u32[]{:S(2)}) async-start(f32[8,32,256]{2,1,0:T(8,128)} %bitcast.77), calls=%async_computation.1 | async-start | bytes 524288 | tf_op jit(solution)/shard_map/all_to_all | solution.py:139
  68.0 7.2 %collective-permute-start.5 = (bf16[32,3584]{1,0:T(8,128)(2,1)S(1)}, bf16[32,3584]{1,0:T(8,128)(2,1)S(1)}, u32[]{:S(2)}, u32[]{:S(2)}) collective-permute-start(bf16[32,3584]{1,0:T(8,128)(2,1)S(1)} %fusion.3), channel_id=1, source_target_pairs={{0,1},{1,0},{2,3},{3,2},{4,5},{5,4},{6,7},{7,6},{8,9},{9,8},{10,11... | collective-permute-start | bytes 688136 | tf_op jit(solution)/shard_map/ppermute | solution.py:146
  75.2 2.2 %all-to-all-done.1 = f32[8,32,256]{2,1,0:T(8,128)S(1)} async-done(((f32[8,32,256]{2,1,0:T(8,128)}), f32[8,32,256]{2,1,0:T(8,128)S(1)}, u32[]{:S(2)}, u32[]{:S(2)}) %all-to-all-start.1) | async-done | bytes 262176 | tf_op jit(solution)/shard_map/all_to_all | solution.py:139
  78.1 6.1 %all-to-all-start.2 = ((f32[8,32,256]{2,1,0:T(8,128)}), f32[8,32,256]{2,1,0:T(8,128)}, u32[]{:S(2)}, u32[]{:S(2)}) async-start(f32[8,32,256]{2,1,0:T(8,128)} %broadcast_in_dim.13), calls=%async_computation.2 | async-start | bytes 524288 | tf_op jit(solution)/shard_map/all_to_all | solution.py:39
  85.3 3.2 %collective-permute-start.6 = (bf16[64,3584]{1,0:T(8,128)(2,1)S(1)}, bf16[64,3584]{1,0:T(8,128)(2,1)S(1)}, u32[]{:S(2)}, u32[]{:S(2)}) collective-permute-start(bf16[64,3584]{1,0:T(8,128)(2,1)S(1)} %bitcast.79), channel_id=1, source_target_pairs={{0,2},{2,0},{4,6},{6,4},{1,3},{3,1},{5,7},{7,5},{8,10},{10,8},{12,... | collective-permute-start | bytes 1376264 | tf_op jit(solution)/shard_map/ppermute | solution.py:149
  88.5 4.6 %collective-permute-start.8 = (bf16[64,3584]{1,0:T(8,128)(2,1)S(1)}, bf16[64,3584]{1,0:T(8,128)(2,1)S(1)}, u32[]{:S(2)}, u32[]{:S(2)}) collective-permute-start(bf16[64,3584]{1,0:T(8,128)(2,1)S(1)} %bitcast.80), channel_id=1, source_target_pairs={{0,6},{2,4},{4,2},{6,0},{1,7},{3,5},{5,3},{7,1},{8,14},{10,12},{12... | collective-permute-start | bytes 1376264 | tf_op jit(solution)/shard_map/ppermute | solution.py:150
  93.1 2.8 %all-to-all-done.2 = f32[8,32,256]{2,1,0:T(8,128)} async-done(((f32[8,32,256]{2,1,0:T(8,128)}), f32[8,32,256]{2,1,0:T(8,128)}, u32[]{:S(2)}, u32[]{:S(2)}) %all-to-all-start.2) | async-done | bytes 262176 | tf_op jit(solution)/shard_map/all_to_all | solution.py:39
  103.7 4.7 %all-to-all-start.3 = ((f32[8,8,448]{2,1,0:T(8,128)}), f32[8,8,448]{2,1,0:T(8,128)S(1)}, u32[]{:S(2)}, u32[]{:S(2)}) async-start(f32[8,8,448]{2,1,0:T(8,128)} %broadcast_in_dim.14), calls=%async_computation.3 | async-start | bytes 262144 | tf_op jit(solution)/shard_map/all_to_all | solution.py:39
  108.5 4.3 %collective-permute-start.11 = (bf16[40,1024]{1,0:T(8,128)(2,1)S(1)}, bf16[40,1024]{1,0:T(8,128)(2,1)S(1)}, u32[]{:S(2)}, u32[]{:S(2)}) collective-permute-start(bf16[40,1024]{1,0:T(8,128)(2,1)S(1)} %fusion.9), channel_id=1, source_target_pairs={{0,8},{8,0},{1,9},{9,1},{2,10},{10,2},{3,11},{11,3},{4,12},{12,4},... | collective-permute-start | bytes 245768 | tf_op jit(solution)/shard_map/ppermute | solution.py:27
  115.1 2.8 %all-to-all-done.3.group_ref = f32[8,8,448]{2,1,0:T(8,128)S(1)} async-done(((f32[8,8,448]{2,1,0:T(8,128)}), f32[8,8,448]{2,1,0:T(8,128)S(1)}, u32[]{:S(2)}, u32[]{:S(2)}) %all-to-all-start.3) | async-done | bytes 114720 | tf_op jit(solution)/shard_map/all_to_all | solution.py:39
  117.9 8.4 %all-to-all-start.5 = ((bf16[32,32,512]{2,1,0:T(8,128)(2,1)}), bf16[32,32,512]{2,1,0:T(8,128)(2,1)}, u32[]{:S(2)}, u32[]{:S(2)}) async-start(bf16[32,32,512]{2,1,0:T(8,128)(2,1)} %shard_map.111), calls=%async_computation.5 | async-start | bytes 2097152 | tf_op jit(solution)/shard_map/all_to_all | solution.py:178
  127.2 4.9 %collective-permute-start.7 = (bf16[32,3584]{1,0:T(8,128)(2,1)}, bf16[32,3584]{1,0:T(8,128)(2,1)}, u32[]{:S(2)}, u32[]{:S(2)}) collective-permute-start(bf16[32,3584]{1,0:T(8,128)(2,1)} %get-tuple-element.41), channel_id=1, source_target_pairs={{0,6},{2,4},{4,2},{6,0},{1,7},{3,5},{5,3},{7,1},{8,14},{10,12},{12... | collective-permute-start | bytes 688136 | tf_op jit(solution)/shard_map/ppermute | solution.py:167
  135.7 3.7 %collective-permute-done.9.refs_3_ = bf16[32,3584]{1,0:T(8,128)(2,1)} collective-permute-done((bf16[32,3584]{1,0:T(8,128)(2,1)}, bf16[32,3584]{1,0:T(8,128)(2,1)}, u32[]{:S(2)}, u32[]{:S(2)}) %collective-permute-start.9) | collective-permute-done | bytes 229408 | tf_op jit(solution)/shard_map/ppermute | solution.py:168
  139.4 2.3 %shard_map.110 = bf16[256,3584]{1,0:T(8,128)(2,1)S(1)} custom-call(s32[1]{0:T(128)} %bitcast.x_ref, f32[8,8,448]{2,1,0:T(8,128)S(1)} %all-to-all-done.3.group_ref, bf16[64,3584]{1,0:T(8,128)(2,1)S(1)} %bitcast.81, bf16[64,3584]{1,0:T(8,128)(2,1)S(1)} %collective-permute-done.6.refs_1_, bf16[32,3584]{1,0:T(8,128)(2,1)} %collective-permute-done.7.refs_2_, ...), custom_call_target="tpu_custom_call" | custom-call | flops 11010048 | bytes 3670016 | tf_op jit(solution)/shard_map/pallas_call | solution.py:75
  143.7 7.5 %collective-permute-start.10 = (bf16[3584,128]{1,0:T(8,128)(2,1)S(1)}, bf16[3584,128]{1,0:T(8,128)(2,1)}, u32[]{:S(2)}, u32[]{:S(2)}) collective-permute-start(bf16[3584,128]{1,0:T(8,128)(2,1)S(1)} %convolution_convert_fusion.1), channel_id=1, source_target_pairs={{0,8},{8,0},{1,9},{9,1},{2,10},{10,2},{3,11},{11,3},{4,12},{12,4},... | collective-permute-start | bytes 2752520 | tf_op jit(solution)/shard_map/ppermute | solution.py:27
  151.3 2.1 %collective-permute-done.10 = bf16[3584,128]{1,0:T(8,128)(2,1)} collective-permute-done((bf16[3584,128]{1,0:T(8,128)(2,1)S(1)}, bf16[3584,128]{1,0:T(8,128)(2,1)}, u32[]{:S(2)}, u32[]{:S(2)}) %collective-permute-start.10) | collective-permute-done | bytes 917536 | tf_op jit(solution)/shard_map/ppermute | solution.py:27
  153.4 2.4 %fusion = bf16[3584,128]{1,0:T(8,128)(2,1)S(1)} fusion(bf16[256,3584]{1,0:T(8,128)(2,1)} %copy-done.1, bf16[3584,128]{1,0:T(8,128)(2,1)} %collective-permute-done.10, bf16[256,256]{1,0:T(8,128)(2,1)S(1)} %bitcast.91, s32[]{:T(128)S(6)} %select_n.100), kind=kOutput, calls=%fused_computation.2 | convolution fusion | flops 236257280 | bytes 3735556 | tf_op jit(solution)/shard_map/dot_general | solution.py:43
  156.8 9.8 %all-to-all-start.4 = ((bf16[32,120,128]{2,1,0:T(8,128)(2,1)}), bf16[32,120,128]{2,1,0:T(8,128)(2,1)S(1)}, u32[]{:S(2)}, u32[]{:S(2)}) async-start(bf16[32,120,128]{2,1,0:T(8,128)(2,1)} %pad_maximum_fusion), calls=%async_computation.4 | async-start | bytes 1966080 | tf_op jit(solution)/shard_map/all_to_all | solution.py:190
  166.6 2.3 %copy.28 = bf16[1024,448]{0,1:T(8,128)(2,1)} copy(bf16[1024,448]{1,0:T(8,128)(2,1)} %bitcast.17) | data formatting | bytes 1835008 | tf_op jit(solution)/shard_map/reshape | solution.py:193
  168.9 2.5 %collective-permute-start.12 = (bf16[1024,448]{0,1:T(8,128)(2,1)}, bf16[1024,448]{0,1:T(8,128)(2,1)}, u32[]{:S(2)}, u32[]{:S(2)}) collective-permute-start(bf16[1024,448]{0,1:T(8,128)(2,1)} %copy.28), channel_id=1, source_target_pairs={{0,8},{8,0},{1,9},{9,1},{2,10},{10,2},{3,11},{11,3},{4,12},{12,4},... | collective-permute-start | bytes 2752520 | tf_op jit(solution)/shard_map/ppermute | solution.py:27
  171.5 2.2 %convolution_convert_fusion.2 = bf16[256,256]{1,0:T(8,128)(2,1)S(1)} fusion(bf16[256,3584]{1,0:T(8,128)(2,1)} %copy-done.1, bf16[256,3584]{1,0:T(8,128)(2,1)S(1)} %copy-done), kind=kOutput, calls=%fused_computation.5 | convolution fusion | flops 469827584 | bytes 3801088 | tf_op jit(solution)/shard_map/dot_general | solution.py:43
  179.8 2.2 %fusion.1 = f32[32,448]{1,0:T(8,128)} fusion(f32[32,448]{1,0:T(8,128)S(1)} %fusion.39, bf16[1024,32]{0,1:T(8,128)(2,1)S(1)} %squeeze.24, bf16[1024,448]{1,0:T(8,128)(2,1)} %bitcast.17), kind=kOutput, calls=%fused_computation.7 | convolution fusion | flops 29388800 | bytes 1097728 | tf_op jit(solution)/shard_map/dot_general | solution.py:43
  182.0 9.5 %all-to-all-done.4 = bf16[32,120,128]{2,1,0:T(8,128)(2,1)S(1)} async-done(((bf16[32,120,128]{2,1,0:T(8,128)(2,1)}), bf16[32,120,128]{2,1,0:T(8,128)(2,1)S(1)}, u32[]{:S(2)}, u32[]{:S(2)}) %all-to-all-start.4) | async-done | bytes 983072 | tf_op jit(solution)/shard_map/all_to_all | solution.py:190
  191.7 5.9 %collective-permute-start.13 = (f32[56,128]{1,0:T(8,128)S(1)}, f32[56,128]{1,0:T(8,128)S(1)}, u32[]{:S(2)}, u32[]{:S(2)}) collective-permute-start(f32[56,128]{1,0:T(8,128)S(1)} %dynamic-slice_bitcast_fusion), channel_id=1, source_target_pairs={{0,8},{8,0},{1,9},{9,1},{2,10},{10,2},{3,11},{11,3},{4,12},{12,4},... | collective-permute-start | bytes 86024 | tf_op jit(solution)/shard_map/ppermute | solution.py:27
  (101 shorter events, 39.1 us)
Async XLA Ops:
  0.6 15.6 %copy-start = (bf16[256,3584]{1,0:T(8,128)(2,1)S(1)}, bf16[256,3584]{1,0:T(8,128)(2,1)}, u32[]{:S(2)}) copy-start(bf16[256,3584]{1,0:T(8,128)(2,1)} %param.14) | copy-start | bytes 5505028
  0.6 15.5 %copy-start.12 = (bf16[256,256]{1,0:T(8,128)(2,1)S(1)}, bf16[256,256]{1,0:T(8,128)(2,1)}, u32[]{:S(2)}) copy-start(bf16[256,256]{1,0:T(8,128)(2,1)} %param.12) | copy-start | bytes 393220
  2.7 39.3 %all-to-all-start = ((bf16[32,32,448]{2,1,0:T(8,128)(2,1)}), bf16[32,32,448]{2,1,0:T(8,128)(2,1)S(1)}, u32[]{:S(2)}, u32[]{:S(2)}) async-start(bf16[32,32,448]{2,1,0:T(8,128)(2,1)} %broadcast_in_dim.11), calls=%async_computation | async-start | bytes 2097152 | tf_op jit(solution)/shard_map/all_to_all | solution.py:39
  16.9 1.3 copy-start.4
  18.2 11.5 %copy-start.13 = (s32[32]{0:T(128)S(1)}, s32[32]{0:T(128)}, u32[]{:S(2)}) copy-start(s32[32]{0:T(128)} %param.11) | copy-start | bytes 388
  19.3 30.4 %collective-permute-start.1 = (bf16[64,3584]{1,0:T(8,128)(2,1)}, bf16[64,3584]{1,0:T(8,128)(2,1)S(1)}, u32[]{:S(2)}, u32[]{:S(2)}) collective-permute-start(bf16[64,3584]{1,0:T(8,128)(2,1)} %get-tuple-element.21), channel_id=1, source_target_pairs={{0,2},{2,0},{4,6},{6,4},{1,3},{3,1},{5,7},{7,5},{8,10},{10,8},{12,... | collective-permute-start | bytes 1376264 | tf_op jit(solution)/shard_map/ppermute | solution.py:124
  22.4 27.3 %collective-permute-start.2 = (bf16[64,3584]{1,0:T(8,128)(2,1)}, bf16[64,3584]{1,0:T(8,128)(2,1)}, u32[]{:S(2)}, u32[]{:S(2)}) collective-permute-start(bf16[64,3584]{1,0:T(8,128)(2,1)} %get-tuple-element.23), channel_id=1, source_target_pairs={{0,4},{2,6},{4,0},{6,2},{1,5},{3,7},{5,1},{7,3},{8,12},{10,14},{12... | collective-permute-start | bytes 1376264 | tf_op jit(solution)/shard_map/ppermute | solution.py:124
  26.8 23.8 %collective-permute-start.3 = (bf16[64,3584]{1,0:T(8,128)(2,1)}, bf16[64,3584]{1,0:T(8,128)(2,1)}, u32[]{:S(2)}, u32[]{:S(2)}) collective-permute-start(bf16[64,3584]{1,0:T(8,128)(2,1)} %get-tuple-element.22), channel_id=1, source_target_pairs={{0,6},{2,4},{4,2},{6,0},{1,7},{3,5},{5,3},{7,1},{8,14},{10,12},{12... | collective-permute-start | bytes 1376264 | tf_op jit(solution)/shard_map/ppermute | solution.py:124
  42.0 18.1 %copy-start.3 = (bf16[32,32,448]{2,1,0:T(8,128)(2,1)}, bf16[32,32,448]{2,1,0:T(8,128)(2,1)S(1)}, u32[]{:S(2)}) copy-start(bf16[32,32,448]{2,1,0:T(8,128)(2,1)S(1)} %all-to-all-done) | copy-start | bytes 2752516
  43.3 16.8 %copy-start.2 = (bf16[32,448]{1,0:T(8,128)(2,1)S(1)}, bf16[32,448]{1,0:T(8,128)(2,1)}, u32[]{:S(2)}) copy-start(bf16[32,448]{1,0:T(8,128)(2,1)} %item_ref.1) | copy-start | bytes 86020
  43.3 17.2 %collective-permute-start = (bf16[1024,448]{0,1:T(8,128)(2,1)}, bf16[1024,448]{0,1:T(8,128)(2,1)S(1)}, u32[]{:S(2)}, u32[]{:S(2)}) collective-permute-start(bf16[1024,448]{0,1:T(8,128)(2,1)} %copy.22), channel_id=1, source_target_pairs={{0,8},{8,0},{1,9},{9,1},{2,10},{10,2},{3,11},{11,3},{4,12},{12,4},... | collective-permute-start | bytes 2752520 | tf_op jit(solution)/shard_map/ppermute | solution.py:27
  52.1 10.4 %copy-start.7 = (f32[64,3584]{1,0:T(8,128)}, f32[64,3584]{1,0:T(8,128)S(1)}, u32[]{:S(2)}) copy-start(f32[64,3584]{1,0:T(8,128)S(1)} %add_add_fusion) | copy-start | bytes 2752516
  52.2 14.6 %collective-permute-start.4 = (bf16[32,3584]{1,0:T(8,128)(2,1)S(1)}, bf16[32,3584]{1,0:T(8,128)(2,1)S(1)}, u32[]{:S(2)}, u32[]{:S(2)}) collective-permute-start(bf16[32,3584]{1,0:T(8,128)(2,1)S(1)} %fusion.7), channel_id=1, source_target_pairs={{0,1},{1,0},{2,3},{3,2},{4,5},{5,4},{6,7},{7,6},{8,9},{9,8},{10,11... | collective-permute-start | bytes 688136 | tf_op jit(solution)/shard_map/ppermute | solution.py:130
  60.5 0.9 copy-start.5
  62.5 14.9 %all-to-all-start.1 = ((f32[8,32,256]{2,1,0:T(8,128)}), f32[8,32,256]{2,1,0:T(8,128)S(1)}, u32[]{:S(2)}, u32[]{:S(2)}) async-start(f32[8,32,256]{2,1,0:T(8,128)} %bitcast.77), calls=%async_computation.1 | async-start | bytes 524288 | tf_op jit(solution)/shard_map/all_to_all | solution.py:139
  68.0 17.1 %collective-permute-start.5 = (bf16[32,3584]{1,0:T(8,128)(2,1)S(1)}, bf16[32,3584]{1,0:T(8,128)(2,1)S(1)}, u32[]{:S(2)}, u32[]{:S(2)}) collective-permute-start(bf16[32,3584]{1,0:T(8,128)(2,1)S(1)} %fusion.3), channel_id=1, source_target_pairs={{0,1},{1,0},{2,3},{3,2},{4,5},{5,4},{6,7},{7,6},{8,9},{9,8},{10,11... | collective-permute-start | bytes 688136 | tf_op jit(solution)/shard_map/ppermute | solution.py:146
  78.1 17.8 %all-to-all-start.2 = ((f32[8,32,256]{2,1,0:T(8,128)}), f32[8,32,256]{2,1,0:T(8,128)}, u32[]{:S(2)}, u32[]{:S(2)}) async-start(f32[8,32,256]{2,1,0:T(8,128)} %broadcast_in_dim.13), calls=%async_computation.2 | async-start | bytes 524288 | tf_op jit(solution)/shard_map/all_to_all | solution.py:39
  85.3 41.0 %collective-permute-start.6 = (bf16[64,3584]{1,0:T(8,128)(2,1)S(1)}, bf16[64,3584]{1,0:T(8,128)(2,1)S(1)}, u32[]{:S(2)}, u32[]{:S(2)}) collective-permute-start(bf16[64,3584]{1,0:T(8,128)(2,1)S(1)} %bitcast.79), channel_id=1, source_target_pairs={{0,2},{2,0},{4,6},{6,4},{1,3},{3,1},{5,7},{7,5},{8,10},{10,8},{12,... | collective-permute-start | bytes 1376264 | tf_op jit(solution)/shard_map/ppermute | solution.py:149
  88.5 37.7 %collective-permute-start.8 = (bf16[64,3584]{1,0:T(8,128)(2,1)S(1)}, bf16[64,3584]{1,0:T(8,128)(2,1)S(1)}, u32[]{:S(2)}, u32[]{:S(2)}) collective-permute-start(bf16[64,3584]{1,0:T(8,128)(2,1)S(1)} %bitcast.80), channel_id=1, source_target_pairs={{0,6},{2,4},{4,2},{6,0},{1,7},{3,5},{5,3},{7,1},{8,14},{10,12},{12... | collective-permute-start | bytes 1376264 | tf_op jit(solution)/shard_map/ppermute | solution.py:150
  98.7 3.9 %copy-start.6 = (bf16[1024,448]{0,1:T(8,128)(2,1)S(1)}, bf16[1024,448]{0,1:T(8,128)(2,1)}, u32[]{:S(2)}) copy-start(bf16[1024,448]{0,1:T(8,128)(2,1)} %copy-done.5) | copy-start | bytes 2752516
  103.7 14.2 %all-to-all-start.3 = ((f32[8,8,448]{2,1,0:T(8,128)}), f32[8,8,448]{2,1,0:T(8,128)S(1)}, u32[]{:S(2)}, u32[]{:S(2)}) async-start(f32[8,8,448]{2,1,0:T(8,128)} %broadcast_in_dim.14), calls=%async_computation.3 | async-start | bytes 262144 | tf_op jit(solution)/shard_map/all_to_all | solution.py:39
  108.5 5.3 %collective-permute-start.11 = (bf16[40,1024]{1,0:T(8,128)(2,1)S(1)}, bf16[40,1024]{1,0:T(8,128)(2,1)S(1)}, u32[]{:S(2)}, u32[]{:S(2)}) collective-permute-start(bf16[40,1024]{1,0:T(8,128)(2,1)S(1)} %fusion.9), channel_id=1, source_target_pairs={{0,8},{8,0},{1,9},{9,1},{2,10},{10,2},{3,11},{11,3},{4,12},{12,4},... | collective-permute-start | bytes 245768 | tf_op jit(solution)/shard_map/ppermute | solution.py:27
  117.9 39.0 %all-to-all-start.5 = ((bf16[32,32,512]{2,1,0:T(8,128)(2,1)}), bf16[32,32,512]{2,1,0:T(8,128)(2,1)}, u32[]{:S(2)}, u32[]{:S(2)}) async-start(bf16[32,32,512]{2,1,0:T(8,128)(2,1)} %shard_map.111), calls=%async_computation.5 | async-start | bytes 2097152 | tf_op jit(solution)/shard_map/all_to_all | solution.py:178
  127.2 8.6 %collective-permute-start.7 = (bf16[32,3584]{1,0:T(8,128)(2,1)}, bf16[32,3584]{1,0:T(8,128)(2,1)}, u32[]{:S(2)}, u32[]{:S(2)}) collective-permute-start(bf16[32,3584]{1,0:T(8,128)(2,1)} %get-tuple-element.41), channel_id=1, source_target_pairs={{0,6},{2,4},{4,2},{6,0},{1,7},{3,5},{5,3},{7,1},{8,14},{10,12},{12... | collective-permute-start | bytes 688136 | tf_op jit(solution)/shard_map/ppermute | solution.py:167
  132.0 7.4 %collective-permute-start.9 = (bf16[32,3584]{1,0:T(8,128)(2,1)}, bf16[32,3584]{1,0:T(8,128)(2,1)}, u32[]{:S(2)}, u32[]{:S(2)}) collective-permute-start(bf16[32,3584]{1,0:T(8,128)(2,1)} %get-tuple-element.40), channel_id=1, source_target_pairs={{0,2},{2,0},{4,6},{6,4},{1,3},{3,1},{5,7},{7,5},{8,10},{10,8},{12,... | collective-permute-start | bytes 688136 | tf_op jit(solution)/shard_map/ppermute | solution.py:168
  139.4 3.6 %copy-start.9 = (bf16[4,64,256]{2,1,0:T(8,128)(2,1)S(1)}, bf16[4,64,256]{2,1,0:T(8,128)(2,1)}, u32[]{:S(2)}) copy-start(bf16[4,64,256]{2,1,0:T(8,128)(2,1)} %copy-done.8) | copy-start | bytes 393220
  141.7 1.3 copy-start.1
  143.0 10.4 %copy-start.10 = (bf16[4,64,256]{2,1,0:T(8,128)(2,1)S(1)}, bf16[4,64,256]{2,1,0:T(8,128)(2,1)}, u32[]{:S(2)}) copy-start(bf16[4,64,256]{2,1,0:T(8,128)(2,1)} %copy-done.8) | copy-start | bytes 393220
  143.7 9.7 %collective-permute-start.10 = (bf16[3584,128]{1,0:T(8,128)(2,1)S(1)}, bf16[3584,128]{1,0:T(8,128)(2,1)}, u32[]{:S(2)}, u32[]{:S(2)}) collective-permute-start(bf16[3584,128]{1,0:T(8,128)(2,1)S(1)} %convolution_convert_fusion.1), channel_id=1, source_target_pairs={{0,8},{8,0},{1,9},{9,1},{2,10},{10,2},{3,11},{11,3},{4,12},{12,4},... | collective-permute-start | bytes 2752520 | tf_op jit(solution)/shard_map/ppermute | solution.py:27
  156.8 34.7 %all-to-all-start.4 = ((bf16[32,120,128]{2,1,0:T(8,128)(2,1)}), bf16[32,120,128]{2,1,0:T(8,128)(2,1)S(1)}, u32[]{:S(2)}, u32[]{:S(2)}) async-start(bf16[32,120,128]{2,1,0:T(8,128)(2,1)} %pad_maximum_fusion), calls=%async_computation.4 | async-start | bytes 1966080 | tf_op jit(solution)/shard_map/all_to_all | solution.py:190
  168.9 9.4 %collective-permute-start.12 = (bf16[1024,448]{0,1:T(8,128)(2,1)}, bf16[1024,448]{0,1:T(8,128)(2,1)}, u32[]{:S(2)}, u32[]{:S(2)}) collective-permute-start(bf16[1024,448]{0,1:T(8,128)(2,1)} %copy.28), channel_id=1, source_target_pairs={{0,8},{8,0},{1,9},{9,1},{2,10},{10,2},{3,11},{11,3},{4,12},{12,4},... | collective-permute-start | bytes 2752520 | tf_op jit(solution)/shard_map/ppermute | solution.py:27
  191.7 7.1 %collective-permute-start.13 = (f32[56,128]{1,0:T(8,128)S(1)}, f32[56,128]{1,0:T(8,128)S(1)}, u32[]{:S(2)}, u32[]{:S(2)}) collective-permute-start(f32[56,128]{1,0:T(8,128)S(1)} %dynamic-slice_bitcast_fusion), channel_id=1, source_target_pairs={{0,8},{8,0},{1,9},{9,1},{2,10},{10,2},{3,11},{11,3},{4,12},{12,4},... | collective-permute-start | bytes 86024 | tf_op jit(solution)/shard_map/ppermute | solution.py:27
  (2 other events, 1.4 us)

commit v10 on v9

--- a/solution.py
+++ b/solution.py
@@ -25,14 +25,6 @@
 
 def swap(value):
     return lax.ppermute(value, **xor("c", 2, 1))
-
-
-def three_terms(value):
-    high = lax.reduce_precision(value, 8, 7)
-    rest = value - high
-    middle = lax.reduce_precision(rest, 8, 7)
-    low = lax.reduce_precision(rest - middle, 8, 7)
-    return high.astype(BF16), middle.astype(BF16), low.astype(BF16)
 
 
 def to_all(value, axes, count):
@@ -85,6 +77,48 @@
     )(x_index.reshape(1), group_rows, *blocks)
 
 
+def softmax_kernel(score_ref, column_ref, own_ref, give_ref):
+    rows, half = own_ref.shape
+    scores = jnp.concatenate([score_ref[t] for t in range(N_T)], axis=1)
+    lane = lax.broadcasted_iota(jnp.int32, scores.shape, 1)
+    target = column_ref[...] == lane
+    top = jnp.max(scores, axis=1, keepdims=True)
+    log_total = top + jnp.log(jnp.sum(jnp.exp(scores - top), axis=1, keepdims=True))
+    picked = jnp.sum(jnp.where(target, scores, F32(0.0)), axis=1, keepdims=True)
+    grad = (jnp.exp(scores - log_total) - target.astype(F32)).astype(BF16)
+    own_ref[...] = grad[:, :half]
+    give_ref[:rows, :] = grad[:, half:]
+    across = lax.broadcasted_iota(jnp.int32, (rows, half), 1)
+    down = lax.broadcasted_iota(jnp.int32, (rows, half), 0)
+    loss = jnp.where(across == down, log_total - picked, F32(0.0))
+    loss = jnp.sum(loss, axis=0, keepdims=True)
+    high = loss.astype(BF16).astype(F32)
+    middle = (loss - high).astype(BF16).astype(F32)
+    low = loss - high - middle
+    row = lax.broadcasted_iota(jnp.int32, (16, half), 0)
+    terms = jnp.where(row == 0, high, jnp.where(row == 1, middle, low))
+    give_ref[rows:, :] = jnp.where(row < 3, terms, F32(0.0)).astype(BF16)
+
+
+def softmax_gradient(scores, column):
+    rows = scores.shape[1]
+    half = N_T * scores.shape[2] // 2
+    whole = pl.BlockSpec(memory_space=pltpu.VMEM)
+    return pl.pallas_call(
+        softmax_kernel,
+        out_shape=(
+            jax.ShapeDtypeStruct((rows, half), BF16),
+            jax.ShapeDtypeStruct((rows + 16, half), BF16),
+        ),
+        in_specs=[whole] * 2,
+        out_specs=(whole, whole),
+        compiler_params=pltpu.CompilerParams(vmem_limit_bytes=12 * 2**20),
+        cost_estimate=pl.CostEstimate(
+            flops=16 * rows * half, bytes_accessed=12 * rows * half, transcendentals=4 * rows * half
+        ),
+    )(scores, column[:, None])
+
+
 def payload_kernel(item_ref, own_ref, other_ref, out_ref):
     rows, feats = item_ref.shape
     both = jnp.concatenate([own_ref[...].astype(F32), other_ref[:rows, :].astype(F32)], axis=0)
@@ -137,7 +171,7 @@
     share = 2 * half // N_T
     partial = partial.reshape(rows, N_T, share).transpose(1, 0, 2)
     scores_own = jnp.sum(lax.all_to_all(partial, TENSOR, 0, 0), axis=0) * LOGIT_SCALE
-    scores = to_all(scores_own, TENSOR, N_T).transpose(1, 0, 2).reshape(rows, 2 * half)
+    scores = to_all(scores_own, TENSOR, N_T)
 
     own_residual = lax.dynamic_slice_in_dim(residual, (2 * x_index + z_index) * rows, rows, 0)
     hidden_own = tie(from_z.astype(F32), partial[0, :, :1]) + own_residual.astype(F32)
@@ -151,14 +185,9 @@
 
     owner, row_in = positive // rows, positive % rows
     column = (owner % 2 != core).astype(jnp.int32) * half + (owner // 2) * rows + row_in
-    maxima = jnp.max(scores, axis=1, keepdims=True)
-    log_total = maxima[:, 0] + jnp.log(jnp.sum(jnp.exp(scores - maxima), axis=1))
-    target = column[:, None] == lax.broadcasted_iota(jnp.int32, (1, 2 * half), 1)
-    picked = jnp.sum(jnp.where(target, scores, F32(0.0)), axis=1)
-    losses = jnp.concatenate(three_terms(log_total - picked))
-    grad = (jnp.exp(scores - log_total[:, None]) - target.astype(F32)).astype(BF16)
+    grad_own, grad_give = softmax_gradient(scores, column)
     item_grad = (
-        dot(grad[:, :half], users[0], ((1,), (0,))) + dot(grad[:, half:], users[1], ((1,), (0,)))
+        dot(grad_own, users[0], ((1,), (0,))) + dot(grad_give[:rows], users[1], ((1,), (0,)))
     ) * LOGIT_SCALE
     t_index = 2 * x_index + z_index
     own_gain = lax.dynamic_slice_in_dim(norm_gain, t_index * feats, feats, 0) / SEQ
@@ -169,12 +198,10 @@
     ]
     hidden = (hidden_0, hidden_1, *hidden_2, hidden_3)
 
-    grad_losses = jnp.zeros((8, half), BF16).at[0, : 3 * rows].set(losses)
-    other = swap(jnp.concatenate([grad[:, half:], grad_losses], axis=0))
-    losses = jnp.concatenate([losses, other[rows, : 3 * rows]])
-    losses = jnp.pad(losses, (0, 2 * rows)).reshape(2, heads // 2)
-    losses = jnp.pad(losses, ((0, 6), (0, 0)))
-    by_plane = plane_payload(item_cache, grad[:, :half], other)
+    other = swap(grad_give)
+    losses = jnp.concatenate([part[rows : rows + 3, : heads // 2] for part in (grad_give, other)])
+    losses = jnp.pad(losses, ((0, 2), (0, 0)))
+    by_plane = plane_payload(item_cache, grad_own, other)
     by_plane = lax.all_to_all(by_plane, PLANE, 0, 0)
 
     stream = stream_gradient(x_index, group_rows, hidden)

time: 202 us -> 201 us (level)
  other arithmetic: 13.2 us -> 8.85 us
  matrix products: 12.2 us -> 14.7 us
    dot_general x10, matrix products: 12.2 us -> 14.7 us  [dot(): return lax.dot_general(a, b, (dims, ((), ())), preferred_element_type=F32)]
    unnamed x28 -> x30, local copies, waits for them, and re-layouts: 3.54 us -> 4.36 us
where the time goes in v10:
time: 201 us; the launch traced here: 199 us
  starting transfers between devices  110 us (55%)
  waiting for transfers between devices  39.1 us (19%)
  local copies, waits for them, and re-layouts  19.9 us (10%)
  matrix products  14.7 us (7%)
  other arithmetic  8.85 us (4%)
  Pallas kernels  3.89 us (2%)
  between operations  2.99 us (1%)
    ppermute x5, starting transfers between devices, swap(): return lax.ppermute(value, **xor('c', 2, 1))  24.7 us
    all_to_all x3, starting transfers between devices, to_all(): lax.all_to_all(jnp.broadcast_to(value[None], (count,) + value.shape), axe...  23.5 us
    all_to_all x3, waiting for transfers between devices, to_all(): lax.all_to_all(jnp.broadcast_to(value[None], (count,) + value.shape), axe...  17.1 us
    dot_general x10, matrix products, dot(): return lax.dot_general(a, b, (dims, ((), ())), preferred_element_type=F32)  14.7 us
    all_to_all x1, starting transfers between devices, per_device(): by_plane = lax.all_to_all(by_plane, PLANE, 0, 0)  9.8 us
    all_to_all x1, starting transfers between devices, per_device(): final = lax.all_to_all(final, PLANE, 0, 0)  9.78 us
    ppermute x3, starting transfers between devices, per_device(): lax.ppermute(mixed[k * x_block:(k + 1) * x_block], **xor('x', 4, k))  9.57 us
    all_to_all x1, waiting for transfers between devices, per_device(): final = lax.all_to_all(final, PLANE, 0, 0)  9.53 us
  transfers between devices with their start and end apart: 20, of which 11 were waited for; matrix products, arithmetic and copies ran while one was open for 18% of the time, Pallas kernels for 2%

profile of v10, /device:TPU:1, one launch (start us, length us, event | category | flops | bytes accessed | tf_op | source)
XLA Modules:
  0.0 199.0 jit_solution(4460924543871830952)
XLA Ops:
  0.7 2.0 %broadcast_in_dim.10 = bf16[32,32,448]{2,1,0:T(8,128)(2,1)} broadcast(bf16[32,448]{1,0:T(8,128)(2,1)} %param.8), dimensions={1,2} | broadcast | bytes 946176 | tf_op jit(solution)/shard_map/broadcast_in_dim | solution.py:31
  2.7 13.5 %all-to-all-start = ((bf16[32,32,448]{2,1,0:T(8,128)(2,1)}), bf16[32,32,448]{2,1,0:T(8,128)(2,1)S(1)}, u32[]{:S(2)}, u32[]{:S(2)}) async-start(bf16[32,32,448]{2,1,0:T(8,128)(2,1)} %broadcast_in_dim.10), calls=%async_computation | async-start | bytes 2097152 | tf_op jit(solution)/shard_map/all_to_all | solution.py:31
  18.1 2.5 %fusion.21 = (bf16[64,3584]{1,0:T(8,128)(2,1)}, bf16[64,3584]{1,0:T(8,128)(2,1)}, bf16[64,3584]{1,0:T(8,128)(2,1)}) fusion(bf16[256,3584]{1,0:T(8,128)(2,1)} %convolution_convert_fusion), kind=kLoop, calls=%fused_computation.73 | loop fusion | bytes 2752512 | tf_op jit(solution)/shard_map/slice | solution.py:158
  20.6 3.1 %collective-permute-start.1 = (bf16[64,3584]{1,0:T(8,128)(2,1)}, bf16[64,3584]{1,0:T(8,128)(2,1)S(1)}, u32[]{:S(2)}, u32[]{:S(2)}) collective-permute-start(bf16[64,3584]{1,0:T(8,128)(2,1)} %get-tuple-element.9), channel_id=1, source_target_pairs={{0,2},{2,0},{4,6},{6,4},{1,3},{3,1},{5,7},{7,5},{8,10},{10,8},{12,... | collective-permute-start | bytes 1376264 | tf_op jit(solution)/shard_map/ppermute | solution.py:158
  23.7 4.4 %collective-permute-start.2 = (bf16[64,3584]{1,0:T(8,128)(2,1)}, bf16[64,3584]{1,0:T(8,128)(2,1)}, u32[]{:S(2)}, u32[]{:S(2)}) collective-permute-start(bf16[64,3584]{1,0:T(8,128)(2,1)} %get-tuple-element.11), channel_id=1, source_target_pairs={{0,4},{2,6},{4,0},{6,2},{1,5},{3,7},{5,1},{7,3},{8,12},{10,14},{12... | collective-permute-start | bytes 1376264 | tf_op jit(solution)/shard_map/ppermute | solution.py:158
  28.1 2.1 %collective-permute-start.3 = (bf16[64,3584]{1,0:T(8,128)(2,1)}, bf16[64,3584]{1,0:T(8,128)(2,1)}, u32[]{:S(2)}, u32[]{:S(2)}) collective-permute-start(bf16[64,3584]{1,0:T(8,128)(2,1)} %get-tuple-element.10), channel_id=1, source_target_pairs={{0,6},{2,4},{4,2},{6,0},{1,7},{3,5},{5,3},{7,1},{8,14},{10,12},{12... | collective-permute-start | bytes 1376264 | tf_op jit(solution)/shard_map/ppermute | solution.py:158
  31.1 10.9 %all-to-all-done = bf16[32,32,448]{2,1,0:T(8,128)(2,1)S(1)} async-done(((bf16[32,32,448]{2,1,0:T(8,128)(2,1)}), bf16[32,32,448]{2,1,0:T(8,128)(2,1)S(1)}, u32[]{:S(2)}, u32[]{:S(2)}) %all-to-all-start) | async-done | bytes 917536 | tf_op jit(solution)/shard_map/all_to_all | solution.py:31
  43.3 6.3 %collective-permute-start = (bf16[1024,448]{0,1:T(8,128)(2,1)}, bf16[1024,448]{0,1:T(8,128)(2,1)S(1)}, u32[]{:S(2)}, u32[]{:S(2)}) collective-permute-start(bf16[1024,448]{0,1:T(8,128)(2,1)} %copy.24), channel_id=1, source_target_pairs={{0,8},{8,0},{1,9},{9,1},{2,10},{10,2},{3,11},{11,3},{4,12},{12,4},... | collective-permute-start | bytes 2752520 | tf_op jit(solution)/shard_map/ppermute | solution.py:27
  49.6 2.3 %collective-permute-done.3 = bf16[64,3584]{1,0:T(8,128)(2,1)} collective-permute-done((bf16[64,3584]{1,0:T(8,128)(2,1)}, bf16[64,3584]{1,0:T(8,128)(2,1)}, u32[]{:S(2)}, u32[]{:S(2)}) %collective-permute-start.3) | collective-permute-done | bytes 458784 | tf_op jit(solution)/shard_map/ppermute | solution.py:158
  53.5 7.9 %collective-permute-start.4 = (bf16[32,3584]{1,0:T(8,128)(2,1)S(1)}, bf16[32,3584]{1,0:T(8,128)(2,1)S(1)}, u32[]{:S(2)}, u32[]{:S(2)}) collective-permute-start(bf16[32,3584]{1,0:T(8,128)(2,1)S(1)} %fusion.4), channel_id=1, source_target_pairs={{0,1},{1,0},{2,3},{3,2},{4,5},{5,4},{6,7},{7,6},{8,9},{9,8},{10,11... | collective-permute-start | bytes 688136 | tf_op jit(solution)/shard_map/ppermute | solution.py:164
  63.8 3.4 %all-to-all-start.1 = ((f32[8,32,256]{2,1,0:T(8,128)}), f32[8,32,256]{2,1,0:T(8,128)S(1)}, u32[]{:S(2)}, u32[]{:S(2)}) async-start(f32[8,32,256]{2,1,0:T(8,128)} %bitcast.63), calls=%async_computation.1 | async-start | bytes 524288 | tf_op jit(solution)/shard_map/all_to_all | solution.py:173
  69.3 7.2 %collective-permute-start.5 = (bf16[32,3584]{1,0:T(8,128)(2,1)S(1)}, bf16[32,3584]{1,0:T(8,128)(2,1)S(1)}, u32[]{:S(2)}, u32[]{:S(2)}) collective-permute-start(bf16[32,3584]{1,0:T(8,128)(2,1)S(1)} %fusion.3), channel_id=1, source_target_pairs={{0,1},{1,0},{2,3},{3,2},{4,5},{5,4},{6,7},{7,6},{8,9},{9,8},{10,11... | collective-permute-start | bytes 688136 | tf_op jit(solution)/shard_map/ppermute | solution.py:180
  76.5 2.1 %all-to-all-done.1 = f32[8,32,256]{2,1,0:T(8,128)S(1)} async-done(((f32[8,32,256]{2,1,0:T(8,128)}), f32[8,32,256]{2,1,0:T(8,128)S(1)}, u32[]{:S(2)}, u32[]{:S(2)}) %all-to-all-start.1) | async-done | bytes 262176 | tf_op jit(solution)/shard_map/all_to_all | solution.py:173
  79.4 6.2 %all-to-all-start.2 = ((f32[8,32,256]{2,1,0:T(8,128)}), f32[8,32,256]{2,1,0:T(8,128)S(1)}, u32[]{:S(2)}, u32[]{:S(2)}) async-start(f32[8,32,256]{2,1,0:T(8,128)} %broadcast_in_dim.11), calls=%async_computation.2 | async-start | bytes 524288 | tf_op jit(solution)/shard_map/all_to_all | solution.py:31
  86.6 3.0 %collective-permute-start.6 = (bf16[64,3584]{1,0:T(8,128)(2,1)S(1)}, bf16[64,3584]{1,0:T(8,128)(2,1)S(1)}, u32[]{:S(2)}, u32[]{:S(2)}) collective-permute-start(bf16[64,3584]{1,0:T(8,128)(2,1)S(1)} %bitcast.65), channel_id=1, source_target_pairs={{0,2},{2,0},{4,6},{6,4},{1,3},{3,1},{5,7},{7,5},{8,10},{10,8},{12,... | collective-permute-start | bytes 1376264 | tf_op jit(solution)/shard_map/ppermute | solution.py:183
  89.7 3.9 %collective-permute-start.8 = (bf16[64,3584]{1,0:T(8,128)(2,1)S(1)}, bf16[64,3584]{1,0:T(8,128)(2,1)S(1)}, u32[]{:S(2)}, u32[]{:S(2)}) collective-permute-start(bf16[64,3584]{1,0:T(8,128)(2,1)S(1)} %bitcast.66), channel_id=1, source_target_pairs={{0,6},{2,4},{4,2},{6,0},{1,7},{3,5},{5,3},{7,1},{8,14},{10,12},{12... | collective-permute-start | bytes 1376264 | tf_op jit(solution)/shard_map/ppermute | solution.py:184
  93.5 4.8 %all-to-all-done.2.score_ref = f32[8,32,256]{2,1,0:T(8,128)S(1)} async-done(((f32[8,32,256]{2,1,0:T(8,128)}), f32[8,32,256]{2,1,0:T(8,128)S(1)}, u32[]{:S(2)}, u32[]{:S(2)}) %all-to-all-start.2) | async-done | bytes 262176 | tf_op jit(solution)/shard_map/all_to_all | solution.py:31
  103.1 3.9 %all-to-all-start.3 = ((f32[8,8,448]{2,1,0:T(8,128)}), f32[8,8,448]{2,1,0:T(8,128)S(1)}, u32[]{:S(2)}, u32[]{:S(2)}) async-start(f32[8,8,448]{2,1,0:T(8,128)} %broadcast_in_dim.13), calls=%async_computation.3 | async-start | bytes 262144 | tf_op jit(solution)/shard_map/all_to_all | solution.py:31
  107.0 4.1 %collective-permute-start.11 = (bf16[48,1024]{1,0:T(8,128)(2,1)}, bf16[48,1024]{1,0:T(8,128)(2,1)S(1)}, u32[]{:S(2)}, u32[]{:S(2)}) collective-permute-start(bf16[48,1024]{1,0:T(8,128)(2,1)} %copy-done.6), channel_id=1, source_target_pairs={{0,8},{8,0},{1,9},{9,1},{2,10},{10,2},{3,11},{11,3},{4,12},{12,4},... | collective-permute-start | bytes 294920 | tf_op jit(solution)/shard_map/ppermute | solution.py:27
  116.5 9.8 %all-to-all-start.5 = ((bf16[32,32,512]{2,1,0:T(8,128)(2,1)}), bf16[32,32,512]{2,1,0:T(8,128)(2,1)}, u32[]{:S(2)}, u32[]{:S(2)}) async-start(bf16[32,32,512]{2,1,0:T(8,128)(2,1)} %shard_map.112), calls=%async_computation.5 | async-start | bytes 2097152 | tf_op jit(solution)/shard_map/all_to_all | solution.py:205
  127.2 4.9 %collective-permute-start.7 = (bf16[32,3584]{1,0:T(8,128)(2,1)}, bf16[32,3584]{1,0:T(8,128)(2,1)}, u32[]{:S(2)}, u32[]{:S(2)}) collective-permute-start(bf16[32,3584]{1,0:T(8,128)(2,1)} %get-tuple-element.25), channel_id=1, source_target_pairs={{0,6},{2,4},{4,2},{6,0},{1,7},{3,5},{5,3},{7,1},{8,14},{10,12},{12... | collective-permute-start | bytes 688136 | tf_op jit(solution)/shard_map/ppermute | solution.py:196
  135.7 3.7 %collective-permute-done.9.refs_3_ = bf16[32,3584]{1,0:T(8,128)(2,1)} collective-permute-done((bf16[32,3584]{1,0:T(8,128)(2,1)}, bf16[32,3584]{1,0:T(8,128)(2,1)}, u32[]{:S(2)}, u32[]{:S(2)}) %collective-permute-start.9) | collective-permute-done | bytes 229408 | tf_op jit(solution)/shard_map/ppermute | solution.py:197
  139.4 2.3 %shard_map.111 = bf16[256,3584]{1,0:T(8,128)(2,1)S(1)} custom-call(s32[1]{0:T(128)} %bitcast.x_ref, f32[8,8,448]{2,1,0:T(8,128)S(1)} %all-to-all-done.3.group_ref, bf16[64,3584]{1,0:T(8,128)(2,1)S(1)} %bitcast.67, bf16[64,3584]{1,0:T(8,128)(2,1)S(1)} %collective-permute-done.6.refs_1_, bf16[32,3584]{1,0:T(8,128)(2,1)} %collective-permute-done.7.refs_2_, ...), custom_call_target="tpu_custom_call" | custom-call | flops 11010048 | bytes 3670016 | tf_op jit(solution)/shard_map/pallas_call | solution.py:67
  143.7 5.9 %collective-permute-start.10 = (bf16[3584,128]{1,0:T(8,128)(2,1)S(1)}, bf16[3584,128]{1,0:T(8,128)(2,1)}, u32[]{:S(2)}, u32[]{:S(2)}) collective-permute-start(bf16[3584,128]{1,0:T(8,128)(2,1)S(1)} %convolution_convert_fusion.1), channel_id=1, source_target_pairs={{0,8},{8,0},{1,9},{9,1},{2,10},{10,2},{3,11},{11,3},{4,12},{12,4},... | collective-permute-start | bytes 2752520 | tf_op jit(solution)/shard_map/ppermute | solution.py:27
  151.8 2.4 %fusion = bf16[3584,128]{1,0:T(8,128)(2,1)S(1)} fusion(bf16[256,3584]{1,0:T(8,128)(2,1)} %copy-done.1, bf16[3584,128]{1,0:T(8,128)(2,1)} %collective-permute-done.10, bf16[256,256]{1,0:T(8,128)(2,1)S(1)} %bitcast.77, s32[]{:T(128)S(6)} %select_n.95), kind=kOutput, calls=%fused_computation.2 | convolution fusion | flops 236257280 | bytes 3735556 | tf_op jit(solution)/shard_map/dot_general | solution.py:35
  155.3 9.8 %all-to-all-start.4 = ((bf16[32,120,128]{2,1,0:T(8,128)(2,1)}), bf16[32,120,128]{2,1,0:T(8,128)(2,1)S(1)}, u32[]{:S(2)}, u32[]{:S(2)}) async-start(bf16[32,120,128]{2,1,0:T(8,128)(2,1)} %pad_maximum_fusion), calls=%async_computation.4 | async-start | bytes 1966080 | tf_op jit(solution)/shard_map/all_to_all | solution.py:217
  165.0 2.2 %copy.30 = bf16[1024,448]{0,1:T(8,128)(2,1)} copy(bf16[1024,448]{1,0:T(8,128)(2,1)} %bitcast.14) | data formatting | bytes 1835008 | tf_op jit(solution)/shard_map/reshape | solution.py:220
  167.3 2.5 %collective-permute-start.12 = (bf16[1024,448]{0,1:T(8,128)(2,1)}, bf16[1024,448]{0,1:T(8,128)(2,1)}, u32[]{:S(2)}, u32[]{:S(2)}) collective-permute-start(bf16[1024,448]{0,1:T(8,128)(2,1)} %copy.30), channel_id=1, source_target_pairs={{0,8},{8,0},{1,9},{9,1},{2,10},{10,2},{3,11},{11,3},{4,12},{12,4},... | collective-permute-start | bytes 2752520 | tf_op jit(solution)/shard_map/ppermute | solution.py:27
  169.8 2.2 %convolution_convert_fusion.2 = bf16[256,256]{1,0:T(8,128)(2,1)S(1)} fusion(bf16[256,3584]{1,0:T(8,128)(2,1)} %copy-done.1, bf16[256,3584]{1,0:T(8,128)(2,1)S(1)} %copy-done), kind=kOutput, calls=%fused_computation.5 | convolution fusion | flops 469827584 | bytes 3801088 | tf_op jit(solution)/shard_map/dot_general | solution.py:35
  178.2 2.2 %fusion.1 = f32[32,448]{1,0:T(8,128)} fusion(f32[32,448]{1,0:T(8,128)S(1)} %fusion.26, bf16[1024,32]{0,1:T(8,128)(2,1)S(1)} %squeeze.20, bf16[1024,448]{1,0:T(8,128)(2,1)} %bitcast.14), kind=kOutput, calls=%fused_computation.7 | convolution fusion | flops 29388800 | bytes 1097728 | tf_op jit(solution)/shard_map/dot_general | solution.py:35
  180.4 9.5 %all-to-all-done.4 = bf16[32,120,128]{2,1,0:T(8,128)(2,1)S(1)} async-done(((bf16[32,120,128]{2,1,0:T(8,128)(2,1)}), bf16[32,120,128]{2,1,0:T(8,128)(2,1)S(1)}, u32[]{:S(2)}, u32[]{:S(2)}) %all-to-all-start.4) | async-done | bytes 983072 | tf_op jit(solution)/shard_map/all_to_all | solution.py:217
  190.1 5.8 %collective-permute-start.13 = (f32[56,128]{1,0:T(8,128)S(1)}, f32[56,128]{1,0:T(8,128)S(1)}, u32[]{:S(2)}, u32[]{:S(2)}) collective-permute-start(f32[56,128]{1,0:T(8,128)S(1)} %dynamic-slice_bitcast_fusion), channel_id=1, source_target_pairs={{0,8},{8,0},{1,9},{9,1},{2,10},{10,2},{3,11},{11,3},{4,12},{12,4},... | collective-permute-start | bytes 86024 | tf_op jit(solution)/shard_map/ppermute | solution.py:27
  (95 shorter events, 39.2 us)
Async XLA Ops:
  0.6 15.6 %copy-start = (bf16[256,3584]{1,0:T(8,128)(2,1)S(1)}, bf16[256,3584]{1,0:T(8,128)(2,1)}, u32[]{:S(2)}) copy-start(bf16[256,3584]{1,0:T(8,128)(2,1)} %param.12) | copy-start | bytes 5505028
  0.6 15.5 %copy-start.13 = (bf16[256,256]{1,0:T(8,128)(2,1)S(1)}, bf16[256,256]{1,0:T(8,128)(2,1)}, u32[]{:S(2)}) copy-start(bf16[256,256]{1,0:T(8,128)(2,1)} %param.10) | copy-start | bytes 393220
  2.7 39.3 %all-to-all-start = ((bf16[32,32,448]{2,1,0:T(8,128)(2,1)}), bf16[32,32,448]{2,1,0:T(8,128)(2,1)S(1)}, u32[]{:S(2)}, u32[]{:S(2)}) async-start(bf16[32,32,448]{2,1,0:T(8,128)(2,1)} %broadcast_in_dim.10), calls=%async_computation | async-start | bytes 2097152 | tf_op jit(solution)/shard_map/all_to_all | solution.py:31
  16.2 1.9 copy-start.10
  18.1 12.1 %copy-start.14 = (s32[32]{0:T(128)S(1)}, s32[32]{0:T(128)}, u32[]{:S(2)}) copy-start(s32[32]{0:T(128)} %param.9) | copy-start | bytes 388
  20.6 29.0 %collective-permute-start.1 = (bf16[64,3584]{1,0:T(8,128)(2,1)}, bf16[64,3584]{1,0:T(8,128)(2,1)S(1)}, u32[]{:S(2)}, u32[]{:S(2)}) collective-permute-start(bf16[64,3584]{1,0:T(8,128)(2,1)} %get-tuple-element.9), channel_id=1, source_target_pairs={{0,2},{2,0},{4,6},{6,4},{1,3},{3,1},{5,7},{7,5},{8,10},{10,8},{12,... | collective-permute-start | bytes 1376264 | tf_op jit(solution)/shard_map/ppermute | solution.py:158
  23.7 25.9 %collective-permute-start.2 = (bf16[64,3584]{1,0:T(8,128)(2,1)}, bf16[64,3584]{1,0:T(8,128)(2,1)}, u32[]{:S(2)}, u32[]{:S(2)}) collective-permute-start(bf16[64,3584]{1,0:T(8,128)(2,1)} %get-tuple-element.11), channel_id=1, source_target_pairs={{0,4},{2,6},{4,0},{6,2},{1,5},{3,7},{5,1},{7,3},{8,12},{10,14},{12... | collective-permute-start | bytes 1376264 | tf_op jit(solution)/shard_map/ppermute | solution.py:158
  28.1 23.8 %collective-permute-start.3 = (bf16[64,3584]{1,0:T(8,128)(2,1)}, bf16[64,3584]{1,0:T(8,128)(2,1)}, u32[]{:S(2)}, u32[]{:S(2)}) collective-permute-start(bf16[64,3584]{1,0:T(8,128)(2,1)} %get-tuple-element.10), channel_id=1, source_target_pairs={{0,6},{2,4},{4,2},{6,0},{1,7},{3,5},{5,3},{7,1},{8,14},{10,12},{12... | collective-permute-start | bytes 1376264 | tf_op jit(solution)/shard_map/ppermute | solution.py:158
  42.0 19.4 %copy-start.7 = (bf16[32,32,448]{2,1,0:T(8,128)(2,1)}, bf16[32,32,448]{2,1,0:T(8,128)(2,1)S(1)}, u32[]{:S(2)}) copy-start(bf16[32,32,448]{2,1,0:T(8,128)(2,1)S(1)} %all-to-all-done) | copy-start | bytes 2752516
  43.3 18.2 %copy-start.2 = (bf16[32,448]{1,0:T(8,128)(2,1)S(1)}, bf16[32,448]{1,0:T(8,128)(2,1)}, u32[]{:S(2)}) copy-start(bf16[32,448]{1,0:T(8,128)(2,1)} %item_ref.1) | copy-start | bytes 86020
  43.3 18.6 %collective-permute-start = (bf16[1024,448]{0,1:T(8,128)(2,1)}, bf16[1024,448]{0,1:T(8,128)(2,1)S(1)}, u32[]{:S(2)}, u32[]{:S(2)}) collective-permute-start(bf16[1024,448]{0,1:T(8,128)(2,1)} %copy.24), channel_id=1, source_target_pairs={{0,8},{8,0},{1,9},{9,1},{2,10},{10,2},{3,11},{11,3},{4,12},{12,4},... | collective-permute-start | bytes 2752520 | tf_op jit(solution)/shard_map/ppermute | solution.py:27
  53.4 10.4 %copy-start.9 = (f32[64,3584]{1,0:T(8,128)}, f32[64,3584]{1,0:T(8,128)S(1)}, u32[]{:S(2)}) copy-start(f32[64,3584]{1,0:T(8,128)S(1)} %add_add_fusion) | copy-start | bytes 2752516
  53.5 14.6 %collective-permute-start.4 = (bf16[32,3584]{1,0:T(8,128)(2,1)S(1)}, bf16[32,3584]{1,0:T(8,128)(2,1)S(1)}, u32[]{:S(2)}, u32[]{:S(2)}) collective-permute-start(bf16[32,3584]{1,0:T(8,128)(2,1)S(1)} %fusion.4), channel_id=1, source_target_pairs={{0,1},{1,0},{2,3},{3,2},{4,5},{5,4},{6,7},{7,6},{8,9},{9,8},{10,11... | collective-permute-start | bytes 688136 | tf_op jit(solution)/shard_map/ppermute | solution.py:164
  61.9 1.0 copy-start.8
  63.8 14.8 %all-to-all-start.1 = ((f32[8,32,256]{2,1,0:T(8,128)}), f32[8,32,256]{2,1,0:T(8,128)S(1)}, u32[]{:S(2)}, u32[]{:S(2)}) async-start(f32[8,32,256]{2,1,0:T(8,128)} %bitcast.63), calls=%async_computation.1 | async-start | bytes 524288 | tf_op jit(solution)/shard_map/all_to_all | solution.py:173
  69.3 17.1 %collective-permute-start.5 = (bf16[32,3584]{1,0:T(8,128)(2,1)S(1)}, bf16[32,3584]{1,0:T(8,128)(2,1)S(1)}, u32[]{:S(2)}, u32[]{:S(2)}) collective-permute-start(bf16[32,3584]{1,0:T(8,128)(2,1)S(1)} %fusion.3), channel_id=1, source_target_pairs={{0,1},{1,0},{2,3},{3,2},{4,5},{5,4},{6,7},{7,6},{8,9},{9,8},{10,11... | collective-permute-start | bytes 688136 | tf_op jit(solution)/shard_map/ppermute | solution.py:180
  79.4 19.0 %all-to-all-start.2 = ((f32[8,32,256]{2,1,0:T(8,128)}), f32[8,32,256]{2,1,0:T(8,128)S(1)}, u32[]{:S(2)}, u32[]{:S(2)}) async-start(f32[8,32,256]{2,1,0:T(8,128)} %broadcast_in_dim.11), calls=%async_computation.2 | async-start | bytes 524288 | tf_op jit(solution)/shard_map/all_to_all | solution.py:31
  86.6 39.6 %collective-permute-start.6 = (bf16[64,3584]{1,0:T(8,128)(2,1)S(1)}, bf16[64,3584]{1,0:T(8,128)(2,1)S(1)}, u32[]{:S(2)}, u32[]{:S(2)}) collective-permute-start(bf16[64,3584]{1,0:T(8,128)(2,1)S(1)} %bitcast.65), channel_id=1, source_target_pairs={{0,2},{2,0},{4,6},{6,4},{1,3},{3,1},{5,7},{7,5},{8,10},{10,8},{12,... | collective-permute-start | bytes 1376264 | tf_op jit(solution)/shard_map/ppermute | solution.py:183
  89.7 36.6 %collective-permute-start.8 = (bf16[64,3584]{1,0:T(8,128)(2,1)S(1)}, bf16[64,3584]{1,0:T(8,128)(2,1)S(1)}, u32[]{:S(2)}, u32[]{:S(2)}) collective-permute-start(bf16[64,3584]{1,0:T(8,128)(2,1)S(1)} %bitcast.66), channel_id=1, source_target_pairs={{0,6},{2,4},{4,2},{6,0},{1,7},{3,5},{5,3},{7,1},{8,14},{10,12},{12... | collective-permute-start | bytes 1376264 | tf_op jit(solution)/shard_map/ppermute | solution.py:184
  98.7 2.2 %copy-start.6 = (bf16[48,1024]{1,0:T(8,128)(2,1)}, bf16[48,1024]{1,0:T(8,128)(2,1)S(1)}, u32[]{:S(2)}) copy-start(bf16[48,1024]{1,0:T(8,128)(2,1)S(1)} %get-tuple-element.8) | copy-start | bytes 294916
  102.4 14.0 %copy-start.12 = (f32[32,448]{1,0:T(8,128)}, f32[32,448]{1,0:T(8,128)S(1)}, u32[]{:S(2)}) copy-start(f32[32,448]{1,0:T(8,128)S(1)} %fusion.2) | copy-start | bytes 172036
  103.1 13.4 %all-to-all-start.3 = ((f32[8,8,448]{2,1,0:T(8,128)}), f32[8,8,448]{2,1,0:T(8,128)S(1)}, u32[]{:S(2)}, u32[]{:S(2)}) async-start(f32[8,8,448]{2,1,0:T(8,128)} %broadcast_in_dim.13), calls=%async_computation.3 | async-start | bytes 262144 | tf_op jit(solution)/shard_map/all_to_all | solution.py:31
  107.0 5.3 %collective-permute-start.11 = (bf16[48,1024]{1,0:T(8,128)(2,1)}, bf16[48,1024]{1,0:T(8,128)(2,1)S(1)}, u32[]{:S(2)}, u32[]{:S(2)}) collective-permute-start(bf16[48,1024]{1,0:T(8,128)(2,1)} %copy-done.6), channel_id=1, source_target_pairs={{0,8},{8,0},{1,9},{9,1},{2,10},{10,2},{3,11},{11,3},{4,12},{12,4},... | collective-permute-start | bytes 294920 | tf_op jit(solution)/shard_map/ppermute | solution.py:27
  116.5 38.8 %all-to-all-start.5 = ((bf16[32,32,512]{2,1,0:T(8,128)(2,1)}), bf16[32,32,512]{2,1,0:T(8,128)(2,1)}, u32[]{:S(2)}, u32[]{:S(2)}) async-start(bf16[32,32,512]{2,1,0:T(8,128)(2,1)} %shard_map.112), calls=%async_computation.5 | async-start | bytes 2097152 | tf_op jit(solution)/shard_map/all_to_all | solution.py:205
  127.2 8.6 %collective-permute-start.7 = (bf16[32,3584]{1,0:T(8,128)(2,1)}, bf16[32,3584]{1,0:T(8,128)(2,1)}, u32[]{:S(2)}, u32[]{:S(2)}) collective-permute-start(bf16[32,3584]{1,0:T(8,128)(2,1)} %get-tuple-element.25), channel_id=1, source_target_pairs={{0,6},{2,4},{4,2},{6,0},{1,7},{3,5},{5,3},{7,1},{8,14},{10,12},{12... | collective-permute-start | bytes 688136 | tf_op jit(solution)/shard_map/ppermute | solution.py:196
  132.0 7.4 %collective-permute-start.9 = (bf16[32,3584]{1,0:T(8,128)(2,1)}, bf16[32,3584]{1,0:T(8,128)(2,1)}, u32[]{:S(2)}, u32[]{:S(2)}) collective-permute-start(bf16[32,3584]{1,0:T(8,128)(2,1)} %get-tuple-element.24), channel_id=1, source_target_pairs={{0,2},{2,0},{4,6},{6,4},{1,3},{3,1},{5,7},{7,5},{8,10},{10,8},{12,... | collective-permute-start | bytes 688136 | tf_op jit(solution)/shard_map/ppermute | solution.py:197
  139.4 3.6 %copy-start.11 = (bf16[4,64,256]{2,1,0:T(8,128)(2,1)S(1)}, bf16[4,64,256]{2,1,0:T(8,128)(2,1)}, u32[]{:S(2)}) copy-start(bf16[4,64,256]{2,1,0:T(8,128)(2,1)} %copy-done.10) | copy-start | bytes 393220
  141.7 1.3 copy-start.1
  143.7 8.1 %collective-permute-start.10 = (bf16[3584,128]{1,0:T(8,128)(2,1)S(1)}, bf16[3584,128]{1,0:T(8,128)(2,1)}, u32[]{:S(2)}, u32[]{:S(2)}) collective-permute-start(bf16[3584,128]{1,0:T(8,128)(2,1)S(1)} %convolution_convert_fusion.1), channel_id=1, source_target_pairs={{0,8},{8,0},{1,9},{9,1},{2,10},{10,2},{3,11},{11,3},{4,12},{12,4},... | collective-permute-start | bytes 2752520 | tf_op jit(solution)/shard_map/ppermute | solution.py:27
  155.3 34.7 %all-to-all-start.4 = ((bf16[32,120,128]{2,1,0:T(8,128)(2,1)}), bf16[32,120,128]{2,1,0:T(8,128)(2,1)S(1)}, u32[]{:S(2)}, u32[]{:S(2)}) async-start(bf16[32,120,128]{2,1,0:T(8,128)(2,1)} %pad_maximum_fusion), calls=%async_computation.4 | async-start | bytes 1966080 | tf_op jit(solution)/shard_map/all_to_all | solution.py:217
  167.3 9.4 %collective-permute-start.12 = (bf16[1024,448]{0,1:T(8,128)(2,1)}, bf16[1024,448]{0,1:T(8,128)(2,1)}, u32[]{:S(2)}, u32[]{:S(2)}) collective-permute-start(bf16[1024,448]{0,1:T(8,128)(2,1)} %copy.30), channel_id=1, source_target_pairs={{0,8},{8,0},{1,9},{9,1},{2,10},{10,2},{3,11},{11,3},{4,12},{12,4},... | collective-permute-start | bytes 2752520 | tf_op jit(solution)/shard_map/ppermute | solution.py:27
  190.1 7.1 %collective-permute-start.13 = (f32[56,128]{1,0:T(8,128)S(1)}, f32[56,128]{1,0:T(8,128)S(1)}, u32[]{:S(2)}, u32[]{:S(2)}) collective-permute-start(f32[56,128]{1,0:T(8,128)S(1)} %dynamic-slice_bitcast_fusion), channel_id=1, source_target_pairs={{0,8},{8,0},{1,9},{9,1},{2,10},{10,2},{3,11},{11,3},{4,12},{12,4},... | collective-permute-start | bytes 86024 | tf_op jit(solution)/shard_map/ppermute | solution.py:27
  (3 other events, 2.1 us)

commit v11 on v10

--- a/solution.py
+++ b/solution.py
@@ -77,7 +77,31 @@
     )(x_index.reshape(1), group_rows, *blocks)
 
 
-def softmax_kernel(score_ref, column_ref, own_ref, give_ref):
+def score_kernel(part_ref, out_ref):
+    total = part_ref[0]
+    for t in range(1, N_T):
+        total += part_ref[t]
+    for t in range(N_T):
+        out_ref[t] = total * LOGIT_SCALE
+
+
+def score_sum(parts):
+    whole = pl.BlockSpec(memory_space=pltpu.VMEM)
+    return pl.pallas_call(
+        score_kernel,
+        out_shape=jax.ShapeDtypeStruct(parts.shape, F32),
+        in_specs=[whole],
+        out_specs=whole,
+        compiler_params=pltpu.CompilerParams(vmem_limit_bytes=12 * 2**20),
+        cost_estimate=pl.CostEstimate(
+            flops=parts.size, bytes_accessed=8 * parts.size, transcendentals=0
+        ),
+    )(parts)
+
+
+def softmax_kernel(
+    score_ref, column_ref, gain_ref, near_ref, far_ref, own_ref, give_ref, item_ref, group_ref
+):
     rows, half = own_ref.shape
     scores = jnp.concatenate([score_ref[t] for t in range(N_T)], axis=1)
     lane = lax.broadcasted_iota(jnp.int32, scores.shape, 1)
@@ -88,6 +112,11 @@
     grad = (jnp.exp(scores - log_total) - target.astype(F32)).astype(BF16)
     own_ref[...] = grad[:, :half]
     give_ref[:rows, :] = grad[:, half:]
+    item = dot(grad[:, :half], near_ref[...], ((1,), (0,)))
+    item = (item + dot(grad[:, half:], far_ref[...], ((1,), (0,)))) * LOGIT_SCALE
+    item_ref[...] = item
+    for t in range(N_T):
+        group_ref[t] = gain_ref[...] * item[:GROUP, :]
     across = lax.broadcasted_iota(jnp.int32, (rows, half), 1)
     down = lax.broadcasted_iota(jnp.int32, (rows, half), 0)
     loss = jnp.where(across == down, log_total - picked, F32(0.0))
@@ -100,8 +129,8 @@
     give_ref[rows:, :] = jnp.where(row < 3, terms, F32(0.0)).astype(BF16)
 
 
-def softmax_gradient(scores, column):
-    rows = scores.shape[1]
+def softmax_gradient(scores, column, gain, users):
+    rows, feats = scores.shape[1], gain.shape[0]
     half = N_T * scores.shape[2] // 2
     whole = pl.BlockSpec(memory_space=pltpu.VMEM)
     return pl.pallas_call(
@@ -109,14 +138,16 @@
         out_shape=(
             jax.ShapeDtypeStruct((rows, half), BF16),
             jax.ShapeDtypeStruct((rows + 16, half), BF16),
-        ),
-        in_specs=[whole] * 2,
-        out_specs=(whole, whole),
-        compiler_params=pltpu.CompilerParams(vmem_limit_bytes=12 * 2**20),
+            jax.ShapeDtypeStruct((rows, feats), F32),
+            jax.ShapeDtypeStruct((N_T, GROUP, feats), F32),
+        ),
+        in_specs=[whole] * 5,
+        out_specs=(whole,) * 4,
+        compiler_params=pltpu.CompilerParams(vmem_limit_bytes=16 * 2**20),
         cost_estimate=pl.CostEstimate(
-            flops=16 * rows * half, bytes_accessed=12 * rows * half, transcendentals=4 * rows * half
-        ),
-    )(scores, column[:, None])
+            flops=4 * rows * half * feats, bytes_accessed=12 * rows * half, transcendentals=4 * rows * half
+        ),
+    )(scores, column[:, None], gain[None, :], *users)
 
 
 def payload_kernel(item_ref, own_ref, other_ref, out_ref):
@@ -170,14 +201,14 @@
     partial = jnp.concatenate(partial, axis=1)
     share = 2 * half // N_T
     partial = partial.reshape(rows, N_T, share).transpose(1, 0, 2)
-    scores_own = jnp.sum(lax.all_to_all(partial, TENSOR, 0, 0), axis=0) * LOGIT_SCALE
-    scores = to_all(scores_own, TENSOR, N_T)
+    scores_own = score_sum(lax.all_to_all(partial, TENSOR, 0, 0))
+    scores = lax.all_to_all(scores_own, TENSOR, 0, 0)
 
     own_residual = lax.dynamic_slice_in_dim(residual, (2 * x_index + z_index) * rows, rows, 0)
     hidden_own = tie(from_z.astype(F32), partial[0, :, :1]) + own_residual.astype(F32)
     hidden_own = (mixed_keep + hidden_own).astype(BF16)
 
-    hidden_z = tie(lax.ppermute(hidden_own, **xor("zh", 2, 1)), scores_own[:, :1])
+    hidden_z = tie(lax.ppermute(hidden_own, **xor("zh", 2, 1)), scores_own[0, :, :1])
     hidden_0 = jnp.stack([hidden_own, hidden_z])
     hidden_0 = jnp.where(z_index == 0, hidden_0, hidden_0[::-1]).reshape(x_block, width)
     hidden_1 = lax.ppermute(hidden_0, **xor("x", 4, 1))
@@ -185,13 +216,10 @@
 
     owner, row_in = positive // rows, positive % rows
     column = (owner % 2 != core).astype(jnp.int32) * half + (owner // 2) * rows + row_in
-    grad_own, grad_give = softmax_gradient(scores, column)
-    item_grad = (
-        dot(grad_own, users[0], ((1,), (0,))) + dot(grad_give[:rows], users[1], ((1,), (0,)))
-    ) * LOGIT_SCALE
     t_index = 2 * x_index + z_index
     own_gain = lax.dynamic_slice_in_dim(norm_gain, t_index * feats, feats, 0) / SEQ
-    group_rows = to_all(own_gain[None, :] * item_grad[:GROUP], TENSOR, N_T)
+    grad_own, grad_give, item_grad, group_rows = softmax_gradient(scores, column, own_gain, users)
+    group_rows = lax.all_to_all(group_rows, TENSOR, 0, 0)
     hidden_2 = [
         lax.ppermute(tie(hidden_1[:rows], item_grad[:, :1]), **xor("x", 4, 3)),
         lax.ppermute(tie(hidden_3[rows:], item_grad[:, :1]), **xor("x", 4, 1)),

time: 201 us -> 204 us (1.015)
  starting transfers between devices: 110 us -> 114 us
  waiting for transfers between devices: 39.1 us -> 35.1 us
  matrix products: 14.7 us -> 11.2 us
  other arithmetic: 8.85 us -> 12.3 us
  Pallas kernels: 3.89 us -> 6.75 us
    all_to_all x1 -> x3, starting transfers between devices: 3.41 us -> 13.9 us  [the longest x1 5.44 us: per_device(): group_rows = lax.all_to_all(group_rows, TENSOR, 0, 0)]
    all_to_all x3 -> x1, starting transfers between devices: 23.5 us -> 13.5 us  [to_all(): lax.all_to_all(jnp.broadcast_to(value[None], (count,) + value.shape), axe...]
    ppermute x5, starting transfers between devices: 24.7 us -> 29.1 us  [swap(): return lax.ppermute(value, **xor('c', 2, 1))]
    all_to_all x3 -> x1, waiting for transfers between devices: 17.1 us -> 13.3 us  [to_all(): lax.all_to_all(jnp.broadcast_to(value[None], (count,) + value.shape), axe...]
    ppermute x1, waiting for transfers between devices: 3.67 us -> 0.01 us  [per_device(): lax.ppermute(tie(hidden_3[rows:], item_grad[:, :1]), **xor('x', 4, 1))]
    dot_general x10 -> x8, matrix products: 14.7 us -> 11.2 us  [dot(): return lax.dot_general(a, b, (dims, ((), ())), preferred_element_type=F32)]
    ppermute x1, waiting for transfers between devices: 1.78 us -> 4.26 us  [per_device(): lax.ppermute(tie(hidden_1[:rows], item_grad[:, :1]), **xor('x', 4, 3))]
    ppermute x3, waiting for transfers between devices: 2.28 us -> 0.01 us  [per_device(): lax.ppermute(mixed[k * x_block:(k + 1) * x_block], **xor('x', 4, k))]
  transfers between devices with their start and end apart: 20 -> 20, of which waited for: 11 -> 9; matrix products, arithmetic and copies ran while one was open for 18% -> 17% of each run, Pallas kernels for 2% -> 3%
where the time goes in v11:
time: 204 us; the launch traced here: 202 us
  starting transfers between devices  114 us (56%)
  waiting for transfers between devices  35.1 us (17%)
  local copies, waits for them, and re-layouts  19.7 us (10%)
  other arithmetic  12.3 us (6%)
  matrix products  11.2 us (5%)
  Pallas kernels  6.75 us (3%)
  between operations  2.94 us (1%)
    ppermute x5, starting transfers between devices, swap(): return lax.ppermute(value, **xor('c', 2, 1))  29.1 us
    all_to_all x1, starting transfers between devices, to_all(): lax.all_to_all(jnp.broadcast_to(value[None], (count,) + value.shape), axe...  13.5 us
    all_to_all x1, waiting for transfers between devices, to_all(): lax.all_to_all(jnp.broadcast_to(value[None], (count,) + value.shape), axe...  13.3 us
    dot_general x8, matrix products, dot(): return lax.dot_general(a, b, (dims, ((), ())), preferred_element_type=F32)  11.2 us
    all_to_all x1, starting transfers between devices, per_device(): by_plane = lax.all_to_all(by_plane, PLANE, 0, 0)  10.2 us
    all_to_all x1, starting transfers between devices, per_device(): final = lax.all_to_all(final, PLANE, 0, 0)  9.78 us
    all_to_all x1, waiting for transfers between devices, per_device(): final = lax.all_to_all(final, PLANE, 0, 0)  9.52 us
    ppermute x3, starting transfers between devices, per_device(): lax.ppermute(mixed[k * x_block:(k + 1) * x_block], **xor('x', 4, k))  9.39 us
  transfers between devices with their start and end apart: 20, of which 9 were waited for; matrix products, arithmetic and copies ran while one was open for 17% of the time, Pallas kernels for 3%

profile of v11, /device:TPU:1, one launch (start us, length us, event | category | flops | bytes accessed | tf_op | source)
XLA Modules:
  0.0 201.7 jit_solution(7952750015407607999)
XLA Ops:
  0.7 2.0 broadcast_in_dim.8
  2.7 13.5 %all-to-all-start = ((bf16[32,32,448]{2,1,0:T(8,128)(2,1)}), bf16[32,32,448]{2,1,0:T(8,128)(2,1)S(1)}, u32[]{:S(2)}, u32[]{:S(2)}) async-start(bf16[32,32,448]{2,1,0:T(8,128)(2,1)} %broadcast_in_dim.8), calls=%async_computation | async-start | bytes 2097152 | tf_op jit(solution)/shard_map/all_to_all | solution.py:31
  19.3 3.1 %collective-permute-start.1 = (bf16[64,3584]{1,0:T(8,128)(2,1)}, bf16[64,3584]{1,0:T(8,128)(2,1)S(1)}, u32[]{:S(2)}, u32[]{:S(2)}) collective-permute-start(bf16[64,3584]{1,0:T(8,128)(2,1)} %get-tuple-element.13), channel_id=1, source_target_pairs={{0,2},{2,0},{4,6},{6,4},{1,3},{3,1},{5,7},{7,5},{8,10},{10,8},{12,... | collective-permute-start | bytes 1376264 | tf_op jit(solution)/shard_map/ppermute | solution.py:189
  22.4 3.7 %collective-permute-start.3 = (bf16[64,3584]{1,0:T(8,128)(2,1)}, bf16[64,3584]{1,0:T(8,128)(2,1)}, u32[]{:S(2)}, u32[]{:S(2)}) collective-permute-start(bf16[64,3584]{1,0:T(8,128)(2,1)} %get-tuple-element.14), channel_id=1, source_target_pairs={{0,6},{2,4},{4,2},{6,0},{1,7},{3,5},{5,3},{7,1},{8,14},{10,12},{12... | collective-permute-start | bytes 1376264 | tf_op jit(solution)/shard_map/ppermute | solution.py:189
  26.1 2.6 %collective-permute-start.2 = (bf16[64,3584]{1,0:T(8,128)(2,1)}, bf16[64,3584]{1,0:T(8,128)(2,1)}, u32[]{:S(2)}, u32[]{:S(2)}) collective-permute-start(bf16[64,3584]{1,0:T(8,128)(2,1)} %get-tuple-element.15), channel_id=1, source_target_pairs={{0,4},{2,6},{4,0},{6,2},{1,5},{3,7},{5,1},{7,3},{8,12},{10,14},{12... | collective-permute-start | bytes 1376264 | tf_op jit(solution)/shard_map/ppermute | solution.py:189
  28.7 13.3 %all-to-all-done = bf16[32,32,448]{2,1,0:T(8,128)(2,1)S(1)} async-done(((bf16[32,32,448]{2,1,0:T(8,128)(2,1)}), bf16[32,32,448]{2,1,0:T(8,128)(2,1)S(1)}, u32[]{:S(2)}, u32[]{:S(2)}) %all-to-all-start) | async-done | bytes 917536 | tf_op jit(solution)/shard_map/all_to_all | solution.py:31
  43.3 6.3 %collective-permute-start = (bf16[1024,448]{0,1:T(8,128)(2,1)}, bf16[1024,448]{0,1:T(8,128)(2,1)S(1)}, u32[]{:S(2)}, u32[]{:S(2)}) collective-permute-start(bf16[1024,448]{0,1:T(8,128)(2,1)} %copy.16), channel_id=1, source_target_pairs={{0,8},{8,0},{1,9},{9,1},{2,10},{10,2},{3,11},{11,3},{4,12},{12,4},... | collective-permute-start | bytes 2752520 | tf_op jit(solution)/shard_map/ppermute | solution.py:27
  51.3 7.9 %collective-permute-start.4 = (bf16[32,3584]{1,0:T(8,128)(2,1)S(1)}, bf16[32,3584]{1,0:T(8,128)(2,1)}, u32[]{:S(2)}, u32[]{:S(2)}) collective-permute-start(bf16[32,3584]{1,0:T(8,128)(2,1)S(1)} %fusion.3), channel_id=1, source_target_pairs={{0,1},{1,0},{2,3},{3,2},{4,5},{5,4},{6,7},{7,6},{8,9},{9,8},{10,11... | collective-permute-start | bytes 688136 | tf_op jit(solution)/shard_map/ppermute | solution.py:195
  61.6 4.0 %all-to-all-start.1 = ((f32[8,32,256]{2,1,0:T(8,128)}), f32[8,32,256]{2,1,0:T(8,128)S(1)}, u32[]{:S(2)}, u32[]{:S(2)}) async-start(f32[8,32,256]{2,1,0:T(8,128)} %bitcast.61), calls=%async_computation.1 | async-start | bytes 524288 | tf_op jit(solution)/shard_map/all_to_all | solution.py:204
  69.5 6.3 %collective-permute-start.5 = (bf16[32,3584]{1,0:T(8,128)(2,1)S(1)}, bf16[32,3584]{1,0:T(8,128)(2,1)}, u32[]{:S(2)}, u32[]{:S(2)}) collective-permute-start(bf16[32,3584]{1,0:T(8,128)(2,1)S(1)} %fusion.2), channel_id=1, source_target_pairs={{0,1},{1,0},{2,3},{3,2},{4,5},{5,4},{6,7},{7,6},{8,9},{9,8},{10,11... | collective-permute-start | bytes 688136 | tf_op jit(solution)/shard_map/ppermute | solution.py:211
  76.9 4.4 %all-to-all-start.2 = ((f32[8,32,256]{2,1,0:T(8,128)}), f32[8,32,256]{2,1,0:T(8,128)}, u32[]{:S(2)}, u32[]{:S(2)}) async-start(f32[8,32,256]{2,1,0:T(8,128)} %shard_map.110), calls=%async_computation.2 | async-start | bytes 524288 | tf_op jit(solution)/shard_map/all_to_all | solution.py:205
  82.1 3.0 %collective-permute-done.5 = bf16[32,3584]{1,0:T(8,128)(2,1)} collective-permute-done((bf16[32,3584]{1,0:T(8,128)(2,1)S(1)}, bf16[32,3584]{1,0:T(8,128)(2,1)}, u32[]{:S(2)}, u32[]{:S(2)}) %collective-permute-start.5) | collective-permute-done | bytes 229408 | tf_op jit(solution)/shard_map/ppermute | solution.py:211
  86.2 4.4 %collective-permute-start.8 = (bf16[64,3584]{1,0:T(8,128)(2,1)S(1)}, bf16[64,3584]{1,0:T(8,128)(2,1)}, u32[]{:S(2)}, u32[]{:S(2)}) collective-permute-start(bf16[64,3584]{1,0:T(8,128)(2,1)S(1)} %bitcast.66), channel_id=1, source_target_pairs={{0,6},{2,4},{4,2},{6,0},{1,7},{3,5},{5,3},{7,1},{8,14},{10,12},{12... | collective-permute-start | bytes 1376264 | tf_op jit(solution)/shard_map/ppermute | solution.py:215
  90.6 1.9 collective-permute-start.6
  93.5 2.3 %copy.19.far_ref = bf16[1024,448]{1,0:T(8,128)(2,1)} copy(bf16[1024,448]{0,1:T(8,128)(2,1)} %copy-done.6) | data formatting | bytes 1835008 | tf_op jit(solution)/shard_map/ppermute | solution.py:27
  96.9 2.3 %shard_map.111 = (bf16[32,1024]{1,0:T(8,128)(2,1)S(1)}, bf16[48,1024]{1,0:T(8,128)(2,1)S(1)}, f32[32,448]{1,0:T(8,128)}, f32[8,8,448]{2,1,0:T(8,128)}) custom-call(f32[8,32,256]{2,1,0:T(8,128)} %all-to-all-done.2.score_ref, s32[32,1]{1,0:T(8,128)S(1)} %copy.18.column_ref, f32[1,448]{1,0:T(1,128)S(1)} %bitcast.69, bf16[1024,448]{1,0:T(8,128)(2,1)S(1)} %bitcast.65, ...), custom_call_target="tpu_custom_call" | custom-call | flops 58720256 | bytes 393216 | tf_op jit(solution)/shard_map/pallas_call | solution.py:136
  99.9 5.4 %all-to-all-start.3 = ((f32[8,8,448]{2,1,0:T(8,128)}), f32[8,8,448]{2,1,0:T(8,128)S(1)}, u32[]{:S(2)}, u32[]{:S(2)}) async-start(f32[8,8,448]{2,1,0:T(8,128)} %get-tuple-element.9), calls=%async_computation.3 | async-start | bytes 262144 | tf_op jit(solution)/shard_map/all_to_all | solution.py:222
  105.3 6.1 %collective-permute-start.11 = (bf16[48,1024]{1,0:T(8,128)(2,1)}, bf16[48,1024]{1,0:T(8,128)(2,1)S(1)}, u32[]{:S(2)}, u32[]{:S(2)}) collective-permute-start(bf16[48,1024]{1,0:T(8,128)(2,1)} %copy-done.4), channel_id=1, source_target_pairs={{0,8},{8,0},{1,9},{9,1},{2,10},{10,2},{3,11},{11,3},{4,12},{12,4},... | collective-permute-start | bytes 294920 | tf_op jit(solution)/shard_map/ppermute | solution.py:27
  114.8 10.2 %all-to-all-start.5 = ((bf16[32,32,512]{2,1,0:T(8,128)(2,1)}), bf16[32,32,512]{2,1,0:T(8,128)(2,1)}, u32[]{:S(2)}, u32[]{:S(2)}) async-start(bf16[32,32,512]{2,1,0:T(8,128)(2,1)} %shard_map.113), calls=%async_computation.5 | async-start | bytes 2097152 | tf_op jit(solution)/shard_map/all_to_all | solution.py:233
  126.9 3.6 %collective-permute-start.9 = (bf16[32,3584]{1,0:T(8,128)(2,1)}, bf16[32,3584]{1,0:T(8,128)(2,1)S(1)}, u32[]{:S(2)}, u32[]{:S(2)}) collective-permute-start(bf16[32,3584]{1,0:T(8,128)(2,1)} %get-tuple-element.28), channel_id=1, source_target_pairs={{0,2},{2,0},{4,6},{6,4},{1,3},{3,1},{5,7},{7,5},{8,10},{10,8},{12,... | collective-permute-start | bytes 688136 | tf_op jit(solution)/shard_map/ppermute | solution.py:225
  130.6 3.7 %collective-permute-start.7 = (bf16[32,3584]{1,0:T(8,128)(2,1)S(1)}, bf16[32,3584]{1,0:T(8,128)(2,1)S(1)}, u32[]{:S(2)}, u32[]{:S(2)}) collective-permute-start(bf16[32,3584]{1,0:T(8,128)(2,1)S(1)} %get-tuple-element.29), channel_id=1, source_target_pairs={{0,6},{2,4},{4,2},{6,0},{1,7},{3,5},{5,3},{7,1},{8,14},{10,12},{12... | collective-permute-start | bytes 688136 | tf_op jit(solution)/shard_map/ppermute | solution.py:224
  134.3 4.3 %collective-permute-done.7.refs_2_ = bf16[32,3584]{1,0:T(8,128)(2,1)S(1)} collective-permute-done((bf16[32,3584]{1,0:T(8,128)(2,1)S(1)}, bf16[32,3584]{1,0:T(8,128)(2,1)S(1)}, u32[]{:S(2)}, u32[]{:S(2)}) %collective-permute-start.7) | collective-permute-done | bytes 229408 | tf_op jit(solution)/shard_map/ppermute | solution.py:224
  138.5 2.4 %shard_map.112 = bf16[256,3584]{1,0:T(8,128)(2,1)S(1)} custom-call(s32[1]{0:T(128)} %bitcast.x_ref, f32[8,8,448]{2,1,0:T(8,128)S(1)} %all-to-all-done.3.group_ref, bf16[64,3584]{1,0:T(8,128)(2,1)S(1)} %bitcast.68, bf16[64,3584]{1,0:T(8,128)(2,1)} %collective-permute-done.6.refs_1_, bf16[32,3584]{1,0:T(8,128)(2,1)S(1)} %collective-permute-done.7.refs_2_, ...), custom_call_target="tpu_custom_call" | custom-call | flops 11010048 | bytes 3670016 | tf_op jit(solution)/shard_map/pallas_call | solution.py:67
  143.9 8.2 %collective-permute-start.10 = (bf16[3584,128]{1,0:T(8,128)(2,1)}, bf16[3584,128]{1,0:T(8,128)(2,1)}, u32[]{:S(2)}, u32[]{:S(2)}) collective-permute-start(bf16[3584,128]{1,0:T(8,128)(2,1)} %convolution_convert_fusion.1), channel_id=1, source_target_pairs={{0,8},{8,0},{1,9},{9,1},{2,10},{10,2},{3,11},{11,3},{4,12},{12,4},... | collective-permute-start | bytes 2752520 | tf_op jit(solution)/shard_map/ppermute | solution.py:27
  154.5 2.4 %fusion = bf16[3584,128]{1,0:T(8,128)(2,1)S(1)} fusion(bf16[256,3584]{1,0:T(8,128)(2,1)} %copy-done.1, bf16[3584,128]{1,0:T(8,128)(2,1)} %collective-permute-done.10, bf16[256,256]{1,0:T(8,128)(2,1)S(1)} %bitcast.76, s32[]{:T(128)S(6)} %select_n.95), kind=kOutput, calls=%fused_computation.2 | convolution fusion | flops 236257280 | bytes 3735556 | tf_op jit(solution)/shard_map/dot_general | solution.py:35
  158.0 9.8 %all-to-all-start.4 = ((bf16[32,120,128]{2,1,0:T(8,128)(2,1)}), bf16[32,120,128]{2,1,0:T(8,128)(2,1)S(1)}, u32[]{:S(2)}, u32[]{:S(2)}) async-start(bf16[32,120,128]{2,1,0:T(8,128)(2,1)} %pad_maximum_fusion), calls=%async_computation.4 | async-start | bytes 1966080 | tf_op jit(solution)/shard_map/all_to_all | solution.py:245
  167.8 2.2 %copy.21 = bf16[1024,448]{0,1:T(8,128)(2,1)} copy(bf16[1024,448]{1,0:T(8,128)(2,1)} %bitcast.15) | data formatting | bytes 1835008 | tf_op jit(solution)/shard_map/reshape | solution.py:248
  170.0 2.5 %collective-permute-start.12 = (bf16[1024,448]{0,1:T(8,128)(2,1)}, bf16[1024,448]{0,1:T(8,128)(2,1)}, u32[]{:S(2)}, u32[]{:S(2)}) collective-permute-start(bf16[1024,448]{0,1:T(8,128)(2,1)} %copy.21), channel_id=1, source_target_pairs={{0,8},{8,0},{1,9},{9,1},{2,10},{10,2},{3,11},{11,3},{4,12},{12,4},... | collective-permute-start | bytes 2752520 | tf_op jit(solution)/shard_map/ppermute | solution.py:27
  172.6 2.2 %convolution_convert_fusion.2 = bf16[256,256]{1,0:T(8,128)(2,1)S(1)} fusion(bf16[256,3584]{1,0:T(8,128)(2,1)} %copy-done.1, bf16[256,3584]{1,0:T(8,128)(2,1)S(1)} %copy-done), kind=kOutput, calls=%fused_computation.5 | convolution fusion | flops 469827584 | bytes 3801088 | tf_op jit(solution)/shard_map/dot_general | solution.py:35
  180.9 2.2 %fusion.1 = f32[32,448]{1,0:T(8,128)} fusion(f32[32,448]{1,0:T(8,128)S(1)} %fusion.22, bf16[1024,32]{0,1:T(8,128)(2,1)S(1)} %squeeze.21, bf16[1024,448]{1,0:T(8,128)(2,1)} %bitcast.15), kind=kOutput, calls=%fused_computation.7 | convolution fusion | flops 29388800 | bytes 1097728 | tf_op jit(solution)/shard_map/dot_general | solution.py:35
  183.1 9.5 %all-to-all-done.4 = bf16[32,120,128]{2,1,0:T(8,128)(2,1)S(1)} async-done(((bf16[32,120,128]{2,1,0:T(8,128)(2,1)}), bf16[32,120,128]{2,1,0:T(8,128)(2,1)S(1)}, u32[]{:S(2)}, u32[]{:S(2)}) %all-to-all-start.4) | async-done | bytes 983072 | tf_op jit(solution)/shard_map/all_to_all | solution.py:245
  192.8 5.9 %collective-permute-start.13 = (f32[56,128]{1,0:T(8,128)S(1)}, f32[56,128]{1,0:T(8,128)S(1)}, u32[]{:S(2)}, u32[]{:S(2)}) collective-permute-start(f32[56,128]{1,0:T(8,128)S(1)} %dynamic-slice_bitcast_fusion), channel_id=1, source_target_pairs={{0,8},{8,0},{1,9},{9,1},{2,10},{10,2},{3,11},{11,3},{4,12},{12,4},... | collective-permute-start | bytes 86024 | tf_op jit(solution)/shard_map/ppermute | solution.py:27
  (84 shorter events, 37.1 us)
Async XLA Ops:
  0.6 15.6 %copy-start = (bf16[256,3584]{1,0:T(8,128)(2,1)S(1)}, bf16[256,3584]{1,0:T(8,128)(2,1)}, u32[]{:S(2)}) copy-start(bf16[256,3584]{1,0:T(8,128)(2,1)} %param.12) | copy-start | bytes 5505028
  0.6 15.5 %copy-start.10 = (bf16[256,256]{1,0:T(8,128)(2,1)S(1)}, bf16[256,256]{1,0:T(8,128)(2,1)}, u32[]{:S(2)}) copy-start(bf16[256,256]{1,0:T(8,128)(2,1)} %param.10) | copy-start | bytes 393220
  2.7 39.3 %all-to-all-start = ((bf16[32,32,448]{2,1,0:T(8,128)(2,1)}), bf16[32,32,448]{2,1,0:T(8,128)(2,1)S(1)}, u32[]{:S(2)}, u32[]{:S(2)}) async-start(bf16[32,32,448]{2,1,0:T(8,128)(2,1)} %broadcast_in_dim.8), calls=%async_computation | async-start | bytes 2097152 | tf_op jit(solution)/shard_map/all_to_all | solution.py:31
  16.2 0.7 copy-start.8
  16.9 1.3 copy-start.5
  19.3 30.4 %collective-permute-start.1 = (bf16[64,3584]{1,0:T(8,128)(2,1)}, bf16[64,3584]{1,0:T(8,128)(2,1)S(1)}, u32[]{:S(2)}, u32[]{:S(2)}) collective-permute-start(bf16[64,3584]{1,0:T(8,128)(2,1)} %get-tuple-element.13), channel_id=1, source_target_pairs={{0,2},{2,0},{4,6},{6,4},{1,3},{3,1},{5,7},{7,5},{8,10},{10,8},{12,... | collective-permute-start | bytes 1376264 | tf_op jit(solution)/shard_map/ppermute | solution.py:189
  22.4 27.3 %collective-permute-start.3 = (bf16[64,3584]{1,0:T(8,128)(2,1)}, bf16[64,3584]{1,0:T(8,128)(2,1)}, u32[]{:S(2)}, u32[]{:S(2)}) collective-permute-start(bf16[64,3584]{1,0:T(8,128)(2,1)} %get-tuple-element.14), channel_id=1, source_target_pairs={{0,6},{2,4},{4,2},{6,0},{1,7},{3,5},{5,3},{7,1},{8,14},{10,12},{12... | collective-permute-start | bytes 1376264 | tf_op jit(solution)/shard_map/ppermute | solution.py:189
  26.1 23.6 %collective-permute-start.2 = (bf16[64,3584]{1,0:T(8,128)(2,1)}, bf16[64,3584]{1,0:T(8,128)(2,1)}, u32[]{:S(2)}, u32[]{:S(2)}) collective-permute-start(bf16[64,3584]{1,0:T(8,128)(2,1)} %get-tuple-element.15), channel_id=1, source_target_pairs={{0,4},{2,6},{4,0},{6,2},{1,5},{3,7},{5,1},{7,3},{8,12},{10,14},{12... | collective-permute-start | bytes 1376264 | tf_op jit(solution)/shard_map/ppermute | solution.py:189
  43.3 15.9 %copy-start.3 = (bf16[32,448]{1,0:T(8,128)(2,1)S(1)}, bf16[32,448]{1,0:T(8,128)(2,1)}, u32[]{:S(2)}) copy-start(bf16[32,448]{1,0:T(8,128)(2,1)} %item_ref.1) | copy-start | bytes 86020
  43.3 16.3 %collective-permute-start = (bf16[1024,448]{0,1:T(8,128)(2,1)}, bf16[1024,448]{0,1:T(8,128)(2,1)S(1)}, u32[]{:S(2)}, u32[]{:S(2)}) collective-permute-start(bf16[1024,448]{0,1:T(8,128)(2,1)} %copy.16), channel_id=1, source_target_pairs={{0,8},{8,0},{1,9},{9,1},{2,10},{10,2},{3,11},{11,3},{4,12},{12,4},... | collective-permute-start | bytes 2752520 | tf_op jit(solution)/shard_map/ppermute | solution.py:27
  51.2 10.4 %copy-start.7 = (f32[64,3584]{1,0:T(8,128)}, f32[64,3584]{1,0:T(8,128)S(1)}, u32[]{:S(2)}) copy-start(f32[64,3584]{1,0:T(8,128)S(1)} %add_add_fusion) | copy-start | bytes 2752516
  51.3 16.9 %collective-permute-start.4 = (bf16[32,3584]{1,0:T(8,128)(2,1)S(1)}, bf16[32,3584]{1,0:T(8,128)(2,1)}, u32[]{:S(2)}, u32[]{:S(2)}) collective-permute-start(bf16[32,3584]{1,0:T(8,128)(2,1)S(1)} %fusion.3), channel_id=1, source_target_pairs={{0,1},{1,0},{2,3},{3,2},{4,5},{5,4},{6,7},{7,6},{8,9},{9,8},{10,11... | collective-permute-start | bytes 688136 | tf_op jit(solution)/shard_map/ppermute | solution.py:195
  59.6 0.9 copy-start.6
  61.6 14.5 %all-to-all-start.1 = ((f32[8,32,256]{2,1,0:T(8,128)}), f32[8,32,256]{2,1,0:T(8,128)S(1)}, u32[]{:S(2)}, u32[]{:S(2)}) async-start(f32[8,32,256]{2,1,0:T(8,128)} %bitcast.61), calls=%async_computation.1 | async-start | bytes 524288 | tf_op jit(solution)/shard_map/all_to_all | solution.py:204
  69.5 23.1 %copy-start.11 = (s32[32]{0:T(128)S(1)}, s32[32]{0:T(128)}, u32[]{:S(2)}) copy-start(s32[32]{0:T(128)} %param.9) | copy-start | bytes 388
  69.5 15.6 %collective-permute-start.5 = (bf16[32,3584]{1,0:T(8,128)(2,1)S(1)}, bf16[32,3584]{1,0:T(8,128)(2,1)}, u32[]{:S(2)}, u32[]{:S(2)}) collective-permute-start(bf16[32,3584]{1,0:T(8,128)(2,1)S(1)} %fusion.2), channel_id=1, source_target_pairs={{0,1},{1,0},{2,3},{3,2},{4,5},{5,4},{6,7},{7,6},{8,9},{9,8},{10,11... | collective-permute-start | bytes 688136 | tf_op jit(solution)/shard_map/ppermute | solution.py:211
  76.9 18.9 %all-to-all-start.2 = ((f32[8,32,256]{2,1,0:T(8,128)}), f32[8,32,256]{2,1,0:T(8,128)}, u32[]{:S(2)}, u32[]{:S(2)}) async-start(f32[8,32,256]{2,1,0:T(8,128)} %shard_map.110), calls=%async_computation.2 | async-start | bytes 524288 | tf_op jit(solution)/shard_map/all_to_all | solution.py:205
  86.2 38.8 %collective-permute-start.8 = (bf16[64,3584]{1,0:T(8,128)(2,1)S(1)}, bf16[64,3584]{1,0:T(8,128)(2,1)}, u32[]{:S(2)}, u32[]{:S(2)}) collective-permute-start(bf16[64,3584]{1,0:T(8,128)(2,1)S(1)} %bitcast.66), channel_id=1, source_target_pairs={{0,6},{2,4},{4,2},{6,0},{1,7},{3,5},{5,3},{7,1},{8,14},{10,12},{12... | collective-permute-start | bytes 1376264 | tf_op jit(solution)/shard_map/ppermute | solution.py:215
  90.6 34.4 %collective-permute-start.6 = (bf16[64,3584]{1,0:T(8,128)(2,1)S(1)}, bf16[64,3584]{1,0:T(8,128)(2,1)}, u32[]{:S(2)}, u32[]{:S(2)}) collective-permute-start(bf16[64,3584]{1,0:T(8,128)(2,1)S(1)} %bitcast.67), channel_id=1, source_target_pairs={{0,2},{2,0},{4,6},{6,4},{1,3},{3,1},{5,7},{7,5},{8,10},{10,8},{12,... | collective-permute-start | bytes 1376264 | tf_op jit(solution)/shard_map/ppermute | solution.py:214
  95.7 1.2 copy-start.2
  99.2 0.6 copy-start.4
  99.9 15.0 %all-to-all-start.3 = ((f32[8,8,448]{2,1,0:T(8,128)}), f32[8,8,448]{2,1,0:T(8,128)S(1)}, u32[]{:S(2)}, u32[]{:S(2)}) async-start(f32[8,8,448]{2,1,0:T(8,128)} %get-tuple-element.9), calls=%async_computation.3 | async-start | bytes 262144 | tf_op jit(solution)/shard_map/all_to_all | solution.py:222
  105.3 7.3 %collective-permute-start.11 = (bf16[48,1024]{1,0:T(8,128)(2,1)}, bf16[48,1024]{1,0:T(8,128)(2,1)S(1)}, u32[]{:S(2)}, u32[]{:S(2)}) collective-permute-start(bf16[48,1024]{1,0:T(8,128)(2,1)} %copy-done.4), channel_id=1, source_target_pairs={{0,8},{8,0},{1,9},{9,1},{2,10},{10,2},{3,11},{11,3},{4,12},{12,4},... | collective-permute-start | bytes 294920 | tf_op jit(solution)/shard_map/ppermute | solution.py:27
  114.8 43.2 %all-to-all-start.5 = ((bf16[32,32,512]{2,1,0:T(8,128)(2,1)}), bf16[32,32,512]{2,1,0:T(8,128)(2,1)}, u32[]{:S(2)}, u32[]{:S(2)}) async-start(bf16[32,32,512]{2,1,0:T(8,128)(2,1)} %shard_map.113), calls=%async_computation.5 | async-start | bytes 2097152 | tf_op jit(solution)/shard_map/all_to_all | solution.py:233
  126.9 7.4 %collective-permute-start.9 = (bf16[32,3584]{1,0:T(8,128)(2,1)}, bf16[32,3584]{1,0:T(8,128)(2,1)S(1)}, u32[]{:S(2)}, u32[]{:S(2)}) collective-permute-start(bf16[32,3584]{1,0:T(8,128)(2,1)} %get-tuple-element.28), channel_id=1, source_target_pairs={{0,2},{2,0},{4,6},{6,4},{1,3},{3,1},{5,7},{7,5},{8,10},{10,8},{12,... | collective-permute-start | bytes 688136 | tf_op jit(solution)/shard_map/ppermute | solution.py:225
  130.6 8.0 %collective-permute-start.7 = (bf16[32,3584]{1,0:T(8,128)(2,1)S(1)}, bf16[32,3584]{1,0:T(8,128)(2,1)S(1)}, u32[]{:S(2)}, u32[]{:S(2)}) collective-permute-start(bf16[32,3584]{1,0:T(8,128)(2,1)S(1)} %get-tuple-element.29), channel_id=1, source_target_pairs={{0,6},{2,4},{4,2},{6,0},{1,7},{3,5},{5,3},{7,1},{8,14},{10,12},{12... | collective-permute-start | bytes 688136 | tf_op jit(solution)/shard_map/ppermute | solution.py:224
  138.5 3.7 %copy-start.9 = (bf16[4,64,256]{2,1,0:T(8,128)(2,1)S(1)}, bf16[4,64,256]{2,1,0:T(8,128)(2,1)}, u32[]{:S(2)}) copy-start(bf16[4,64,256]{2,1,0:T(8,128)(2,1)} %copy-done.8) | copy-start | bytes 393220
  141.0 1.3 copy-start.1
  143.9 10.7 %collective-permute-start.10 = (bf16[3584,128]{1,0:T(8,128)(2,1)}, bf16[3584,128]{1,0:T(8,128)(2,1)}, u32[]{:S(2)}, u32[]{:S(2)}) collective-permute-start(bf16[3584,128]{1,0:T(8,128)(2,1)} %convolution_convert_fusion.1), channel_id=1, source_target_pairs={{0,8},{8,0},{1,9},{9,1},{2,10},{10,2},{3,11},{11,3},{4,12},{12,4},... | collective-permute-start | bytes 2752520 | tf_op jit(solution)/shard_map/ppermute | solution.py:27
  158.0 34.7 %all-to-all-start.4 = ((bf16[32,120,128]{2,1,0:T(8,128)(2,1)}), bf16[32,120,128]{2,1,0:T(8,128)(2,1)S(1)}, u32[]{:S(2)}, u32[]{:S(2)}) async-start(bf16[32,120,128]{2,1,0:T(8,128)(2,1)} %pad_maximum_fusion), calls=%async_computation.4 | async-start | bytes 1966080 | tf_op jit(solution)/shard_map/all_to_all | solution.py:245
  170.0 9.4 %collective-permute-start.12 = (bf16[1024,448]{0,1:T(8,128)(2,1)}, bf16[1024,448]{0,1:T(8,128)(2,1)}, u32[]{:S(2)}, u32[]{:S(2)}) collective-permute-start(bf16[1024,448]{0,1:T(8,128)(2,1)} %copy.21), channel_id=1, source_target_pairs={{0,8},{8,0},{1,9},{9,1},{2,10},{10,2},{3,11},{11,3},{4,12},{12,4},... | collective-permute-start | bytes 2752520 | tf_op jit(solution)/shard_map/ppermute | solution.py:27
  192.8 7.1 %collective-permute-start.13 = (f32[56,128]{1,0:T(8,128)S(1)}, f32[56,128]{1,0:T(8,128)S(1)}, u32[]{:S(2)}, u32[]{:S(2)}) collective-permute-start(f32[56,128]{1,0:T(8,128)S(1)} %dynamic-slice_bitcast_fusion), channel_id=1, source_target_pairs={{0,8},{8,0},{1,9},{9,1},{2,10},{10,2},{3,11},{11,3},{4,12},{12,4},... | collective-permute-start | bytes 86024 | tf_op jit(solution)/shard_map/ppermute | solution.py:27

commit v12 on v10

--- a/solution.py
+++ b/solution.py
@@ -45,13 +45,12 @@
 
 
 def stream_kernel(x_ref, group_ref, *refs):
-    first, second, third_0, third_1, fourth, out_ref, up_ref = refs
-    halves = (first, first, second, second, third_0, third_1, fourth, fourth)
+    blocks, out_ref, up_ref = refs[:4], refs[4], refs[5]
     width = out_ref.shape[1]
     up_ref[...] = jnp.concatenate([group_ref[t] for t in range(N_T)], axis=1)
     for item in range(GROUP):
-        start = 0 if halves[item].shape[0] == SEQ else item % 2 * SEQ
-        tokens = halves[item][start : start + SEQ, :].astype(F32)
+        start = item % 2 * SEQ
+        tokens = blocks[item // 2][start : start + SEQ, :].astype(F32)
         which = (x_ref[0] ^ (item // 2)) * 2 + item % 2
         up = up_ref[pl.ds(which, 1), :]
         mean = jnp.sum(tokens * tokens, axis=1, keepdims=True) / width
@@ -67,7 +66,7 @@
     return pl.pallas_call(
         stream_kernel,
         out_shape=jax.ShapeDtypeStruct((tokens, width), BF16),
-        in_specs=[pl.BlockSpec(memory_space=pltpu.SMEM)] + [whole] * 6,
+        in_specs=[pl.BlockSpec(memory_space=pltpu.SMEM)] + [whole] * 5,
         out_specs=whole,
         scratch_shapes=[pltpu.VMEM((GROUP, width), F32)],
         compiler_params=pltpu.CompilerParams(vmem_limit_bytes=24 * 2**20),
@@ -192,16 +191,14 @@
     t_index = 2 * x_index + z_index
     own_gain = lax.dynamic_slice_in_dim(norm_gain, t_index * feats, feats, 0) / SEQ
     group_rows = to_all(own_gain[None, :] * item_grad[:GROUP], TENSOR, N_T)
-    hidden_2 = [
-        lax.ppermute(tie(hidden_1[:rows], item_grad[:, :1]), **xor("x", 4, 3)),
-        lax.ppermute(tie(hidden_3[rows:], item_grad[:, :1]), **xor("x", 4, 1)),
-    ]
-    hidden = (hidden_0, hidden_1, *hidden_2, hidden_3)
+    hidden_2 = lax.ppermute(hidden_0, **xor("x", 4, 2))
+    hidden = (hidden_0, hidden_1, hidden_2, hidden_3)
 
     other = swap(grad_give)
     losses = jnp.concatenate([part[rows : rows + 3, : heads // 2] for part in (grad_give, other)])
     losses = jnp.pad(losses, ((0, 2), (0, 0)))
-    by_plane = plane_payload(item_cache, grad_own, other)
+    near = hidden_1[:rows, :1] + hidden_3[:rows, :1]
+    by_plane = plane_payload(tie(item_cache, near), grad_own, other)
     by_plane = lax.all_to_all(by_plane, PLANE, 0, 0)
 
     stream = stream_gradient(x_index, group_rows, hidden)

time: 201 us -> 213 us (1.060)
  waiting for transfers between devices: 39.1 us -> 49.4 us
  other arithmetic: 8.85 us -> 11.2 us
    all_to_all x1, waiting for transfers between devices: 0.01 us -> 11.6 us  [per_device(): by_plane = lax.all_to_all(by_plane, PLANE, 0, 0)]
    ppermute x2 -> x1, waiting for transfers between devices: 5.44 us -> 0.01 us  [per_device(): hidden_2 = lax.ppermute(hidden_0, **xor('x', 4, 2))]
    all_to_all x1, starting transfers between devices: 9.8 us -> 13 us  [per_device(): by_plane = lax.all_to_all(by_plane, PLANE, 0, 0)]
    all_to_all x1, waiting for transfers between devices: 9.53 us -> 12.3 us  [per_device(): final = lax.all_to_all(final, PLANE, 0, 0)]
    all_to_all x3, starting transfers between devices: 23.5 us -> 26 us  [to_all(): lax.all_to_all(jnp.broadcast_to(value[None], (count,) + value.shape), axe...]
    ppermute x2 -> x1, starting transfers between devices: 6.77 us -> 4.4 us  [per_device(): hidden_2 = lax.ppermute(hidden_0, **xor('x', 4, 2))]
    ppermute x1, waiting for transfers between devices: 0.01 us -> 2.18 us  [per_device(): hidden_3 = lax.ppermute(hidden_0, **xor('x', 4, 3))]
    unnamed x30 -> x24, local copies, waits for them, and re-layouts: 4.36 us -> 2.24 us
  transfers between devices with their start and end apart: 20 -> 19, of which waited for: 11 -> 10; matrix products, arithmetic and copies ran while one was open for 18% -> 18% of each run, Pallas kernels for 2% -> 2%
where the time goes in v12:
time: 213 us; the launch traced here: 211 us
  starting transfers between devices  110 us (52%)
  waiting for transfers between devices  49.4 us (23%)
  local copies, waits for them, and re-layouts  17.9 us (8%)
  matrix products  14.7 us (7%)
  other arithmetic  11.2 us (5%)
  Pallas kernels  4.5 us (2%)
  between operations  2.91 us (1%)
    all_to_all x3, starting transfers between devices, to_all(): lax.all_to_all(jnp.broadcast_to(value[None], (count,) + value.shape), axe...  26 us
    ppermute x5, starting transfers between devices, swap(): return lax.ppermute(value, **xor('c', 2, 1))  25.2 us
    all_to_all x3, waiting for transfers between devices, to_all(): lax.all_to_all(jnp.broadcast_to(value[None], (count,) + value.shape), axe...  16.7 us
    dot_general x10, matrix products, dot(): return lax.dot_general(a, b, (dims, ((), ())), preferred_element_type=F32)  14.7 us
    all_to_all x1, starting transfers between devices, per_device(): by_plane = lax.all_to_all(by_plane, PLANE, 0, 0)  13 us
    all_to_all x1, waiting for transfers between devices, per_device(): final = lax.all_to_all(final, PLANE, 0, 0)  12.3 us
    all_to_all x1, waiting for transfers between devices, per_device(): by_plane = lax.all_to_all(by_plane, PLANE, 0, 0)  11.6 us
    ppermute x3, starting transfers between devices, per_device(): lax.ppermute(mixed[k * x_block:(k + 1) * x_block], **xor('x', 4, k))  9.57 us
  transfers between devices with their start and end apart: 19, of which 10 were waited for; matrix products, arithmetic and copies ran while one was open for 18% of the time, Pallas kernels for 2%

profile of v12, /device:TPU:1, one launch (start us, length us, event | category | flops | bytes accessed | tf_op | source)
XLA Modules:
  0.0 210.7 jit_solution(6726247274095247895)
XLA Ops:
  2.7 13.5 %all-to-all-start = ((bf16[32,32,448]{2,1,0:T(8,128)(2,1)}), bf16[32,32,448]{2,1,0:T(8,128)(2,1)S(1)}, u32[]{:S(2)}, u32[]{:S(2)}) async-start(bf16[32,32,448]{2,1,0:T(8,128)(2,1)} %broadcast_in_dim.10), calls=%async_computation | async-start | bytes 2097152 | tf_op jit(solution)/shard_map/all_to_all | solution.py:31
  18.2 2.4 %fusion.21 = (bf16[64,3584]{1,0:T(8,128)(2,1)}, bf16[64,3584]{1,0:T(8,128)(2,1)}, bf16[64,3584]{1,0:T(8,128)(2,1)}) fusion(bf16[256,3584]{1,0:T(8,128)(2,1)} %convolution_convert_fusion), kind=kLoop, calls=%fused_computation.72 | loop fusion | bytes 2752512 | tf_op jit(solution)/shard_map/slice | solution.py:157
  20.6 3.1 %collective-permute-start.1 = (bf16[64,3584]{1,0:T(8,128)(2,1)}, bf16[64,3584]{1,0:T(8,128)(2,1)S(1)}, u32[]{:S(2)}, u32[]{:S(2)}) collective-permute-start(bf16[64,3584]{1,0:T(8,128)(2,1)} %get-tuple-element.9), channel_id=1, source_target_pairs={{0,2},{2,0},{4,6},{6,4},{1,3},{3,1},{5,7},{7,5},{8,10},{10,8},{12,... | collective-permute-start | bytes 1376264 | tf_op jit(solution)/shard_map/ppermute | solution.py:157
  23.7 4.4 %collective-permute-start.2 = (bf16[64,3584]{1,0:T(8,128)(2,1)}, bf16[64,3584]{1,0:T(8,128)(2,1)}, u32[]{:S(2)}, u32[]{:S(2)}) collective-permute-start(bf16[64,3584]{1,0:T(8,128)(2,1)} %get-tuple-element.11), channel_id=1, source_target_pairs={{0,4},{2,6},{4,0},{6,2},{1,5},{3,7},{5,1},{7,3},{8,12},{10,14},{12... | collective-permute-start | bytes 1376264 | tf_op jit(solution)/shard_map/ppermute | solution.py:157
  28.1 2.1 collective-permute-start.3
  31.7 10.3 %all-to-all-done = bf16[32,32,448]{2,1,0:T(8,128)(2,1)S(1)} async-done(((bf16[32,32,448]{2,1,0:T(8,128)(2,1)}), bf16[32,32,448]{2,1,0:T(8,128)(2,1)S(1)}, u32[]{:S(2)}, u32[]{:S(2)}) %all-to-all-start) | async-done | bytes 917536 | tf_op jit(solution)/shard_map/all_to_all | solution.py:31
  43.3 6.3 %collective-permute-start = (bf16[1024,448]{0,1:T(8,128)(2,1)}, bf16[1024,448]{0,1:T(8,128)(2,1)S(1)}, u32[]{:S(2)}, u32[]{:S(2)}) collective-permute-start(bf16[1024,448]{0,1:T(8,128)(2,1)} %copy.36), channel_id=1, source_target_pairs={{0,8},{8,0},{1,9},{9,1},{2,10},{10,2},{3,11},{11,3},{4,12},{12,4},... | collective-permute-start | bytes 2752520 | tf_op jit(solution)/shard_map/ppermute | solution.py:27
  49.7 2.2 %collective-permute-done.3 = bf16[64,3584]{1,0:T(8,128)(2,1)} collective-permute-done((bf16[64,3584]{1,0:T(8,128)(2,1)}, bf16[64,3584]{1,0:T(8,128)(2,1)}, u32[]{:S(2)}, u32[]{:S(2)}) %collective-permute-start.3) | collective-permute-done | bytes 458784 | tf_op jit(solution)/shard_map/ppermute | solution.py:157
  54.2 7.9 %collective-permute-start.4 = (bf16[32,3584]{1,0:T(8,128)(2,1)}, bf16[32,3584]{1,0:T(8,128)(2,1)}, u32[]{:S(2)}, u32[]{:S(2)}) collective-permute-start(bf16[32,3584]{1,0:T(8,128)(2,1)} %fusion.4), channel_id=1, source_target_pairs={{0,1},{1,0},{2,3},{3,2},{4,5},{5,4},{6,7},{7,6},{8,9},{9,8},{10,11... | collective-permute-start | bytes 688136 | tf_op jit(solution)/shard_map/ppermute | solution.py:163
  64.6 3.4 %all-to-all-start.1 = ((f32[8,32,256]{2,1,0:T(8,128)}), f32[8,32,256]{2,1,0:T(8,128)S(1)}, u32[]{:S(2)}, u32[]{:S(2)}) async-start(f32[8,32,256]{2,1,0:T(8,128)} %bitcast.63), calls=%async_computation.1 | async-start | bytes 524288 | tf_op jit(solution)/shard_map/all_to_all | solution.py:172
  70.2 7.2 %collective-permute-start.5 = (bf16[32,3584]{1,0:T(8,128)(2,1)S(1)}, bf16[32,3584]{1,0:T(8,128)(2,1)}, u32[]{:S(2)}, u32[]{:S(2)}) collective-permute-start(bf16[32,3584]{1,0:T(8,128)(2,1)S(1)} %fusion.3), channel_id=1, source_target_pairs={{0,1},{1,0},{2,3},{3,2},{4,5},{5,4},{6,7},{7,6},{8,9},{9,8},{10,11... | collective-permute-start | bytes 688136 | tf_op jit(solution)/shard_map/ppermute | solution.py:179
  77.4 2.1 %all-to-all-done.1 = f32[8,32,256]{2,1,0:T(8,128)S(1)} async-done(((f32[8,32,256]{2,1,0:T(8,128)}), f32[8,32,256]{2,1,0:T(8,128)S(1)}, u32[]{:S(2)}, u32[]{:S(2)}) %all-to-all-start.1) | async-done | bytes 262176 | tf_op jit(solution)/shard_map/all_to_all | solution.py:172
  80.3 6.2 %all-to-all-start.2 = ((f32[8,32,256]{2,1,0:T(8,128)}), f32[8,32,256]{2,1,0:T(8,128)S(1)}, u32[]{:S(2)}, u32[]{:S(2)}) async-start(f32[8,32,256]{2,1,0:T(8,128)} %broadcast_in_dim.11), calls=%async_computation.2 | async-start | bytes 524288 | tf_op jit(solution)/shard_map/all_to_all | solution.py:31
  88.6 3.0 %collective-permute-start.6 = (bf16[64,3584]{1,0:T(8,128)(2,1)S(1)}, bf16[64,3584]{1,0:T(8,128)(2,1)S(1)}, u32[]{:S(2)}, u32[]{:S(2)}) collective-permute-start(bf16[64,3584]{1,0:T(8,128)(2,1)S(1)} %bitcast.65), channel_id=1, source_target_pairs={{0,2},{2,0},{4,6},{6,4},{1,3},{3,1},{5,7},{7,5},{8,10},{10,8},{12,... | collective-permute-start | bytes 1376264 | tf_op jit(solution)/shard_map/ppermute | solution.py:182
  91.6 4.4 %collective-permute-start.7 = (bf16[64,3584]{1,0:T(8,128)(2,1)S(1)}, bf16[64,3584]{1,0:T(8,128)(2,1)}, u32[]{:S(2)}, u32[]{:S(2)}) collective-permute-start(bf16[64,3584]{1,0:T(8,128)(2,1)S(1)} %bitcast.66), channel_id=1, source_target_pairs={{0,4},{2,6},{4,0},{6,2},{1,5},{3,7},{5,1},{7,3},{8,12},{10,14},{12... | collective-permute-start | bytes 1376264 | tf_op jit(solution)/shard_map/ppermute | solution.py:194
  96.0 2.2 %collective-permute-start.8 = (bf16[64,3584]{1,0:T(8,128)(2,1)S(1)}, bf16[64,3584]{1,0:T(8,128)(2,1)S(1)}, u32[]{:S(2)}, u32[]{:S(2)}) collective-permute-start(bf16[64,3584]{1,0:T(8,128)(2,1)S(1)} %bitcast.67), channel_id=1, source_target_pairs={{0,6},{2,4},{4,2},{6,0},{1,7},{3,5},{5,3},{7,1},{8,14},{10,12},{12... | collective-permute-start | bytes 1376264 | tf_op jit(solution)/shard_map/ppermute | solution.py:183
  101.9 5.8 %collective-permute-start.10 = (bf16[48,1024]{1,0:T(8,128)(2,1)}, bf16[48,1024]{1,0:T(8,128)(2,1)S(1)}, u32[]{:S(2)}, u32[]{:S(2)}) collective-permute-start(bf16[48,1024]{1,0:T(8,128)(2,1)} %get-tuple-element.8), channel_id=1, source_target_pairs={{0,8},{8,0},{1,9},{9,1},{2,10},{10,2},{3,11},{11,3},{4,12},{12,4},... | collective-permute-start | bytes 294920 | tf_op jit(solution)/shard_map/ppermute | solution.py:27
  110.7 6.3 %all-to-all-start.3 = ((f32[8,8,448]{2,1,0:T(8,128)}), f32[8,8,448]{2,1,0:T(8,128)S(1)}, u32[]{:S(2)}, u32[]{:S(2)}) async-start(f32[8,8,448]{2,1,0:T(8,128)} %broadcast_in_dim.13), calls=%async_computation.3 | async-start | bytes 262144 | tf_op jit(solution)/shard_map/all_to_all | solution.py:31
  117.0 2.2 %collective-permute-done.8.refs_3_ = bf16[64,3584]{1,0:T(8,128)(2,1)S(1)} collective-permute-done((bf16[64,3584]{1,0:T(8,128)(2,1)S(1)}, bf16[64,3584]{1,0:T(8,128)(2,1)S(1)}, u32[]{:S(2)}, u32[]{:S(2)}) %collective-permute-start.8) | collective-permute-done | bytes 458784 | tf_op jit(solution)/shard_map/ppermute | solution.py:183
  121.4 5.0 %all-to-all-done.3.group_ref = f32[8,8,448]{2,1,0:T(8,128)S(1)} async-done(((f32[8,8,448]{2,1,0:T(8,128)}), f32[8,8,448]{2,1,0:T(8,128)S(1)}, u32[]{:S(2)}, u32[]{:S(2)}) %all-to-all-start.3) | async-done | bytes 114720 | tf_op jit(solution)/shard_map/all_to_all | solution.py:31
  126.4 13.0 %all-to-all-start.5 = ((bf16[32,32,512]{2,1,0:T(8,128)(2,1)}), bf16[32,32,512]{2,1,0:T(8,128)(2,1)}, u32[]{:S(2)}, u32[]{:S(2)}) async-start(bf16[32,32,512]{2,1,0:T(8,128)(2,1)} %shard_map.112), calls=%async_computation.5 | async-start | bytes 2097152 | tf_op jit(solution)/shard_map/all_to_all | solution.py:202
  139.5 2.3 %shard_map.111 = bf16[256,3584]{1,0:T(8,128)(2,1)S(1)} custom-call(s32[1]{0:T(128)} %bitcast.x_ref, f32[8,8,448]{2,1,0:T(8,128)S(1)} %all-to-all-done.3.group_ref, bf16[64,3584]{1,0:T(8,128)(2,1)S(1)} %bitcast.68, bf16[64,3584]{1,0:T(8,128)(2,1)S(1)} %collective-permute-done.6.refs_1_, bf16[64,3584]{1,0:T(8,128)(2,1)} %collective-permute-done.7.refs_2_, ...), custom_call_target="tpu_custom_call" | custom-call | flops 11010048 | bytes 3670016 | tf_op jit(solution)/shard_map/pallas_call | solution.py:66
  143.7 3.6 %collective-permute-start.9 = (bf16[3584,128]{1,0:T(8,128)(2,1)S(1)}, bf16[3584,128]{1,0:T(8,128)(2,1)}, u32[]{:S(2)}, u32[]{:S(2)}) collective-permute-start(bf16[3584,128]{1,0:T(8,128)(2,1)S(1)} %convolution_convert_fusion.1), channel_id=1, source_target_pairs={{0,8},{8,0},{1,9},{9,1},{2,10},{10,2},{3,11},{11,3},{4,12},{12,4},... | collective-permute-start | bytes 2752520 | tf_op jit(solution)/shard_map/ppermute | solution.py:27
  149.6 2.4 %fusion = bf16[3584,128]{1,0:T(8,128)(2,1)S(1)} fusion(bf16[256,3584]{1,0:T(8,128)(2,1)} %copy-done.1, bf16[3584,128]{1,0:T(8,128)(2,1)} %collective-permute-done.9, bf16[256,256]{1,0:T(8,128)(2,1)S(1)} %bitcast.78, s32[]{:T(128)S(6)} %select_n.95), kind=kOutput, calls=%fused_computation.2 | convolution fusion | flops 236257280 | bytes 3735556 | tf_op jit(solution)/shard_map/dot_general | solution.py:35
  153.1 11.6 %all-to-all-done.5 = bf16[32,32,512]{2,1,0:T(8,128)(2,1)} async-done(((bf16[32,32,512]{2,1,0:T(8,128)(2,1)}), bf16[32,32,512]{2,1,0:T(8,128)(2,1)}, u32[]{:S(2)}, u32[]{:S(2)}) %all-to-all-start.5) | async-done | bytes 1048608 | tf_op jit(solution)/shard_map/all_to_all | solution.py:202
  164.6 8.2 %all-to-all-start.4 = ((bf16[32,120,128]{2,1,0:T(8,128)(2,1)}), bf16[32,120,128]{2,1,0:T(8,128)(2,1)S(1)}, u32[]{:S(2)}, u32[]{:S(2)}) async-start(bf16[32,120,128]{2,1,0:T(8,128)(2,1)} %pad_maximum_fusion), calls=%async_computation.4 | async-start | bytes 1966080 | tf_op jit(solution)/shard_map/all_to_all | solution.py:214
  172.9 2.3 %copy.40 = bf16[1024,448]{0,1:T(8,128)(2,1)} copy(bf16[1024,448]{1,0:T(8,128)(2,1)} %bitcast.14) | data formatting | bytes 1835008 | tf_op jit(solution)/shard_map/reshape | solution.py:217
  175.1 3.1 %collective-permute-start.11 = (bf16[1024,448]{0,1:T(8,128)(2,1)}, bf16[1024,448]{0,1:T(8,128)(2,1)}, u32[]{:S(2)}, u32[]{:S(2)}) collective-permute-start(bf16[1024,448]{0,1:T(8,128)(2,1)} %copy.40), channel_id=1, source_target_pairs={{0,8},{8,0},{1,9},{9,1},{2,10},{10,2},{3,11},{11,3},{4,12},{12,4},... | collective-permute-start | bytes 2752520 | tf_op jit(solution)/shard_map/ppermute | solution.py:27
  178.2 2.2 %convolution_convert_fusion.2 = bf16[256,256]{1,0:T(8,128)(2,1)S(1)} fusion(bf16[256,3584]{1,0:T(8,128)(2,1)} %copy-done.1, bf16[256,3584]{1,0:T(8,128)(2,1)S(1)} %copy-done), kind=kOutput, calls=%fused_computation.5 | convolution fusion | flops 469827584 | bytes 3801088 | tf_op jit(solution)/shard_map/dot_general | solution.py:35
  185.0 12.3 %all-to-all-done.4 = bf16[32,120,128]{2,1,0:T(8,128)(2,1)S(1)} async-done(((bf16[32,120,128]{2,1,0:T(8,128)(2,1)}), bf16[32,120,128]{2,1,0:T(8,128)(2,1)S(1)}, u32[]{:S(2)}, u32[]{:S(2)}) %all-to-all-start.4) | async-done | bytes 983072 | tf_op jit(solution)/shard_map/all_to_all | solution.py:214
  197.5 6.4 %collective-permute-start.12 = (f32[56,128]{1,0:T(8,128)S(1)}, f32[56,128]{1,0:T(8,128)S(1)}, u32[]{:S(2)}, u32[]{:S(2)}) collective-permute-start(f32[56,128]{1,0:T(8,128)S(1)} %dynamic-slice_bitcast_fusion), channel_id=1, source_target_pairs={{0,8},{8,0},{1,9},{9,1},{2,10},{10,2},{3,11},{11,3},{4,12},{12,4},... | collective-permute-start | bytes 86024 | tf_op jit(solution)/shard_map/ppermute | solution.py:27
  206.8 2.2 %fusion.1 = f32[32,448]{1,0:T(8,128)} fusion(f32[32,448]{1,0:T(8,128)S(1)} %fusion.26, bf16[1024,32]{0,1:T(8,128)(2,1)S(1)} %squeeze.20, bf16[1024,448]{1,0:T(8,128)(2,1)} %bitcast.14), kind=kOutput, calls=%fused_computation.7 | convolution fusion | flops 29388800 | bytes 1097728 | tf_op jit(solution)/shard_map/dot_general | solution.py:35
  (87 shorter events, 38.2 us)
Async XLA Ops:
  0.6 15.6 %copy-start = (bf16[256,3584]{1,0:T(8,128)(2,1)S(1)}, bf16[256,3584]{1,0:T(8,128)(2,1)}, u32[]{:S(2)}) copy-start(bf16[256,3584]{1,0:T(8,128)(2,1)} %param.12) | copy-start | bytes 5505028
  0.6 15.5 %copy-start.9 = (bf16[256,256]{1,0:T(8,128)(2,1)S(1)}, bf16[256,256]{1,0:T(8,128)(2,1)}, u32[]{:S(2)}) copy-start(bf16[256,256]{1,0:T(8,128)(2,1)} %param.10) | copy-start | bytes 393220
  2.7 39.3 %all-to-all-start = ((bf16[32,32,448]{2,1,0:T(8,128)(2,1)}), bf16[32,32,448]{2,1,0:T(8,128)(2,1)S(1)}, u32[]{:S(2)}, u32[]{:S(2)}) async-start(bf16[32,32,448]{2,1,0:T(8,128)(2,1)} %broadcast_in_dim.10), calls=%async_computation | async-start | bytes 2097152 | tf_op jit(solution)/shard_map/all_to_all | solution.py:31
  16.2 1.9 copy-start.5
  18.2 12.0 %copy-start.11 = (s32[32]{0:T(128)S(1)}, s32[32]{0:T(128)}, u32[]{:S(2)}) copy-start(s32[32]{0:T(128)} %param.9) | copy-start | bytes 388
  20.6 29.1 %collective-permute-start.1 = (bf16[64,3584]{1,0:T(8,128)(2,1)}, bf16[64,3584]{1,0:T(8,128)(2,1)S(1)}, u32[]{:S(2)}, u32[]{:S(2)}) collective-permute-start(bf16[64,3584]{1,0:T(8,128)(2,1)} %get-tuple-element.9), channel_id=1, source_target_pairs={{0,2},{2,0},{4,6},{6,4},{1,3},{3,1},{5,7},{7,5},{8,10},{10,8},{12,... | collective-permute-start | bytes 1376264 | tf_op jit(solution)/shard_map/ppermute | solution.py:157
  23.7 26.0 %collective-permute-start.2 = (bf16[64,3584]{1,0:T(8,128)(2,1)}, bf16[64,3584]{1,0:T(8,128)(2,1)}, u32[]{:S(2)}, u32[]{:S(2)}) collective-permute-start(bf16[64,3584]{1,0:T(8,128)(2,1)} %get-tuple-element.11), channel_id=1, source_target_pairs={{0,4},{2,6},{4,0},{6,2},{1,5},{3,7},{5,1},{7,3},{8,12},{10,14},{12... | collective-permute-start | bytes 1376264 | tf_op jit(solution)/shard_map/ppermute | solution.py:157
  28.1 23.8 %collective-permute-start.3 = (bf16[64,3584]{1,0:T(8,128)(2,1)}, bf16[64,3584]{1,0:T(8,128)(2,1)}, u32[]{:S(2)}, u32[]{:S(2)}) collective-permute-start(bf16[64,3584]{1,0:T(8,128)(2,1)} %get-tuple-element.10), channel_id=1, source_target_pairs={{0,6},{2,4},{4,2},{6,0},{1,7},{3,5},{5,3},{7,1},{8,14},{10,12},{12... | collective-permute-start | bytes 1376264 | tf_op jit(solution)/shard_map/ppermute | solution.py:157
  42.0 38.3 %copy-start.2 = (bf16[32,32,448]{2,1,0:T(8,128)(2,1)}, bf16[32,32,448]{2,1,0:T(8,128)(2,1)S(1)}, u32[]{:S(2)}) copy-start(bf16[32,32,448]{2,1,0:T(8,128)(2,1)S(1)} %all-to-all-done) | copy-start | bytes 2752516
  43.3 18.9 %copy-start.8 = (bf16[32,448]{1,0:T(8,128)(2,1)S(1)}, bf16[32,448]{1,0:T(8,128)(2,1)}, u32[]{:S(2)}) copy-start(bf16[32,448]{1,0:T(8,128)(2,1)} %param.7) | copy-start | bytes 86020
  43.3 19.3 %collective-permute-start = (bf16[1024,448]{0,1:T(8,128)(2,1)}, bf16[1024,448]{0,1:T(8,128)(2,1)S(1)}, u32[]{:S(2)}, u32[]{:S(2)}) collective-permute-start(bf16[1024,448]{0,1:T(8,128)(2,1)} %copy.36), channel_id=1, source_target_pairs={{0,8},{8,0},{1,9},{9,1},{2,10},{10,2},{3,11},{11,3},{4,12},{12,4},... | collective-permute-start | bytes 2752520 | tf_op jit(solution)/shard_map/ppermute | solution.py:27
  53.4 11.2 %copy-start.4 = (f32[64,3584]{1,0:T(8,128)}, f32[64,3584]{1,0:T(8,128)S(1)}, u32[]{:S(2)}) copy-start(f32[64,3584]{1,0:T(8,128)S(1)} %add_add_fusion) | copy-start | bytes 2752516
  54.2 14.6 %collective-permute-start.4 = (bf16[32,3584]{1,0:T(8,128)(2,1)}, bf16[32,3584]{1,0:T(8,128)(2,1)}, u32[]{:S(2)}, u32[]{:S(2)}) collective-permute-start(bf16[32,3584]{1,0:T(8,128)(2,1)} %fusion.4), channel_id=1, source_target_pairs={{0,1},{1,0},{2,3},{3,2},{4,5},{5,4},{6,7},{7,6},{8,9},{9,8},{10,11... | collective-permute-start | bytes 688136 | tf_op jit(solution)/shard_map/ppermute | solution.py:163
  62.6 0.9 copy-start.3
  64.6 15.0 %all-to-all-start.1 = ((f32[8,32,256]{2,1,0:T(8,128)}), f32[8,32,256]{2,1,0:T(8,128)S(1)}, u32[]{:S(2)}, u32[]{:S(2)}) async-start(f32[8,32,256]{2,1,0:T(8,128)} %bitcast.63), calls=%async_computation.1 | async-start | bytes 524288 | tf_op jit(solution)/shard_map/all_to_all | solution.py:172
  70.2 17.2 %collective-permute-start.5 = (bf16[32,3584]{1,0:T(8,128)(2,1)S(1)}, bf16[32,3584]{1,0:T(8,128)(2,1)}, u32[]{:S(2)}, u32[]{:S(2)}) collective-permute-start(bf16[32,3584]{1,0:T(8,128)(2,1)S(1)} %fusion.3), channel_id=1, source_target_pairs={{0,1},{1,0},{2,3},{3,2},{4,5},{5,4},{6,7},{7,6},{8,9},{9,8},{10,11... | collective-permute-start | bytes 688136 | tf_op jit(solution)/shard_map/ppermute | solution.py:179
  80.3 19.2 %all-to-all-start.2 = ((f32[8,32,256]{2,1,0:T(8,128)}), f32[8,32,256]{2,1,0:T(8,128)S(1)}, u32[]{:S(2)}, u32[]{:S(2)}) async-start(f32[8,32,256]{2,1,0:T(8,128)} %broadcast_in_dim.11), calls=%async_computation.2 | async-start | bytes 524288 | tf_op jit(solution)/shard_map/all_to_all | solution.py:31
  88.6 28.4 %collective-permute-start.6 = (bf16[64,3584]{1,0:T(8,128)(2,1)S(1)}, bf16[64,3584]{1,0:T(8,128)(2,1)S(1)}, u32[]{:S(2)}, u32[]{:S(2)}) collective-permute-start(bf16[64,3584]{1,0:T(8,128)(2,1)S(1)} %bitcast.65), channel_id=1, source_target_pairs={{0,2},{2,0},{4,6},{6,4},{1,3},{3,1},{5,7},{7,5},{8,10},{10,8},{12,... | collective-permute-start | bytes 1376264 | tf_op jit(solution)/shard_map/ppermute | solution.py:182
  91.6 47.8 %collective-permute-start.7 = (bf16[64,3584]{1,0:T(8,128)(2,1)S(1)}, bf16[64,3584]{1,0:T(8,128)(2,1)}, u32[]{:S(2)}, u32[]{:S(2)}) collective-permute-start(bf16[64,3584]{1,0:T(8,128)(2,1)S(1)} %bitcast.66), channel_id=1, source_target_pairs={{0,4},{2,6},{4,0},{6,2},{1,5},{3,7},{5,1},{7,3},{8,12},{10,14},{12... | collective-permute-start | bytes 1376264 | tf_op jit(solution)/shard_map/ppermute | solution.py:194
  96.0 23.1 %collective-permute-start.8 = (bf16[64,3584]{1,0:T(8,128)(2,1)S(1)}, bf16[64,3584]{1,0:T(8,128)(2,1)S(1)}, u32[]{:S(2)}, u32[]{:S(2)}) collective-permute-start(bf16[64,3584]{1,0:T(8,128)(2,1)S(1)} %bitcast.67), channel_id=1, source_target_pairs={{0,6},{2,4},{4,2},{6,0},{1,7},{3,5},{5,3},{7,1},{8,14},{10,12},{12... | collective-permute-start | bytes 1376264 | tf_op jit(solution)/shard_map/ppermute | solution.py:183
  101.9 18.2 %collective-permute-start.10 = (bf16[48,1024]{1,0:T(8,128)(2,1)}, bf16[48,1024]{1,0:T(8,128)(2,1)S(1)}, u32[]{:S(2)}, u32[]{:S(2)}) collective-permute-start(bf16[48,1024]{1,0:T(8,128)(2,1)} %get-tuple-element.8), channel_id=1, source_target_pairs={{0,8},{8,0},{1,9},{9,1},{2,10},{10,2},{3,11},{11,3},{4,12},{12,4},... | collective-permute-start | bytes 294920 | tf_op jit(solution)/shard_map/ppermute | solution.py:27
  109.3 1.4 copy-start.10
  110.7 15.7 %all-to-all-start.3 = ((f32[8,8,448]{2,1,0:T(8,128)}), f32[8,8,448]{2,1,0:T(8,128)S(1)}, u32[]{:S(2)}, u32[]{:S(2)}) async-start(f32[8,8,448]{2,1,0:T(8,128)} %broadcast_in_dim.13), calls=%async_computation.3 | async-start | bytes 262144 | tf_op jit(solution)/shard_map/all_to_all | solution.py:31
  126.4 38.2 %all-to-all-start.5 = ((bf16[32,32,512]{2,1,0:T(8,128)(2,1)}), bf16[32,32,512]{2,1,0:T(8,128)(2,1)}, u32[]{:S(2)}, u32[]{:S(2)}) async-start(bf16[32,32,512]{2,1,0:T(8,128)(2,1)} %shard_map.112), calls=%async_computation.5 | async-start | bytes 2097152 | tf_op jit(solution)/shard_map/all_to_all | solution.py:202
  139.4 3.6 %copy-start.6 = (bf16[4,64,256]{2,1,0:T(8,128)(2,1)S(1)}, bf16[4,64,256]{2,1,0:T(8,128)(2,1)}, u32[]{:S(2)}) copy-start(bf16[4,64,256]{2,1,0:T(8,128)(2,1)} %copy-done.5) | copy-start | bytes 393220
  141.7 1.3 copy-start.1
  143.0 6.6 %copy-start.7 = (bf16[4,64,256]{2,1,0:T(8,128)(2,1)S(1)}, bf16[4,64,256]{2,1,0:T(8,128)(2,1)}, u32[]{:S(2)}) copy-start(bf16[4,64,256]{2,1,0:T(8,128)(2,1)} %copy-done.5) | copy-start | bytes 393220
  143.7 5.9 %collective-permute-start.9 = (bf16[3584,128]{1,0:T(8,128)(2,1)S(1)}, bf16[3584,128]{1,0:T(8,128)(2,1)}, u32[]{:S(2)}, u32[]{:S(2)}) collective-permute-start(bf16[3584,128]{1,0:T(8,128)(2,1)S(1)} %convolution_convert_fusion.1), channel_id=1, source_target_pairs={{0,8},{8,0},{1,9},{9,1},{2,10},{10,2},{3,11},{11,3},{4,12},{12,4},... | collective-permute-start | bytes 2752520 | tf_op jit(solution)/shard_map/ppermute | solution.py:27
  164.6 32.7 %all-to-all-start.4 = ((bf16[32,120,128]{2,1,0:T(8,128)(2,1)}), bf16[32,120,128]{2,1,0:T(8,128)(2,1)S(1)}, u32[]{:S(2)}, u32[]{:S(2)}) async-start(bf16[32,120,128]{2,1,0:T(8,128)(2,1)} %pad_maximum_fusion), calls=%async_computation.4 | async-start | bytes 1966080 | tf_op jit(solution)/shard_map/all_to_all | solution.py:214
  175.1 30.1 %collective-permute-start.11 = (bf16[1024,448]{0,1:T(8,128)(2,1)}, bf16[1024,448]{0,1:T(8,128)(2,1)}, u32[]{:S(2)}, u32[]{:S(2)}) collective-permute-start(bf16[1024,448]{0,1:T(8,128)(2,1)} %copy.40), channel_id=1, source_target_pairs={{0,8},{8,0},{1,9},{9,1},{2,10},{10,2},{3,11},{11,3},{4,12},{12,4},... | collective-permute-start | bytes 2752520 | tf_op jit(solution)/shard_map/ppermute | solution.py:27
  197.5 11.4 %collective-permute-start.12 = (f32[56,128]{1,0:T(8,128)S(1)}, f32[56,128]{1,0:T(8,128)S(1)}, u32[]{:S(2)}, u32[]{:S(2)}) collective-permute-start(f32[56,128]{1,0:T(8,128)S(1)} %dynamic-slice_bitcast_fusion), channel_id=1, source_target_pairs={{0,8},{8,0},{1,9},{9,1},{2,10},{10,2},{3,11},{11,3},{4,12},{12,4},... | collective-permute-start | bytes 86024 | tf_op jit(solution)/shard_map/ppermute | solution.py:27

commit v13 on v10

--- a/solution.py
+++ b/solution.py
@@ -75,6 +75,28 @@
             flops=12 * tokens * width, bytes_accessed=4 * tokens * width, transcendentals=0
         ),
     )(x_index.reshape(1), group_rows, *blocks)
+
+
+def score_kernel(part_ref, out_ref):
+    total = part_ref[0]
+    for t in range(1, N_T):
+        total += part_ref[t]
+    for t in range(N_T):
+        out_ref[t] = total * LOGIT_SCALE
+
+
+def score_sum(parts):
+    whole = pl.BlockSpec(memory_space=pltpu.VMEM)
+    return pl.pallas_call(
+        score_kernel,
+        out_shape=jax.ShapeDtypeStruct(parts.shape, F32),
+        in_specs=[whole],
+        out_specs=whole,
+        compiler_params=pltpu.CompilerParams(vmem_limit_bytes=12 * 2**20),
+        cost_estimate=pl.CostEstimate(
+            flops=parts.size, bytes_accessed=8 * parts.size, transcendentals=0
+        ),
+    )(parts)
 
 
 def softmax_kernel(score_ref, column_ref, own_ref, give_ref):
@@ -170,14 +192,14 @@
     partial = jnp.concatenate(partial, axis=1)
     share = 2 * half // N_T
     partial = partial.reshape(rows, N_T, share).transpose(1, 0, 2)
-    scores_own = jnp.sum(lax.all_to_all(partial, TENSOR, 0, 0), axis=0) * LOGIT_SCALE
-    scores = to_all(scores_own, TENSOR, N_T)
+    scores_own = score_sum(lax.all_to_all(partial, TENSOR, 0, 0))
+    scores = lax.all_to_all(scores_own, TENSOR, 0, 0)
 
     own_residual = lax.dynamic_slice_in_dim(residual, (2 * x_index + z_index) * rows, rows, 0)
     hidden_own = tie(from_z.astype(F32), partial[0, :, :1]) + own_residual.astype(F32)
     hidden_own = (mixed_keep + hidden_own).astype(BF16)
 
-    hidden_z = tie(lax.ppermute(hidden_own, **xor("zh", 2, 1)), scores_own[:, :1])
+    hidden_z = tie(lax.ppermute(hidden_own, **xor("zh", 2, 1)), scores_own[0, :, :1])
     hidden_0 = jnp.stack([hidden_own, hidden_z])
     hidden_0 = jnp.where(z_index == 0, hidden_0, hidden_0[::-1]).reshape(x_block, width)
     hidden_1 = lax.ppermute(hidden_0, **xor("x", 4, 1))

time: 201 us -> 201 us (level)
    all_to_all x3 -> x2, starting transfers between devices: 23.5 us -> 17.2 us  [to_all(): lax.all_to_all(jnp.broadcast_to(value[None], (count,) + value.shape), axe...]
    all_to_all x1 -> x2, starting transfers between devices: 3.41 us -> 9.55 us  [the longest x1 6.14 us: per_device(): scores = lax.all_to_all(scores_own, TENSOR, 0, 0)]
    all_to_all x3 -> x2, waiting for transfers between devices: 17.1 us -> 12.9 us  [to_all(): lax.all_to_all(jnp.broadcast_to(value[None], (count,) + value.shape), axe...]
    all_to_all x1 -> x2, waiting for transfers between devices: 2.1 us -> 6.03 us  [the longest x1 4.79 us: per_device(): scores = lax.all_to_all(scores_own, TENSOR, 0, 0)]
  transfers between devices with their start and end apart: 20 -> 20, of which waited for: 11 -> 10; matrix products, arithmetic and copies ran while one was open for 18% -> 18% of each run, Pallas kernels for 2% -> 2%
where the time goes in v13:
time: 201 us; the launch traced here: 199 us
  starting transfers between devices  110 us (55%)
  waiting for transfers between devices  38.1 us (19%)
  local copies, waits for them, and re-layouts  19.1 us (10%)
  matrix products  14.7 us (7%)
  other arithmetic  9.55 us (5%)
  Pallas kernels  4.64 us (2%)
  between operations  2.99 us (1%)
    ppermute x5, starting transfers between devices, swap(): return lax.ppermute(value, **xor('c', 2, 1))  24.9 us
    all_to_all x2, starting transfers between devices, to_all(): lax.all_to_all(jnp.broadcast_to(value[None], (count,) + value.shape), axe...  17.2 us
    dot_general x10, matrix products, dot(): return lax.dot_general(a, b, (dims, ((), ())), preferred_element_type=F32)  14.7 us
    all_to_all x2, waiting for transfers between devices, to_all(): lax.all_to_all(jnp.broadcast_to(value[None], (count,) + value.shape), axe...  12.9 us
    all_to_all x1, starting transfers between devices, per_device(): by_plane = lax.all_to_all(by_plane, PLANE, 0, 0)  9.98 us
    all_to_all x1, starting transfers between devices, per_device(): final = lax.all_to_all(final, PLANE, 0, 0)  9.78 us
    ppermute x3, starting transfers between devices, per_device(): lax.ppermute(mixed[k * x_block:(k + 1) * x_block], **xor('x', 4, k))  9.57 us
    all_to_all x1, waiting for transfers between devices, per_device(): final = lax.all_to_all(final, PLANE, 0, 0)  9.55 us
  transfers between devices with their start and end apart: 20, of which 10 were waited for; matrix products, arithmetic and copies ran while one was open for 18% of the time, Pallas kernels for 2%

profile of v13, /device:TPU:1, one launch (start us, length us, event | category | flops | bytes accessed | tf_op | source)
XLA Modules:
  0.0 199.1 jit_solution(4968726144078500805)
XLA Ops:
  0.7 2.0 broadcast_in_dim.8
  2.6 13.5 %all-to-all-start = ((bf16[32,32,448]{2,1,0:T(8,128)(2,1)}), bf16[32,32,448]{2,1,0:T(8,128)(2,1)S(1)}, u32[]{:S(2)}, u32[]{:S(2)}) async-start(bf16[32,32,448]{2,1,0:T(8,128)(2,1)} %broadcast_in_dim.8), calls=%async_computation | async-start | bytes 2097152 | tf_op jit(solution)/shard_map/all_to_all | solution.py:31
  18.1 2.4 %fusion.21 = (bf16[64,3584]{1,0:T(8,128)(2,1)}, bf16[64,3584]{1,0:T(8,128)(2,1)}, bf16[64,3584]{1,0:T(8,128)(2,1)}) fusion(bf16[256,3584]{1,0:T(8,128)(2,1)} %convolution_convert_fusion), kind=kLoop, calls=%fused_computation.72 | loop fusion | bytes 2752512 | tf_op jit(solution)/shard_map/slice | solution.py:180
  20.6 3.1 %collective-permute-start.1 = (bf16[64,3584]{1,0:T(8,128)(2,1)}, bf16[64,3584]{1,0:T(8,128)(2,1)S(1)}, u32[]{:S(2)}, u32[]{:S(2)}) collective-permute-start(bf16[64,3584]{1,0:T(8,128)(2,1)} %get-tuple-element.9), channel_id=1, source_target_pairs={{0,2},{2,0},{4,6},{6,4},{1,3},{3,1},{5,7},{7,5},{8,10},{10,8},{12,... | collective-permute-start | bytes 1376264 | tf_op jit(solution)/shard_map/ppermute | solution.py:180
  23.7 4.4 %collective-permute-start.2 = (bf16[64,3584]{1,0:T(8,128)(2,1)}, bf16[64,3584]{1,0:T(8,128)(2,1)}, u32[]{:S(2)}, u32[]{:S(2)}) collective-permute-start(bf16[64,3584]{1,0:T(8,128)(2,1)} %get-tuple-element.11), channel_id=1, source_target_pairs={{0,4},{2,6},{4,0},{6,2},{1,5},{3,7},{5,1},{7,3},{8,12},{10,14},{12... | collective-permute-start | bytes 1376264 | tf_op jit(solution)/shard_map/ppermute | solution.py:180
  28.1 2.1 %collective-permute-start.3 = (bf16[64,3584]{1,0:T(8,128)(2,1)}, bf16[64,3584]{1,0:T(8,128)(2,1)}, u32[]{:S(2)}, u32[]{:S(2)}) collective-permute-start(bf16[64,3584]{1,0:T(8,128)(2,1)} %get-tuple-element.10), channel_id=1, source_target_pairs={{0,6},{2,4},{4,2},{6,0},{1,7},{3,5},{5,3},{7,1},{8,14},{10,12},{12... | collective-permute-start | bytes 1376264 | tf_op jit(solution)/shard_map/ppermute | solution.py:180
  30.2 11.8 %all-to-all-done = bf16[32,32,448]{2,1,0:T(8,128)(2,1)S(1)} async-done(((bf16[32,32,448]{2,1,0:T(8,128)(2,1)}), bf16[32,32,448]{2,1,0:T(8,128)(2,1)S(1)}, u32[]{:S(2)}, u32[]{:S(2)}) %all-to-all-start) | async-done | bytes 917536 | tf_op jit(solution)/shard_map/all_to_all | solution.py:31
  43.3 6.3 %collective-permute-start = (bf16[1024,448]{0,1:T(8,128)(2,1)}, bf16[1024,448]{0,1:T(8,128)(2,1)S(1)}, u32[]{:S(2)}, u32[]{:S(2)}) collective-permute-start(bf16[1024,448]{0,1:T(8,128)(2,1)} %copy.21), channel_id=1, source_target_pairs={{0,8},{8,0},{1,9},{9,1},{2,10},{10,2},{3,11},{11,3},{4,12},{12,4},... | collective-permute-start | bytes 2752520 | tf_op jit(solution)/shard_map/ppermute | solution.py:27
  49.6 2.2 %collective-permute-done.3 = bf16[64,3584]{1,0:T(8,128)(2,1)} collective-permute-done((bf16[64,3584]{1,0:T(8,128)(2,1)}, bf16[64,3584]{1,0:T(8,128)(2,1)}, u32[]{:S(2)}, u32[]{:S(2)}) %collective-permute-start.3) | collective-permute-done | bytes 458784 | tf_op jit(solution)/shard_map/ppermute | solution.py:180
  53.4 7.9 %collective-permute-start.4 = (bf16[32,3584]{1,0:T(8,128)(2,1)S(1)}, bf16[32,3584]{1,0:T(8,128)(2,1)S(1)}, u32[]{:S(2)}, u32[]{:S(2)}) collective-permute-start(bf16[32,3584]{1,0:T(8,128)(2,1)S(1)} %fusion.4), channel_id=1, source_target_pairs={{0,1},{1,0},{2,3},{3,2},{4,5},{5,4},{6,7},{7,6},{8,9},{9,8},{10,11... | collective-permute-start | bytes 688136 | tf_op jit(solution)/shard_map/ppermute | solution.py:186
  63.8 3.4 %all-to-all-start.1 = ((f32[8,32,256]{2,1,0:T(8,128)}), f32[8,32,256]{2,1,0:T(8,128)S(1)}, u32[]{:S(2)}, u32[]{:S(2)}) async-start(f32[8,32,256]{2,1,0:T(8,128)} %bitcast.63), calls=%async_computation.1 | async-start | bytes 524288 | tf_op jit(solution)/shard_map/all_to_all | solution.py:195
  69.3 7.2 %collective-permute-start.5 = (bf16[32,3584]{1,0:T(8,128)(2,1)S(1)}, bf16[32,3584]{1,0:T(8,128)(2,1)S(1)}, u32[]{:S(2)}, u32[]{:S(2)}) collective-permute-start(bf16[32,3584]{1,0:T(8,128)(2,1)S(1)} %fusion.3), channel_id=1, source_target_pairs={{0,1},{1,0},{2,3},{3,2},{4,5},{5,4},{6,7},{7,6},{8,9},{9,8},{10,11... | collective-permute-start | bytes 688136 | tf_op jit(solution)/shard_map/ppermute | solution.py:202
  79.4 6.1 %all-to-all-start.2 = ((f32[8,32,256]{2,1,0:T(8,128)}), f32[8,32,256]{2,1,0:T(8,128)S(1)}, u32[]{:S(2)}, u32[]{:S(2)}) async-start(f32[8,32,256]{2,1,0:T(8,128)} %shard_map.110), calls=%async_computation.2 | async-start | bytes 524288 | tf_op jit(solution)/shard_map/all_to_all | solution.py:196
  86.6 3.4 %collective-permute-start.6 = (bf16[64,3584]{1,0:T(8,128)(2,1)S(1)}, bf16[64,3584]{1,0:T(8,128)(2,1)S(1)}, u32[]{:S(2)}, u32[]{:S(2)}) collective-permute-start(bf16[64,3584]{1,0:T(8,128)(2,1)S(1)} %bitcast.65), channel_id=1, source_target_pairs={{0,2},{2,0},{4,6},{6,4},{1,3},{3,1},{5,7},{7,5},{8,10},{10,8},{12,... | collective-permute-start | bytes 1376264 | tf_op jit(solution)/shard_map/ppermute | solution.py:205
  90.0 3.7 %collective-permute-start.8 = (bf16[64,3584]{1,0:T(8,128)(2,1)S(1)}, bf16[64,3584]{1,0:T(8,128)(2,1)S(1)}, u32[]{:S(2)}, u32[]{:S(2)}) collective-permute-start(bf16[64,3584]{1,0:T(8,128)(2,1)S(1)} %bitcast.66), channel_id=1, source_target_pairs={{0,6},{2,4},{4,2},{6,0},{1,7},{3,5},{5,3},{7,1},{8,14},{10,12},{12... | collective-permute-start | bytes 1376264 | tf_op jit(solution)/shard_map/ppermute | solution.py:206
  93.7 4.8 %all-to-all-done.2.score_ref = f32[8,32,256]{2,1,0:T(8,128)S(1)} async-done(((f32[8,32,256]{2,1,0:T(8,128)}), f32[8,32,256]{2,1,0:T(8,128)S(1)}, u32[]{:S(2)}, u32[]{:S(2)}) %all-to-all-start.2) | async-done | bytes 262176 | tf_op jit(solution)/shard_map/all_to_all | solution.py:196
  103.2 3.8 %all-to-all-start.3 = ((f32[8,8,448]{2,1,0:T(8,128)}), f32[8,8,448]{2,1,0:T(8,128)S(1)}, u32[]{:S(2)}, u32[]{:S(2)}) async-start(f32[8,8,448]{2,1,0:T(8,128)} %broadcast_in_dim.10), calls=%async_computation.3 | async-start | bytes 262144 | tf_op jit(solution)/shard_map/all_to_all | solution.py:31
  107.0 4.4 %collective-permute-start.11 = (bf16[48,1024]{1,0:T(8,128)(2,1)}, bf16[48,1024]{1,0:T(8,128)(2,1)S(1)}, u32[]{:S(2)}, u32[]{:S(2)}) collective-permute-start(bf16[48,1024]{1,0:T(8,128)(2,1)} %copy-done.6), channel_id=1, source_target_pairs={{0,8},{8,0},{1,9},{9,1},{2,10},{10,2},{3,11},{11,3},{4,12},{12,4},... | collective-permute-start | bytes 294920 | tf_op jit(solution)/shard_map/ppermute | solution.py:27
  116.4 10.0 %all-to-all-start.5 = ((bf16[32,32,512]{2,1,0:T(8,128)(2,1)}), bf16[32,32,512]{2,1,0:T(8,128)(2,1)}, u32[]{:S(2)}, u32[]{:S(2)}) async-start(bf16[32,32,512]{2,1,0:T(8,128)(2,1)} %shard_map.113), calls=%async_computation.5 | async-start | bytes 2097152 | tf_op jit(solution)/shard_map/all_to_all | solution.py:227
  127.3 4.9 %collective-permute-start.7 = (bf16[32,3584]{1,0:T(8,128)(2,1)}, bf16[32,3584]{1,0:T(8,128)(2,1)}, u32[]{:S(2)}, u32[]{:S(2)}) collective-permute-start(bf16[32,3584]{1,0:T(8,128)(2,1)} %get-tuple-element.25), channel_id=1, source_target_pairs={{0,6},{2,4},{4,2},{6,0},{1,7},{3,5},{5,3},{7,1},{8,14},{10,12},{12... | collective-permute-start | bytes 688136 | tf_op jit(solution)/shard_map/ppermute | solution.py:218
  132.2 1.9 collective-permute-start.9
  135.9 3.7 %collective-permute-done.9.refs_3_ = bf16[32,3584]{1,0:T(8,128)(2,1)} collective-permute-done((bf16[32,3584]{1,0:T(8,128)(2,1)}, bf16[32,3584]{1,0:T(8,128)(2,1)}, u32[]{:S(2)}, u32[]{:S(2)}) %collective-permute-start.9) | collective-permute-done | bytes 229408 | tf_op jit(solution)/shard_map/ppermute | solution.py:219
  139.5 2.3 %shard_map.112 = bf16[256,3584]{1,0:T(8,128)(2,1)S(1)} custom-call(s32[1]{0:T(128)} %bitcast.x_ref, f32[8,8,448]{2,1,0:T(8,128)S(1)} %all-to-all-done.3.group_ref, bf16[64,3584]{1,0:T(8,128)(2,1)S(1)} %bitcast.67, bf16[64,3584]{1,0:T(8,128)(2,1)S(1)} %collective-permute-done.6.refs_1_, bf16[32,3584]{1,0:T(8,128)(2,1)} %collective-permute-done.7.refs_2_, ...), custom_call_target="tpu_custom_call" | custom-call | flops 11010048 | bytes 3670016 | tf_op jit(solution)/shard_map/pallas_call | solution.py:67
  143.8 5.8 %collective-permute-start.10 = (bf16[3584,128]{1,0:T(8,128)(2,1)S(1)}, bf16[3584,128]{1,0:T(8,128)(2,1)}, u32[]{:S(2)}, u32[]{:S(2)}) collective-permute-start(bf16[3584,128]{1,0:T(8,128)(2,1)S(1)} %convolution_convert_fusion.1), channel_id=1, source_target_pairs={{0,8},{8,0},{1,9},{9,1},{2,10},{10,2},{3,11},{11,3},{4,12},{12,4},... | collective-permute-start | bytes 2752520 | tf_op jit(solution)/shard_map/ppermute | solution.py:27
  151.9 2.4 %fusion = bf16[3584,128]{1,0:T(8,128)(2,1)S(1)} fusion(bf16[256,3584]{1,0:T(8,128)(2,1)} %copy-done.1, bf16[3584,128]{1,0:T(8,128)(2,1)} %collective-permute-done.10, bf16[256,256]{1,0:T(8,128)(2,1)S(1)} %bitcast.77, s32[]{:T(128)S(6)} %select_n.95), kind=kOutput, calls=%fused_computation.2 | convolution fusion | flops 236257280 | bytes 3735556 | tf_op jit(solution)/shard_map/dot_general | solution.py:35
  155.3 9.8 %all-to-all-start.4 = ((bf16[32,120,128]{2,1,0:T(8,128)(2,1)}), bf16[32,120,128]{2,1,0:T(8,128)(2,1)S(1)}, u32[]{:S(2)}, u32[]{:S(2)}) async-start(bf16[32,120,128]{2,1,0:T(8,128)(2,1)} %pad_maximum_fusion), calls=%async_computation.4 | async-start | bytes 1966080 | tf_op jit(solution)/shard_map/all_to_all | solution.py:239
  165.1 2.2 %copy.25 = bf16[1024,448]{0,1:T(8,128)(2,1)} copy(bf16[1024,448]{1,0:T(8,128)(2,1)} %bitcast.14) | data formatting | bytes 1835008 | tf_op jit(solution)/shard_map/reshape | solution.py:242
  167.4 2.5 %collective-permute-start.12 = (bf16[1024,448]{0,1:T(8,128)(2,1)}, bf16[1024,448]{0,1:T(8,128)(2,1)}, u32[]{:S(2)}, u32[]{:S(2)}) collective-permute-start(bf16[1024,448]{0,1:T(8,128)(2,1)} %copy.25), channel_id=1, source_target_pairs={{0,8},{8,0},{1,9},{9,1},{2,10},{10,2},{3,11},{11,3},{4,12},{12,4},... | collective-permute-start | bytes 2752520 | tf_op jit(solution)/shard_map/ppermute | solution.py:27
  169.9 2.2 %convolution_convert_fusion.2 = bf16[256,256]{1,0:T(8,128)(2,1)S(1)} fusion(bf16[256,3584]{1,0:T(8,128)(2,1)} %copy-done.1, bf16[256,3584]{1,0:T(8,128)(2,1)S(1)} %copy-done), kind=kOutput, calls=%fused_computation.5 | convolution fusion | flops 469827584 | bytes 3801088 | tf_op jit(solution)/shard_map/dot_general | solution.py:35
  178.3 2.2 %fusion.1 = f32[32,448]{1,0:T(8,128)} fusion(f32[32,448]{1,0:T(8,128)S(1)} %fusion.26, bf16[1024,32]{0,1:T(8,128)(2,1)S(1)} %squeeze.21, bf16[1024,448]{1,0:T(8,128)(2,1)} %bitcast.14), kind=kOutput, calls=%fused_computation.7 | convolution fusion | flops 29388800 | bytes 1097728 | tf_op jit(solution)/shard_map/dot_general | solution.py:35
  180.5 9.5 %all-to-all-done.4 = bf16[32,120,128]{2,1,0:T(8,128)(2,1)S(1)} async-done(((bf16[32,120,128]{2,1,0:T(8,128)(2,1)}), bf16[32,120,128]{2,1,0:T(8,128)(2,1)S(1)}, u32[]{:S(2)}, u32[]{:S(2)}) %all-to-all-start.4) | async-done | bytes 983072 | tf_op jit(solution)/shard_map/all_to_all | solution.py:239
  190.2 5.9 %collective-permute-start.13 = (f32[56,128]{1,0:T(8,128)S(1)}, f32[56,128]{1,0:T(8,128)S(1)}, u32[]{:S(2)}, u32[]{:S(2)}) collective-permute-start(f32[56,128]{1,0:T(8,128)S(1)} %dynamic-slice_bitcast_fusion), channel_id=1, source_target_pairs={{0,8},{8,0},{1,9},{9,1},{2,10},{10,2},{3,11},{11,3},{4,12},{12,4},... | collective-permute-start | bytes 86024 | tf_op jit(solution)/shard_map/ppermute | solution.py:27
  (93 shorter events, 38.3 us)
Async XLA Ops:
  0.6 15.6 %copy-start = (bf16[256,3584]{1,0:T(8,128)(2,1)S(1)}, bf16[256,3584]{1,0:T(8,128)(2,1)}, u32[]{:S(2)}) copy-start(bf16[256,3584]{1,0:T(8,128)(2,1)} %param.12) | copy-start | bytes 5505028
  0.6 15.5 %copy-start.13 = (bf16[256,256]{1,0:T(8,128)(2,1)S(1)}, bf16[256,256]{1,0:T(8,128)(2,1)}, u32[]{:S(2)}) copy-start(bf16[256,256]{1,0:T(8,128)(2,1)} %param.10) | copy-start | bytes 393220
  2.6 39.3 %all-to-all-start = ((bf16[32,32,448]{2,1,0:T(8,128)(2,1)}), bf16[32,32,448]{2,1,0:T(8,128)(2,1)S(1)}, u32[]{:S(2)}, u32[]{:S(2)}) async-start(bf16[32,32,448]{2,1,0:T(8,128)(2,1)} %broadcast_in_dim.8), calls=%async_computation | async-start | bytes 2097152 | tf_op jit(solution)/shard_map/all_to_all | solution.py:31
  16.2 1.9 copy-start.10
  20.6 29.0 %collective-permute-start.1 = (bf16[64,3584]{1,0:T(8,128)(2,1)}, bf16[64,3584]{1,0:T(8,128)(2,1)S(1)}, u32[]{:S(2)}, u32[]{:S(2)}) collective-permute-start(bf16[64,3584]{1,0:T(8,128)(2,1)} %get-tuple-element.9), channel_id=1, source_target_pairs={{0,2},{2,0},{4,6},{6,4},{1,3},{3,1},{5,7},{7,5},{8,10},{10,8},{12,... | collective-permute-start | bytes 1376264 | tf_op jit(solution)/shard_map/ppermute | solution.py:180
  23.7 25.9 %collective-permute-start.2 = (bf16[64,3584]{1,0:T(8,128)(2,1)}, bf16[64,3584]{1,0:T(8,128)(2,1)}, u32[]{:S(2)}, u32[]{:S(2)}) collective-permute-start(bf16[64,3584]{1,0:T(8,128)(2,1)} %get-tuple-element.11), channel_id=1, source_target_pairs={{0,4},{2,6},{4,0},{6,2},{1,5},{3,7},{5,1},{7,3},{8,12},{10,14},{12... | collective-permute-start | bytes 1376264 | tf_op jit(solution)/shard_map/ppermute | solution.py:180
  28.1 23.8 %collective-permute-start.3 = (bf16[64,3584]{1,0:T(8,128)(2,1)}, bf16[64,3584]{1,0:T(8,128)(2,1)}, u32[]{:S(2)}, u32[]{:S(2)}) collective-permute-start(bf16[64,3584]{1,0:T(8,128)(2,1)} %get-tuple-element.10), channel_id=1, source_target_pairs={{0,6},{2,4},{4,2},{6,0},{1,7},{3,5},{5,3},{7,1},{8,14},{10,12},{12... | collective-permute-start | bytes 1376264 | tf_op jit(solution)/shard_map/ppermute | solution.py:180
  42.0 19.4 %copy-start.7 = (bf16[32,32,448]{2,1,0:T(8,128)(2,1)}, bf16[32,32,448]{2,1,0:T(8,128)(2,1)S(1)}, u32[]{:S(2)}) copy-start(bf16[32,32,448]{2,1,0:T(8,128)(2,1)S(1)} %all-to-all-done) | copy-start | bytes 2752516
  43.3 18.1 %copy-start.2 = (bf16[32,448]{1,0:T(8,128)(2,1)S(1)}, bf16[32,448]{1,0:T(8,128)(2,1)}, u32[]{:S(2)}) copy-start(bf16[32,448]{1,0:T(8,128)(2,1)} %item_ref.1) | copy-start | bytes 86020
  43.3 18.6 %collective-permute-start = (bf16[1024,448]{0,1:T(8,128)(2,1)}, bf16[1024,448]{0,1:T(8,128)(2,1)S(1)}, u32[]{:S(2)}, u32[]{:S(2)}) collective-permute-start(bf16[1024,448]{0,1:T(8,128)(2,1)} %copy.21), channel_id=1, source_target_pairs={{0,8},{8,0},{1,9},{9,1},{2,10},{10,2},{3,11},{11,3},{4,12},{12,4},... | collective-permute-start | bytes 2752520 | tf_op jit(solution)/shard_map/ppermute | solution.py:27
  53.4 10.4 %copy-start.9 = (f32[64,3584]{1,0:T(8,128)}, f32[64,3584]{1,0:T(8,128)S(1)}, u32[]{:S(2)}) copy-start(f32[64,3584]{1,0:T(8,128)S(1)} %add_add_fusion) | copy-start | bytes 2752516
  53.4 14.6 %collective-permute-start.4 = (bf16[32,3584]{1,0:T(8,128)(2,1)S(1)}, bf16[32,3584]{1,0:T(8,128)(2,1)S(1)}, u32[]{:S(2)}, u32[]{:S(2)}) collective-permute-start(bf16[32,3584]{1,0:T(8,128)(2,1)S(1)} %fusion.4), channel_id=1, source_target_pairs={{0,1},{1,0},{2,3},{3,2},{4,5},{5,4},{6,7},{7,6},{8,9},{9,8},{10,11... | collective-permute-start | bytes 688136 | tf_op jit(solution)/shard_map/ppermute | solution.py:186
  61.8 14.7 %copy-start.14 = (s32[32]{0:T(128)S(1)}, s32[32]{0:T(128)}, u32[]{:S(2)}) copy-start(s32[32]{0:T(128)} %param.9) | copy-start | bytes 388
  61.8 0.9 copy-start.8
  63.8 14.8 %all-to-all-start.1 = ((f32[8,32,256]{2,1,0:T(8,128)}), f32[8,32,256]{2,1,0:T(8,128)S(1)}, u32[]{:S(2)}, u32[]{:S(2)}) async-start(f32[8,32,256]{2,1,0:T(8,128)} %bitcast.63), calls=%async_computation.1 | async-start | bytes 524288 | tf_op jit(solution)/shard_map/all_to_all | solution.py:195
  69.3 17.1 %collective-permute-start.5 = (bf16[32,3584]{1,0:T(8,128)(2,1)S(1)}, bf16[32,3584]{1,0:T(8,128)(2,1)S(1)}, u32[]{:S(2)}, u32[]{:S(2)}) collective-permute-start(bf16[32,3584]{1,0:T(8,128)(2,1)S(1)} %fusion.3), channel_id=1, source_target_pairs={{0,1},{1,0},{2,3},{3,2},{4,5},{5,4},{6,7},{7,6},{8,9},{9,8},{10,11... | collective-permute-start | bytes 688136 | tf_op jit(solution)/shard_map/ppermute | solution.py:202
  79.4 19.1 %all-to-all-start.2 = ((f32[8,32,256]{2,1,0:T(8,128)}), f32[8,32,256]{2,1,0:T(8,128)S(1)}, u32[]{:S(2)}, u32[]{:S(2)}) async-start(f32[8,32,256]{2,1,0:T(8,128)} %shard_map.110), calls=%async_computation.2 | async-start | bytes 524288 | tf_op jit(solution)/shard_map/all_to_all | solution.py:196
  86.6 39.8 %collective-permute-start.6 = (bf16[64,3584]{1,0:T(8,128)(2,1)S(1)}, bf16[64,3584]{1,0:T(8,128)(2,1)S(1)}, u32[]{:S(2)}, u32[]{:S(2)}) collective-permute-start(bf16[64,3584]{1,0:T(8,128)(2,1)S(1)} %bitcast.65), channel_id=1, source_target_pairs={{0,2},{2,0},{4,6},{6,4},{1,3},{3,1},{5,7},{7,5},{8,10},{10,8},{12,... | collective-permute-start | bytes 1376264 | tf_op jit(solution)/shard_map/ppermute | solution.py:205
  90.0 36.5 %collective-permute-start.8 = (bf16[64,3584]{1,0:T(8,128)(2,1)S(1)}, bf16[64,3584]{1,0:T(8,128)(2,1)S(1)}, u32[]{:S(2)}, u32[]{:S(2)}) collective-permute-start(bf16[64,3584]{1,0:T(8,128)(2,1)S(1)} %bitcast.66), channel_id=1, source_target_pairs={{0,6},{2,4},{4,2},{6,0},{1,7},{3,5},{5,3},{7,1},{8,14},{10,12},{12... | collective-permute-start | bytes 1376264 | tf_op jit(solution)/shard_map/ppermute | solution.py:206
  98.7 2.2 %copy-start.6 = (bf16[48,1024]{1,0:T(8,128)(2,1)}, bf16[48,1024]{1,0:T(8,128)(2,1)S(1)}, u32[]{:S(2)}) copy-start(bf16[48,1024]{1,0:T(8,128)(2,1)S(1)} %get-tuple-element.8) | copy-start | bytes 294916
  102.5 13.9 %copy-start.12 = (f32[32,448]{1,0:T(8,128)}, f32[32,448]{1,0:T(8,128)S(1)}, u32[]{:S(2)}) copy-start(f32[32,448]{1,0:T(8,128)S(1)} %fusion.2) | copy-start | bytes 172036
  103.2 13.2 %all-to-all-start.3 = ((f32[8,8,448]{2,1,0:T(8,128)}), f32[8,8,448]{2,1,0:T(8,128)S(1)}, u32[]{:S(2)}, u32[]{:S(2)}) async-start(f32[8,8,448]{2,1,0:T(8,128)} %broadcast_in_dim.10), calls=%async_computation.3 | async-start | bytes 262144 | tf_op jit(solution)/shard_map/all_to_all | solution.py:31
  107.0 5.5 %collective-permute-start.11 = (bf16[48,1024]{1,0:T(8,128)(2,1)}, bf16[48,1024]{1,0:T(8,128)(2,1)S(1)}, u32[]{:S(2)}, u32[]{:S(2)}) collective-permute-start(bf16[48,1024]{1,0:T(8,128)(2,1)} %copy-done.6), channel_id=1, source_target_pairs={{0,8},{8,0},{1,9},{9,1},{2,10},{10,2},{3,11},{11,3},{4,12},{12,4},... | collective-permute-start | bytes 294920 | tf_op jit(solution)/shard_map/ppermute | solution.py:27
  116.4 38.9 %all-to-all-start.5 = ((bf16[32,32,512]{2,1,0:T(8,128)(2,1)}), bf16[32,32,512]{2,1,0:T(8,128)(2,1)}, u32[]{:S(2)}, u32[]{:S(2)}) async-start(bf16[32,32,512]{2,1,0:T(8,128)(2,1)} %shard_map.113), calls=%async_computation.5 | async-start | bytes 2097152 | tf_op jit(solution)/shard_map/all_to_all | solution.py:227
  127.3 8.6 %collective-permute-start.7 = (bf16[32,3584]{1,0:T(8,128)(2,1)}, bf16[32,3584]{1,0:T(8,128)(2,1)}, u32[]{:S(2)}, u32[]{:S(2)}) collective-permute-start(bf16[32,3584]{1,0:T(8,128)(2,1)} %get-tuple-element.25), channel_id=1, source_target_pairs={{0,6},{2,4},{4,2},{6,0},{1,7},{3,5},{5,3},{7,1},{8,14},{10,12},{12... | collective-permute-start | bytes 688136 | tf_op jit(solution)/shard_map/ppermute | solution.py:218
  132.2 7.4 %collective-permute-start.9 = (bf16[32,3584]{1,0:T(8,128)(2,1)}, bf16[32,3584]{1,0:T(8,128)(2,1)}, u32[]{:S(2)}, u32[]{:S(2)}) collective-permute-start(bf16[32,3584]{1,0:T(8,128)(2,1)} %get-tuple-element.24), channel_id=1, source_target_pairs={{0,2},{2,0},{4,6},{6,4},{1,3},{3,1},{5,7},{7,5},{8,10},{10,8},{12,... | collective-permute-start | bytes 688136 | tf_op jit(solution)/shard_map/ppermute | solution.py:219
  139.5 3.6 %copy-start.11 = (bf16[4,64,256]{2,1,0:T(8,128)(2,1)S(1)}, bf16[4,64,256]{2,1,0:T(8,128)(2,1)}, u32[]{:S(2)}) copy-start(bf16[4,64,256]{2,1,0:T(8,128)(2,1)} %copy-done.10) | copy-start | bytes 393220
  141.9 1.3 copy-start.1
  143.8 8.1 %collective-permute-start.10 = (bf16[3584,128]{1,0:T(8,128)(2,1)S(1)}, bf16[3584,128]{1,0:T(8,128)(2,1)}, u32[]{:S(2)}, u32[]{:S(2)}) collective-permute-start(bf16[3584,128]{1,0:T(8,128)(2,1)S(1)} %convolution_convert_fusion.1), channel_id=1, source_target_pairs={{0,8},{8,0},{1,9},{9,1},{2,10},{10,2},{3,11},{11,3},{4,12},{12,4},... | collective-permute-start | bytes 2752520 | tf_op jit(solution)/shard_map/ppermute | solution.py:27
  155.3 34.7 %all-to-all-start.4 = ((bf16[32,120,128]{2,1,0:T(8,128)(2,1)}), bf16[32,120,128]{2,1,0:T(8,128)(2,1)S(1)}, u32[]{:S(2)}, u32[]{:S(2)}) async-start(bf16[32,120,128]{2,1,0:T(8,128)(2,1)} %pad_maximum_fusion), calls=%async_computation.4 | async-start | bytes 1966080 | tf_op jit(solution)/shard_map/all_to_all | solution.py:239
  167.4 9.4 %collective-permute-start.12 = (bf16[1024,448]{0,1:T(8,128)(2,1)}, bf16[1024,448]{0,1:T(8,128)(2,1)}, u32[]{:S(2)}, u32[]{:S(2)}) collective-permute-start(bf16[1024,448]{0,1:T(8,128)(2,1)} %copy.25), channel_id=1, source_target_pairs={{0,8},{8,0},{1,9},{9,1},{2,10},{10,2},{3,11},{11,3},{4,12},{12,4},... | collective-permute-start | bytes 2752520 | tf_op jit(solution)/shard_map/ppermute | solution.py:27
  190.2 7.1 %collective-permute-start.13 = (f32[56,128]{1,0:T(8,128)S(1)}, f32[56,128]{1,0:T(8,128)S(1)}, u32[]{:S(2)}, u32[]{:S(2)}) collective-permute-start(f32[56,128]{1,0:T(8,128)S(1)} %dynamic-slice_bitcast_fusion), channel_id=1, source_target_pairs={{0,8},{8,0},{1,9},{9,1},{2,10},{10,2},{3,11},{11,3},{4,12},{12,4},... | collective-permute-start | bytes 86024 | tf_op jit(solution)/shard_map/ppermute | solution.py:27
  (3 other events, 2.1 us)
